TPU v7x, 32 devices: a whole 2x2x4 slice. The times are simulated.
32 devices in a mesh: win: 8 (over z, y), lat: 4 (over x, core).
Axes of the slice: x: 2, y: 2, z: 4, core: 2. Of those that a mesh axis runs over, the one named last changes fastest.
Arguments:
- model_rhs: float32 [8, 3, 32, 1536], P('win', None, 'lat'), may hold values from -6 to 6
- obs_rhs: float32 [8, 3, 32, 1536], P('win', None, 'lat'), may hold values from -6 to 6
- model_var: float32 [8, 3, 32, 1536], P('win', None, 'lat'), may hold values from 0.3 to 3
- obs_var: float32 [8, 3, 32, 1536], P('win', None, 'lat'), may hold values from 0.3 to 3
- obs_weight: float32 [8, 3, 32, 1536], P('win', None, 'lat'), may hold values from 0.2 to 1.5
- depth: float32 [8, 32, 1536], P('win', 'lat'), may hold values from 0.5 to 1.5
Outputs:
- dual_model: float32 [8, 3, 32, 1536], P('win', None, 'lat')
- dual_obs: float32 [8, 3, 32, 1536], P('win', None, 'lat')
- increment: float32 [8, 3, 32, 1536], P('win', None, 'lat')
All inputs are finite; a program needn't handle non-finite values.
Results may differ from a plain program's by a relative error of at most 0.0001.
Values sent between devices are 32-bit elements; how exact they have to be, the bound alone decides.
No kernel may reach another device: no remote copies, remote signals or barrier semaphores. Data moves between devices by JAX's collectives and lax.ppermute only.
A program may use at most 64 MiB of HBM per device.

v0:
```python
import jax
import jax.numpy as jnp
from jax import lax
from jax.sharding import PartitionSpec as P

GRID_ROWS = 768
STEPS = 4
ITERS = 2


mass_rate = 0.5
press_rate = 0.5
spin_rate = 0.4


def extended(block, sides, width):
    for axis, dim in sides:
        count = lax.axis_size(axis)
        forward = [(i, i + 1) for i in range(count - 1)]
        backward = [(target, source) for source, target in forward]
        low = lax.ppermute(
            lax.slice_in_dim(block, block.shape[dim] - width, None, axis=dim), axis, forward
        )
        high = lax.ppermute(lax.slice_in_dim(block, 0, width, axis=dim), axis, backward)
        block = jnp.concatenate([low, block, high], axis=dim)
    return block


def shifted(value, axis, steps):
    count = lax.axis_size(axis)
    initial, last = (max(0, -steps), min(count, count - steps))
    return lax.ppermute(value, axis, [(source, source + steps) for source in range(initial, last)])


def along_lon(field):
    return 0.5 * (jnp.roll(field, -1, axis=-1) - jnp.roll(field, 1, axis=-1))


def lat_slopes(padded):
    return 0.5 * (padded[:, 2:] - padded[:, :-2])


def local_inner(left, right):
    return jnp.sum(left[0] * right[0]) + jnp.sum(left[1] * right[1]) + jnp.sum(left[2] * right[2])


def least_squares(beta, columns):
    count = len(columns)
    cosines, sines, upper_cols = ([], [], [])
    target = [beta]
    for index, (proj, tail) in enumerate(columns):
        column = list(proj)
        for prior in range(index):
            top = cosines[prior] * column[prior] + sines[prior] * column[prior + 1]
            bottom = -sines[prior] * column[prior] + cosines[prior] * column[prior + 1]
            column[prior] = top
            column[prior + 1] = bottom
        radius = jnp.sqrt(column[index] * column[index] + tail * tail)
        cosine = column[index] / radius
        sine = tail / radius
        column[index] = radius
        cosines.append(cosine)
        sines.append(sine)
        target.append(-sine * target[index])
        target[index] = cosine * target[index]
        upper_cols.append(column)
    coeffs = [None] * count
    for row in reversed(range(count)):
        accum = target[row]
        for later in range(row + 1, count):
            accum = accum - upper_cols[later][row] * coeffs[later]
        coeffs[row] = accum / upper_cols[row][row]
    return coeffs


def joint_sweep(state, depth_fwd, adjoint, depth_adj, spin):
    height, east, north = (state[0], state[1], state[2])
    adj_height, adj_east, adj_north = (adjoint[0], adjoint[1], adjoint[2])
    for step in range(STEPS):
        edges = extended(jnp.stack([depth_fwd * north, adj_north]), (("lat", 1),), 1)
        slopes = lat_slopes(edges)
        height = height - mass_rate * (along_lon(depth_fwd * east) + slopes[0])
        adj_mid = adj_east - mass_rate * spin * adj_north
        adj_rest = adj_height + press_rate * (slopes[1] + along_lon(adj_mid))
        edges = extended(jnp.stack([height, adj_rest]), (("lat", 1),), 1)
        slopes = lat_slopes(edges)
        east = east + mass_rate * spin * north - press_rate * along_lon(height)
        north = north - mass_rate * spin * east - press_rate * slopes[0]
        adj_height = adj_rest
        adj_new_north = adj_north + mass_rate * spin * adj_mid + mass_rate * depth_adj * slopes[1]
        adj_east = adj_mid + mass_rate * depth_adj * along_lon(adj_rest)
        adj_north = adj_new_north
    return (jnp.stack([height, east, north]), jnp.stack([adj_height, adj_east, adj_north]))


def body(model_rhs, obs_rhs, model_var, obs_var, obs_weight, depth):
    rows = model_rhs.shape[2]
    total_rows = rows * lax.axis_size("lat")
    offset = (GRID_ROWS - total_rows) // 2
    global_rows = lax.axis_index("lat") * rows + jnp.arange(rows, dtype=jnp.int32)
    latitude = -jnp.pi / 2 + (global_rows.astype(jnp.float32) + offset + 0.5) * (jnp.pi / GRID_ROWS)
    spin = (spin_rate * jnp.sin(latitude))[:, None]
    own_depth = depth[0]
    first = (model_rhs, obs_rhs, jnp.zeros_like(model_rhs))
    beta = jnp.sqrt(lax.psum(local_inner(first, first), ("win", "lat")))
    basis = [tuple((part / beta for part in first))]
    columns = []
    for index in range(ITERS):
        dual_model, dual_obs, increment = basis[index]
        upcoming = shifted(dual_model, "win", -1)
        own_end, back = joint_sweep(increment[0], own_depth, upcoming[0], own_depth, spin)
        carried = shifted(own_end[None], "win", 1)[0]
        image = (
            model_var * dual_model + increment - carried[None],
            obs_var * dual_obs + obs_weight * increment,
            dual_model - back[None] + obs_weight * dual_obs,
        )
        partials = jnp.stack([local_inner(image, vec) for vec in basis])
        totals = lax.psum(partials, ("win", "lat"))
        proj = [totals[slot] for slot in range(len(basis))]
        for factor, vec in zip(proj, basis):
            image = tuple((a - factor * b for a, b in zip(image, vec)))
        tail = jnp.sqrt(lax.psum(local_inner(image, image), ("win", "lat")))
        columns.append((proj, tail))
        if index + 1 < ITERS:
            basis.append(tuple((part / tail for part in image)))
    coeffs = least_squares(beta, columns)
    result = [jnp.zeros_like(model_rhs) for part in range(3)]
    for factor, vec in zip(coeffs, basis):
        result = [accum + factor * part for accum, part in zip(result, vec)]
    return (result[0], result[1], result[2])


def solution(mesh):
    in_specs = (
        P("win", None, "lat", None),
        P("win", None, "lat", None),
        P("win", None, "lat", None),
        P("win", None, "lat", None),
        P("win", None, "lat", None),
        P("win", "lat", None),
    )
    out_specs = (
        P("win", None, "lat", None),
        P("win", None, "lat", None),
        P("win", None, "lat", None),
    )
    return jax.shard_map(body, mesh=mesh, in_specs=in_specs, out_specs=out_specs, check_vma=False)
```

profile of v0, /device:TPU:0, one launch (start us, length us, event | category | flops | bytes accessed | tf_op | source)
XLA Modules:
  0.0 384.8 jit_solution(5219906573985783762)
XLA Ops:
  0.6 1.7 multiply_reduce_fusion.15
  3.6 42.0 %psum.35 = f32[]{:T(128)} all-reduce(f32[]{:T(128)S(6)} %add.562), channel_id=1, replica_groups=mesh['win'=8,'lat'=4] {'win','lat'}, use_global_device_ids=true, to_apply=%region_2.0 | all-reduce | flops 1 | bytes 8 | tf_op jit(solution)/shard_map/psum | solution.py:105
  48.0 5.8 %collective-permute-done = f32[1,3,8,1536]{3,2,1,0:T(8,128)S(1)} collective-permute-done((f32[1,3,8,1536]{3,2,1,0:T(8,128)S(1)}, f32[1,3,8,1536]{3,2,1,0:T(8,128)S(1)}, u32[]{:S(2)}, u32[]{:S(2)}) %collective-permute-start) | collective-permute-done | bytes 147488 | tf_op jit(solution)/shard_map/ppermute | solution.py:32
  55.2 3.0 collective-permute-start.2
  59.5 1.3 collective-permute-start.3
  60.8 4.0 %collective-permute-start.4 = (f32[2,1,1536]{2,1,0:T(1,128)S(1)}, f32[2,1,1536]{2,1,0:T(1,128)S(1)}, u32[]{:S(2)}, u32[]{:S(2)}) collective-permute-start(f32[2,1,1536]{2,1,0:T(1,128)S(1)} %get-tuple-element.130), channel_id=1, source_target_pairs={{0,1},{1,2},{2,3},{4,5},{5,6},{6,7},{8,9},{9,10},{10,11},{12,13},{... | collective-permute-start | bytes 36872 | tf_op jit(solution)/shard_map/ppermute | solution.py:21
  67.3 4.8 %collective-permute-start.6 = (f32[2,1,1536]{2,1,0:T(1,128)S(1)}, f32[2,1,1536]{2,1,0:T(1,128)S(1)}, u32[]{:S(2)}, u32[]{:S(2)}) collective-permute-start(f32[2,1,1536]{2,1,0:T(1,128)S(1)} %get-tuple-element.126), channel_id=1, source_target_pairs={{0,1},{1,2},{2,3},{4,5},{5,6},{6,7},{8,9},{9,10},{10,11},{12,13},{... | collective-permute-start | bytes 36872 | tf_op jit(solution)/shard_map/ppermute | solution.py:21
  74.7 4.8 %collective-permute-start.8 = (f32[2,1,1536]{2,1,0:T(1,128)S(1)}, f32[2,1,1536]{2,1,0:T(1,128)S(1)}, u32[]{:S(2)}, u32[]{:S(2)}) collective-permute-start(f32[2,1,1536]{2,1,0:T(1,128)S(1)} %get-tuple-element.122), channel_id=1, source_target_pairs={{0,1},{1,2},{2,3},{4,5},{5,6},{6,7},{8,9},{9,10},{10,11},{12,13},{... | collective-permute-start | bytes 36872 | tf_op jit(solution)/shard_map/ppermute | solution.py:21
  81.0 4.2 %collective-permute-start.10 = (f32[2,1,1536]{2,1,0:T(1,128)S(1)}, f32[2,1,1536]{2,1,0:T(1,128)S(1)}, u32[]{:S(2)}, u32[]{:S(2)}) collective-permute-start(f32[2,1,1536]{2,1,0:T(1,128)S(1)} %get-tuple-element.118), channel_id=1, source_target_pairs={{0,1},{1,2},{2,3},{4,5},{5,6},{6,7},{8,9},{9,10},{10,11},{12,13},{... | collective-permute-start | bytes 36872 | tf_op jit(solution)/shard_map/ppermute | solution.py:21
  86.6 3.4 collective-permute-done.9
  91.9 5.0 %collective-permute-start.12 = (f32[2,1,1536]{2,1,0:T(1,128)S(1)}, f32[2,1,1536]{2,1,0:T(1,128)S(1)}, u32[]{:S(2)}, u32[]{:S(2)}) collective-permute-start(f32[2,1,1536]{2,1,0:T(1,128)S(1)} %get-tuple-element.114), channel_id=1, source_target_pairs={{0,1},{1,2},{2,3},{4,5},{5,6},{6,7},{8,9},{9,10},{10,11},{12,13},{... | collective-permute-start | bytes 36872 | tf_op jit(solution)/shard_map/ppermute | solution.py:21
  99.4 4.3 %collective-permute-start.14 = (f32[2,1,1536]{2,1,0:T(1,128)S(1)}, f32[2,1,1536]{2,1,0:T(1,128)S(1)}, u32[]{:S(2)}, u32[]{:S(2)}) collective-permute-start(f32[2,1,1536]{2,1,0:T(1,128)S(1)} %get-tuple-element.110), channel_id=1, source_target_pairs={{0,1},{1,2},{2,3},{4,5},{5,6},{6,7},{8,9},{9,10},{10,11},{12,13},{... | collective-permute-start | bytes 36872 | tf_op jit(solution)/shard_map/ppermute | solution.py:21
  106.4 4.8 %collective-permute-start.16 = (f32[2,1,1536]{2,1,0:T(1,128)S(1)}, f32[2,1,1536]{2,1,0:T(1,128)S(1)}, u32[]{:S(2)}, u32[]{:S(2)}) collective-permute-start(f32[2,1,1536]{2,1,0:T(1,128)S(1)} %get-tuple-element.106), channel_id=1, source_target_pairs={{0,1},{1,2},{2,3},{4,5},{5,6},{6,7},{8,9},{9,10},{10,11},{12,13},{... | collective-permute-start | bytes 36872 | tf_op jit(solution)/shard_map/ppermute | solution.py:21
  112.2 3.7 collective-permute-start.17
  115.9 2.8 collective-permute-done.17
  121.4 44.0 %psum.36 = f32[]{:T(128)} all-reduce(f32[]{:T(128)S(6)} %add.623), channel_id=1, replica_groups=mesh['win'=8,'lat'=4] {'win','lat'}, use_global_device_ids=true, to_apply=%region_6.7 | all-reduce | flops 1 | bytes 8 | tf_op jit(solution)/shard_map/psum | solution.py:119
  171.1 39.9 %psum.37 = f32[]{:T(128)} all-reduce(f32[]{:T(128)S(6)} %add.625), channel_id=1, replica_groups=mesh['win'=8,'lat'=4] {'win','lat'}, use_global_device_ids=true, to_apply=%region_10.11 | all-reduce | flops 1 | bytes 8 | tf_op jit(solution)/shard_map/psum | solution.py:123
  213.9 6.0 %collective-permute-done.18 = f32[1,3,8,1536]{3,2,1,0:T(8,128)S(1)} collective-permute-done((f32[1,3,8,1536]{3,2,1,0:T(8,128)S(1)}, f32[1,3,8,1536]{3,2,1,0:T(8,128)S(1)}, u32[]{:S(2)}, u32[]{:S(2)}) %collective-permute-start.18) | collective-permute-done | bytes 147488 | tf_op jit(solution)/shard_map/ppermute | solution.py:32
  221.2 3.0 collective-permute-start.20
  226.8 4.0 %collective-permute-start.22 = (f32[2,1,1536]{2,1,0:T(1,128)S(1)}, f32[2,1,1536]{2,1,0:T(1,128)S(1)}, u32[]{:S(2)}, u32[]{:S(2)}) collective-permute-start(f32[2,1,1536]{2,1,0:T(1,128)S(1)} %get-tuple-element.98), channel_id=1, source_target_pairs={{0,1},{1,2},{2,3},{4,5},{5,6},{6,7},{8,9},{9,10},{10,11},{12,13},{... | collective-permute-start | bytes 36872 | tf_op jit(solution)/shard_map/ppermute | solution.py:21
  233.4 4.8 %collective-permute-start.24 = (f32[2,1,1536]{2,1,0:T(1,128)S(1)}, f32[2,1,1536]{2,1,0:T(1,128)S(1)}, u32[]{:S(2)}, u32[]{:S(2)}) collective-permute-start(f32[2,1,1536]{2,1,0:T(1,128)S(1)} %get-tuple-element.94), channel_id=1, source_target_pairs={{0,1},{1,2},{2,3},{4,5},{5,6},{6,7},{8,9},{9,10},{10,11},{12,13},{... | collective-permute-start | bytes 36872 | tf_op jit(solution)/shard_map/ppermute | solution.py:21
  240.8 4.8 %collective-permute-start.26 = (f32[2,1,1536]{2,1,0:T(1,128)S(1)}, f32[2,1,1536]{2,1,0:T(1,128)S(1)}, u32[]{:S(2)}, u32[]{:S(2)}) collective-permute-start(f32[2,1,1536]{2,1,0:T(1,128)S(1)} %get-tuple-element.90), channel_id=1, source_target_pairs={{0,1},{1,2},{2,3},{4,5},{5,6},{6,7},{8,9},{9,10},{10,11},{12,13},{... | collective-permute-start | bytes 36872 | tf_op jit(solution)/shard_map/ppermute | solution.py:21
  248.2 4.8 %collective-permute-start.28 = (f32[2,1,1536]{2,1,0:T(1,128)S(1)}, f32[2,1,1536]{2,1,0:T(1,128)S(1)}, u32[]{:S(2)}, u32[]{:S(2)}) collective-permute-start(f32[2,1,1536]{2,1,0:T(1,128)S(1)} %get-tuple-element.86), channel_id=1, source_target_pairs={{0,1},{1,2},{2,3},{4,5},{5,6},{6,7},{8,9},{9,10},{10,11},{12,13},{... | collective-permute-start | bytes 36872 | tf_op jit(solution)/shard_map/ppermute | solution.py:21
  255.8 4.8 %collective-permute-start.30 = (f32[2,1,1536]{2,1,0:T(1,128)S(1)}, f32[2,1,1536]{2,1,0:T(1,128)S(1)}, u32[]{:S(2)}, u32[]{:S(2)}) collective-permute-start(f32[2,1,1536]{2,1,0:T(1,128)S(1)} %get-tuple-element.82), channel_id=1, source_target_pairs={{0,1},{1,2},{2,3},{4,5},{5,6},{6,7},{8,9},{9,10},{10,11},{12,13},{... | collective-permute-start | bytes 36872 | tf_op jit(solution)/shard_map/ppermute | solution.py:21
  263.1 4.8 %collective-permute-start.32 = (f32[2,1,1536]{2,1,0:T(1,128)S(1)}, f32[2,1,1536]{2,1,0:T(1,128)S(1)}, u32[]{:S(2)}, u32[]{:S(2)}) collective-permute-start(f32[2,1,1536]{2,1,0:T(1,128)S(1)} %get-tuple-element.78), channel_id=1, source_target_pairs={{0,1},{1,2},{2,3},{4,5},{5,6},{6,7},{8,9},{9,10},{10,11},{12,13},{... | collective-permute-start | bytes 36872 | tf_op jit(solution)/shard_map/ppermute | solution.py:21
  270.6 4.8 %collective-permute-start.34 = (f32[2,1,1536]{2,1,0:T(1,128)S(1)}, f32[2,1,1536]{2,1,0:T(1,128)S(1)}, u32[]{:S(2)}, u32[]{:S(2)}) collective-permute-start(f32[2,1,1536]{2,1,0:T(1,128)S(1)} %get-tuple-element.74), channel_id=1, source_target_pairs={{0,1},{1,2},{2,3},{4,5},{5,6},{6,7},{8,9},{9,10},{10,11},{12,13},{... | collective-permute-start | bytes 36872 | tf_op jit(solution)/shard_map/ppermute | solution.py:21
  276.4 3.9 %collective-permute-start.35 = (f32[1,3,8,1536]{3,2,1,0:T(8,128)S(1)}, f32[1,3,8,1536]{3,2,1,0:T(8,128)S(1)}, u32[]{:S(2)}, u32[]{:S(2)}) collective-permute-start(f32[1,3,8,1536]{3,2,1,0:T(8,128)S(1)} %maximum_bitcast_fusion.2), channel_id=1, source_target_pairs={{0,4},{4,8},{8,12},{12,16},{16,20},{20,24},{24,28},{1,5},{5,9},{9,... | collective-permute-start | bytes 442376 | tf_op jit(solution)/shard_map/ppermute | solution.py:32
  287.7 43.9 %psum.38 = f32[2]{0:T(128)S(1)} all-reduce(f32[2]{0:T(128)S(1)} %pad_maximum_fusion.96), channel_id=1, replica_groups=mesh['win'=8,'lat'=4] {'win','lat'}, use_global_device_ids=true, to_apply=%region_17.18 | all-reduce | flops 2 | bytes 16 | tf_op jit(solution)/shard_map/psum | solution.py:119
  334.8 1.9 multiply_reduce_fusion.1
  336.7 1.9 multiply_reduce_fusion.2
  338.7 1.3 multiply_reduce_fusion
  342.4 39.4 %psum.39 = f32[]{:T(128)} all-reduce(f32[]{:T(128)S(6)} %add.689), channel_id=1, replica_groups=mesh['win'=8,'lat'=4] {'win','lat'}, use_global_device_ids=true, to_apply=%region_21.22 | all-reduce | flops 1 | bytes 8 | tf_op jit(solution)/shard_map/psum | solution.py:123
  (217 shorter events, 50.6 us)
Async XLA Ops:
  46.4 7.5 %collective-permute-start = (f32[1,3,8,1536]{3,2,1,0:T(8,128)S(1)}, f32[1,3,8,1536]{3,2,1,0:T(8,128)S(1)}, u32[]{:S(2)}, u32[]{:S(2)}) collective-permute-start(f32[1,3,8,1536]{3,2,1,0:T(8,128)S(1)} %broadcast_divide_fusion.3), channel_id=1, source_target_pairs={{4,0},{8,4},{12,8},{16,12},{20,16},{24,20},{28,24},{5,1},{9,5},{13... | collective-permute-start | bytes 442376 | tf_op jit(solution)/shard_map/ppermute | solution.py:32
  59.5 5.4 %collective-permute-start.3 = (f32[2,1,1536]{2,1,0:T(1,128)S(1)}, f32[2,1,1536]{2,1,0:T(1,128)S(1)}, u32[]{:S(2)}, u32[]{:S(2)}) collective-permute-start(f32[2,1,1536]{2,1,0:T(1,128)S(1)} %get-tuple-element.129), channel_id=1, source_target_pairs={{1,0},{2,1},{3,2},{5,4},{6,5},{7,6},{9,8},{10,9},{11,10},{13,12},{... | collective-permute-start | bytes 36872 | tf_op jit(solution)/shard_map/ppermute | solution.py:24
  60.8 4.8 %collective-permute-start.4 = (f32[2,1,1536]{2,1,0:T(1,128)S(1)}, f32[2,1,1536]{2,1,0:T(1,128)S(1)}, u32[]{:S(2)}, u32[]{:S(2)}) collective-permute-start(f32[2,1,1536]{2,1,0:T(1,128)S(1)} %get-tuple-element.130), channel_id=1, source_target_pairs={{0,1},{1,2},{2,3},{4,5},{5,6},{6,7},{8,9},{9,10},{10,11},{12,13},{... | collective-permute-start | bytes 36872 | tf_op jit(solution)/shard_map/ppermute | solution.py:21
  66.0 6.3 %collective-permute-start.5 = (f32[2,1,1536]{2,1,0:T(1,128)S(1)}, f32[2,1,1536]{2,1,0:T(1,128)S(1)}, u32[]{:S(2)}, u32[]{:S(2)}) collective-permute-start(f32[2,1,1536]{2,1,0:T(1,128)S(1)} %get-tuple-element.125), channel_id=1, source_target_pairs={{1,0},{2,1},{3,2},{5,4},{6,5},{7,6},{9,8},{10,9},{11,10},{13,12},{... | collective-permute-start | bytes 36872 | tf_op jit(solution)/shard_map/ppermute | solution.py:24
  67.3 5.6 %collective-permute-start.6 = (f32[2,1,1536]{2,1,0:T(1,128)S(1)}, f32[2,1,1536]{2,1,0:T(1,128)S(1)}, u32[]{:S(2)}, u32[]{:S(2)}) collective-permute-start(f32[2,1,1536]{2,1,0:T(1,128)S(1)} %get-tuple-element.126), channel_id=1, source_target_pairs={{0,1},{1,2},{2,3},{4,5},{5,6},{6,7},{8,9},{9,10},{10,11},{12,13},{... | collective-permute-start | bytes 36872 | tf_op jit(solution)/shard_map/ppermute | solution.py:21
  73.4 6.3 %collective-permute-start.7 = (f32[2,1,1536]{2,1,0:T(1,128)S(1)}, f32[2,1,1536]{2,1,0:T(1,128)S(1)}, u32[]{:S(2)}, u32[]{:S(2)}) collective-permute-start(f32[2,1,1536]{2,1,0:T(1,128)S(1)} %get-tuple-element.121), channel_id=1, source_target_pairs={{1,0},{2,1},{3,2},{5,4},{6,5},{7,6},{9,8},{10,9},{11,10},{13,12},{... | collective-permute-start | bytes 36872 | tf_op jit(solution)/shard_map/ppermute | solution.py:24
  74.7 5.6 %collective-permute-start.8 = (f32[2,1,1536]{2,1,0:T(1,128)S(1)}, f32[2,1,1536]{2,1,0:T(1,128)S(1)}, u32[]{:S(2)}, u32[]{:S(2)}) collective-permute-start(f32[2,1,1536]{2,1,0:T(1,128)S(1)} %get-tuple-element.122), channel_id=1, source_target_pairs={{0,1},{1,2},{2,3},{4,5},{5,6},{6,7},{8,9},{9,10},{10,11},{12,13},{... | collective-permute-start | bytes 36872 | tf_op jit(solution)/shard_map/ppermute | solution.py:21
  81.0 5.7 %collective-permute-start.10 = (f32[2,1,1536]{2,1,0:T(1,128)S(1)}, f32[2,1,1536]{2,1,0:T(1,128)S(1)}, u32[]{:S(2)}, u32[]{:S(2)}) collective-permute-start(f32[2,1,1536]{2,1,0:T(1,128)S(1)} %get-tuple-element.118), channel_id=1, source_target_pairs={{0,1},{1,2},{2,3},{4,5},{5,6},{6,7},{8,9},{9,10},{10,11},{12,13},{... | collective-permute-start | bytes 36872 | tf_op jit(solution)/shard_map/ppermute | solution.py:21
  85.2 4.9 %collective-permute-start.9 = (f32[2,1,1536]{2,1,0:T(1,128)S(1)}, f32[2,1,1536]{2,1,0:T(1,128)S(1)}, u32[]{:S(2)}, u32[]{:S(2)}) collective-permute-start(f32[2,1,1536]{2,1,0:T(1,128)S(1)} %get-tuple-element.117), channel_id=1, source_target_pairs={{1,0},{2,1},{3,2},{5,4},{6,5},{7,6},{9,8},{10,9},{11,10},{13,12},{... | collective-permute-start | bytes 36872 | tf_op jit(solution)/shard_map/ppermute | solution.py:24
  90.6 6.5 %collective-permute-start.11 = (f32[2,1,1536]{2,1,0:T(1,128)S(1)}, f32[2,1,1536]{2,1,0:T(1,128)S(1)}, u32[]{:S(2)}, u32[]{:S(2)}) collective-permute-start(f32[2,1,1536]{2,1,0:T(1,128)S(1)} %get-tuple-element.113), channel_id=1, source_target_pairs={{1,0},{2,1},{3,2},{5,4},{6,5},{7,6},{9,8},{10,9},{11,10},{13,12},{... | collective-permute-start | bytes 36872 | tf_op jit(solution)/shard_map/ppermute | solution.py:24
  91.9 5.8 %collective-permute-start.12 = (f32[2,1,1536]{2,1,0:T(1,128)S(1)}, f32[2,1,1536]{2,1,0:T(1,128)S(1)}, u32[]{:S(2)}, u32[]{:S(2)}) collective-permute-start(f32[2,1,1536]{2,1,0:T(1,128)S(1)} %get-tuple-element.114), channel_id=1, source_target_pairs={{0,1},{1,2},{2,3},{4,5},{5,6},{6,7},{8,9},{9,10},{10,11},{12,13},{... | collective-permute-start | bytes 36872 | tf_op jit(solution)/shard_map/ppermute | solution.py:21
  98.1 5.6 %collective-permute-start.13 = (f32[2,1,1536]{2,1,0:T(1,128)S(1)}, f32[2,1,1536]{2,1,0:T(1,128)S(1)}, u32[]{:S(2)}, u32[]{:S(2)}) collective-permute-start(f32[2,1,1536]{2,1,0:T(1,128)S(1)} %get-tuple-element.109), channel_id=1, source_target_pairs={{1,0},{2,1},{3,2},{5,4},{6,5},{7,6},{9,8},{10,9},{11,10},{13,12},{... | collective-permute-start | bytes 36872 | tf_op jit(solution)/shard_map/ppermute | solution.py:24
  99.4 5.1 %collective-permute-start.14 = (f32[2,1,1536]{2,1,0:T(1,128)S(1)}, f32[2,1,1536]{2,1,0:T(1,128)S(1)}, u32[]{:S(2)}, u32[]{:S(2)}) collective-permute-start(f32[2,1,1536]{2,1,0:T(1,128)S(1)} %get-tuple-element.110), channel_id=1, source_target_pairs={{0,1},{1,2},{2,3},{4,5},{5,6},{6,7},{8,9},{9,10},{10,11},{12,13},{... | collective-permute-start | bytes 36872 | tf_op jit(solution)/shard_map/ppermute | solution.py:21
  105.1 6.3 %collective-permute-start.15 = (f32[2,1,1536]{2,1,0:T(1,128)S(1)}, f32[2,1,1536]{2,1,0:T(1,128)S(1)}, u32[]{:S(2)}, u32[]{:S(2)}) collective-permute-start(f32[2,1,1536]{2,1,0:T(1,128)S(1)} %get-tuple-element.105), channel_id=1, source_target_pairs={{1,0},{2,1},{3,2},{5,4},{6,5},{7,6},{9,8},{10,9},{11,10},{13,12},{... | collective-permute-start | bytes 36872 | tf_op jit(solution)/shard_map/ppermute | solution.py:24
  106.4 5.6 %collective-permute-start.16 = (f32[2,1,1536]{2,1,0:T(1,128)S(1)}, f32[2,1,1536]{2,1,0:T(1,128)S(1)}, u32[]{:S(2)}, u32[]{:S(2)}) collective-permute-start(f32[2,1,1536]{2,1,0:T(1,128)S(1)} %get-tuple-element.106), channel_id=1, source_target_pairs={{0,1},{1,2},{2,3},{4,5},{5,6},{6,7},{8,9},{9,10},{10,11},{12,13},{... | collective-permute-start | bytes 36872 | tf_op jit(solution)/shard_map/ppermute | solution.py:21
  112.2 6.5 %collective-permute-start.17 = (f32[1,3,8,1536]{3,2,1,0:T(8,128)S(1)}, f32[1,3,8,1536]{3,2,1,0:T(8,128)S(1)}, u32[]{:S(2)}, u32[]{:S(2)}) collective-permute-start(f32[1,3,8,1536]{3,2,1,0:T(8,128)S(1)} %maximum_bitcast_fusion), channel_id=1, source_target_pairs={{0,4},{4,8},{8,12},{12,16},{16,20},{20,24},{24,28},{1,5},{5,9},{9,... | collective-permute-start | bytes 442376 | tf_op jit(solution)/shard_map/ppermute | solution.py:32
  212.4 7.5 %collective-permute-start.18 = (f32[1,3,8,1536]{3,2,1,0:T(8,128)S(1)}, f32[1,3,8,1536]{3,2,1,0:T(8,128)S(1)}, u32[]{:S(2)}, u32[]{:S(2)}) collective-permute-start(f32[1,3,8,1536]{3,2,1,0:T(8,128)S(1)} %broadcast_divide_fusion.1), channel_id=1, source_target_pairs={{4,0},{8,4},{12,8},{16,12},{20,16},{24,20},{28,24},{5,1},{9,5},{13... | collective-permute-start | bytes 442376 | tf_op jit(solution)/shard_map/ppermute | solution.py:32
  225.5 5.4 %collective-permute-start.21 = (f32[2,1,1536]{2,1,0:T(1,128)S(1)}, f32[2,1,1536]{2,1,0:T(1,128)S(1)}, u32[]{:S(2)}, u32[]{:S(2)}) collective-permute-start(f32[2,1,1536]{2,1,0:T(1,128)S(1)} %get-tuple-element.97), channel_id=1, source_target_pairs={{1,0},{2,1},{3,2},{5,4},{6,5},{7,6},{9,8},{10,9},{11,10},{13,12},{... | collective-permute-start | bytes 36872 | tf_op jit(solution)/shard_map/ppermute | solution.py:24
  226.8 4.8 %collective-permute-start.22 = (f32[2,1,1536]{2,1,0:T(1,128)S(1)}, f32[2,1,1536]{2,1,0:T(1,128)S(1)}, u32[]{:S(2)}, u32[]{:S(2)}) collective-permute-start(f32[2,1,1536]{2,1,0:T(1,128)S(1)} %get-tuple-element.98), channel_id=1, source_target_pairs={{0,1},{1,2},{2,3},{4,5},{5,6},{6,7},{8,9},{9,10},{10,11},{12,13},{... | collective-permute-start | bytes 36872 | tf_op jit(solution)/shard_map/ppermute | solution.py:21
  232.1 6.3 %collective-permute-start.23 = (f32[2,1,1536]{2,1,0:T(1,128)S(1)}, f32[2,1,1536]{2,1,0:T(1,128)S(1)}, u32[]{:S(2)}, u32[]{:S(2)}) collective-permute-start(f32[2,1,1536]{2,1,0:T(1,128)S(1)} %get-tuple-element.93), channel_id=1, source_target_pairs={{1,0},{2,1},{3,2},{5,4},{6,5},{7,6},{9,8},{10,9},{11,10},{13,12},{... | collective-permute-start | bytes 36872 | tf_op jit(solution)/shard_map/ppermute | solution.py:24
  233.4 5.6 %collective-permute-start.24 = (f32[2,1,1536]{2,1,0:T(1,128)S(1)}, f32[2,1,1536]{2,1,0:T(1,128)S(1)}, u32[]{:S(2)}, u32[]{:S(2)}) collective-permute-start(f32[2,1,1536]{2,1,0:T(1,128)S(1)} %get-tuple-element.94), channel_id=1, source_target_pairs={{0,1},{1,2},{2,3},{4,5},{5,6},{6,7},{8,9},{9,10},{10,11},{12,13},{... | collective-permute-start | bytes 36872 | tf_op jit(solution)/shard_map/ppermute | solution.py:21
  239.5 6.3 %collective-permute-start.25 = (f32[2,1,1536]{2,1,0:T(1,128)S(1)}, f32[2,1,1536]{2,1,0:T(1,128)S(1)}, u32[]{:S(2)}, u32[]{:S(2)}) collective-permute-start(f32[2,1,1536]{2,1,0:T(1,128)S(1)} %get-tuple-element.89), channel_id=1, source_target_pairs={{1,0},{2,1},{3,2},{5,4},{6,5},{7,6},{9,8},{10,9},{11,10},{13,12},{... | collective-permute-start | bytes 36872 | tf_op jit(solution)/shard_map/ppermute | solution.py:24
  240.8 5.6 %collective-permute-start.26 = (f32[2,1,1536]{2,1,0:T(1,128)S(1)}, f32[2,1,1536]{2,1,0:T(1,128)S(1)}, u32[]{:S(2)}, u32[]{:S(2)}) collective-permute-start(f32[2,1,1536]{2,1,0:T(1,128)S(1)} %get-tuple-element.90), channel_id=1, source_target_pairs={{0,1},{1,2},{2,3},{4,5},{5,6},{6,7},{8,9},{9,10},{10,11},{12,13},{... | collective-permute-start | bytes 36872 | tf_op jit(solution)/shard_map/ppermute | solution.py:21
  246.9 6.3 %collective-permute-start.27 = (f32[2,1,1536]{2,1,0:T(1,128)S(1)}, f32[2,1,1536]{2,1,0:T(1,128)S(1)}, u32[]{:S(2)}, u32[]{:S(2)}) collective-permute-start(f32[2,1,1536]{2,1,0:T(1,128)S(1)} %get-tuple-element.85), channel_id=1, source_target_pairs={{1,0},{2,1},{3,2},{5,4},{6,5},{7,6},{9,8},{10,9},{11,10},{13,12},{... | collective-permute-start | bytes 36872 | tf_op jit(solution)/shard_map/ppermute | solution.py:24
  248.2 5.6 %collective-permute-start.28 = (f32[2,1,1536]{2,1,0:T(1,128)S(1)}, f32[2,1,1536]{2,1,0:T(1,128)S(1)}, u32[]{:S(2)}, u32[]{:S(2)}) collective-permute-start(f32[2,1,1536]{2,1,0:T(1,128)S(1)} %get-tuple-element.86), channel_id=1, source_target_pairs={{0,1},{1,2},{2,3},{4,5},{5,6},{6,7},{8,9},{9,10},{10,11},{12,13},{... | collective-permute-start | bytes 36872 | tf_op jit(solution)/shard_map/ppermute | solution.py:21
  254.5 6.4 %collective-permute-start.29 = (f32[2,1,1536]{2,1,0:T(1,128)S(1)}, f32[2,1,1536]{2,1,0:T(1,128)S(1)}, u32[]{:S(2)}, u32[]{:S(2)}) collective-permute-start(f32[2,1,1536]{2,1,0:T(1,128)S(1)} %get-tuple-element.81), channel_id=1, source_target_pairs={{1,0},{2,1},{3,2},{5,4},{6,5},{7,6},{9,8},{10,9},{11,10},{13,12},{... | collective-permute-start | bytes 36872 | tf_op jit(solution)/shard_map/ppermute | solution.py:24
  255.8 5.6 %collective-permute-start.30 = (f32[2,1,1536]{2,1,0:T(1,128)S(1)}, f32[2,1,1536]{2,1,0:T(1,128)S(1)}, u32[]{:S(2)}, u32[]{:S(2)}) collective-permute-start(f32[2,1,1536]{2,1,0:T(1,128)S(1)} %get-tuple-element.82), channel_id=1, source_target_pairs={{0,1},{1,2},{2,3},{4,5},{5,6},{6,7},{8,9},{9,10},{10,11},{12,13},{... | collective-permute-start | bytes 36872 | tf_op jit(solution)/shard_map/ppermute | solution.py:21
  261.8 6.2 %collective-permute-start.31 = (f32[2,1,1536]{2,1,0:T(1,128)S(1)}, f32[2,1,1536]{2,1,0:T(1,128)S(1)}, u32[]{:S(2)}, u32[]{:S(2)}) collective-permute-start(f32[2,1,1536]{2,1,0:T(1,128)S(1)} %get-tuple-element.77), channel_id=1, source_target_pairs={{1,0},{2,1},{3,2},{5,4},{6,5},{7,6},{9,8},{10,9},{11,10},{13,12},{... | collective-permute-start | bytes 36872 | tf_op jit(solution)/shard_map/ppermute | solution.py:24
  263.1 5.6 %collective-permute-start.32 = (f32[2,1,1536]{2,1,0:T(1,128)S(1)}, f32[2,1,1536]{2,1,0:T(1,128)S(1)}, u32[]{:S(2)}, u32[]{:S(2)}) collective-permute-start(f32[2,1,1536]{2,1,0:T(1,128)S(1)} %get-tuple-element.78), channel_id=1, source_target_pairs={{0,1},{1,2},{2,3},{4,5},{5,6},{6,7},{8,9},{9,10},{10,11},{12,13},{... | collective-permute-start | bytes 36872 | tf_op jit(solution)/shard_map/ppermute | solution.py:21
  269.3 6.3 %collective-permute-start.33 = (f32[2,1,1536]{2,1,0:T(1,128)S(1)}, f32[2,1,1536]{2,1,0:T(1,128)S(1)}, u32[]{:S(2)}, u32[]{:S(2)}) collective-permute-start(f32[2,1,1536]{2,1,0:T(1,128)S(1)} %get-tuple-element.73), channel_id=1, source_target_pairs={{1,0},{2,1},{3,2},{5,4},{6,5},{7,6},{9,8},{10,9},{11,10},{13,12},{... | collective-permute-start | bytes 36872 | tf_op jit(solution)/shard_map/ppermute | solution.py:24
  270.6 5.6 %collective-permute-start.34 = (f32[2,1,1536]{2,1,0:T(1,128)S(1)}, f32[2,1,1536]{2,1,0:T(1,128)S(1)}, u32[]{:S(2)}, u32[]{:S(2)}) collective-permute-start(f32[2,1,1536]{2,1,0:T(1,128)S(1)} %get-tuple-element.74), channel_id=1, source_target_pairs={{0,1},{1,2},{2,3},{4,5},{5,6},{6,7},{8,9},{9,10},{10,11},{12,13},{... | collective-permute-start | bytes 36872 | tf_op jit(solution)/shard_map/ppermute | solution.py:21
  276.4 6.7 %collective-permute-start.35 = (f32[1,3,8,1536]{3,2,1,0:T(8,128)S(1)}, f32[1,3,8,1536]{3,2,1,0:T(8,128)S(1)}, u32[]{:S(2)}, u32[]{:S(2)}) collective-permute-start(f32[1,3,8,1536]{3,2,1,0:T(8,128)S(1)} %maximum_bitcast_fusion.2), channel_id=1, source_target_pairs={{0,4},{4,8},{8,12},{12,16},{16,20},{20,24},{24,28},{1,5},{5,9},{9,... | collective-permute-start | bytes 442376 | tf_op jit(solution)/shard_map/ppermute | solution.py:32
  (10 other events, 90.4 us)
where the time goes:
time: 387 us; the launch traced here: 385 us
  blocking collectives  209 us (54%)
  starting transfers between devices  102 us (26%)
  waiting for transfers between devices  28.6 us (7%)
  between operations  20.4 us (5%)
  other arithmetic  19.5 us (5%)
  local copies, waits for them, and re-layouts  5.5 us (1%)
    psum x2, blocking collectives, body(): totals = lax.psum(partials, ('win', 'lat'))  87.9 us
    psum x2, blocking collectives, body(): tail = jnp.sqrt(lax.psum(local_inner(image, image), ('win', 'lat')))  79.3 us
    ppermute x16, starting transfers between devices, extended(): lax.ppermute(lax.slice_in_dim(block, block.shape[dim] - width, None, axis...  70.8 us
    psum x1, blocking collectives, body(): beta = jnp.sqrt(lax.psum(local_inner(first, first), ('win', 'lat')))  42 us
    ppermute x16, starting transfers between devices, extended(): lax.ppermute(lax.slice_in_dim(block, 0, width, axis=dim), axis, backward)  20.7 us
    ppermute x4, waiting for transfers between devices, shifted(): lax.ppermute(value, axis, [(source, source + steps) for source in range(i...  15.5 us
    ppermute x4, starting transfers between devices, shifted(): lax.ppermute(value, axis, [(source, source + steps) for source in range(i...  10.1 us
    ppermute x16, waiting for transfers between devices, extended(): lax.ppermute(lax.slice_in_dim(block, block.shape[dim] - width, None, axis...  9.59 us
  transfers between devices with their start and end apart: 36, of which 20 were waited for; matrix products, arithmetic and copies ran while one was open for 1% of the time, Pallas kernels for 0%

commit v1 on v0

v1 whole, which is shorter than its diff:
```python
import jax
import jax.numpy as jnp
from jax import lax
from jax.sharding import PartitionSpec as P

GRID_ROWS = 768
STEPS = 4
REACH = 2 * STEPS

mass_rate = 0.5
press_rate = 0.5
spin_rate = 0.4


def halo(block):
    count = lax.axis_size("lat")
    forward = [(i, i + 1) for i in range(count - 1)]
    backward = [(j, i) for i, j in forward]
    rows = block.shape[-2]
    low = lax.ppermute(block[..., rows - REACH:, :], "lat", forward)
    high = lax.ppermute(block[..., :REACH, :], "lat", backward)
    return jnp.concatenate([low, block, high], axis=-2)


def shifted(value, axis, steps):
    count = lax.axis_size(axis)
    initial, last = (max(0, -steps), min(count, count - steps))
    return lax.ppermute(value, axis, [(source, source + steps) for source in range(initial, last)])


def along_lon(field):
    return 0.5 * (jnp.roll(field, -1, axis=-1) - jnp.roll(field, 1, axis=-1))


def along_lat(field):
    padded = jnp.pad(field, [(0, 0)] * (field.ndim - 2) + [(1, 1), (0, 0)])
    return 0.5 * (padded[..., 2:, :] - padded[..., :-2, :])


def adjoint(adj_height, adj_east, adj_north, depth, spin, inside):
    for step in range(STEPS):
        adj_mid = adj_east - mass_rate * spin * adj_north
        adj_rest = inside * (adj_height + press_rate * (along_lat(adj_north) + along_lon(adj_mid)))
        adj_height = adj_rest
        adj_north = inside * (adj_north + mass_rate * spin * adj_mid + mass_rate * depth * along_lat(adj_rest))
        adj_east = adj_mid + mass_rate * depth * along_lon(adj_rest)
    return adj_height, adj_east, adj_north


def forward(height, east, north, depth, spin, inside):
    for step in range(STEPS):
        height = inside * (height - mass_rate * (along_lon(depth * east) + along_lat(depth * north)))
        east = east + mass_rate * spin * north - press_rate * along_lon(height)
        north = north - mass_rate * spin * east - press_rate * along_lat(height)
    return height, east, north


def total(value):
    return jnp.sum(value)


def body(model_rhs, obs_rhs, model_var, obs_var, obs_weight, depth):
    rows = model_rhs.shape[2]
    total_rows = rows * lax.axis_size("lat")
    offset = (GRID_ROWS - total_rows) // 2
    local_rows = lax.axis_index("lat") * rows - REACH + jnp.arange(rows + 2 * REACH, dtype=jnp.int32)
    latitude = -jnp.pi / 2 + (local_rows.astype(jnp.float32) + offset + 0.5) * (jnp.pi / GRID_ROWS)
    inside = ((local_rows >= 0) & (local_rows < total_rows)).astype(jnp.float32)[:, None]
    spin = inside * (spin_rate * jnp.sin(latitude))[:, None]
    p, m, dvar, rvar, hobs = model_rhs[0], obs_rhs[0], model_var[0], obs_var[0], obs_weight[0]
    axes = ("win", "lat")
    up = dvar * p
    um = rvar * m
    first = total(up * p) + total(um * m)
    wide_depth = halo(depth[0])
    pair = shifted(jnp.stack([p, up], axis=1), "win", -1)
    wide = halo(pair)
    back = adjoint(wide[0], wide[1], wide[2], wide_depth, spin, inside)
    back = jnp.stack(back)[:, :, REACH:REACH + rows]
    ux = p - back[:, 0] + hobs * m
    far = shifted(dvar * up + ux, "win", -1)
    wide = halo(ux)
    end = jnp.stack(forward(wide[0], wide[1], wide[2], wide_depth, spin, inside))[:, REACH:REACH + rows]
    zx = up - back[:, 1] + hobs * um
    zm = rvar * um + hobs * ux
    window = lax.axis_index("win")
    lead = jnp.where(window == 0, 1.0, 0.0)
    zp = far - jnp.where(window == lax.axis_size("win") - 1, 0.0, 1.0) * end
    own = dvar * up + ux
    uu = total(up * up) + total(um * um) + total(ux * ux)
    uz = total(dvar * up * up) + total(rvar * um * um) + 2.0 * total(zx * ux)
    zz = total(zp * zp) + lead * total(own * own) + total(zm * zm) + total(zx * zx)
    ranks = lax.axis_size("win") * lax.axis_size("lat")
    parts = jnp.stack([first, uu, uz, zz])
    sent = jnp.broadcast_to(jnp.pad(parts, (0, 124))[None], (ranks, 128))
    sums = jnp.sum(lax.all_to_all(sent, axes, 0, 0, tiled=True), axis=0)
    m1, m2, m3, m4 = sums[0], sums[1], sums[2], sums[3]
    tau, sigma, rho = m1 / m2, m3 / m2, m4 / m2
    gap = rho - sigma * sigma
    y1 = (tau * rho - sigma) / gap
    y2 = (1.0 - sigma * tau) / gap
    return ((y1 * p + y2 * up)[None], (y1 * m + y2 * um)[None], (y2 * ux)[None])


def solution(mesh):
    split = P("win", None, "lat", None)
    in_specs = (split,) * 5 + (P("win", "lat", None),)
    return jax.shard_map(body, mesh=mesh, in_specs=in_specs, out_specs=(split,) * 3, check_vma=False)
```

time: 387 us -> 69.2 us (0.18)
  blocking collectives: 209 us -> 15.5 us
  starting transfers between devices: 102 us -> 17.1 us
  waiting for transfers between devices: 28.6 us -> 10.9 us
  other arithmetic: 19.5 us -> 7.63 us
  between operations: 20.4 us -> 12.8 us
    psum x5 -> x0, blocking collectives: 209 us -> none  [the longest x2 87.9 us: body(): totals = lax.psum(partials, ('win', 'lat'))]
    ppermute x32 -> x6, starting transfers between devices: 91.5 us -> 14.5 us  [the longest x3 10.6 us: halo(): low = lax.ppermute(block[..., rows - REACH:, :], 'lat', forward)]
    all_to_all x0 -> x1, blocking collectives: none -> 15.5 us  [body(): sums = jnp.sum(lax.all_to_all(sent, axes, 0, 0, tiled=True), axis=0)]
    reduce_sum x10 -> x5, other arithmetic: 12.2 us -> 2.79 us  [the longest x4 2.77 us: total(): return jnp.sum(value)]
    ppermute x32 -> x6, waiting for transfers between devices: 13 us -> 4.04 us  [the longest x3 4.04 us: halo(): high = lax.ppermute(block[..., :REACH, :], 'lat', backward)]
    ppermute x4 -> x2, waiting for transfers between devices: 15.5 us -> 6.84 us  [shifted(): lax.ppermute(value, axis, [(source, source + steps) for source in range(i...]
    ppermute x4 -> x2, starting transfers between devices: 10.1 us -> 2.57 us  [shifted(): lax.ppermute(value, axis, [(source, source + steps) for source in range(i...]
  transfers between devices with their start and end apart: 36 -> 8, of which waited for: 20 -> 2; matrix products, arithmetic and copies ran while one was open for 1% -> 5% of each run, Pallas kernels for 0% -> 0%
where the time goes in v1:
time: 69.2 us; the launch traced here: 68.7 us
  starting transfers between devices  17.1 us (25%)
  blocking collectives  15.5 us (22%)
  between operations  12.8 us (18%)
  waiting for transfers between devices  10.9 us (16%)
  other arithmetic  7.63 us (11%)
  local copies, waits for them, and re-layouts  4.71 us (7%)
    all_to_all x1, blocking collectives, body(): sums = jnp.sum(lax.all_to_all(sent, axes, 0, 0, tiled=True), axis=0)  15.5 us
    ppermute x3, starting transfers between devices, halo(): low = lax.ppermute(block[..., rows - REACH:, :], 'lat', forward)  10.6 us
    ppermute x2, waiting for transfers between devices, shifted(): lax.ppermute(value, axis, [(source, source + steps) for source in range(i...  6.84 us
    ppermute x3, waiting for transfers between devices, halo(): high = lax.ppermute(block[..., :REACH, :], 'lat', backward)  4.04 us
    ppermute x3, starting transfers between devices, halo(): high = lax.ppermute(block[..., :REACH, :], 'lat', backward)  3.88 us
    slice x32, local copies, waits for them, and re-layouts, along_lon(): return 0.5 * (jnp.roll(field, -1, axis=-1) - jnp.roll(field, 1, axis=-1))  3.07 us
    reduce_sum x4, other arithmetic, total(): return jnp.sum(value)  2.77 us
    ppermute x2, starting transfers between devices, shifted(): lax.ppermute(value, axis, [(source, source + steps) for source in range(i...  2.57 us
  transfers between devices with their start and end apart: 8, of which 2 were waited for; matrix products, arithmetic and copies ran while one was open for 5% of the time, Pallas kernels for 0%

profile of v1, /device:TPU:0, one launch (start us, length us, event | category | flops | bytes accessed | tf_op | source)
XLA Modules:
  0.0 68.7 jit_solution(5067476566806919553)
XLA Ops:
  0.6 1.0 %bitcast_multiply_fusion.3 = f32[3,1,8,1536]{3,2,1,0:T(8,128)S(1)} fusion(f32[1,3,8,1536]{3,2,1,0:T(8,128)} %param.8, f32[1,3,8,1536]{3,2,1,0:T(8,128)} %param.6), kind=kLoop, calls=%fused_computation.171 | loop fusion | flops 36864 | bytes 442368 | tf_op jit(solution)/shard_map/mul | solution.py:72
  1.7 1.3 %collective-permute-start = (f32[3,2,8,1536]{3,2,1,0:T(8,128)S(1)}, f32[3,2,8,1536]{3,2,1,0:T(8,128)S(1)}, u32[]{:S(2)}, u32[]{:S(2)}) collective-permute-start(f32[3,2,8,1536]{3,2,1,0:T(8,128)S(1)} %pad_maximum_fusion.1), channel_id=1, source_target_pairs={{4,0},{8,4},{12,8},{16,12},{20,16},{24,20},{28,24},{5,1},{9,5},{13... | collective-permute-start | bytes 884744 | tf_op jit(solution)/shard_map/ppermute | solution.py:28
  3.0 2.4 %collective-permute-start.3 = (f32[8,1536]{1,0:T(8,128)S(1)}, f32[8,1536]{1,0:T(8,128)S(1)}, u32[]{:S(2)}, u32[]{:S(2)}) collective-permute-start(f32[8,1536]{1,0:T(8,128)S(1)} %bitcast.172), channel_id=1, source_target_pairs={{0,1},{1,2},{2,3},{4,5},{5,6},{6,7},{8,9},{9,10},{10,11},{12,13},{... | collective-permute-start | bytes 147464 | tf_op jit(solution)/shard_map/ppermute | solution.py:20
  5.4 1.3 %collective-permute-start.4 = (f32[8,1536]{1,0:T(8,128)S(1)}, f32[8,1536]{1,0:T(8,128)S(1)}, u32[]{:S(2)}, u32[]{:S(2)}) collective-permute-start(f32[8,1536]{1,0:T(8,128)S(1)} %bitcast.173), channel_id=1, source_target_pairs={{1,0},{2,1},{3,2},{5,4},{6,5},{7,6},{9,8},{10,9},{11,10},{13,12},{... | collective-permute-start | bytes 147464 | tf_op jit(solution)/shard_map/ppermute | solution.py:21
  6.8 6.8 %collective-permute-done = f32[3,2,8,1536]{3,2,1,0:T(8,128)S(1)} collective-permute-done((f32[3,2,8,1536]{3,2,1,0:T(8,128)S(1)}, f32[3,2,8,1536]{3,2,1,0:T(8,128)S(1)}, u32[]{:S(2)}, u32[]{:S(2)}) %collective-permute-start) | collective-permute-done | bytes 294944 | tf_op jit(solution)/shard_map/ppermute | solution.py:28
  13.6 1.3 %collective-permute-start.1 = (f32[3,2,8,1536]{3,2,1,0:T(8,128)S(1)}, f32[3,2,8,1536]{3,2,1,0:T(8,128)S(1)}, u32[]{:S(2)}, u32[]{:S(2)}) collective-permute-start(f32[3,2,8,1536]{3,2,1,0:T(8,128)S(1)} %collective-permute-done), channel_id=1, source_target_pairs={{0,1},{1,2},{2,3},{4,5},{5,6},{6,7},{8,9},{9,10},{10,11},{12,13},{... | collective-permute-start | bytes 884744 | tf_op jit(solution)/shard_map/ppermute | solution.py:20
  15.0 1.3 %collective-permute-start.2 = (f32[3,2,8,1536]{3,2,1,0:T(8,128)S(1)}, f32[3,2,8,1536]{3,2,1,0:T(8,128)S(1)}, u32[]{:S(2)}, u32[]{:S(2)}) collective-permute-start(f32[3,2,8,1536]{3,2,1,0:T(8,128)S(1)} %collective-permute-done), channel_id=1, source_target_pairs={{1,0},{2,1},{3,2},{5,4},{6,5},{7,6},{9,8},{10,9},{11,10},{13,12},{... | collective-permute-start | bytes 884744 | tf_op jit(solution)/shard_map/ppermute | solution.py:21
  16.4 4.0 %collective-permute-done.2 = f32[3,2,8,1536]{3,2,1,0:T(8,128)S(1)} collective-permute-done((f32[3,2,8,1536]{3,2,1,0:T(8,128)S(1)}, f32[3,2,8,1536]{3,2,1,0:T(8,128)S(1)}, u32[]{:S(2)}, u32[]{:S(2)}) %collective-permute-start.2) | collective-permute-done | bytes 294944 | tf_op jit(solution)/shard_map/ppermute | solution.py:21
  20.5 0.1 fusion.143
  20.8 0.2 fusion.4
  20.9 0.1 fusion.141
  21.1 0.2 fusion.40
  21.4 0.1 fusion.139
  21.6 0.2 fusion.13
  21.8 0.1 fusion.137
  22.0 0.2 fusion.43
  22.2 0.1 fusion.135
  22.4 0.2 fusion.22
  22.8 0.2 fusion.46
  23.2 0.2 fusion.31
  23.6 0.2 fusion.49
  23.8 0.7 %copy-done.2 = f32[1,3,8,1536]{3,2,1,0:T(8,128)S(1)} copy-done((f32[1,3,8,1536]{3,2,1,0:T(8,128)S(1)}, f32[1,3,8,1536]{3,2,1,0:T(8,128)}, u32[]{:S(2)}) %copy-start.2) | copy-done | bytes 147480
  24.7 0.7 fusion.105
  25.4 0.8 %fusion.104 = (f32[]{:T(128)}, f32[]{:T(128)}, f32[]{:T(128)}, f32[]{:T(128)}, f32[]{:T(128)}, /*index=5*/f32[]{:T(128)}, f32[]{:T(128)}, f32[3,8,1536]{2,1,0:T(8,128)S(1)}, f32[3,1,8,1536]{3,2,0,1:T(8,128)S(1)}) fusion(f32[1,3,8,1536]{3,2,1,0:T(8,128)S(1)} %copy-done.3, f32[1,3,8,1536]{3,2,1,0:T(8,128)S(1)} %copy-done.4, ...), kind=kLoop, calls=%fused_computation.174 | loop fusion | flops 847865 | bytes 1916956 | tf_op jit(solution)/shard_map/reduce_sum | solution.py:59
  26.2 7.0 %collective-permute-start.6 = (f32[3,8,1536]{2,1,0:T(8,128)S(1)}, f32[3,8,1536]{2,1,0:T(8,128)S(1)}, u32[]{:S(2)}, u32[]{:S(2)}) collective-permute-start(f32[3,8,1536]{2,1,0:T(8,128)S(1)} %get-tuple-element.13), channel_id=1, source_target_pairs={{0,1},{1,2},{2,3},{4,5},{5,6},{6,7},{8,9},{9,10},{10,11},{12,13},{... | collective-permute-start | bytes 442376 | tf_op jit(solution)/shard_map/ppermute | solution.py:20
  33.2 1.3 %collective-permute-start.7 = (f32[3,8,1536]{2,1,0:T(8,128)S(1)}, f32[3,8,1536]{2,1,0:T(8,128)S(1)}, u32[]{:S(2)}, u32[]{:S(2)}) collective-permute-start(f32[3,8,1536]{2,1,0:T(8,128)S(1)} %get-tuple-element.13), channel_id=1, source_target_pairs={{1,0},{2,1},{3,2},{5,4},{6,5},{7,6},{9,8},{10,9},{11,10},{13,12},{... | collective-permute-start | bytes 442376 | tf_op jit(solution)/shard_map/ppermute | solution.py:21
  34.5 0.6 multiply_reduce_fusion.1
  35.1 1.3 %collective-permute-start.5 = (f32[3,8,1536]{2,1,0:T(8,128)S(1)}, f32[3,8,1536]{2,1,0:T(8,128)S(1)}, u32[]{:S(2)}, u32[]{:S(2)}) collective-permute-start(f32[3,8,1536]{2,1,0:T(8,128)S(1)} %get-tuple-element.16), channel_id=1, source_target_pairs={{4,0},{8,4},{12,8},{16,12},{20,16},{24,20},{28,24},{5,1},{9,5},{13... | collective-permute-start | bytes 442376 | tf_op jit(solution)/shard_map/ppermute | solution.py:28
  45.0 0.6 fusion.86
  47.7 15.5 %all_to_all.6 = f32[32,1,128]{2,1,0:T(1,128)S(1)} all-to-all(f32[32,1,128]{2,1,0:T(1,128)S(1)} %broadcast_in_dim.2), channel_id=1, replica_groups=mesh['win'=8,'lat'=4] {'win','lat'}, dimensions={0} | all-to-all | bytes 32768 | tf_op jit(solution)/shard_map/all_to_all | solution.py:96
  63.2 0.6 fusion.160
  67.9 0.8 %fusion.99 = (f32[1,3,8,1536]{3,2,1,0:T(8,128)}, f32[1,3,8,1536]{3,2,1,0:T(8,128)}, f32[1,3,8,1536]{3,2,1,0:T(8,128)}) fusion(f32[1,3,8,1536]{3,2,1,0:T(8,128)S(1)} %copy-done, f32[3,1,8,1536]{3,2,0,1:T(8,128)S(1)} %get-tuple-element.14, f32[1,3,8,1536]{3,2,1,0:T(8,128)S(1)} %copy-done.5, f32[1,3,8,1536]{3,2,1,0:T(8,128)S(1)} %copy-done.3, f32[]{:T(128)S(6)} %div.31, ...), kind=kLoop, calls=%fused_computation.162 | loop fusion | flops 442368 | bytes 1327112 | tf_op jit(solution)/shard_map/mul | solution.py:102
  (69 shorter events, 4.4 us)
Async XLA Ops:
  0.6 1.1 %copy-start = (f32[1,3,8,1536]{3,2,1,0:T(8,128)S(1)}, f32[1,3,8,1536]{3,2,1,0:T(8,128)}, u32[]{:S(2)}) copy-start(f32[1,3,8,1536]{3,2,1,0:T(8,128)} %param.6) | copy-start | bytes 442372
  1.7 1.3 %copy-start.1 = (f32[1,8,1536]{2,1,0:T(8,128)S(1)}, f32[1,8,1536]{2,1,0:T(8,128)}, u32[]{:S(2)}) copy-start(f32[1,8,1536]{2,1,0:T(8,128)} %param.11) | copy-start | bytes 147460
  1.7 11.9 %collective-permute-start = (f32[3,2,8,1536]{3,2,1,0:T(8,128)S(1)}, f32[3,2,8,1536]{3,2,1,0:T(8,128)S(1)}, u32[]{:S(2)}, u32[]{:S(2)}) collective-permute-start(f32[3,2,8,1536]{3,2,1,0:T(8,128)S(1)} %pad_maximum_fusion.1), channel_id=1, source_target_pairs={{4,0},{8,4},{12,8},{16,12},{20,16},{24,20},{28,24},{5,1},{9,5},{13... | collective-permute-start | bytes 884744 | tf_op jit(solution)/shard_map/ppermute | solution.py:28
  3.0 11.9 %collective-permute-start.3 = (f32[8,1536]{1,0:T(8,128)S(1)}, f32[8,1536]{1,0:T(8,128)S(1)}, u32[]{:S(2)}, u32[]{:S(2)}) collective-permute-start(f32[8,1536]{1,0:T(8,128)S(1)} %bitcast.172), channel_id=1, source_target_pairs={{0,1},{1,2},{2,3},{4,5},{5,6},{6,7},{8,9},{9,10},{10,11},{12,13},{... | collective-permute-start | bytes 147464 | tf_op jit(solution)/shard_map/ppermute | solution.py:20
  5.4 9.5 %collective-permute-start.4 = (f32[8,1536]{1,0:T(8,128)S(1)}, f32[8,1536]{1,0:T(8,128)S(1)}, u32[]{:S(2)}, u32[]{:S(2)}) collective-permute-start(f32[8,1536]{1,0:T(8,128)S(1)} %bitcast.173), channel_id=1, source_target_pairs={{1,0},{2,1},{3,2},{5,4},{6,5},{7,6},{9,8},{10,9},{11,10},{13,12},{... | collective-permute-start | bytes 147464 | tf_op jit(solution)/shard_map/ppermute | solution.py:21
  13.6 2.7 %collective-permute-start.1 = (f32[3,2,8,1536]{3,2,1,0:T(8,128)S(1)}, f32[3,2,8,1536]{3,2,1,0:T(8,128)S(1)}, u32[]{:S(2)}, u32[]{:S(2)}) collective-permute-start(f32[3,2,8,1536]{3,2,1,0:T(8,128)S(1)} %collective-permute-done), channel_id=1, source_target_pairs={{0,1},{1,2},{2,3},{4,5},{5,6},{6,7},{8,9},{9,10},{10,11},{12,13},{... | collective-permute-start | bytes 884744 | tf_op jit(solution)/shard_map/ppermute | solution.py:20
  15.0 5.4 %collective-permute-start.2 = (f32[3,2,8,1536]{3,2,1,0:T(8,128)S(1)}, f32[3,2,8,1536]{3,2,1,0:T(8,128)S(1)}, u32[]{:S(2)}, u32[]{:S(2)}) collective-permute-start(f32[3,2,8,1536]{3,2,1,0:T(8,128)S(1)} %collective-permute-done), channel_id=1, source_target_pairs={{1,0},{2,1},{3,2},{5,4},{6,5},{7,6},{9,8},{10,9},{11,10},{13,12},{... | collective-permute-start | bytes 884744 | tf_op jit(solution)/shard_map/ppermute | solution.py:21
  23.6 0.9 %copy-start.2 = (f32[1,3,8,1536]{3,2,1,0:T(8,128)S(1)}, f32[1,3,8,1536]{3,2,1,0:T(8,128)}, u32[]{:S(2)}) copy-start(f32[1,3,8,1536]{3,2,1,0:T(8,128)} %param.8) | copy-start | bytes 442372
  23.6 1.0 %copy-start.3 = (f32[1,3,8,1536]{3,2,1,0:T(8,128)S(1)}, f32[1,3,8,1536]{3,2,1,0:T(8,128)}, u32[]{:S(2)}) copy-start(f32[1,3,8,1536]{3,2,1,0:T(8,128)} %param.7) | copy-start | bytes 442372
  23.6 1.1 %copy-start.4 = (f32[1,3,8,1536]{3,2,1,0:T(8,128)S(1)}, f32[1,3,8,1536]{3,2,1,0:T(8,128)}, u32[]{:S(2)}) copy-start(f32[1,3,8,1536]{3,2,1,0:T(8,128)} %param.9) | copy-start | bytes 442372
  23.6 1.1 %copy-start.5 = (f32[1,3,8,1536]{3,2,1,0:T(8,128)S(1)}, f32[1,3,8,1536]{3,2,1,0:T(8,128)}, u32[]{:S(2)}) copy-start(f32[1,3,8,1536]{3,2,1,0:T(8,128)} %param.10) | copy-start | bytes 442372
  26.2 15.9 %collective-permute-start.6 = (f32[3,8,1536]{2,1,0:T(8,128)S(1)}, f32[3,8,1536]{2,1,0:T(8,128)S(1)}, u32[]{:S(2)}, u32[]{:S(2)}) collective-permute-start(f32[3,8,1536]{2,1,0:T(8,128)S(1)} %get-tuple-element.13), channel_id=1, source_target_pairs={{0,1},{1,2},{2,3},{4,5},{5,6},{6,7},{8,9},{9,10},{10,11},{12,13},{... | collective-permute-start | bytes 442376 | tf_op jit(solution)/shard_map/ppermute | solution.py:20
  33.2 8.9 %collective-permute-start.7 = (f32[3,8,1536]{2,1,0:T(8,128)S(1)}, f32[3,8,1536]{2,1,0:T(8,128)S(1)}, u32[]{:S(2)}, u32[]{:S(2)}) collective-permute-start(f32[3,8,1536]{2,1,0:T(8,128)S(1)} %get-tuple-element.13), channel_id=1, source_target_pairs={{1,0},{2,1},{3,2},{5,4},{6,5},{7,6},{9,8},{10,9},{11,10},{13,12},{... | collective-permute-start | bytes 442376 | tf_op jit(solution)/shard_map/ppermute | solution.py:21
  35.1 9.8 %collective-permute-start.5 = (f32[3,8,1536]{2,1,0:T(8,128)S(1)}, f32[3,8,1536]{2,1,0:T(8,128)S(1)}, u32[]{:S(2)}, u32[]{:S(2)}) collective-permute-start(f32[3,8,1536]{2,1,0:T(8,128)S(1)} %get-tuple-element.16), channel_id=1, source_target_pairs={{4,0},{8,4},{12,8},{16,12},{20,16},{24,20},{28,24},{5,1},{9,5},{13... | collective-permute-start | bytes 442376 | tf_op jit(solution)/shard_map/ppermute | solution.py:28

commit v2 on v1

v2 whole, which is shorter than its diff:
```python
import jax
import jax.numpy as jnp
from jax import lax
from jax.experimental import pallas as pl
from jax.experimental.pallas import tpu as pltpu
from jax.sharding import PartitionSpec as P

GRID_ROWS = 768
STEPS = 4

mass_rate = 0.5
press_rate = 0.5
spin_rate = 0.4


def lon_gap(field):
    width = field.shape[-1]
    return pltpu.roll(field, width - 1, 1) - pltpu.roll(field, 1, 1)


def lat_gap(field):
    rows = field.shape[0]
    return pltpu.roll(field, rows - 1, 0) - pltpu.roll(field, 1, 0)


def stacked(low, own, high, index):
    return jnp.concatenate([low[index], own[index], high[index]], axis=0)


def prep_kernel(p, m, dvar, hobs, depth, pair, straight):
    for part in range(3):
        pair[part] = p[0, part]
        pair[3 + part] = dvar[0, part] * p[0, part]
        straight[1 + part] = p[0, part] + hobs[0, part] * m[0, part]
    straight[0] = depth[0]


def adjoint_kernel(pair, pair_low, pair_high, straight, depth_low, depth_high, spin, inside, state, back):
    depth = 0.25 * jnp.concatenate([depth_low[0], straight[0], depth_high[0]], axis=0)
    turn, keep = spin[...], inside[...]
    rows = pair.shape[1]
    for which in range(2):
        base = 3 * which
        adj_height = stacked(pair_low, pair, pair_high, base)
        adj_east = stacked(pair_low, pair, pair_high, base + 1)
        adj_north = stacked(pair_low, pair, pair_high, base + 2)
        for step in range(STEPS):
            adj_mid = adj_east - turn * adj_north
            adj_height = keep * (adj_height + 0.25 * (lat_gap(adj_north) + lon_gap(adj_mid)))
            adj_north = adj_north + turn * adj_mid + depth * lat_gap(adj_height)
            adj_east = adj_mid + depth * lon_gap(adj_height)
        for part, value in enumerate((adj_height, adj_east, adj_north)):
            own = value[rows:2 * rows]
            back[base + part] = own
            if which == 0:
                state[part] = straight[1 + part] - own


def forward_kernel(state, state_low, state_high, straight, depth_low, depth_high, spin, inside, end):
    depth = 0.25 * jnp.concatenate([depth_low[0], straight[0], depth_high[0]], axis=0)
    turn, keep = spin[...], inside[...]
    rows = state.shape[1]
    height = stacked(state_low, state, state_high, 0)
    east = stacked(state_low, state, state_high, 1)
    north = stacked(state_low, state, state_high, 2)
    for step in range(STEPS):
        height = keep * (height - (lon_gap(depth * east) + lat_gap(depth * north)))
        east = east + turn * north - 0.25 * lon_gap(height)
        north = north - turn * east - 0.25 * lat_gap(height)
    for part, value in enumerate((height, east, north)):
        end[part] = value[rows:2 * rows]


def lane_sum(value):
    rows, width = value.shape
    total = value[:, :128]
    for start in range(128, width, 128):
        total = total + value[:, start:start + 128]
    return total


def inner_kernel(p, m, dvar, rvar, hobs, back, end, linked, sent):
    moments = [0.0, 0.0, 0.0, 0.0]
    link = linked[...]
    for part in range(3):
        dv, rv, hv = dvar[0, part], rvar[0, part], hobs[0, part]
        pv, mv = p[0, part], m[0, part]
        up, um = dv * pv, rv * mv
        ux = pv - back[part] + hv * mv
        zp = dv * up + ux - link * end[part]
        zm = rv * um + hv * ux
        zx = up - back[3 + part] + hv * um
        moments[0] += lane_sum(up * pv + um * mv)
        moments[1] += lane_sum(up * up + um * um + ux * ux)
        moments[2] += lane_sum(dv * up * up + rv * um * um + 2.0 * (zx * ux))
        moments[3] += lane_sum(zp * zp + zm * zm + zx * zx)
    rows = [jnp.sum(value, axis=0, keepdims=True) for value in moments]
    tile = jnp.concatenate(rows + rows, axis=0)
    for rank in range(sent.shape[0] // 8):
        sent[8 * rank:8 * rank + 8] = tile


def two_sum(a, b):
    total = a + b
    part = total - a
    return total, (a - (total - part)) + (b - part)


def split(a):
    wide = 4097.0 * a
    top = wide - (wide - a)
    return top, a - top


def two_product(a, b):
    product = a * b
    a_top, a_low = split(a)
    b_top, b_low = split(b)
    return product, ((a_top * b_top - product) + a_top * b_low + a_low * b_top) + a_low * b_low


def pair_product(a, b):
    product, rest = two_product(a[0], b[0])
    return product, rest + (a[0] * b[1] + a[1] * b[0])


def pair_gap(a, b):
    total, rest = two_sum(a[0], -b[0])
    return total + (rest + (a[1] - b[1]))


def coefficients(gathered):
    top = gathered[0:8]
    for rank in range(1, gathered.shape[0] // 8):
        top = top + gathered[8 * rank:8 * rank + 8]
    low = jnp.zeros_like(top)
    shift = 64
    while shift:
        total, rest = two_sum(top, pltpu.roll(top, shift, 1))
        low = low + pltpu.roll(low, shift, 1) + rest
        top = total
        shift //= 2
    scale = 1.0 / top[1:2, :128]
    moments = []
    for row in range(4):
        product, rest = two_product(top[row:row + 1], scale)
        moments.append((product, rest + low[row:row + 1] * scale))
    m1, m2, m3, m4 = moments
    gap = pair_gap(pair_product(m2, m4), pair_product(m3, m3))
    y1 = pair_gap(pair_product(m1, m4), pair_product(m2, m3)) / gap
    y2 = pair_gap(pair_product(m2, m2), pair_product(m1, m3)) / gap
    return y1, y2


def combine_kernel(gathered, p, m, dvar, rvar, hobs, back, dual_model, dual_obs, increment):
    y1, y2 = coefficients(gathered)
    rows, width = p.shape[2:]
    y1 = jnp.broadcast_to(jnp.concatenate([y1] * (width // 128), axis=1), (rows, width))
    y2 = jnp.broadcast_to(jnp.concatenate([y2] * (width // 128), axis=1), (rows, width))
    for part in range(3):
        pv, mv = p[0, part], m[0, part]
        dual_model[0, part] = (y1 + y2 * dvar[0, part]) * pv
        dual_obs[0, part] = (y1 + y2 * rvar[0, part]) * mv
        increment[0, part] = y2 * (pv - back[part] + hobs[0, part] * mv)


def run(kernel, out_shapes, *operands):
    shapes = [jax.ShapeDtypeStruct(shape, jnp.float32) for shape in out_shapes]
    size = sum(4 * operand.size for operand in operands) + sum(4 * shape.size for shape in shapes)
    return pl.pallas_call(
        kernel,
        out_shape=shapes,
        in_specs=[pl.BlockSpec(memory_space=pltpu.VMEM)] * len(operands),
        out_specs=[pl.BlockSpec(memory_space=pltpu.VMEM)] * len(shapes),
        compiler_params=pltpu.CompilerParams(vmem_limit_bytes=32 * 1024 * 1024),
        cost_estimate=pl.CostEstimate(flops=4 * size, bytes_accessed=size, transcendentals=0),
    )(*operands)


def moved(value, win_step, lat_step):
    wins, lats = lax.axis_size("win"), lax.axis_size("lat")
    pairs = []
    for win in range(wins):
        for lat in range(lats):
            if 0 <= win + win_step < wins and 0 <= lat + lat_step < lats:
                pairs.append((win * lats + lat, (win + win_step) * lats + lat + lat_step))
    return lax.ppermute(value, ("win", "lat"), pairs)


def body(model_rhs, obs_rhs, model_var, obs_var, obs_weight, depth):
    rows, width = model_rhs.shape[2:]
    ranks = lax.axis_size("win") * lax.axis_size("lat")
    total_rows = rows * lax.axis_size("lat")
    offset = (GRID_ROWS - total_rows) // 2
    local_rows = lax.axis_index("lat") * rows - rows + jnp.arange(3 * rows, dtype=jnp.int32)
    latitude = -jnp.pi / 2 + (local_rows.astype(jnp.float32) + offset + 0.5) * (jnp.pi / GRID_ROWS)
    inside = ((local_rows >= 0) & (local_rows < total_rows)).astype(jnp.float32)
    spin = inside * (mass_rate * spin_rate * jnp.sin(latitude))
    inside = jnp.broadcast_to(inside[:, None], (3 * rows, width))
    spin = jnp.broadcast_to(spin[:, None], (3 * rows, width))
    linked = jnp.full((rows, width), jnp.where(lax.axis_index("win") > 0, 1.0, 0.0))

    depth_low, depth_high = moved(depth, 1, 1), moved(depth, 1, -1)
    pair, straight = run(
        prep_kernel, [(6, rows, width), (4, rows, width)], model_rhs, obs_rhs, model_var, obs_weight, depth
    )
    pair_low, pair_high = moved(pair, 0, 1), moved(pair, 0, -1)
    came = moved(straight, 1, 0)
    state, back = run(
        adjoint_kernel, [(3, rows, width), (6, rows, width)],
        pair, pair_low, pair_high, came, depth_low, depth_high, spin, inside,
    )
    state_low, state_high = moved(state, 0, 1), moved(state, 0, -1)
    back = moved(back, -1, 0)
    (end,) = run(
        forward_kernel, [(3, rows, width)], state, state_low, state_high, came, depth_low, depth_high, spin, inside
    )
    (sent,) = run(
        inner_kernel, [(8 * ranks, 128)],
        model_rhs, obs_rhs, model_var, obs_var, obs_weight, back, end, linked,
    )
    gathered = lax.all_to_all(sent, ("win", "lat"), 0, 0, tiled=True)
    return run(
        combine_kernel, [model_rhs.shape] * 3,
        gathered, model_rhs, obs_rhs, model_var, obs_var, obs_weight, back,
    )


def solution(mesh):
    split_spec = P("win", None, "lat", None)
    in_specs = (split_spec,) * 5 + (P("win", "lat", None),)
    return jax.shard_map(body, mesh=mesh, in_specs=in_specs, out_specs=(split_spec,) * 3, check_vma=False)
```

time: 69.2 us -> 57.9 us (0.84)
  between operations: 12.8 us -> 0.83 us
  other arithmetic: 7.63 us -> 0.06 us
  Pallas kernels: 0 us -> 5.92 us
  starting transfers between devices: 17.1 us -> 20.4 us
  blocking collectives: 15.5 us -> 16.9 us
  waiting for transfers between devices: 10.9 us -> 9.6 us
  local copies, waits for them, and re-layouts: 4.71 us -> 3.81 us
    pallas_call x0 -> x5, Pallas kernels: none -> 5.92 us  [run(): pl.pallas_call(kernel, out_shape=shapes, in_specs=[pl.BlockSpec(memory_sp...]
    slice x33 -> x0, local copies, waits for them, and re-layouts: 3.66 us -> none  [the longest x32 3.07 us: along_lon(): return 0.5 * (jnp.roll(field, -1, axis=-1) - jnp.roll(field, 1, axis=-1))]
    mul x19 -> x1, other arithmetic: 3.71 us -> 0.05 us  [body(): spin = inside * (mass_rate * spin_rate * jnp.sin(latitude))]
    ppermute x8, starting transfers between devices: 17.1 us -> 20.4 us  [moved(): return lax.ppermute(value, ('win', 'lat'), pairs)]
    reduce_sum x5 -> x0, other arithmetic: 2.79 us -> none  [the longest x4 2.77 us: total(): return jnp.sum(value)]
    unnamed x14 -> x18, local copies, waits for them, and re-layouts: 0.99 us -> 3.65 us
    all_to_all x1, blocking collectives: 15.5 us -> 16.9 us  [body(): gathered = lax.all_to_all(sent, ('win', 'lat'), 0, 0, tiled=True)]
    ppermute x8, waiting for transfers between devices: 10.9 us -> 9.6 us  [moved(): return lax.ppermute(value, ('win', 'lat'), pairs)]
  transfers between devices with their start and end apart: 8 -> 8, of which waited for: 2 -> 3; matrix products, arithmetic and copies ran while one was open for 5% -> 0% of each run, Pallas kernels for 0% -> 2%
where the time goes in v2:
time: 57.9 us; the launch traced here: 57.5 us
  starting transfers between devices  20.4 us (35%)
  blocking collectives  16.9 us (29%)
  waiting for transfers between devices  9.6 us (17%)
  Pallas kernels  5.92 us (10%)
  local copies, waits for them, and re-layouts  3.81 us (7%)
  between operations  0.83 us (1%)
    ppermute x8, starting transfers between devices, moved(): return lax.ppermute(value, ('win', 'lat'), pairs)  20.4 us
    all_to_all x1, blocking collectives, body(): gathered = lax.all_to_all(sent, ('win', 'lat'), 0, 0, tiled=True)  16.9 us
    ppermute x8, waiting for transfers between devices, moved(): return lax.ppermute(value, ('win', 'lat'), pairs)  9.6 us
    pallas_call x5, Pallas kernels, run(): pl.pallas_call(kernel, out_shape=shapes, in_specs=[pl.BlockSpec(memory_sp...  5.92 us
    unnamed x18, local copies, waits for them, and re-layouts  3.65 us
  transfers between devices with their start and end apart: 8, of which 3 were waited for; matrix products, arithmetic and copies ran while one was open for 0% of the time, Pallas kernels for 2%

profile of v2, /device:TPU:0, one launch (start us, length us, event | category | flops | bytes accessed | tf_op | source)
XLA Modules:
  0.0 57.5 jit_solution(7468420839742267667)
XLA Ops:
  0.6 0.0 copy-start
  0.6 0.9 %copy-done = f32[1,3,8,1536]{3,2,1,0:T(8,128)S(1)} copy-done((f32[1,3,8,1536]{3,2,1,0:T(8,128)S(1)}, f32[1,3,8,1536]{3,2,1,0:T(8,128)}, u32[]{:S(2)}) %copy-start) | copy-done | bytes 147480
  1.5 0.9 %copy-done.2 = f32[1,3,8,1536]{3,2,1,0:T(8,128)S(1)} copy-done((f32[1,3,8,1536]{3,2,1,0:T(8,128)S(1)}, f32[1,3,8,1536]{3,2,1,0:T(8,128)}, u32[]{:S(2)}) %copy-start.2) | copy-done | bytes 147480
  2.5 0.9 %copy-done.4 = f32[1,3,8,1536]{3,2,1,0:T(8,128)S(1)} copy-done((f32[1,3,8,1536]{3,2,1,0:T(8,128)S(1)}, f32[1,3,8,1536]{3,2,1,0:T(8,128)}, u32[]{:S(2)}) %copy-start.4) | copy-done | bytes 147480
  3.4 0.9 %copy-done.6 = f32[1,3,8,1536]{3,2,1,0:T(8,128)S(1)} copy-done((f32[1,3,8,1536]{3,2,1,0:T(8,128)S(1)}, f32[1,3,8,1536]{3,2,1,0:T(8,128)}, u32[]{:S(2)}) %copy-start.6) | copy-done | bytes 147480
  4.3 0.8 %shard_map.85 = (f32[6,8,1536]{2,1,0:T(8,128)S(1)}, f32[4,8,1536]{2,1,0:T(8,128)S(1)}) custom-call(f32[1,3,8,1536]{3,2,1,0:T(8,128)S(1)} %copy-done, f32[1,3,8,1536]{3,2,1,0:T(8,128)S(1)} %copy-done.2, f32[1,3,8,1536]{3,2,1,0:T(8,128)S(1)} %copy-done.4, f32[1,3,8,1536]{3,2,1,0:T(8,128)S(1)} %copy-done.6, f32[1,8,1536]{2,1,0:T(8,128)} %depth.1), custom_call_target="tpu_custom_call" | custom-call | flops 4521984 | bytes 1130496 | tf_op jit(solution)/shard_map/pallas_call | solution.py:170
  5.1 2.4 %collective-permute-start = (f32[6,8,1536]{2,1,0:T(8,128)S(1)}, f32[6,8,1536]{2,1,0:T(8,128)S(1)}, u32[]{:S(2)}, u32[]{:S(2)}) collective-permute-start(f32[6,8,1536]{2,1,0:T(8,128)S(1)} %get-tuple-element.7.pair), channel_id=1, source_target_pairs={{0,1},{1,2},{2,3},{4,5},{5,6},{6,7},{8,9},{9,10},{10,11},{12,13},{... | collective-permute-start | bytes 884744 | tf_op jit(solution)/shard_map/ppermute | solution.py:187
  7.5 1.3 %collective-permute-start.1 = (f32[6,8,1536]{2,1,0:T(8,128)S(1)}, f32[6,8,1536]{2,1,0:T(8,128)S(1)}, u32[]{:S(2)}, u32[]{:S(2)}) collective-permute-start(f32[6,8,1536]{2,1,0:T(8,128)S(1)} %get-tuple-element.7.pair), channel_id=1, source_target_pairs={{1,0},{2,1},{3,2},{5,4},{6,5},{7,6},{9,8},{10,9},{11,10},{13,12},{... | collective-permute-start | bytes 884744 | tf_op jit(solution)/shard_map/ppermute | solution.py:187
  8.8 6.2 %collective-permute-start.3 = (f32[1,8,1536]{2,1,0:T(8,128)}, f32[1,8,1536]{2,1,0:T(8,128)S(1)}, u32[]{:S(2)}, u32[]{:S(2)}) collective-permute-start(f32[1,8,1536]{2,1,0:T(8,128)} %depth.1), channel_id=1, source_target_pairs={{0,5},{1,6},{2,7},{4,9},{5,10},{6,11},{8,13},{9,14},{10,15},{12,17... | collective-permute-start | bytes 147464 | tf_op jit(solution)/shard_map/ppermute | solution.py:187
  15.1 0.7 %collective-permute-start.4 = (f32[1,8,1536]{2,1,0:T(8,128)}, f32[1,8,1536]{2,1,0:T(8,128)S(1)}, u32[]{:S(2)}, u32[]{:S(2)}) collective-permute-start(f32[1,8,1536]{2,1,0:T(8,128)} %depth.1), channel_id=1, source_target_pairs={{1,4},{2,5},{3,6},{5,8},{6,9},{7,10},{9,12},{10,13},{11,14},{13,16... | collective-permute-start | bytes 147464 | tf_op jit(solution)/shard_map/ppermute | solution.py:187
  15.7 4.1 %collective-permute-start.2 = (f32[4,8,1536]{2,1,0:T(8,128)S(1)}, f32[4,8,1536]{2,1,0:T(8,128)S(1)}, u32[]{:S(2)}, u32[]{:S(2)}) collective-permute-start(f32[4,8,1536]{2,1,0:T(8,128)S(1)} %get-tuple-element.8), channel_id=1, source_target_pairs={{0,4},{1,5},{2,6},{3,7},{4,8},{5,9},{6,10},{7,11},{8,12},{9,13},{1... | collective-permute-start | bytes 589832 | tf_op jit(solution)/shard_map/ppermute | solution.py:187
  19.9 0.0 collective-permute-done.3.depth_low
  19.9 0.0 collective-permute-done.4.depth_high
  19.9 4.6 %collective-permute-done.2.straight = f32[4,8,1536]{2,1,0:T(8,128)S(1)} collective-permute-done((f32[4,8,1536]{2,1,0:T(8,128)S(1)}, f32[4,8,1536]{2,1,0:T(8,128)S(1)}, u32[]{:S(2)}, u32[]{:S(2)}) %collective-permute-start.2) | collective-permute-done | bytes 196640 | tf_op jit(solution)/shard_map/ppermute | solution.py:187
  24.5 0.0 collective-permute-done.pair_low
  24.5 0.0 collective-permute-done.1.pair_high
  24.5 0.1 broadcast_in_dim.6.spin
  24.6 0.1 broadcast_in_dim.7.inside
  24.6 2.3 %shard_map.86 = (f32[3,8,1536]{2,1,0:T(8,128)S(1)}, f32[6,8,1536]{2,1,0:T(8,128)S(1)}) custom-call(f32[6,8,1536]{2,1,0:T(8,128)S(1)} %get-tuple-element.7.pair, f32[6,8,1536]{2,1,0:T(8,128)S(1)} %collective-permute-done.pair_low, f32[6,8,1536]{2,1,0:T(8,128)S(1)} %collective-permute-done.1.pair_high, f32[4,8,1536]{2,1,0:T(8,128)S(1)} %collective-permute-done.2.straight, ...), custom_call_target="tpu_custom_call" | custom-call | flops 7667712 | bytes 1916928 | tf_op jit(solution)/shard_map/pallas_call | solution.py:170
  27.0 1.3 %collective-permute-start.5 = (f32[6,8,1536]{2,1,0:T(8,128)S(1)}, f32[6,8,1536]{2,1,0:T(8,128)S(1)}, u32[]{:S(2)}, u32[]{:S(2)}) collective-permute-start(f32[6,8,1536]{2,1,0:T(8,128)S(1)} %get-tuple-element.9), channel_id=1, source_target_pairs={{4,0},{5,1},{6,2},{7,3},{8,4},{9,5},{10,6},{11,7},{12,8},{13,9},{1... | collective-permute-start | bytes 884744 | tf_op jit(solution)/shard_map/ppermute | solution.py:187
  28.3 3.2 %collective-permute-start.6 = (f32[3,8,1536]{2,1,0:T(8,128)S(1)}, f32[3,8,1536]{2,1,0:T(8,128)S(1)}, u32[]{:S(2)}, u32[]{:S(2)}) collective-permute-start(f32[3,8,1536]{2,1,0:T(8,128)S(1)} %get-tuple-element.10.state), channel_id=1, source_target_pairs={{0,1},{1,2},{2,3},{4,5},{5,6},{6,7},{8,9},{9,10},{10,11},{12,13},{... | collective-permute-start | bytes 442376 | tf_op jit(solution)/shard_map/ppermute | solution.py:187
  31.4 1.3 %collective-permute-start.7 = (f32[3,8,1536]{2,1,0:T(8,128)S(1)}, f32[3,8,1536]{2,1,0:T(8,128)S(1)}, u32[]{:S(2)}, u32[]{:S(2)}) collective-permute-start(f32[3,8,1536]{2,1,0:T(8,128)S(1)} %get-tuple-element.10.state), channel_id=1, source_target_pairs={{1,0},{2,1},{3,2},{5,4},{6,5},{7,6},{9,8},{10,9},{11,10},{13,12},{... | collective-permute-start | bytes 442376 | tf_op jit(solution)/shard_map/ppermute | solution.py:187
  32.7 0.0 collective-permute-done.6.state_low
  32.7 3.6 %collective-permute-done.7.state_high = f32[3,8,1536]{2,1,0:T(8,128)S(1)} collective-permute-done((f32[3,8,1536]{2,1,0:T(8,128)S(1)}, f32[3,8,1536]{2,1,0:T(8,128)S(1)}, u32[]{:S(2)}, u32[]{:S(2)}) %collective-permute-start.7) | collective-permute-done | bytes 147488 | tf_op jit(solution)/shard_map/ppermute | solution.py:187
  36.3 0.0 copy-start.8
  36.4 1.2 %shard_map.87.end = f32[3,8,1536]{2,1,0:T(8,128)S(1)} custom-call(f32[3,8,1536]{2,1,0:T(8,128)S(1)} %get-tuple-element.10.state, f32[3,8,1536]{2,1,0:T(8,128)S(1)} %collective-permute-done.6.state_low, f32[3,8,1536]{2,1,0:T(8,128)S(1)} %collective-permute-done.7.state_high, f32[4,8,1536]{2,1,0:T(8,128)S(1)} %collective-permute-done.2.straight, ...), custom_call_target="tpu_custom_call" | custom-call | flops 4718592 | bytes 1179648 | tf_op jit(solution)/shard_map/pallas_call | solution.py:170
  37.5 1.4 %collective-permute-done.5.back = f32[6,8,1536]{2,1,0:T(8,128)S(1)} collective-permute-done((f32[6,8,1536]{2,1,0:T(8,128)S(1)}, f32[6,8,1536]{2,1,0:T(8,128)S(1)}, u32[]{:S(2)}, u32[]{:S(2)}) %collective-permute-start.5) | collective-permute-done | bytes 294944 | tf_op jit(solution)/shard_map/ppermute | solution.py:187
  39.0 0.0 copy-done.1
  39.0 0.0 copy-done.5
  39.0 0.3 shard_map.88
  39.3 16.9 %all_to_all.11 = f32[32,8,128]{2,1,0:T(8,128)S(1)} all-to-all(f32[32,8,128]{2,1,0:T(8,128)S(1)} %bitcast.3), channel_id=1, replica_groups=mesh['win'=8,'lat'=4] {'win','lat'}, dimensions={0} | all-to-all | bytes 262144 | tf_op jit(solution)/shard_map/all_to_all | solution.py:222
  56.1 1.3 %shard_map.89 = (f32[1,3,8,1536]{3,2,1,0:T(8,128)}, f32[1,3,8,1536]{3,2,1,0:T(8,128)}, f32[1,3,8,1536]{3,2,1,0:T(8,128)}) custom-call(f32[256,128]{1,0:T(8,128)S(1)} %bitcast.2, f32[1,3,8,1536]{3,2,1,0:T(8,128)S(1)} %copy-done.1, f32[1,3,8,1536]{3,2,1,0:T(8,128)S(1)} %copy-done.3, f32[1,3,8,1536]{3,2,1,0:T(8,128)S(1)} %copy-done.5, ...), custom_call_target="tpu_custom_call" | custom-call | flops 6422528 | bytes 1605632 | tf_op jit(solution)/shard_map/pallas_call | solution.py:170
  (13 shorter events, 0.1 us)
Async XLA Ops:
  0.6 0.9 %copy-start = (f32[1,3,8,1536]{3,2,1,0:T(8,128)S(1)}, f32[1,3,8,1536]{3,2,1,0:T(8,128)}, u32[]{:S(2)}) copy-start(f32[1,3,8,1536]{3,2,1,0:T(8,128)} %p.5) | copy-start | bytes 442372
  1.5 0.9 %copy-start.2 = (f32[1,3,8,1536]{3,2,1,0:T(8,128)S(1)}, f32[1,3,8,1536]{3,2,1,0:T(8,128)}, u32[]{:S(2)}) copy-start(f32[1,3,8,1536]{3,2,1,0:T(8,128)} %m.5) | copy-start | bytes 442372
  2.5 0.9 %copy-start.4 = (f32[1,3,8,1536]{3,2,1,0:T(8,128)S(1)}, f32[1,3,8,1536]{3,2,1,0:T(8,128)}, u32[]{:S(2)}) copy-start(f32[1,3,8,1536]{3,2,1,0:T(8,128)} %dvar.5) | copy-start | bytes 442372
  3.4 0.9 %copy-start.6 = (f32[1,3,8,1536]{3,2,1,0:T(8,128)S(1)}, f32[1,3,8,1536]{3,2,1,0:T(8,128)}, u32[]{:S(2)}) copy-start(f32[1,3,8,1536]{3,2,1,0:T(8,128)} %hobs.5) | copy-start | bytes 442372
  5.1 19.4 %collective-permute-start = (f32[6,8,1536]{2,1,0:T(8,128)S(1)}, f32[6,8,1536]{2,1,0:T(8,128)S(1)}, u32[]{:S(2)}, u32[]{:S(2)}) collective-permute-start(f32[6,8,1536]{2,1,0:T(8,128)S(1)} %get-tuple-element.7.pair), channel_id=1, source_target_pairs={{0,1},{1,2},{2,3},{4,5},{5,6},{6,7},{8,9},{9,10},{10,11},{12,13},{... | collective-permute-start | bytes 884744 | tf_op jit(solution)/shard_map/ppermute | solution.py:187
  7.5 17.0 %collective-permute-start.1 = (f32[6,8,1536]{2,1,0:T(8,128)S(1)}, f32[6,8,1536]{2,1,0:T(8,128)S(1)}, u32[]{:S(2)}, u32[]{:S(2)}) collective-permute-start(f32[6,8,1536]{2,1,0:T(8,128)S(1)} %get-tuple-element.7.pair), channel_id=1, source_target_pairs={{1,0},{2,1},{3,2},{5,4},{6,5},{7,6},{9,8},{10,9},{11,10},{13,12},{... | collective-permute-start | bytes 884744 | tf_op jit(solution)/shard_map/ppermute | solution.py:187
  8.8 11.1 %collective-permute-start.3 = (f32[1,8,1536]{2,1,0:T(8,128)}, f32[1,8,1536]{2,1,0:T(8,128)S(1)}, u32[]{:S(2)}, u32[]{:S(2)}) collective-permute-start(f32[1,8,1536]{2,1,0:T(8,128)} %depth.1), channel_id=1, source_target_pairs={{0,5},{1,6},{2,7},{4,9},{5,10},{6,11},{8,13},{9,14},{10,15},{12,17... | collective-permute-start | bytes 147464 | tf_op jit(solution)/shard_map/ppermute | solution.py:187
  15.1 4.8 %collective-permute-start.4 = (f32[1,8,1536]{2,1,0:T(8,128)}, f32[1,8,1536]{2,1,0:T(8,128)S(1)}, u32[]{:S(2)}, u32[]{:S(2)}) collective-permute-start(f32[1,8,1536]{2,1,0:T(8,128)} %depth.1), channel_id=1, source_target_pairs={{1,4},{2,5},{3,6},{5,8},{6,9},{7,10},{9,12},{10,13},{11,14},{13,16... | collective-permute-start | bytes 147464 | tf_op jit(solution)/shard_map/ppermute | solution.py:187
  15.7 8.7 %collective-permute-start.2 = (f32[4,8,1536]{2,1,0:T(8,128)S(1)}, f32[4,8,1536]{2,1,0:T(8,128)S(1)}, u32[]{:S(2)}, u32[]{:S(2)}) collective-permute-start(f32[4,8,1536]{2,1,0:T(8,128)S(1)} %get-tuple-element.8), channel_id=1, source_target_pairs={{0,4},{1,5},{2,6},{3,7},{4,8},{5,9},{6,10},{7,11},{8,12},{9,13},{1... | collective-permute-start | bytes 589832 | tf_op jit(solution)/shard_map/ppermute | solution.py:187
  27.0 12.0 %collective-permute-start.5 = (f32[6,8,1536]{2,1,0:T(8,128)S(1)}, f32[6,8,1536]{2,1,0:T(8,128)S(1)}, u32[]{:S(2)}, u32[]{:S(2)}) collective-permute-start(f32[6,8,1536]{2,1,0:T(8,128)S(1)} %get-tuple-element.9), channel_id=1, source_target_pairs={{4,0},{5,1},{6,2},{7,3},{8,4},{9,5},{10,6},{11,7},{12,8},{13,9},{1... | collective-permute-start | bytes 884744 | tf_op jit(solution)/shard_map/ppermute | solution.py:187
  28.3 4.5 %collective-permute-start.6 = (f32[3,8,1536]{2,1,0:T(8,128)S(1)}, f32[3,8,1536]{2,1,0:T(8,128)S(1)}, u32[]{:S(2)}, u32[]{:S(2)}) collective-permute-start(f32[3,8,1536]{2,1,0:T(8,128)S(1)} %get-tuple-element.10.state), channel_id=1, source_target_pairs={{0,1},{1,2},{2,3},{4,5},{5,6},{6,7},{8,9},{9,10},{10,11},{12,13},{... | collective-permute-start | bytes 442376 | tf_op jit(solution)/shard_map/ppermute | solution.py:187
  31.4 4.9 %collective-permute-start.7 = (f32[3,8,1536]{2,1,0:T(8,128)S(1)}, f32[3,8,1536]{2,1,0:T(8,128)S(1)}, u32[]{:S(2)}, u32[]{:S(2)}) collective-permute-start(f32[3,8,1536]{2,1,0:T(8,128)S(1)} %get-tuple-element.10.state), channel_id=1, source_target_pairs={{1,0},{2,1},{3,2},{5,4},{6,5},{7,6},{9,8},{10,9},{11,10},{13,12},{... | collective-permute-start | bytes 442376 | tf_op jit(solution)/shard_map/ppermute | solution.py:187
  36.3 2.6 %copy-start.1 = (f32[1,3,8,1536]{3,2,1,0:T(8,128)S(1)}, f32[1,3,8,1536]{3,2,1,0:T(8,128)}, u32[]{:S(2)}) copy-start(f32[1,3,8,1536]{3,2,1,0:T(8,128)} %p.5) | copy-start | bytes 442372
  36.3 2.6 %copy-start.3 = (f32[1,3,8,1536]{3,2,1,0:T(8,128)S(1)}, f32[1,3,8,1536]{3,2,1,0:T(8,128)}, u32[]{:S(2)}) copy-start(f32[1,3,8,1536]{3,2,1,0:T(8,128)} %m.5) | copy-start | bytes 442372
  36.3 2.6 %copy-start.5 = (f32[1,3,8,1536]{3,2,1,0:T(8,128)S(1)}, f32[1,3,8,1536]{3,2,1,0:T(8,128)}, u32[]{:S(2)}) copy-start(f32[1,3,8,1536]{3,2,1,0:T(8,128)} %dvar.5) | copy-start | bytes 442372
  36.3 2.6 %copy-start.7 = (f32[1,3,8,1536]{3,2,1,0:T(8,128)S(1)}, f32[1,3,8,1536]{3,2,1,0:T(8,128)}, u32[]{:S(2)}) copy-start(f32[1,3,8,1536]{3,2,1,0:T(8,128)} %hobs.5) | copy-start | bytes 442372
  36.3 2.6 %copy-start.8 = (f32[1,3,8,1536]{3,2,1,0:T(8,128)S(1)}, f32[1,3,8,1536]{3,2,1,0:T(8,128)}, u32[]{:S(2)}) copy-start(f32[1,3,8,1536]{3,2,1,0:T(8,128)} %rvar.3) | copy-start | bytes 442372

commit v3 on v2

--- a/solution.py
+++ b/solution.py
@@ -23,50 +23,85 @@
     return pltpu.roll(field, rows - 1, 0) - pltpu.roll(field, 1, 0)
 
 
-def stacked(low, own, high, index):
-    return jnp.concatenate([low[index], own[index], high[index]], axis=0)
-
-
-def prep_kernel(p, m, dvar, hobs, depth, pair, straight):
+def even_lat():
+    return lax.axis_index("lat") % 2 == 0
+
+
+def has_previous():
+    return lax.axis_index("win") > 0
+
+
+def stacked(own, near, far, index):
+    even = even_lat()
+    low = jnp.where(even, far[index], near[index])
+    high = jnp.where(even, near[index], far[index])
+    return jnp.concatenate([low, own[index], high], axis=0)
+
+
+def prep_kernel(p, m, dvar, rvar, hobs, depth, pair, straight, pv, mv, dv, rv, hv, sems):
+    copies = [
+        pltpu.make_async_copy(p, pv, sems.at[0]),
+        pltpu.make_async_copy(dvar, dv, sems.at[1]),
+        pltpu.make_async_copy(m, mv, sems.at[2]),
+        pltpu.make_async_copy(hobs, hv, sems.at[3]),
+        pltpu.make_async_copy(rvar, rv, sems.at[4]),
+        pltpu.make_async_copy(depth, straight.at[0:1], sems.at[5]),
+    ]
+    for copy in copies:
+        copy.start()
+    for copy in copies:
+        copy.wait()
     for part in range(3):
-        pair[part] = p[0, part]
-        pair[3 + part] = dvar[0, part] * p[0, part]
-        straight[1 + part] = p[0, part] + hobs[0, part] * m[0, part]
-    straight[0] = depth[0]
-
-
-def adjoint_kernel(pair, pair_low, pair_high, straight, depth_low, depth_high, spin, inside, state, back):
-    depth = 0.25 * jnp.concatenate([depth_low[0], straight[0], depth_high[0]], axis=0)
+        up = dv[0, part] * pv[0, part]
+        seen = hv[0, part] * mv[0, part]
+        pair[part] = pv[0, part]
+        pair[3 + part] = up
+        straight[1 + part] = pv[0, part] + seen
+        straight[4 + part] = up + rv[0, part] * seen
+
+
+def adjoint(pair, pair_near, pair_far, straight, depth_near, depth_far, spin, inside, base):
+    depth = 0.25 * stacked(straight, depth_near, depth_far, 0)
     turn, keep = spin[...], inside[...]
+    adj_height, adj_east, adj_north = [stacked(pair, pair_near, pair_far, base + part) for part in range(3)]
+    for step in range(STEPS):
+        adj_mid = adj_east - turn * adj_north
+        adj_height = keep * (adj_height + 0.25 * (lat_gap(adj_north) + lon_gap(adj_mid)))
+        adj_north = adj_north + turn * adj_mid + depth * lat_gap(adj_height)
+        adj_east = adj_mid + depth * lon_gap(adj_height)
     rows = pair.shape[1]
-    for which in range(2):
-        base = 3 * which
-        adj_height = stacked(pair_low, pair, pair_high, base)
-        adj_east = stacked(pair_low, pair, pair_high, base + 1)
-        adj_north = stacked(pair_low, pair, pair_high, base + 2)
-        for step in range(STEPS):
-            adj_mid = adj_east - turn * adj_north
-            adj_height = keep * (adj_height + 0.25 * (lat_gap(adj_north) + lon_gap(adj_mid)))
-            adj_north = adj_north + turn * adj_mid + depth * lat_gap(adj_height)
-            adj_east = adj_mid + depth * lon_gap(adj_height)
-        for part, value in enumerate((adj_height, adj_east, adj_north)):
-            own = value[rows:2 * rows]
-            back[base + part] = own
-            if which == 0:
-                state[part] = straight[1 + part] - own
-
-
-def forward_kernel(state, state_low, state_high, straight, depth_low, depth_high, spin, inside, end):
-    depth = 0.25 * jnp.concatenate([depth_low[0], straight[0], depth_high[0]], axis=0)
+    return [value[rows:2 * rows] for value in (adj_height, adj_east, adj_north)]
+
+
+def first_adjoint_kernel(pair, pair_near, pair_far, straight, depth_near, depth_far, spin, inside, state, back):
+    swept = adjoint(pair, pair_near, pair_far, straight, depth_near, depth_far, spin, inside, 0)
+    link = has_previous()
+    for part, value in enumerate(swept):
+        back[part] = value
+        state[part] = jnp.where(link, straight[1 + part] - value, 0.0)
+
+
+def second_adjoint_kernel(pair, pair_near, pair_far, straight, depth_near, depth_far, spin, inside, state, tally):
+    swept = adjoint(pair, pair_near, pair_far, straight, depth_near, depth_far, spin, inside, 3)
+    link = has_previous()
+    cross = square = 0.0
+    for part, value in enumerate(swept):
+        zx = jnp.where(link, straight[4 + part] - value, 0.0)
+        cross += lane_sum(zx * state[part])
+        square += lane_sum(zx * zx)
+    tally[0] = cross
+    tally[1] = square
+
+
+def forward_kernel(state, state_near, state_far, straight, depth_near, depth_far, spin, inside, end):
+    depth = 0.25 * stacked(straight, depth_near, depth_far, 0)
     turn, keep = spin[...], inside[...]
-    rows = state.shape[1]
-    height = stacked(state_low, state, state_high, 0)
-    east = stacked(state_low, state, state_high, 1)
-    north = stacked(state_low, state, state_high, 2)
+    height, east, north = [stacked(state, state_near, state_far, part) for part in range(3)]
     for step in range(STEPS):
         height = keep * (height - (lon_gap(depth * east) + lat_gap(depth * north)))
         east = east + turn * north - 0.25 * lon_gap(height)
         north = north - turn * east - 0.25 * lat_gap(height)
+    rows = state.shape[1]
     for part, value in enumerate((height, east, north)):
         end[part] = value[rows:2 * rows]
 
@@ -79,17 +114,17 @@
     return total
 
 
-def inner_kernel(p, m, dvar, rvar, hobs, back, end, linked, sent):
-    moments = [0.0, 0.0, 0.0, 0.0]
-    link = linked[...]
+def inner_kernel(p, m, dvar, rvar, hobs, back, end, tally, sent):
+    last = lax.axis_index("win") == lax.axis_size("win") - 1
+    moments = [0.0, 0.0, 2.0 * tally[0], tally[1]]
     for part in range(3):
         dv, rv, hv = dvar[0, part], rvar[0, part], hobs[0, part]
         pv, mv = p[0, part], m[0, part]
         up, um = dv * pv, rv * mv
         ux = pv - back[part] + hv * mv
-        zp = dv * up + ux - link * end[part]
+        zp = dv * up + ux - end[part]
         zm = rv * um + hv * ux
-        zx = up - back[3 + part] + hv * um
+        zx = jnp.where(last, up + hv * um, 0.0)
         moments[0] += lane_sum(up * pv + um * mv)
         moments[1] += lane_sum(up * up + um * um + ux * ux)
         moments[2] += lane_sum(dv * up * up + rv * um * um + 2.0 * (zx * ux))
@@ -164,26 +199,33 @@
         increment[0, part] = y2 * (pv - back[part] + hobs[0, part] * mv)
 
 
-def run(kernel, out_shapes, *operands):
+def run(kernel, out_shapes, *operands, scratch=(), space=pltpu.VMEM, limit=32):
     shapes = [jax.ShapeDtypeStruct(shape, jnp.float32) for shape in out_shapes]
     size = sum(4 * operand.size for operand in operands) + sum(4 * shape.size for shape in shapes)
     return pl.pallas_call(
         kernel,
         out_shape=shapes,
-        in_specs=[pl.BlockSpec(memory_space=pltpu.VMEM)] * len(operands),
+        in_specs=[pl.BlockSpec(memory_space=space)] * len(operands),
         out_specs=[pl.BlockSpec(memory_space=pltpu.VMEM)] * len(shapes),
-        compiler_params=pltpu.CompilerParams(vmem_limit_bytes=32 * 1024 * 1024),
+        scratch_shapes=scratch,
+        compiler_params=pltpu.CompilerParams(vmem_limit_bytes=limit * 1024 * 1024),
         cost_estimate=pl.CostEstimate(flops=4 * size, bytes_accessed=size, transcendentals=0),
     )(*operands)
 
 
-def moved(value, win_step, lat_step):
+def shifted(value, step):
+    count = lax.axis_size("win")
+    initial, last = (max(0, -step), min(count, count - step))
+    return lax.ppermute(value, "win", [(source, source + step) for source in range(initial, last)])
+
+
+def swapped(value, first, win_step=0):
     wins, lats = lax.axis_size("win"), lax.axis_size("lat")
     pairs = []
-    for win in range(wins):
-        for lat in range(lats):
-            if 0 <= win + win_step < wins and 0 <= lat + lat_step < lats:
-                pairs.append((win * lats + lat, (win + win_step) * lats + lat + lat_step))
+    for win in range(wins - win_step):
+        for lat in range(first, lats - 1, 2):
+            for source, target in ((lat, lat + 1), (lat + 1, lat)):
+                pairs.append((win * lats + source, (win + win_step) * lats + target))
     return lax.ppermute(value, ("win", "lat"), pairs)
 
 
@@ -198,26 +240,26 @@
     spin = inside * (mass_rate * spin_rate * jnp.sin(latitude))
     inside = jnp.broadcast_to(inside[:, None], (3 * rows, width))
     spin = jnp.broadcast_to(spin[:, None], (3 * rows, width))
-    linked = jnp.full((rows, width), jnp.where(lax.axis_index("win") > 0, 1.0, 0.0))
-
-    depth_low, depth_high = moved(depth, 1, 1), moved(depth, 1, -1)
+    fields = (3, rows, width)
+
+    depth_near, depth_far = swapped(depth, 0, 1), swapped(depth, 1, 1)
     pair, straight = run(
-        prep_kernel, [(6, rows, width), (4, rows, width)], model_rhs, obs_rhs, model_var, obs_weight, depth
+        prep_kernel, [(6, rows, width), (7, rows, width)],
+        model_rhs, obs_rhs, model_var, obs_var, obs_weight, depth,
+        scratch=[pltpu.VMEM(model_rhs.shape, jnp.float32)] * 5 + [pltpu.SemaphoreType.DMA((6,))],
+        space=pltpu.HBM, limit=60,
     )
-    pair_low, pair_high = moved(pair, 0, 1), moved(pair, 0, -1)
-    came = moved(straight, 1, 0)
-    state, back = run(
-        adjoint_kernel, [(3, rows, width), (6, rows, width)],
-        pair, pair_low, pair_high, came, depth_low, depth_high, spin, inside,
-    )
-    state_low, state_high = moved(state, 0, 1), moved(state, 0, -1)
-    back = moved(back, -1, 0)
-    (end,) = run(
-        forward_kernel, [(3, rows, width)], state, state_low, state_high, came, depth_low, depth_high, spin, inside
-    )
+    came = shifted(straight, 1)
+    pair_near, pair_far = swapped(pair, 0), swapped(pair, 1)
+    known = (pair, pair_near, pair_far, came, depth_near, depth_far, spin, inside)
+    state, back = run(first_adjoint_kernel, [fields, fields], *known)
+    back = shifted(back, -1)
+    state_near, state_far = swapped(state, 0), swapped(state, 1)
+    (tally,) = run(second_adjoint_kernel, [(2, rows, 128)], *known, state)
+    (end,) = run(forward_kernel, [fields], state, state_near, state_far, came, depth_near, depth_far, spin, inside)
     (sent,) = run(
         inner_kernel, [(8 * ranks, 128)],
-        model_rhs, obs_rhs, model_var, obs_var, obs_weight, back, end, linked,
+        model_rhs, obs_rhs, model_var, obs_var, obs_weight, back, end, tally,
     )
     gathered = lax.all_to_all(sent, ("win", "lat"), 0, 0, tiled=True)
     return run(

time: 57.9 us -> 45.9 us (0.79)
  starting transfers between devices: 20.4 us -> 15.9 us
  local copies, waits for them, and re-layouts: 3.81 us -> 0.19 us
  waiting for transfers between devices: 9.6 us -> 6.02 us
  blocking collectives: 16.9 us -> 15.4 us
  Pallas kernels: 5.92 us -> 7.21 us
    ppermute x8, starting transfers between devices: 20.4 us -> 15.9 us  [the longest x6 9.6 us: swapped(): return lax.ppermute(value, ('win', 'lat'), pairs)]
    unnamed x18 -> x14, local copies, waits for them, and re-layouts: 3.65 us -> 0.04 us
    ppermute x8, waiting for transfers between devices: 9.6 us -> 6.02 us  [the longest x2 4.84 us: shifted(): lax.ppermute(value, 'win', [(source, source + step) for source in range(i...]
    all_to_all x1, blocking collectives: 16.9 us -> 15.4 us  [body(): gathered = lax.all_to_all(sent, ('win', 'lat'), 0, 0, tiled=True)]
    pallas_call x5 -> x6, Pallas kernels: 5.92 us -> 7.21 us  [run(): pl.pallas_call(kernel, out_shape=shapes, in_specs=[pl.BlockSpec(memory_sp...]
  transfers between devices with their start and end apart: 8 -> 8, of which waited for: 3 -> 2; matrix products, arithmetic and copies ran while one was open for 0% -> 0% of each run, Pallas kernels for 2% -> 5%
where the time goes in v3:
time: 45.9 us; the launch traced here: 45.6 us
  starting transfers between devices  15.9 us (35%)
  blocking collectives  15.4 us (34%)
  Pallas kernels  7.21 us (16%)
  waiting for transfers between devices  6.02 us (13%)
  between operations  0.87 us (2%)
    all_to_all x1, blocking collectives, body(): gathered = lax.all_to_all(sent, ('win', 'lat'), 0, 0, tiled=True)  15.4 us
    ppermute x6, starting transfers between devices, swapped(): return lax.ppermute(value, ('win', 'lat'), pairs)  9.6 us
    pallas_call x6, Pallas kernels, run(): pl.pallas_call(kernel, out_shape=shapes, in_specs=[pl.BlockSpec(memory_sp...  7.21 us
    ppermute x2, starting transfers between devices, shifted(): lax.ppermute(value, 'win', [(source, source + step) for source in range(i...  6.32 us
    ppermute x2, waiting for transfers between devices, shifted(): lax.ppermute(value, 'win', [(source, source + step) for source in range(i...  4.84 us
    ppermute x6, waiting for transfers between devices, swapped(): return lax.ppermute(value, ('win', 'lat'), pairs)  1.19 us
  transfers between devices with their start and end apart: 8, of which 2 were waited for; matrix products, arithmetic and copies ran while one was open for 0% of the time, Pallas kernels for 5%

profile of v3, /device:TPU:0, one launch (start us, length us, event | category | flops | bytes accessed | tf_op | source)
XLA Modules:
  0.0 45.6 jit_solution(3997364537269243939)
XLA Ops:
  0.6 2.2 %shard_map.85 = (f32[6,8,1536]{2,1,0:T(8,128)}, f32[7,8,1536]{2,1,0:T(8,128)}) custom-call(f32[1,3,8,1536]{3,2,1,0:T(8,128)} %p.5, f32[1,3,8,1536]{3,2,1,0:T(8,128)} %m.5, f32[1,3,8,1536]{3,2,1,0:T(8,128)} %dvar.5, f32[1,3,8,1536]{3,2,1,0:T(8,128)} %rvar.5, f32[1,3,8,1536]{3,2,1,0:T(8,128)} %hobs.5, f32[1,8,1536]{2,1,0:T(8,128)} %depth.1), custom_call_target="tpu_custom_call" | custom-call | flops 5701632 | bytes 1425408 | tf_op jit(solution)/shard_map/pallas_call | solution.py:205
  2.8 5.0 %collective-permute-start.2 = (f32[7,8,1536]{2,1,0:T(8,128)}, f32[7,8,1536]{2,1,0:T(8,128)S(1)}, u32[]{:S(2)}, u32[]{:S(2)}) collective-permute-start(f32[7,8,1536]{2,1,0:T(8,128)} %get-tuple-element.8), channel_id=1, source_target_pairs={{0,4},{4,8},{8,12},{12,16},{16,20},{20,24},{24,28},{1,5},{5,9},{9,... | collective-permute-start | bytes 1032200 | tf_op jit(solution)/shard_map/ppermute | solution.py:219
  7.8 0.1 collective-permute-start
  7.9 0.7 %collective-permute-start.1 = (f32[6,8,1536]{2,1,0:T(8,128)}, f32[6,8,1536]{2,1,0:T(8,128)S(1)}, u32[]{:S(2)}, u32[]{:S(2)}) collective-permute-start(f32[6,8,1536]{2,1,0:T(8,128)} %get-tuple-element.7.pair), channel_id=1, source_target_pairs={{1,2},{2,1},{5,6},{6,5},{9,10},{10,9},{13,14},{14,13},{17,18},{18,... | collective-permute-start | bytes 884744 | tf_op jit(solution)/shard_map/ppermute | solution.py:229
  8.6 5.8 %collective-permute-start.3 = (f32[1,8,1536]{2,1,0:T(8,128)S(1)}, f32[1,8,1536]{2,1,0:T(8,128)S(1)}, u32[]{:S(2)}, u32[]{:S(2)}) collective-permute-start(f32[1,8,1536]{2,1,0:T(8,128)S(1)} %copy-done.6), channel_id=1, source_target_pairs={{0,5},{1,4},{2,7},{3,6},{4,9},{5,8},{6,11},{7,10},{8,13},{9,12},{1... | collective-permute-start | bytes 147464 | tf_op jit(solution)/shard_map/ppermute | solution.py:229
  14.5 0.7 %collective-permute-start.4 = (f32[1,8,1536]{2,1,0:T(8,128)S(1)}, f32[1,8,1536]{2,1,0:T(8,128)S(1)}, u32[]{:S(2)}, u32[]{:S(2)}) collective-permute-start(f32[1,8,1536]{2,1,0:T(8,128)S(1)} %copy-done.6), channel_id=1, source_target_pairs={{1,6},{2,5},{5,10},{6,9},{9,14},{10,13},{13,18},{14,17},{17,22},{1... | collective-permute-start | bytes 147464 | tf_op jit(solution)/shard_map/ppermute | solution.py:229
  15.2 1.2 %collective-permute-done.3.depth_near = f32[1,8,1536]{2,1,0:T(8,128)S(1)} collective-permute-done((f32[1,8,1536]{2,1,0:T(8,128)S(1)}, f32[1,8,1536]{2,1,0:T(8,128)S(1)}, u32[]{:S(2)}, u32[]{:S(2)}) %collective-permute-start.3) | collective-permute-done | bytes 49184 | tf_op jit(solution)/shard_map/ppermute | solution.py:229
  16.4 0.0 collective-permute-done.4.depth_far
  16.4 0.0 collective-permute-done.pair_near
  16.4 0.0 collective-permute-done.1.pair_far
  16.4 0.0 collective-permute-done.2.straight
  16.4 0.1 broadcast_in_dim.4.spin
  16.5 0.1 broadcast_in_dim.5.inside
  16.6 0.0 copy-done.5
  16.6 1.2 %shard_map.86 = (f32[3,8,1536]{2,1,0:T(8,128)S(1)}, f32[3,8,1536]{2,1,0:T(8,128)S(1)}) custom-call(f32[6,8,1536]{2,1,0:T(8,128)S(1)} %copy-done.5, f32[6,8,1536]{2,1,0:T(8,128)S(1)} %collective-permute-done.pair_near, f32[6,8,1536]{2,1,0:T(8,128)S(1)} %collective-permute-done.1.pair_far, f32[7,8,1536]{2,1,0:T(8,128)S(1)} %collective-permute-done.2.straight, ...), custom_call_target="tpu_custom_call" | custom-call | flops 7667712 | bytes 1916928 | tf_op jit(solution)/shard_map/pallas_call | solution.py:205
  17.8 1.7 %collective-permute-start.6 = (f32[3,8,1536]{2,1,0:T(8,128)S(1)}, f32[3,8,1536]{2,1,0:T(8,128)S(1)}, u32[]{:S(2)}, u32[]{:S(2)}) collective-permute-start(f32[3,8,1536]{2,1,0:T(8,128)S(1)} %get-tuple-element.10.state), channel_id=1, source_target_pairs={{0,1},{1,0},{2,3},{3,2},{4,5},{5,4},{6,7},{7,6},{8,9},{9,8},{10,11... | collective-permute-start | bytes 442376 | tf_op jit(solution)/shard_map/ppermute | solution.py:229
  19.4 0.7 %collective-permute-start.7 = (f32[3,8,1536]{2,1,0:T(8,128)S(1)}, f32[3,8,1536]{2,1,0:T(8,128)S(1)}, u32[]{:S(2)}, u32[]{:S(2)}) collective-permute-start(f32[3,8,1536]{2,1,0:T(8,128)S(1)} %get-tuple-element.10.state), channel_id=1, source_target_pairs={{1,2},{2,1},{5,6},{6,5},{9,10},{10,9},{13,14},{14,13},{17,18},{18,... | collective-permute-start | bytes 442376 | tf_op jit(solution)/shard_map/ppermute | solution.py:229
  20.1 1.3 %collective-permute-start.5 = (f32[3,8,1536]{2,1,0:T(8,128)S(1)}, f32[3,8,1536]{2,1,0:T(8,128)S(1)}, u32[]{:S(2)}, u32[]{:S(2)}) collective-permute-start(f32[3,8,1536]{2,1,0:T(8,128)S(1)} %get-tuple-element.9), channel_id=1, source_target_pairs={{4,0},{8,4},{12,8},{16,12},{20,16},{24,20},{28,24},{5,1},{9,5},{13... | collective-permute-start | bytes 442376 | tf_op jit(solution)/shard_map/ppermute | solution.py:219
  21.4 1.2 %shard_map.88.tally = f32[2,8,128]{2,1,0:T(8,128)S(1)} custom-call(f32[6,8,1536]{2,1,0:T(8,128)S(1)} %copy-done.5, f32[6,8,1536]{2,1,0:T(8,128)S(1)} %collective-permute-done.pair_near, f32[6,8,1536]{2,1,0:T(8,128)S(1)} %collective-permute-done.1.pair_far, f32[7,8,1536]{2,1,0:T(8,128)S(1)} %collective-permute-done.2.straight, ...), custom_call_target="tpu_custom_call" | custom-call | flops 7110656 | bytes 1777664 | tf_op jit(solution)/shard_map/pallas_call | solution.py:205
  22.6 0.0 copy-start
  22.6 0.0 copy-start.1
  22.6 0.0 copy-start.2
  22.6 0.0 copy-start.3
  22.6 0.0 copy-start.4
  22.6 0.0 collective-permute-done.6.state_near
  22.7 0.0 collective-permute-done.7.state_far
  22.7 1.1 %shard_map.87.end = f32[3,8,1536]{2,1,0:T(8,128)S(1)} custom-call(f32[3,8,1536]{2,1,0:T(8,128)S(1)} %get-tuple-element.10.state, f32[3,8,1536]{2,1,0:T(8,128)S(1)} %collective-permute-done.6.state_near, f32[3,8,1536]{2,1,0:T(8,128)S(1)} %collective-permute-done.7.state_far, f32[7,8,1536]{2,1,0:T(8,128)S(1)} %collective-permute-done.2.straight, ...), custom_call_target="tpu_custom_call" | custom-call | flops 5308416 | bytes 1327104 | tf_op jit(solution)/shard_map/pallas_call | solution.py:205
  23.8 4.8 %collective-permute-done.5.back = f32[3,8,1536]{2,1,0:T(8,128)S(1)} collective-permute-done((f32[3,8,1536]{2,1,0:T(8,128)S(1)}, f32[3,8,1536]{2,1,0:T(8,128)S(1)}, u32[]{:S(2)}, u32[]{:S(2)}) %collective-permute-start.5) | collective-permute-done | bytes 147488 | tf_op jit(solution)/shard_map/ppermute | solution.py:219
  28.7 0.0 copy-done.1
  28.7 0.2 shard_map.89
  28.9 15.4 %all_to_all.11 = f32[32,8,128]{2,1,0:T(8,128)S(1)} all-to-all(f32[32,8,128]{2,1,0:T(8,128)S(1)} %bitcast.2), channel_id=1, replica_groups=mesh['win'=8,'lat'=4] {'win','lat'}, dimensions={0} | all-to-all | bytes 262144 | tf_op jit(solution)/shard_map/all_to_all | solution.py:264
  44.3 1.3 %shard_map.90 = (f32[1,3,8,1536]{3,2,1,0:T(8,128)}, f32[1,3,8,1536]{3,2,1,0:T(8,128)}, f32[1,3,8,1536]{3,2,1,0:T(8,128)}) custom-call(f32[256,128]{1,0:T(8,128)S(1)} %bitcast.3, f32[1,3,8,1536]{3,2,1,0:T(8,128)S(1)} %copy-done, f32[1,3,8,1536]{3,2,1,0:T(8,128)S(1)} %copy-done.1, f32[1,3,8,1536]{3,2,1,0:T(8,128)S(1)} %copy-done.2, ...), custom_call_target="tpu_custom_call" | custom-call | flops 5832704 | bytes 1458176 | tf_op jit(solution)/shard_map/pallas_call | solution.py:205
  (9 shorter events, 0.1 us)
Async XLA Ops:
  0.6 8.0 %copy-start.6 = (f32[1,8,1536]{2,1,0:T(8,128)S(1)}, f32[1,8,1536]{2,1,0:T(8,128)}, u32[]{:S(2)}) copy-start(f32[1,8,1536]{2,1,0:T(8,128)} %depth.1) | copy-start | bytes 147460
  2.8 13.8 %copy-start.5 = (f32[6,8,1536]{2,1,0:T(8,128)S(1)}, f32[6,8,1536]{2,1,0:T(8,128)}, u32[]{:S(2)}) copy-start(f32[6,8,1536]{2,1,0:T(8,128)} %get-tuple-element.7.pair) | copy-start | bytes 884740
  2.8 13.6 %collective-permute-start.2 = (f32[7,8,1536]{2,1,0:T(8,128)}, f32[7,8,1536]{2,1,0:T(8,128)S(1)}, u32[]{:S(2)}, u32[]{:S(2)}) collective-permute-start(f32[7,8,1536]{2,1,0:T(8,128)} %get-tuple-element.8), channel_id=1, source_target_pairs={{0,4},{4,8},{8,12},{12,16},{16,20},{20,24},{24,28},{1,5},{5,9},{9,... | collective-permute-start | bytes 1032200 | tf_op jit(solution)/shard_map/ppermute | solution.py:219
  7.8 8.6 %collective-permute-start = (f32[6,8,1536]{2,1,0:T(8,128)}, f32[6,8,1536]{2,1,0:T(8,128)S(1)}, u32[]{:S(2)}, u32[]{:S(2)}) collective-permute-start(f32[6,8,1536]{2,1,0:T(8,128)} %get-tuple-element.7.pair), channel_id=1, source_target_pairs={{0,1},{1,0},{2,3},{3,2},{4,5},{5,4},{6,7},{7,6},{8,9},{9,8},{10,11... | collective-permute-start | bytes 884744 | tf_op jit(solution)/shard_map/ppermute | solution.py:229
  7.9 8.5 %collective-permute-start.1 = (f32[6,8,1536]{2,1,0:T(8,128)}, f32[6,8,1536]{2,1,0:T(8,128)S(1)}, u32[]{:S(2)}, u32[]{:S(2)}) collective-permute-start(f32[6,8,1536]{2,1,0:T(8,128)} %get-tuple-element.7.pair), channel_id=1, source_target_pairs={{1,2},{2,1},{5,6},{6,5},{9,10},{10,9},{13,14},{14,13},{17,18},{18,... | collective-permute-start | bytes 884744 | tf_op jit(solution)/shard_map/ppermute | solution.py:229
  8.6 7.8 %collective-permute-start.3 = (f32[1,8,1536]{2,1,0:T(8,128)S(1)}, f32[1,8,1536]{2,1,0:T(8,128)S(1)}, u32[]{:S(2)}, u32[]{:S(2)}) collective-permute-start(f32[1,8,1536]{2,1,0:T(8,128)S(1)} %copy-done.6), channel_id=1, source_target_pairs={{0,5},{1,4},{2,7},{3,6},{4,9},{5,8},{6,11},{7,10},{8,13},{9,12},{1... | collective-permute-start | bytes 147464 | tf_op jit(solution)/shard_map/ppermute | solution.py:229
  14.5 1.9 %collective-permute-start.4 = (f32[1,8,1536]{2,1,0:T(8,128)S(1)}, f32[1,8,1536]{2,1,0:T(8,128)S(1)}, u32[]{:S(2)}, u32[]{:S(2)}) collective-permute-start(f32[1,8,1536]{2,1,0:T(8,128)S(1)} %copy-done.6), channel_id=1, source_target_pairs={{1,6},{2,5},{5,10},{6,9},{9,14},{10,13},{13,18},{14,17},{17,22},{1... | collective-permute-start | bytes 147464 | tf_op jit(solution)/shard_map/ppermute | solution.py:229
  17.8 4.9 %collective-permute-start.6 = (f32[3,8,1536]{2,1,0:T(8,128)S(1)}, f32[3,8,1536]{2,1,0:T(8,128)S(1)}, u32[]{:S(2)}, u32[]{:S(2)}) collective-permute-start(f32[3,8,1536]{2,1,0:T(8,128)S(1)} %get-tuple-element.10.state), channel_id=1, source_target_pairs={{0,1},{1,0},{2,3},{3,2},{4,5},{5,4},{6,7},{7,6},{8,9},{9,8},{10,11... | collective-permute-start | bytes 442376 | tf_op jit(solution)/shard_map/ppermute | solution.py:229
  19.4 3.2 %collective-permute-start.7 = (f32[3,8,1536]{2,1,0:T(8,128)S(1)}, f32[3,8,1536]{2,1,0:T(8,128)S(1)}, u32[]{:S(2)}, u32[]{:S(2)}) collective-permute-start(f32[3,8,1536]{2,1,0:T(8,128)S(1)} %get-tuple-element.10.state), channel_id=1, source_target_pairs={{1,2},{2,1},{5,6},{6,5},{9,10},{10,9},{13,14},{14,13},{17,18},{18,... | collective-permute-start | bytes 442376 | tf_op jit(solution)/shard_map/ppermute | solution.py:229
  20.1 8.6 %collective-permute-start.5 = (f32[3,8,1536]{2,1,0:T(8,128)S(1)}, f32[3,8,1536]{2,1,0:T(8,128)S(1)}, u32[]{:S(2)}, u32[]{:S(2)}) collective-permute-start(f32[3,8,1536]{2,1,0:T(8,128)S(1)} %get-tuple-element.9), channel_id=1, source_target_pairs={{4,0},{8,4},{12,8},{16,12},{20,16},{24,20},{28,24},{5,1},{9,5},{13... | collective-permute-start | bytes 442376 | tf_op jit(solution)/shard_map/ppermute | solution.py:219
  22.6 6.1 %copy-start = (f32[1,3,8,1536]{3,2,1,0:T(8,128)S(1)}, f32[1,3,8,1536]{3,2,1,0:T(8,128)}, u32[]{:S(2)}) copy-start(f32[1,3,8,1536]{3,2,1,0:T(8,128)} %p.5) | copy-start | bytes 442372
  22.6 6.1 %copy-start.1 = (f32[1,3,8,1536]{3,2,1,0:T(8,128)S(1)}, f32[1,3,8,1536]{3,2,1,0:T(8,128)}, u32[]{:S(2)}) copy-start(f32[1,3,8,1536]{3,2,1,0:T(8,128)} %m.5) | copy-start | bytes 442372
  22.6 6.1 %copy-start.2 = (f32[1,3,8,1536]{3,2,1,0:T(8,128)S(1)}, f32[1,3,8,1536]{3,2,1,0:T(8,128)}, u32[]{:S(2)}) copy-start(f32[1,3,8,1536]{3,2,1,0:T(8,128)} %dvar.5) | copy-start | bytes 442372
  22.6 6.0 %copy-start.3 = (f32[1,3,8,1536]{3,2,1,0:T(8,128)S(1)}, f32[1,3,8,1536]{3,2,1,0:T(8,128)}, u32[]{:S(2)}) copy-start(f32[1,3,8,1536]{3,2,1,0:T(8,128)} %rvar.5) | copy-start | bytes 442372
  22.6 6.0 %copy-start.4 = (f32[1,3,8,1536]{3,2,1,0:T(8,128)S(1)}, f32[1,3,8,1536]{3,2,1,0:T(8,128)}, u32[]{:S(2)}) copy-start(f32[1,3,8,1536]{3,2,1,0:T(8,128)} %hobs.5) | copy-start | bytes 442372

commit v4 on v3

--- a/solution.py
+++ b/solution.py
@@ -131,8 +131,7 @@
         moments[3] += lane_sum(zp * zp + zm * zm + zx * zx)
     rows = [jnp.sum(value, axis=0, keepdims=True) for value in moments]
     tile = jnp.concatenate(rows + rows, axis=0)
-    for rank in range(sent.shape[0] // 8):
-        sent[8 * rank:8 * rank + 8] = tile
+    sent[...] = tile
 
 
 def two_sum(a, b):
@@ -231,7 +230,6 @@
 
 def body(model_rhs, obs_rhs, model_var, obs_var, obs_weight, depth):
     rows, width = model_rhs.shape[2:]
-    ranks = lax.axis_size("win") * lax.axis_size("lat")
     total_rows = rows * lax.axis_size("lat")
     offset = (GRID_ROWS - total_rows) // 2
     local_rows = lax.axis_index("lat") * rows - rows + jnp.arange(3 * rows, dtype=jnp.int32)
@@ -258,10 +256,10 @@
     (tally,) = run(second_adjoint_kernel, [(2, rows, 128)], *known, state)
     (end,) = run(forward_kernel, [fields], state, state_near, state_far, came, depth_near, depth_far, spin, inside)
     (sent,) = run(
-        inner_kernel, [(8 * ranks, 128)],
+        inner_kernel, [(8, 128)],
         model_rhs, obs_rhs, model_var, obs_var, obs_weight, back, end, tally,
     )
-    gathered = lax.all_to_all(sent, ("win", "lat"), 0, 0, tiled=True)
+    gathered = lax.all_gather(sent, ("win", "lat"), axis=0, tiled=True)
     return run(
         combine_kernel, [model_rhs.shape] * 3,
         gathered, model_rhs, obs_rhs, model_var, obs_var, obs_weight, back,

time: 45.9 us -> 73.1 us (1.59)
  blocking collectives: 15.4 us -> 42.6 us
    all_gather x0 -> x1, blocking collectives: none -> 42.6 us  [body(): gathered = lax.all_gather(sent, ('win', 'lat'), axis=0, tiled=True)]
    all_to_all x1 -> x0, blocking collectives: 15.4 us -> none  [body(): gathered = lax.all_to_all(sent, ('win', 'lat'), 0, 0, tiled=True)]
  transfers between devices with their start and end apart: 8 -> 8, of which waited for: 2 -> 2; matrix products, arithmetic and copies ran while one was open for 0% -> 0% of each run, Pallas kernels for 5% -> 3%
where the time goes in v4:
time: 73.1 us; the launch traced here: 72.9 us
  blocking collectives  42.6 us (58%)
  starting transfers between devices  15.9 us (22%)
  Pallas kernels  7.2 us (10%)
  waiting for transfers between devices  6.02 us (8%)
  between operations  0.86 us (1%)
    all_gather x1, blocking collectives, body(): gathered = lax.all_gather(sent, ('win', 'lat'), axis=0, tiled=True)  42.6 us
    ppermute x6, starting transfers between devices, swapped(): return lax.ppermute(value, ('win', 'lat'), pairs)  9.6 us
    pallas_call x6, Pallas kernels, run(): pl.pallas_call(kernel, out_shape=shapes, in_specs=[pl.BlockSpec(memory_sp...  7.2 us
    ppermute x2, starting transfers between devices, shifted(): lax.ppermute(value, 'win', [(source, source + step) for source in range(i...  6.32 us
    ppermute x2, waiting for transfers between devices, shifted(): lax.ppermute(value, 'win', [(source, source + step) for source in range(i...  4.84 us
  transfers between devices with their start and end apart: 8, of which 2 were waited for; matrix products, arithmetic and copies ran while one was open for 0% of the time, Pallas kernels for 3%

profile of v4, /device:TPU:0, one launch (start us, length us, event | category | flops | bytes accessed | tf_op | source)
XLA Modules:
  0.0 72.9 jit_solution(14740221558099504460)
XLA Ops:
  0.6 0.0 copy-start.6
  0.6 2.2 %shard_map.85 = (f32[6,8,1536]{2,1,0:T(8,128)}, f32[7,8,1536]{2,1,0:T(8,128)}) custom-call(f32[1,3,8,1536]{3,2,1,0:T(8,128)} %p.5, f32[1,3,8,1536]{3,2,1,0:T(8,128)} %m.5, f32[1,3,8,1536]{3,2,1,0:T(8,128)} %dvar.5, f32[1,3,8,1536]{3,2,1,0:T(8,128)} %rvar.5, f32[1,3,8,1536]{3,2,1,0:T(8,128)} %hobs.5, f32[1,8,1536]{2,1,0:T(8,128)} %depth.1), custom_call_target="tpu_custom_call" | custom-call | flops 5701632 | bytes 1425408 | tf_op jit(solution)/shard_map/pallas_call | solution.py:204
  2.8 0.0 copy-start.5
  2.8 5.0 %collective-permute-start.2 = (f32[7,8,1536]{2,1,0:T(8,128)}, f32[7,8,1536]{2,1,0:T(8,128)S(1)}, u32[]{:S(2)}, u32[]{:S(2)}) collective-permute-start(f32[7,8,1536]{2,1,0:T(8,128)} %get-tuple-element.8), channel_id=1, source_target_pairs={{0,4},{4,8},{8,12},{12,16},{16,20},{20,24},{24,28},{1,5},{5,9},{9,... | collective-permute-start | bytes 1032200 | tf_op jit(solution)/shard_map/ppermute | solution.py:218
  7.8 0.1 collective-permute-start
  7.9 0.7 collective-permute-start.1
  8.6 5.8 %collective-permute-start.3 = (f32[1,8,1536]{2,1,0:T(8,128)S(1)}, f32[1,8,1536]{2,1,0:T(8,128)S(1)}, u32[]{:S(2)}, u32[]{:S(2)}) collective-permute-start(f32[1,8,1536]{2,1,0:T(8,128)S(1)} %copy-done.6), channel_id=1, source_target_pairs={{0,5},{1,4},{2,7},{3,6},{4,9},{5,8},{6,11},{7,10},{8,13},{9,12},{1... | collective-permute-start | bytes 147464 | tf_op jit(solution)/shard_map/ppermute | solution.py:228
  14.5 0.7 collective-permute-start.4
  15.2 1.2 %collective-permute-done.3.depth_near = f32[1,8,1536]{2,1,0:T(8,128)S(1)} collective-permute-done((f32[1,8,1536]{2,1,0:T(8,128)S(1)}, f32[1,8,1536]{2,1,0:T(8,128)S(1)}, u32[]{:S(2)}, u32[]{:S(2)}) %collective-permute-start.3) | collective-permute-done | bytes 49184 | tf_op jit(solution)/shard_map/ppermute | solution.py:228
  16.4 0.0 collective-permute-done.4.depth_far
  16.4 0.0 collective-permute-done.pair_near
  16.4 0.0 collective-permute-done.1.pair_far
  16.4 0.0 collective-permute-done.2.straight
  16.4 0.1 broadcast_in_dim.4.spin
  16.5 0.1 broadcast_in_dim.5.inside
  16.6 1.2 %shard_map.86 = (f32[3,8,1536]{2,1,0:T(8,128)S(1)}, f32[3,8,1536]{2,1,0:T(8,128)S(1)}) custom-call(f32[6,8,1536]{2,1,0:T(8,128)S(1)} %copy-done.5, f32[6,8,1536]{2,1,0:T(8,128)S(1)} %collective-permute-done.pair_near, f32[6,8,1536]{2,1,0:T(8,128)S(1)} %collective-permute-done.1.pair_far, f32[7,8,1536]{2,1,0:T(8,128)S(1)} %collective-permute-done.2.straight, ...), custom_call_target="tpu_custom_call" | custom-call | flops 7667712 | bytes 1916928 | tf_op jit(solution)/shard_map/pallas_call | solution.py:204
  17.8 1.7 %collective-permute-start.6 = (f32[3,8,1536]{2,1,0:T(8,128)S(1)}, f32[3,8,1536]{2,1,0:T(8,128)S(1)}, u32[]{:S(2)}, u32[]{:S(2)}) collective-permute-start(f32[3,8,1536]{2,1,0:T(8,128)S(1)} %get-tuple-element.10.state), channel_id=1, source_target_pairs={{0,1},{1,0},{2,3},{3,2},{4,5},{5,4},{6,7},{7,6},{8,9},{9,8},{10,11... | collective-permute-start | bytes 442376 | tf_op jit(solution)/shard_map/ppermute | solution.py:228
  19.4 0.7 collective-permute-start.7
  20.1 1.3 %collective-permute-start.5 = (f32[3,8,1536]{2,1,0:T(8,128)S(1)}, f32[3,8,1536]{2,1,0:T(8,128)S(1)}, u32[]{:S(2)}, u32[]{:S(2)}) collective-permute-start(f32[3,8,1536]{2,1,0:T(8,128)S(1)} %get-tuple-element.9), channel_id=1, source_target_pairs={{4,0},{8,4},{12,8},{16,12},{20,16},{24,20},{28,24},{5,1},{9,5},{13... | collective-permute-start | bytes 442376 | tf_op jit(solution)/shard_map/ppermute | solution.py:218
  21.4 1.2 %shard_map.88.tally = f32[2,8,128]{2,1,0:T(8,128)S(1)} custom-call(f32[6,8,1536]{2,1,0:T(8,128)S(1)} %copy-done.5, f32[6,8,1536]{2,1,0:T(8,128)S(1)} %collective-permute-done.pair_near, f32[6,8,1536]{2,1,0:T(8,128)S(1)} %collective-permute-done.1.pair_far, f32[7,8,1536]{2,1,0:T(8,128)S(1)} %collective-permute-done.2.straight, ...), custom_call_target="tpu_custom_call" | custom-call | flops 7110656 | bytes 1777664 | tf_op jit(solution)/shard_map/pallas_call | solution.py:204
  22.6 0.0 copy-start
  22.6 0.0 copy-start.1
  22.6 0.0 copy-start.2
  22.6 0.0 copy-start.3
  22.6 0.0 copy-start.4
  22.6 0.0 collective-permute-done.6.state_near
  22.7 0.0 collective-permute-done.7.state_far
  22.7 1.1 %shard_map.87.end = f32[3,8,1536]{2,1,0:T(8,128)S(1)} custom-call(f32[3,8,1536]{2,1,0:T(8,128)S(1)} %get-tuple-element.10.state, f32[3,8,1536]{2,1,0:T(8,128)S(1)} %collective-permute-done.6.state_near, f32[3,8,1536]{2,1,0:T(8,128)S(1)} %collective-permute-done.7.state_far, f32[7,8,1536]{2,1,0:T(8,128)S(1)} %collective-permute-done.2.straight, ...), custom_call_target="tpu_custom_call" | custom-call | flops 5308416 | bytes 1327104 | tf_op jit(solution)/shard_map/pallas_call | solution.py:204
  23.8 4.8 %collective-permute-done.5.back = f32[3,8,1536]{2,1,0:T(8,128)S(1)} collective-permute-done((f32[3,8,1536]{2,1,0:T(8,128)S(1)}, f32[3,8,1536]{2,1,0:T(8,128)S(1)}, u32[]{:S(2)}, u32[]{:S(2)}) %collective-permute-start.5) | collective-permute-done | bytes 147488 | tf_op jit(solution)/shard_map/ppermute | solution.py:218
  28.7 0.2 shard_map.89
  28.9 42.6 %all_gather.3.gathered = f32[256,128]{1,0:T(8,128)S(1)} all-gather(f32[8,128]{1,0:T(8,128)S(1)} %shard_map.89), channel_id=1, replica_groups=mesh['win'=8,'lat'=4] {'win','lat'}, dimensions={0}, use_global_device_ids=true | all-gather | bytes 135168 | tf_op jit(solution)/shard_map/all_gather | solution.py:262
  71.5 1.3 %shard_map.90 = (f32[1,3,8,1536]{3,2,1,0:T(8,128)}, f32[1,3,8,1536]{3,2,1,0:T(8,128)}, f32[1,3,8,1536]{3,2,1,0:T(8,128)}) custom-call(f32[256,128]{1,0:T(8,128)S(1)} %all_gather.3.gathered, f32[1,3,8,1536]{3,2,1,0:T(8,128)S(1)} %copy-done, f32[1,3,8,1536]{3,2,1,0:T(8,128)S(1)} %copy-done.1, f32[1,3,8,1536]{3,2,1,0:T(8,128)S(1)} %copy-done.2, ...), custom_call_target="tpu_custom_call" | custom-call | flops 5832704 | bytes 1458176 | tf_op jit(solution)/shard_map/pallas_call | solution.py:204
  (9 shorter events, 0.1 us)
Async XLA Ops:
  0.6 8.0 %copy-start.6 = (f32[1,8,1536]{2,1,0:T(8,128)S(1)}, f32[1,8,1536]{2,1,0:T(8,128)}, u32[]{:S(2)}) copy-start(f32[1,8,1536]{2,1,0:T(8,128)} %depth.1) | copy-start | bytes 147460
  2.8 13.8 %copy-start.5 = (f32[6,8,1536]{2,1,0:T(8,128)S(1)}, f32[6,8,1536]{2,1,0:T(8,128)}, u32[]{:S(2)}) copy-start(f32[6,8,1536]{2,1,0:T(8,128)} %get-tuple-element.7.pair) | copy-start | bytes 884740
  2.8 13.6 %collective-permute-start.2 = (f32[7,8,1536]{2,1,0:T(8,128)}, f32[7,8,1536]{2,1,0:T(8,128)S(1)}, u32[]{:S(2)}, u32[]{:S(2)}) collective-permute-start(f32[7,8,1536]{2,1,0:T(8,128)} %get-tuple-element.8), channel_id=1, source_target_pairs={{0,4},{4,8},{8,12},{12,16},{16,20},{20,24},{24,28},{1,5},{5,9},{9,... | collective-permute-start | bytes 1032200 | tf_op jit(solution)/shard_map/ppermute | solution.py:218
  7.8 8.6 %collective-permute-start = (f32[6,8,1536]{2,1,0:T(8,128)}, f32[6,8,1536]{2,1,0:T(8,128)S(1)}, u32[]{:S(2)}, u32[]{:S(2)}) collective-permute-start(f32[6,8,1536]{2,1,0:T(8,128)} %get-tuple-element.7.pair), channel_id=1, source_target_pairs={{0,1},{1,0},{2,3},{3,2},{4,5},{5,4},{6,7},{7,6},{8,9},{9,8},{10,11... | collective-permute-start | bytes 884744 | tf_op jit(solution)/shard_map/ppermute | solution.py:228
  7.9 8.5 %collective-permute-start.1 = (f32[6,8,1536]{2,1,0:T(8,128)}, f32[6,8,1536]{2,1,0:T(8,128)S(1)}, u32[]{:S(2)}, u32[]{:S(2)}) collective-permute-start(f32[6,8,1536]{2,1,0:T(8,128)} %get-tuple-element.7.pair), channel_id=1, source_target_pairs={{1,2},{2,1},{5,6},{6,5},{9,10},{10,9},{13,14},{14,13},{17,18},{18,... | collective-permute-start | bytes 884744 | tf_op jit(solution)/shard_map/ppermute | solution.py:228
  8.6 7.8 %collective-permute-start.3 = (f32[1,8,1536]{2,1,0:T(8,128)S(1)}, f32[1,8,1536]{2,1,0:T(8,128)S(1)}, u32[]{:S(2)}, u32[]{:S(2)}) collective-permute-start(f32[1,8,1536]{2,1,0:T(8,128)S(1)} %copy-done.6), channel_id=1, source_target_pairs={{0,5},{1,4},{2,7},{3,6},{4,9},{5,8},{6,11},{7,10},{8,13},{9,12},{1... | collective-permute-start | bytes 147464 | tf_op jit(solution)/shard_map/ppermute | solution.py:228
  14.5 1.9 %collective-permute-start.4 = (f32[1,8,1536]{2,1,0:T(8,128)S(1)}, f32[1,8,1536]{2,1,0:T(8,128)S(1)}, u32[]{:S(2)}, u32[]{:S(2)}) collective-permute-start(f32[1,8,1536]{2,1,0:T(8,128)S(1)} %copy-done.6), channel_id=1, source_target_pairs={{1,6},{2,5},{5,10},{6,9},{9,14},{10,13},{13,18},{14,17},{17,22},{1... | collective-permute-start | bytes 147464 | tf_op jit(solution)/shard_map/ppermute | solution.py:228
  17.8 4.9 %collective-permute-start.6 = (f32[3,8,1536]{2,1,0:T(8,128)S(1)}, f32[3,8,1536]{2,1,0:T(8,128)S(1)}, u32[]{:S(2)}, u32[]{:S(2)}) collective-permute-start(f32[3,8,1536]{2,1,0:T(8,128)S(1)} %get-tuple-element.10.state), channel_id=1, source_target_pairs={{0,1},{1,0},{2,3},{3,2},{4,5},{5,4},{6,7},{7,6},{8,9},{9,8},{10,11... | collective-permute-start | bytes 442376 | tf_op jit(solution)/shard_map/ppermute | solution.py:228
  19.4 3.2 %collective-permute-start.7 = (f32[3,8,1536]{2,1,0:T(8,128)S(1)}, f32[3,8,1536]{2,1,0:T(8,128)S(1)}, u32[]{:S(2)}, u32[]{:S(2)}) collective-permute-start(f32[3,8,1536]{2,1,0:T(8,128)S(1)} %get-tuple-element.10.state), channel_id=1, source_target_pairs={{1,2},{2,1},{5,6},{6,5},{9,10},{10,9},{13,14},{14,13},{17,18},{18,... | collective-permute-start | bytes 442376 | tf_op jit(solution)/shard_map/ppermute | solution.py:228
  20.1 8.6 %collective-permute-start.5 = (f32[3,8,1536]{2,1,0:T(8,128)S(1)}, f32[3,8,1536]{2,1,0:T(8,128)S(1)}, u32[]{:S(2)}, u32[]{:S(2)}) collective-permute-start(f32[3,8,1536]{2,1,0:T(8,128)S(1)} %get-tuple-element.9), channel_id=1, source_target_pairs={{4,0},{8,4},{12,8},{16,12},{20,16},{24,20},{28,24},{5,1},{9,5},{13... | collective-permute-start | bytes 442376 | tf_op jit(solution)/shard_map/ppermute | solution.py:218
  22.6 6.1 %copy-start = (f32[1,3,8,1536]{3,2,1,0:T(8,128)S(1)}, f32[1,3,8,1536]{3,2,1,0:T(8,128)}, u32[]{:S(2)}) copy-start(f32[1,3,8,1536]{3,2,1,0:T(8,128)} %p.5) | copy-start | bytes 442372
  22.6 6.1 %copy-start.1 = (f32[1,3,8,1536]{3,2,1,0:T(8,128)S(1)}, f32[1,3,8,1536]{3,2,1,0:T(8,128)}, u32[]{:S(2)}) copy-start(f32[1,3,8,1536]{3,2,1,0:T(8,128)} %m.5) | copy-start | bytes 442372
  22.6 6.1 %copy-start.2 = (f32[1,3,8,1536]{3,2,1,0:T(8,128)S(1)}, f32[1,3,8,1536]{3,2,1,0:T(8,128)}, u32[]{:S(2)}) copy-start(f32[1,3,8,1536]{3,2,1,0:T(8,128)} %dvar.5) | copy-start | bytes 442372
  22.6 6.0 %copy-start.3 = (f32[1,3,8,1536]{3,2,1,0:T(8,128)S(1)}, f32[1,3,8,1536]{3,2,1,0:T(8,128)}, u32[]{:S(2)}) copy-start(f32[1,3,8,1536]{3,2,1,0:T(8,128)} %rvar.5) | copy-start | bytes 442372
  22.6 6.0 %copy-start.4 = (f32[1,3,8,1536]{3,2,1,0:T(8,128)S(1)}, f32[1,3,8,1536]{3,2,1,0:T(8,128)}, u32[]{:S(2)}) copy-start(f32[1,3,8,1536]{3,2,1,0:T(8,128)} %hobs.5) | copy-start | bytes 442372

commit v5 on v3

v5 whole, which is shorter than its diff:
```python
import jax
import jax.numpy as jnp
from jax import lax
from jax.experimental import pallas as pl
from jax.experimental.pallas import tpu as pltpu
from jax.sharding import Mesh, PartitionSpec as P

GRID_ROWS = 768
STEPS = 4

mass_rate = 0.5
press_rate = 0.5
spin_rate = 0.4


def lon_gap(field):
    width = field.shape[-1]
    return pltpu.roll(field, width - 1, 1) - pltpu.roll(field, 1, 1)


def lat_gap(field):
    rows = field.shape[0]
    return pltpu.roll(field, rows - 1, 0) - pltpu.roll(field, 1, 0)


def even_lat():
    return lax.axis_index("half") == 0


def stacked(own, near, far, index):
    even = even_lat()
    low = jnp.where(even, far[index], near[index])
    high = jnp.where(even, near[index], far[index])
    return jnp.concatenate([low, own[index], high], axis=0)


def scale_kernel(p, dvar, scaled, pv, dv, sems):
    copies = [pltpu.make_async_copy(p, pv, sems.at[0]), pltpu.make_async_copy(dvar, dv, sems.at[1])]
    for copy in copies:
        copy.start()
    for copy in copies:
        copy.wait()
    for part in range(3):
        scaled[0, part] = dv[0, part] * pv[0, part]


def adjoint(own, near, far, depth, turn, keep):
    adj_height, adj_east, adj_north = [
        stacked(own.at[0], near.at[0], far.at[0], part) for part in range(3)
    ]
    for step in range(STEPS):
        adj_mid = adj_east - turn * adj_north
        adj_height = keep * (adj_height + 0.25 * (lat_gap(adj_north) + lon_gap(adj_mid)))
        adj_north = adj_north + turn * adj_mid + depth * lat_gap(adj_height)
        adj_east = adj_mid + depth * lon_gap(adj_height)
    rows = own.shape[2]
    return [value[rows:2 * rows] for value in (adj_height, adj_east, adj_north)]


def first_adjoint_kernel(own, near, far, depth, depth_near, depth_far, spin, inside, p, m, dvar, hobs, state, lead):
    quarter = 0.25 * stacked(depth, depth_near, depth_far, 0)
    swept = adjoint(own, near, far, quarter, spin[...], inside[...])
    for part, value in enumerate(swept):
        pv, dv = p[0, part], dvar[0, part]
        ux = pv - value + hobs[0, part] * m[0, part]
        state[0, part] = ux
        lead[0, part] = dv * (dv * pv) + ux


def second_adjoint_kernel(
    own, near, far, depth, depth_near, depth_far, spin, inside, p, m, dvar, rvar, hobs, state, lead, tally
):
    quarter = 0.25 * stacked(depth, depth_near, depth_far, 0)
    swept = adjoint(own, near, far, quarter, spin[...], inside[...])
    first = lax.axis_index("win") == 0
    moments = [0.0, 0.0, 0.0, 0.0]
    for part, value in enumerate(swept):
        dv, rv, hv = dvar[0, part], rvar[0, part], hobs[0, part]
        pv, mv, ux = p[0, part], m[0, part], state[0, part]
        up, um = dv * pv, rv * mv
        zp = jnp.where(first, lead[0, part], 0.0)
        zm = rv * um + hv * ux
        zx = up - value + hv * um
        moments[0] += lane_sum(up * pv + um * mv)
        moments[1] += lane_sum(up * up + um * um + ux * ux)
        moments[2] += lane_sum(dv * up * up + rv * um * um + 2.0 * (zx * ux))
        moments[3] += lane_sum(zp * zp + zm * zm + zx * zx)
    for row, value in enumerate(moments):
        tally[row] = value


def forward_kernel(state, near, far, depth, depth_near, depth_far, spin, inside, tally, end):
    quarter = 0.25 * stacked(depth, depth_near, depth_far, 0)
    turn, keep = spin[...], inside[...]
    height, east, north = [stacked(state.at[0], near.at[0], far.at[0], part) for part in range(3)]
    for step in range(STEPS):
        height = keep * (height - (lon_gap(quarter * east) + lat_gap(quarter * north)))
        east = east + turn * north - 0.25 * lon_gap(height)
        north = north - turn * east - 0.25 * lat_gap(height)
    rows = state.shape[2]
    for part, value in enumerate((height, east, north)):
        end[0, part] = value[rows:2 * rows]


def lane_sum(value):
    rows, width = value.shape
    total = value[:, :128]
    for start in range(128, width, 128):
        total = total + value[:, start:start + 128]
    return total


def inner_kernel(lead, end, tally, tile):
    last = lax.axis_index("win") == lax.axis_size("win") - 1
    square = 0.0
    for part in range(3):
        zp = lead[0, part] - end[0, part]
        square += lane_sum(zp * zp)
    moments = [tally[0], tally[1], tally[2], tally[3] + jnp.where(last, 0.0, square)]
    rows = [jnp.sum(value, axis=0, keepdims=True) for value in moments]
    tile[...] = jnp.concatenate(rows + rows, axis=0)


def spread_kernel(own, other, sent):
    tile = own[...] + other[...]
    for rank in range(sent.shape[0] // 8):
        sent[8 * rank:8 * rank + 8] = tile


def two_sum(a, b):
    total = a + b
    part = total - a
    return total, (a - (total - part)) + (b - part)


def split(a):
    wide = 4097.0 * a
    top = wide - (wide - a)
    return top, a - top


def two_product(a, b):
    product = a * b
    a_top, a_low = split(a)
    b_top, b_low = split(b)
    return product, ((a_top * b_top - product) + a_top * b_low + a_low * b_top) + a_low * b_low


def pair_product(a, b):
    product, rest = two_product(a[0], b[0])
    return product, rest + (a[0] * b[1] + a[1] * b[0])


def pair_gap(a, b):
    total, rest = two_sum(a[0], -b[0])
    return total + (rest + (a[1] - b[1]))


def coefficients(gathered):
    top = gathered[0:8]
    for rank in range(1, gathered.shape[0] // 8):
        top = top + gathered[8 * rank:8 * rank + 8]
    low = jnp.zeros_like(top)
    shift = 64
    while shift:
        total, rest = two_sum(top, pltpu.roll(top, shift, 1))
        low = low + pltpu.roll(low, shift, 1) + rest
        top = total
        shift //= 2
    scale = 1.0 / top[1:2, :128]
    moments = []
    for row in range(4):
        product, rest = two_product(top[row:row + 1], scale)
        moments.append((product, rest + low[row:row + 1] * scale))
    m1, m2, m3, m4 = moments
    gap = pair_gap(pair_product(m2, m4), pair_product(m3, m3))
    y1 = pair_gap(pair_product(m1, m4), pair_product(m2, m3)) / gap
    y2 = pair_gap(pair_product(m2, m2), pair_product(m1, m3)) / gap
    return y1, y2


def combine_kernel(gathered, p, m, dvar, rvar, state, dual_model, dual_obs, increment):
    y1, y2 = coefficients(gathered)
    rows, width = p.shape[2:]
    y1 = jnp.broadcast_to(jnp.concatenate([y1] * (width // 128), axis=1), (rows, width))
    y2 = jnp.broadcast_to(jnp.concatenate([y2] * (width // 128), axis=1), (rows, width))
    for part in range(3):
        dual_model[0, part] = (y1 + y2 * dvar[0, part]) * p[0, part]
        dual_obs[0, part] = (y1 + y2 * rvar[0, part]) * m[0, part]
        increment[0, part] = y2 * state[0, part]


def run(kernel, out_shapes, *operands, scratch=(), space=pltpu.VMEM, work=4):
    shapes = [jax.ShapeDtypeStruct(shape, jnp.float32) for shape in out_shapes]
    size = sum(4 * operand.size for operand in operands) + sum(4 * shape.size for shape in shapes)
    if space is not pltpu.VMEM:
        operands = [pltpu.with_memory_space_constraint(operand, space) for operand in operands]
    return pl.pallas_call(
        kernel,
        out_shape=shapes,
        in_specs=[pl.BlockSpec(memory_space=space)] * len(operands),
        out_specs=[pl.BlockSpec(memory_space=pltpu.VMEM)] * len(shapes),
        scratch_shapes=scratch,
        compiler_params=pltpu.CompilerParams(vmem_limit_bytes=32 * 1024 * 1024),
        cost_estimate=pl.CostEstimate(flops=work * size, bytes_accessed=size, transcendentals=0),
    )(*operands)


def shifted(value, step):
    count = lax.axis_size("win")
    initial, last = (max(0, -step), min(count, count - step))
    return lax.ppermute(value, "win", [(source, source + step) for source in range(initial, last)])


def lat_count():
    return lax.axis_size("band") * lax.axis_size("half")


def lat_index():
    return lax.axis_index("band") * lax.axis_size("half") + lax.axis_index("half")


def swapped(value, first, win_step=0):
    wins, lats = lax.axis_size("win"), lat_count()
    pairs = []
    for win in range(max(0, -win_step), min(wins, wins - win_step)):
        for lat in range(first, lats - 1, 2):
            for source, target in ((lat, lat + 1), (lat + 1, lat)):
                pairs.append((win * lats + source, (win + win_step) * lats + target))
    return lax.ppermute(value, ("win", "band", "half"), pairs)


def body(model_rhs, obs_rhs, model_var, obs_var, obs_weight, depth):
    rows, width = model_rhs.shape[2:]
    ranks = lax.axis_size("win") * lax.axis_size("band")
    total_rows = rows * lat_count()
    offset = (GRID_ROWS - total_rows) // 2
    local_rows = lat_index() * rows - rows + jnp.arange(3 * rows, dtype=jnp.int32)
    latitude = -jnp.pi / 2 + (local_rows.astype(jnp.float32) + offset + 0.5) * (jnp.pi / GRID_ROWS)
    inside = ((local_rows >= 0) & (local_rows < total_rows)).astype(jnp.float32)
    spin = inside * (mass_rate * spin_rate * jnp.sin(latitude))
    inside = jnp.broadcast_to(inside[:, None], (3 * rows, width))
    spin = jnp.broadcast_to(spin[:, None], (3 * rows, width))
    field = model_rhs.shape
    came = shifted(model_rhs, -1)
    came_far = swapped(model_rhs, 1, -1)
    place = (depth, swapped(depth, 0), swapped(depth, 1), spin, inside)
    (scaled,) = run(
        scale_kernel, [field], model_rhs, model_var, space=pltpu.HBM,
        scratch=[pltpu.VMEM(field, jnp.float32)] * 2 + [pltpu.SemaphoreType.DMA((2,))],
    )
    scaled_came = shifted(scaled, -1)
    scaled_far = swapped(scaled, 1, -1)
    state, lead = run(
        first_adjoint_kernel, [field, field],
        came, swapped(came, 0), came_far, *place, model_rhs, obs_rhs, model_var, obs_weight,
    )
    near, far = swapped(state, 0), swapped(state, 1)
    lead_came = shifted(lead, -1)
    held, _ = lax.optimization_barrier((scaled_came, state))
    (tally,) = run(
        second_adjoint_kernel, [(4, rows, 128)],
        scaled_came, swapped(held, 0), scaled_far, *place,
        model_rhs, obs_rhs, model_var, obs_var, obs_weight, state, lead,
    )
    (end,) = run(forward_kernel, [field], state, near, far, *place, tally)
    (tile,) = run(inner_kernel, [(8, 128)], lead_came, end, tally)
    (sent,) = run(spread_kernel, [(8 * ranks, 128)], tile, swapped(tile, 0))
    gathered = lax.all_to_all(sent, ("win", "band"), 0, 0, tiled=True)
    return run(combine_kernel, [field] * 3, gathered, model_rhs, obs_rhs, model_var, obs_var, state)


def solution(mesh):
    wins, lats = mesh.devices.shape
    mesh = Mesh(mesh.devices.reshape(wins, lats // 2, 2), ("win", "band", "half"))
    lat = ("band", "half")
    field = P("win", None, lat, None)
    in_specs = (field,) * 5 + (P("win", lat, None),)
    return jax.shard_map(body, mesh=mesh, in_specs=in_specs, out_specs=(field,) * 3, check_vma=False)
```

time: 45.9 us -> 47.3 us (1.031)
  waiting for transfers between devices: 6.02 us -> 9.12 us
  starting transfers between devices: 15.9 us -> 14.3 us
  Pallas kernels: 7.21 us -> 5.98 us
  blocking collectives: 15.4 us -> 16.4 us
    ppermute x2 -> x3, waiting for transfers between devices: 4.84 us -> 8.2 us  [shifted(): lax.ppermute(value, 'win', [(source, source + step) for source in range(i...]
    ppermute x2 -> x3, starting transfers between devices: 6.32 us -> 3.88 us  [shifted(): lax.ppermute(value, 'win', [(source, source + step) for source in range(i...]
    pallas_call x6 -> x7, Pallas kernels: 7.21 us -> 5.98 us  [run(): pl.pallas_call(kernel, out_shape=shapes, in_specs=[pl.BlockSpec(memory_sp...]
    all_to_all x1, blocking collectives: 15.4 us -> 16.4 us  [body(): gathered = lax.all_to_all(sent, ('win', 'band'), 0, 0, tiled=True)]
    ppermute x6 -> x9, starting transfers between devices: 9.6 us -> 10.5 us  [swapped(): return lax.ppermute(value, ('win', 'band', 'half'), pairs)]
    ppermute x6 -> x9, waiting for transfers between devices: 1.19 us -> 0.92 us  [swapped(): return lax.ppermute(value, ('win', 'band', 'half'), pairs)]
  transfers between devices with their start and end apart: 8 -> 12, of which waited for: 2 -> 4; matrix products, arithmetic and copies ran while one was open for 0% -> 0% of each run, Pallas kernels for 5% -> 10%
where the time goes in v5:
time: 47.3 us; the launch traced here: 47 us
  blocking collectives  16.4 us (35%)
  starting transfers between devices  14.3 us (30%)
  waiting for transfers between devices  9.12 us (19%)
  Pallas kernels  5.98 us (13%)
  between operations  0.9 us (2%)
    all_to_all x1, blocking collectives, body(): gathered = lax.all_to_all(sent, ('win', 'band'), 0, 0, tiled=True)  16.4 us
    ppermute x9, starting transfers between devices, swapped(): return lax.ppermute(value, ('win', 'band', 'half'), pairs)  10.5 us
    ppermute x3, waiting for transfers between devices, shifted(): lax.ppermute(value, 'win', [(source, source + step) for source in range(i...  8.2 us
    pallas_call x7, Pallas kernels, run(): pl.pallas_call(kernel, out_shape=shapes, in_specs=[pl.BlockSpec(memory_sp...  5.98 us
    ppermute x3, starting transfers between devices, shifted(): lax.ppermute(value, 'win', [(source, source + step) for source in range(i...  3.88 us
  transfers between devices with their start and end apart: 12, of which 4 were waited for; matrix products, arithmetic and copies ran while one was open for 0% of the time, Pallas kernels for 10%

profile of v5, /device:TPU:0, one launch (start us, length us, event | category | flops | bytes accessed | tf_op | source)
XLA Modules:
  0.0 47.0 jit_solution(10963548096390687906)
XLA Ops:
  0.6 1.3 %collective-permute-start = (f32[1,3,8,1536]{3,2,1,0:T(8,128)}, f32[1,3,8,1536]{3,2,1,0:T(8,128)S(1)}, u32[]{:S(2)}, u32[]{:S(2)}) collective-permute-start(f32[1,3,8,1536]{3,2,1,0:T(8,128)} %p.7), channel_id=1, source_target_pairs={{4,0},{8,4},{12,8},{16,12},{20,16},{24,20},{28,24},{5,1},{9,5},{13... | collective-permute-start | bytes 442376 | tf_op jit(solution)/shard_map/ppermute | solution.py:212
  1.9 0.5 %collective-permute-start.3 = (f32[1,8,1536]{2,1,0:T(8,128)}, f32[1,8,1536]{2,1,0:T(8,128)S(1)}, u32[]{:S(2)}, u32[]{:S(2)}) collective-permute-start(f32[1,8,1536]{2,1,0:T(8,128)} %depth.5), channel_id=1, source_target_pairs={{0,1},{1,0},{2,3},{3,2},{4,5},{5,4},{6,7},{7,6},{8,9},{9,8},{10,11... | collective-permute-start | bytes 147464 | tf_op jit(solution)/shard_map/ppermute | solution.py:230
  2.4 0.7 %collective-permute-start.4 = (f32[1,8,1536]{2,1,0:T(8,128)}, f32[1,8,1536]{2,1,0:T(8,128)S(1)}, u32[]{:S(2)}, u32[]{:S(2)}) collective-permute-start(f32[1,8,1536]{2,1,0:T(8,128)} %depth.5), channel_id=1, source_target_pairs={{1,2},{2,1},{5,6},{6,5},{9,10},{10,9},{13,14},{14,13},{17,18},{18,... | collective-permute-start | bytes 147464 | tf_op jit(solution)/shard_map/ppermute | solution.py:230
  3.1 0.7 %collective-permute-start.2 = (f32[1,3,8,1536]{3,2,1,0:T(8,128)}, f32[1,3,8,1536]{3,2,1,0:T(8,128)S(1)}, u32[]{:S(2)}, u32[]{:S(2)}) collective-permute-start(f32[1,3,8,1536]{3,2,1,0:T(8,128)} %p.7), channel_id=1, source_target_pairs={{5,2},{6,1},{9,6},{10,5},{13,10},{14,9},{17,14},{18,13},{21,18},{2... | collective-permute-start | bytes 442376 | tf_op jit(solution)/shard_map/ppermute | solution.py:230
  3.8 1.1 %shard_map.86 = f32[1,3,8,1536]{3,2,1,0:T(8,128)S(1)} custom-call(f32[1,3,8,1536]{3,2,1,0:T(8,128)} %p.7, f32[1,3,8,1536]{3,2,1,0:T(8,128)} %dvar.7), custom_call_target="tpu_custom_call" | custom-call | flops 1769472 | bytes 442368 | tf_op jit(solution)/shard_map/pallas_call | solution.py:198
  4.9 1.3 %collective-permute-start.8 = (f32[1,3,8,1536]{3,2,1,0:T(8,128)S(1)}, f32[1,3,8,1536]{3,2,1,0:T(8,128)S(1)}, u32[]{:S(2)}, u32[]{:S(2)}) collective-permute-start(f32[1,3,8,1536]{3,2,1,0:T(8,128)S(1)} %shard_map.86), channel_id=1, source_target_pairs={{4,0},{8,4},{12,8},{16,12},{20,16},{24,20},{28,24},{5,1},{9,5},{13... | collective-permute-start | bytes 442376 | tf_op jit(solution)/shard_map/ppermute | solution.py:212
  6.2 3.4 %collective-permute-done.own = f32[1,3,8,1536]{3,2,1,0:T(8,128)S(1)} collective-permute-done((f32[1,3,8,1536]{3,2,1,0:T(8,128)}, f32[1,3,8,1536]{3,2,1,0:T(8,128)S(1)}, u32[]{:S(2)}, u32[]{:S(2)}) %collective-permute-start) | collective-permute-done | bytes 147488 | tf_op jit(solution)/shard_map/ppermute | solution.py:212
  9.6 1.2 %collective-permute-start.1 = (f32[1,3,8,1536]{3,2,1,0:T(8,128)S(1)}, f32[1,3,8,1536]{3,2,1,0:T(8,128)S(1)}, u32[]{:S(2)}, u32[]{:S(2)}) collective-permute-start(f32[1,3,8,1536]{3,2,1,0:T(8,128)S(1)} %collective-permute-done.own), channel_id=1, source_target_pairs={{0,1},{1,0},{2,3},{3,2},{4,5},{5,4},{6,7},{7,6},{8,9},{9,8},{10,11... | collective-permute-start | bytes 442376 | tf_op jit(solution)/shard_map/ppermute | solution.py:230
  10.8 0.0 copy-start
  10.8 0.0 copy-start.1
  10.8 0.0 collective-permute-done.3.depth_near
  10.9 0.8 %collective-permute-start.10 = (f32[1,3,8,1536]{3,2,1,0:T(8,128)S(1)}, f32[1,3,8,1536]{3,2,1,0:T(8,128)S(1)}, u32[]{:S(2)}, u32[]{:S(2)}) collective-permute-start(f32[1,3,8,1536]{3,2,1,0:T(8,128)S(1)} %shard_map.86), channel_id=1, source_target_pairs={{5,2},{6,1},{9,6},{10,5},{13,10},{14,9},{17,14},{18,13},{21,18},{2... | collective-permute-start | bytes 442376 | tf_op jit(solution)/shard_map/ppermute | solution.py:230
  11.7 0.0 collective-permute-done.4.depth_far
  11.7 0.1 collective-permute-done.1.near
  11.8 0.1 broadcast_in_dim.4.spin
  11.8 0.1 broadcast_in_dim.5.inside
  12.0 0.0 copy-start.4
  12.0 1.2 %shard_map.85 = (f32[1,3,8,1536]{3,2,1,0:T(8,128)S(1)}, f32[1,3,8,1536]{3,2,1,0:T(8,128)S(1)}) custom-call(f32[1,3,8,1536]{3,2,1,0:T(8,128)S(1)} %collective-permute-done.own, f32[1,3,8,1536]{3,2,1,0:T(8,128)S(1)} %collective-permute-done.1.near, f32[1,3,8,1536]{3,2,1,0:T(8,128)S(1)} %collective-permute-done.2.far, f32[1,8,1536]{2,1,0:T(8,128)S(1)} %copy-done.5, ...), custom_call_target="tpu_custom_call" | custom-call | flops 7077888 | bytes 1769472 | tf_op jit(solution)/shard_map/pallas_call | solution.py:198
  13.2 0.0 collective-permute-done.8.own
  13.2 3.6 %collective-permute-start.9 = (f32[1,3,8,1536]{3,2,1,0:T(8,128)S(1)}, f32[1,3,8,1536]{3,2,1,0:T(8,128)S(1)}, u32[]{:S(2)}, u32[]{:S(2)}) collective-permute-start(f32[1,3,8,1536]{3,2,1,0:T(8,128)S(1)} %collective-permute-done.8.own), channel_id=1, source_target_pairs={{0,1},{1,0},{2,3},{3,2},{4,5},{5,4},{6,7},{7,6},{8,9},{9,8},{10,11... | collective-permute-start | bytes 442376 | tf_op jit(solution)/shard_map/ppermute | solution.py:230
  16.8 0.0 collective-permute-start.6
  16.8 0.7 %collective-permute-start.7 = (f32[1,3,8,1536]{3,2,1,0:T(8,128)S(1)}, f32[1,3,8,1536]{3,2,1,0:T(8,128)S(1)}, u32[]{:S(2)}, u32[]{:S(2)}) collective-permute-start(f32[1,3,8,1536]{3,2,1,0:T(8,128)S(1)} %get-tuple-element.7.state), channel_id=1, source_target_pairs={{1,2},{2,1},{5,6},{6,5},{9,10},{10,9},{13,14},{14,13},{17,18},{18,... | collective-permute-start | bytes 442376 | tf_op jit(solution)/shard_map/ppermute | solution.py:230
  17.5 1.3 %collective-permute-start.5 = (f32[1,3,8,1536]{3,2,1,0:T(8,128)S(1)}, f32[1,3,8,1536]{3,2,1,0:T(8,128)S(1)}, u32[]{:S(2)}, u32[]{:S(2)}) collective-permute-start(f32[1,3,8,1536]{3,2,1,0:T(8,128)S(1)} %get-tuple-element.6.lead), channel_id=1, source_target_pairs={{4,0},{8,4},{12,8},{16,12},{20,16},{24,20},{28,24},{5,1},{9,5},{13... | collective-permute-start | bytes 442376 | tf_op jit(solution)/shard_map/ppermute | solution.py:212
  18.8 0.0 collective-permute-done.10.far
  18.8 1.2 %shard_map.87.tally = f32[4,8,128]{2,1,0:T(8,128)S(1)} custom-call(f32[1,3,8,1536]{3,2,1,0:T(8,128)S(1)} %collective-permute-done.8.own, f32[1,3,8,1536]{3,2,1,0:T(8,128)S(1)} %collective-permute-done.9.near, f32[1,3,8,1536]{3,2,1,0:T(8,128)S(1)} %collective-permute-done.10.far, f32[1,8,1536]{2,1,0:T(8,128)S(1)} %copy-done.5, ...), custom_call_target="tpu_custom_call" | custom-call | flops 7733248 | bytes 1933312 | tf_op jit(solution)/shard_map/pallas_call | solution.py:198
  20.0 0.0 collective-permute-done.6.near
  20.1 1.2 %shard_map.88.end = f32[1,3,8,1536]{3,2,1,0:T(8,128)S(1)} custom-call(f32[1,3,8,1536]{3,2,1,0:T(8,128)S(1)} %get-tuple-element.7.state, f32[1,3,8,1536]{3,2,1,0:T(8,128)S(1)} %collective-permute-done.6.near, f32[1,3,8,1536]{3,2,1,0:T(8,128)S(1)} %collective-permute-done.7.far, f32[1,8,1536]{2,1,0:T(8,128)S(1)} %copy-done.5, ...), custom_call_target="tpu_custom_call" | custom-call | flops 4194304 | bytes 1048576 | tf_op jit(solution)/shard_map/pallas_call | solution.py:198
  21.2 4.8 %collective-permute-done.5.lead = f32[1,3,8,1536]{3,2,1,0:T(8,128)S(1)} collective-permute-done((f32[1,3,8,1536]{3,2,1,0:T(8,128)S(1)}, f32[1,3,8,1536]{3,2,1,0:T(8,128)S(1)}, u32[]{:S(2)}, u32[]{:S(2)}) %collective-permute-start.5) | collective-permute-done | bytes 147488 | tf_op jit(solution)/shard_map/ppermute | solution.py:212
  26.1 2.3 %collective-permute-start.11 = (f32[8,128]{1,0:T(8,128)S(1)}, f32[8,128]{1,0:T(8,128)S(1)}, u32[]{:S(2)}, u32[]{:S(2)}) collective-permute-start(f32[8,128]{1,0:T(8,128)S(1)} %shard_map.89.own), channel_id=1, source_target_pairs={{0,1},{1,0},{2,3},{3,2},{4,5},{5,4},{6,7},{7,6},{8,9},{9,8},{10,11... | collective-permute-start | bytes 12296 | tf_op jit(solution)/shard_map/ppermute | solution.py:230
  28.4 0.8 %collective-permute-done.11.other = f32[8,128]{1,0:T(8,128)S(1)} collective-permute-done((f32[8,128]{1,0:T(8,128)S(1)}, f32[8,128]{1,0:T(8,128)S(1)}, u32[]{:S(2)}, u32[]{:S(2)}) %collective-permute-start.11) | collective-permute-done | bytes 4128 | tf_op jit(solution)/shard_map/ppermute | solution.py:230
  29.3 16.4 %all_to_all.11 = f32[16,8,128]{2,1,0:T(8,128)S(1)} all-to-all(f32[16,8,128]{2,1,0:T(8,128)S(1)} %bitcast.3), channel_id=1, replica_groups=mesh['win'=8,'band'=2,'half'=2] {'win','band'}, dimensions={0} | all-to-all | bytes 131072 | tf_op jit(solution)/shard_map/all_to_all | solution.py:269
  45.7 1.3 %shard_map.91 = (f32[1,3,8,1536]{3,2,1,0:T(8,128)}, f32[1,3,8,1536]{3,2,1,0:T(8,128)}, f32[1,3,8,1536]{3,2,1,0:T(8,128)}) custom-call(f32[128,128]{1,0:T(8,128)S(1)} %bitcast.2, f32[1,3,8,1536]{3,2,1,0:T(8,128)S(1)} %copy-done, f32[1,3,8,1536]{3,2,1,0:T(8,128)S(1)} %copy-done.2, f32[1,3,8,1536]{3,2,1,0:T(8,128)S(1)} %copy-done.1, ...), custom_call_target="tpu_custom_call" | custom-call | flops 4980736 | bytes 1245184 | tf_op jit(solution)/shard_map/pallas_call | solution.py:198
  (16 shorter events, 0.1 us)
Async XLA Ops:
  0.6 8.9 %collective-permute-start = (f32[1,3,8,1536]{3,2,1,0:T(8,128)}, f32[1,3,8,1536]{3,2,1,0:T(8,128)S(1)}, u32[]{:S(2)}, u32[]{:S(2)}) collective-permute-start(f32[1,3,8,1536]{3,2,1,0:T(8,128)} %p.7), channel_id=1, source_target_pairs={{4,0},{8,4},{12,8},{16,12},{20,16},{24,20},{28,24},{5,1},{9,5},{13... | collective-permute-start | bytes 442376 | tf_op jit(solution)/shard_map/ppermute | solution.py:212
  1.9 8.9 %collective-permute-start.3 = (f32[1,8,1536]{2,1,0:T(8,128)}, f32[1,8,1536]{2,1,0:T(8,128)S(1)}, u32[]{:S(2)}, u32[]{:S(2)}) collective-permute-start(f32[1,8,1536]{2,1,0:T(8,128)} %depth.5), channel_id=1, source_target_pairs={{0,1},{1,0},{2,3},{3,2},{4,5},{5,4},{6,7},{7,6},{8,9},{9,8},{10,11... | collective-permute-start | bytes 147464 | tf_op jit(solution)/shard_map/ppermute | solution.py:230
  2.4 9.2 %collective-permute-start.4 = (f32[1,8,1536]{2,1,0:T(8,128)}, f32[1,8,1536]{2,1,0:T(8,128)S(1)}, u32[]{:S(2)}, u32[]{:S(2)}) collective-permute-start(f32[1,8,1536]{2,1,0:T(8,128)} %depth.5), channel_id=1, source_target_pairs={{1,2},{2,1},{5,6},{6,5},{9,10},{10,9},{13,14},{14,13},{17,18},{18,... | collective-permute-start | bytes 147464 | tf_op jit(solution)/shard_map/ppermute | solution.py:230
  3.1 8.6 %collective-permute-start.2 = (f32[1,3,8,1536]{3,2,1,0:T(8,128)}, f32[1,3,8,1536]{3,2,1,0:T(8,128)S(1)}, u32[]{:S(2)}, u32[]{:S(2)}) collective-permute-start(f32[1,3,8,1536]{3,2,1,0:T(8,128)} %p.7), channel_id=1, source_target_pairs={{5,2},{6,1},{9,6},{10,5},{13,10},{14,9},{17,14},{18,13},{21,18},{2... | collective-permute-start | bytes 442376 | tf_op jit(solution)/shard_map/ppermute | solution.py:230
  3.8 8.1 %copy-start.2 = (f32[1,3,8,1536]{3,2,1,0:T(8,128)S(1)}, f32[1,3,8,1536]{3,2,1,0:T(8,128)}, u32[]{:S(2)}) copy-start(f32[1,3,8,1536]{3,2,1,0:T(8,128)} %m.5) | copy-start | bytes 442372
  3.8 8.1 %copy-start.3 = (f32[1,3,8,1536]{3,2,1,0:T(8,128)S(1)}, f32[1,3,8,1536]{3,2,1,0:T(8,128)}, u32[]{:S(2)}) copy-start(f32[1,3,8,1536]{3,2,1,0:T(8,128)} %hobs.3) | copy-start | bytes 442372
  3.8 8.1 %copy-start.5 = (f32[1,8,1536]{2,1,0:T(8,128)S(1)}, f32[1,8,1536]{2,1,0:T(8,128)}, u32[]{:S(2)}) copy-start(f32[1,8,1536]{2,1,0:T(8,128)} %depth.5) | copy-start | bytes 147460
  4.9 8.3 %collective-permute-start.8 = (f32[1,3,8,1536]{3,2,1,0:T(8,128)S(1)}, f32[1,3,8,1536]{3,2,1,0:T(8,128)S(1)}, u32[]{:S(2)}, u32[]{:S(2)}) collective-permute-start(f32[1,3,8,1536]{3,2,1,0:T(8,128)S(1)} %shard_map.86), channel_id=1, source_target_pairs={{4,0},{8,4},{12,8},{16,12},{20,16},{24,20},{28,24},{5,1},{9,5},{13... | collective-permute-start | bytes 442376 | tf_op jit(solution)/shard_map/ppermute | solution.py:212
  9.6 2.2 %collective-permute-start.1 = (f32[1,3,8,1536]{3,2,1,0:T(8,128)S(1)}, f32[1,3,8,1536]{3,2,1,0:T(8,128)S(1)}, u32[]{:S(2)}, u32[]{:S(2)}) collective-permute-start(f32[1,3,8,1536]{3,2,1,0:T(8,128)S(1)} %collective-permute-done.own), channel_id=1, source_target_pairs={{0,1},{1,0},{2,3},{3,2},{4,5},{5,4},{6,7},{7,6},{8,9},{9,8},{10,11... | collective-permute-start | bytes 442376 | tf_op jit(solution)/shard_map/ppermute | solution.py:230
  10.8 1.1 %copy-start = (f32[1,3,8,1536]{3,2,1,0:T(8,128)S(1)}, f32[1,3,8,1536]{3,2,1,0:T(8,128)}, u32[]{:S(2)}) copy-start(f32[1,3,8,1536]{3,2,1,0:T(8,128)} %p.7) | copy-start | bytes 442372
  10.8 1.1 %copy-start.1 = (f32[1,3,8,1536]{3,2,1,0:T(8,128)S(1)}, f32[1,3,8,1536]{3,2,1,0:T(8,128)}, u32[]{:S(2)}) copy-start(f32[1,3,8,1536]{3,2,1,0:T(8,128)} %dvar.7) | copy-start | bytes 442372
  10.9 7.9 %collective-permute-start.10 = (f32[1,3,8,1536]{3,2,1,0:T(8,128)S(1)}, f32[1,3,8,1536]{3,2,1,0:T(8,128)S(1)}, u32[]{:S(2)}, u32[]{:S(2)}) collective-permute-start(f32[1,3,8,1536]{3,2,1,0:T(8,128)S(1)} %shard_map.86), channel_id=1, source_target_pairs={{5,2},{6,1},{9,6},{10,5},{13,10},{14,9},{17,14},{18,13},{21,18},{2... | collective-permute-start | bytes 442376 | tf_op jit(solution)/shard_map/ppermute | solution.py:230
  12.0 6.8 %copy-start.4 = (f32[1,3,8,1536]{3,2,1,0:T(8,128)S(1)}, f32[1,3,8,1536]{3,2,1,0:T(8,128)}, u32[]{:S(2)}) copy-start(f32[1,3,8,1536]{3,2,1,0:T(8,128)} %rvar.3) | copy-start | bytes 442372
  13.2 5.6 %collective-permute-start.9 = (f32[1,3,8,1536]{3,2,1,0:T(8,128)S(1)}, f32[1,3,8,1536]{3,2,1,0:T(8,128)S(1)}, u32[]{:S(2)}, u32[]{:S(2)}) collective-permute-start(f32[1,3,8,1536]{3,2,1,0:T(8,128)S(1)} %collective-permute-done.8.own), channel_id=1, source_target_pairs={{0,1},{1,0},{2,3},{3,2},{4,5},{5,4},{6,7},{7,6},{8,9},{9,8},{10,11... | collective-permute-start | bytes 442376 | tf_op jit(solution)/shard_map/ppermute | solution.py:230
  16.8 3.2 %collective-permute-start.6 = (f32[1,3,8,1536]{3,2,1,0:T(8,128)S(1)}, f32[1,3,8,1536]{3,2,1,0:T(8,128)S(1)}, u32[]{:S(2)}, u32[]{:S(2)}) collective-permute-start(f32[1,3,8,1536]{3,2,1,0:T(8,128)S(1)} %get-tuple-element.7.state), channel_id=1, source_target_pairs={{0,1},{1,0},{2,3},{3,2},{4,5},{5,4},{6,7},{7,6},{8,9},{9,8},{10,11... | collective-permute-start | bytes 442376 | tf_op jit(solution)/shard_map/ppermute | solution.py:230
  16.8 3.2 %collective-permute-start.7 = (f32[1,3,8,1536]{3,2,1,0:T(8,128)S(1)}, f32[1,3,8,1536]{3,2,1,0:T(8,128)S(1)}, u32[]{:S(2)}, u32[]{:S(2)}) collective-permute-start(f32[1,3,8,1536]{3,2,1,0:T(8,128)S(1)} %get-tuple-element.7.state), channel_id=1, source_target_pairs={{1,2},{2,1},{5,6},{6,5},{9,10},{10,9},{13,14},{14,13},{17,18},{18,... | collective-permute-start | bytes 442376 | tf_op jit(solution)/shard_map/ppermute | solution.py:230
  17.5 8.6 %collective-permute-start.5 = (f32[1,3,8,1536]{3,2,1,0:T(8,128)S(1)}, f32[1,3,8,1536]{3,2,1,0:T(8,128)S(1)}, u32[]{:S(2)}, u32[]{:S(2)}) collective-permute-start(f32[1,3,8,1536]{3,2,1,0:T(8,128)S(1)} %get-tuple-element.6.lead), channel_id=1, source_target_pairs={{4,0},{8,4},{12,8},{16,12},{20,16},{24,20},{28,24},{5,1},{9,5},{13... | collective-permute-start | bytes 442376 | tf_op jit(solution)/shard_map/ppermute | solution.py:212
  26.1 3.2 %collective-permute-start.11 = (f32[8,128]{1,0:T(8,128)S(1)}, f32[8,128]{1,0:T(8,128)S(1)}, u32[]{:S(2)}, u32[]{:S(2)}) collective-permute-start(f32[8,128]{1,0:T(8,128)S(1)} %shard_map.89.own), channel_id=1, source_target_pairs={{0,1},{1,0},{2,3},{3,2},{4,5},{5,4},{6,7},{7,6},{8,9},{9,8},{10,11... | collective-permute-start | bytes 12296 | tf_op jit(solution)/shard_map/ppermute | solution.py:230

commit v6 on v5

--- a/solution.py
+++ b/solution.py
@@ -23,31 +23,25 @@
     return pltpu.roll(field, rows - 1, 0) - pltpu.roll(field, 1, 0)
 
 
-def even_lat():
-    return lax.axis_index("half") == 0
+def is_middle():
+    return lax.axis_index("band") != lax.axis_index("half")
 
 
 def stacked(own, near, far, index):
-    even = even_lat()
-    low = jnp.where(even, far[index], near[index])
-    high = jnp.where(even, near[index], far[index])
+    even = lax.axis_index("half") == 0
+    outer = jnp.where(is_middle(), far[index], 0.0)
+    low = jnp.where(even, outer, near[index])
+    high = jnp.where(even, near[index], outer)
     return jnp.concatenate([low, own[index], high], axis=0)
 
 
-def scale_kernel(p, dvar, scaled, pv, dv, sems):
-    copies = [pltpu.make_async_copy(p, pv, sems.at[0]), pltpu.make_async_copy(dvar, dv, sems.at[1])]
-    for copy in copies:
-        copy.start()
-    for copy in copies:
-        copy.wait()
-    for part in range(3):
-        scaled[0, part] = dv[0, part] * pv[0, part]
-
-
-def adjoint(own, near, far, depth, turn, keep):
-    adj_height, adj_east, adj_north = [
-        stacked(own.at[0], near.at[0], far.at[0], part) for part in range(3)
-    ]
+def stretched(depth, depth_near, depth_far):
+    return 0.25 * stacked(depth, depth_near, depth_far, 0)
+
+
+def adjoint(own, near, far, far_start, depth, turn, keep):
+    outer = far.at[0, far_start:far_start + 3]
+    adj_height, adj_east, adj_north = [stacked(own.at[0], near.at[0], outer, part) for part in range(3)]
     for step in range(STEPS):
         adj_mid = adj_east - turn * adj_north
         adj_height = keep * (adj_height + 0.25 * (lat_gap(adj_north) + lon_gap(adj_mid)))
@@ -58,8 +52,7 @@
 
 
 def first_adjoint_kernel(own, near, far, depth, depth_near, depth_far, spin, inside, p, m, dvar, hobs, state, lead):
-    quarter = 0.25 * stacked(depth, depth_near, depth_far, 0)
-    swept = adjoint(own, near, far, quarter, spin[...], inside[...])
+    swept = adjoint(own, near, far, 0, stretched(depth, depth_near, depth_far), spin[...], inside[...])
     for part, value in enumerate(swept):
         pv, dv = p[0, part], dvar[0, part]
         ux = pv - value + hobs[0, part] * m[0, part]
@@ -70,8 +63,7 @@
 def second_adjoint_kernel(
     own, near, far, depth, depth_near, depth_far, spin, inside, p, m, dvar, rvar, hobs, state, lead, tally
 ):
-    quarter = 0.25 * stacked(depth, depth_near, depth_far, 0)
-    swept = adjoint(own, near, far, quarter, spin[...], inside[...])
+    swept = adjoint(own, near, far, 3, stretched(depth, depth_near, depth_far), spin[...], inside[...])
     first = lax.axis_index("win") == 0
     moments = [0.0, 0.0, 0.0, 0.0]
     for part, value in enumerate(swept):
@@ -89,8 +81,8 @@
         tally[row] = value
 
 
-def forward_kernel(state, near, far, depth, depth_near, depth_far, spin, inside, tally, end):
-    quarter = 0.25 * stacked(depth, depth_near, depth_far, 0)
+def forward_kernel(state, near, far, depth, depth_near, depth_far, spin, inside, lead, tally, sent):
+    quarter = stretched(depth, depth_near, depth_far)
     turn, keep = spin[...], inside[...]
     height, east, north = [stacked(state.at[0], near.at[0], far.at[0], part) for part in range(3)]
     for step in range(STEPS):
@@ -98,8 +90,20 @@
         east = east + turn * north - 0.25 * lon_gap(height)
         north = north - turn * east - 0.25 * lat_gap(height)
     rows = state.shape[2]
+    square = 0.0
     for part, value in enumerate((height, east, north)):
-        end[0, part] = value[rows:2 * rows]
+        zp = lead[0, part] - value[rows:2 * rows]
+        square += lane_sum(zp * zp)
+    last = lax.axis_index("win") == lax.axis_size("win") - 1
+    moments = [tally[0], tally[1], tally[2], tally[3] + jnp.where(last, 0.0, square)]
+    lane = lax.broadcasted_iota(jnp.int32, (1, 128), 1)
+    row = 0.0
+    for slot, value in enumerate(moments):
+        folded = jnp.sum(value, axis=0, keepdims=True)
+        folded = folded + pltpu.roll(folded, 64, 1)
+        folded = folded + pltpu.roll(folded, 32, 1)
+        row = jnp.where(lane // 32 == slot, folded, row)
+    sent[...] = jnp.broadcast_to(row, sent.shape)
 
 
 def lane_sum(value):
@@ -110,23 +114,6 @@
     return total
 
 
-def inner_kernel(lead, end, tally, tile):
-    last = lax.axis_index("win") == lax.axis_size("win") - 1
-    square = 0.0
-    for part in range(3):
-        zp = lead[0, part] - end[0, part]
-        square += lane_sum(zp * zp)
-    moments = [tally[0], tally[1], tally[2], tally[3] + jnp.where(last, 0.0, square)]
-    rows = [jnp.sum(value, axis=0, keepdims=True) for value in moments]
-    tile[...] = jnp.concatenate(rows + rows, axis=0)
-
-
-def spread_kernel(own, other, sent):
-    tile = own[...] + other[...]
-    for rank in range(sent.shape[0] // 8):
-        sent[8 * rank:8 * rank + 8] = tile
-
-
 def two_sum(a, b):
     total = a + b
     part = total - a
@@ -157,21 +144,20 @@
 
 
 def coefficients(gathered):
-    top = gathered[0:8]
-    for rank in range(1, gathered.shape[0] // 8):
-        top = top + gathered[8 * rank:8 * rank + 8]
+    top = jnp.sum(gathered[...], axis=0, keepdims=True)
     low = jnp.zeros_like(top)
-    shift = 64
-    while shift:
-        total, rest = two_sum(top, pltpu.roll(top, shift, 1))
+    shift = 1
+    while shift < 32:
+        top, rest = two_sum(top, pltpu.roll(top, shift, 1))
         low = low + pltpu.roll(low, shift, 1) + rest
-        top = total
-        shift //= 2
-    scale = 1.0 / top[1:2, :128]
+        shift *= 2
+    tops = [jnp.broadcast_to(top[:, lane:lane + 1], (1, 128)) for lane in range(31, 128, 32)]
+    lows = [jnp.broadcast_to(low[:, lane:lane + 1], (1, 128)) for lane in range(31, 128, 32)]
+    scale = 1.0 / tops[1]
     moments = []
-    for row in range(4):
-        product, rest = two_product(top[row:row + 1], scale)
-        moments.append((product, rest + low[row:row + 1] * scale))
+    for value, rest in zip(tops, lows):
+        product, error = two_product(value, scale)
+        moments.append((product, error + rest * scale))
     m1, m2, m3, m4 = moments
     gap = pair_gap(pair_product(m2, m4), pair_product(m3, m3))
     y1 = pair_gap(pair_product(m1, m4), pair_product(m2, m3)) / gap
@@ -220,19 +206,26 @@
     return lax.axis_index("band") * lax.axis_size("half") + lax.axis_index("half")
 
 
-def swapped(value, first, win_step=0):
-    wins, lats = lax.axis_size("win"), lat_count()
+def swapped(value, first):
     pairs = []
-    for win in range(max(0, -win_step), min(wins, wins - win_step)):
-        for lat in range(first, lats - 1, 2):
-            for source, target in ((lat, lat + 1), (lat + 1, lat)):
-                pairs.append((win * lats + source, (win + win_step) * lats + target))
+    for lat in range(first, lat_count() - 1, 2):
+        pairs += [(lat, lat + 1), (lat + 1, lat)]
+    return lax.ppermute(value, ("band", "half"), pairs)
+
+
+def crossed(value, middle_step, edge_step):
+    wins = lax.axis_size("win")
+    pairs = []
+    for win in range(wins):
+        for source, target, step in ((1, 2, middle_step), (2, 1, middle_step), (0, 3, edge_step), (3, 0, edge_step)):
+            if step is not None and 0 <= win + step < wins:
+                pairs.append((4 * win + source, 4 * (win + step) + target))
     return lax.ppermute(value, ("win", "band", "half"), pairs)
 
 
 def body(model_rhs, obs_rhs, model_var, obs_var, obs_weight, depth):
     rows, width = model_rhs.shape[2:]
-    ranks = lax.axis_size("win") * lax.axis_size("band")
+    ranks = lax.axis_size("win") * lat_count()
     total_rows = rows * lat_count()
     offset = (GRID_ROWS - total_rows) // 2
     local_rows = lat_index() * rows - rows + jnp.arange(3 * rows, dtype=jnp.int32)
@@ -242,31 +235,31 @@
     inside = jnp.broadcast_to(inside[:, None], (3 * rows, width))
     spin = jnp.broadcast_to(spin[:, None], (3 * rows, width))
     field = model_rhs.shape
+    depth_near = swapped(depth, 0)
     came = shifted(model_rhs, -1)
-    came_far = swapped(model_rhs, 1, -1)
-    place = (depth, swapped(depth, 0), swapped(depth, 1), spin, inside)
-    (scaled,) = run(
-        scale_kernel, [field], model_rhs, model_var, space=pltpu.HBM,
-        scratch=[pltpu.VMEM(field, jnp.float32)] * 2 + [pltpu.SemaphoreType.DMA((2,))],
+    scaled = model_rhs * model_var
+    pair = jnp.concatenate([model_rhs, scaled], axis=1)
+    edges = jnp.where(is_middle(), pair, depth_near[:, None])
+    far = crossed(edges, -1, 0)
+    place = (depth, depth_near, swapped(far[:, 0], 0), spin, inside)
+    held_scaled, _ = lax.optimization_barrier((scaled, edges))
+    scaled_came = shifted(held_scaled, -1)
+    state, lead = run(
+        first_adjoint_kernel, [field] * 2,
+        came, swapped(came, 0), far, *place, model_rhs, obs_rhs, model_var, obs_weight,
     )
-    scaled_came = shifted(scaled, -1)
-    scaled_far = swapped(scaled, 1, -1)
-    state, lead = run(
-        first_adjoint_kernel, [field, field],
-        came, swapped(came, 0), came_far, *place, model_rhs, obs_rhs, model_var, obs_weight,
-    )
-    near, far = swapped(state, 0), swapped(state, 1)
     lead_came = shifted(lead, -1)
     held, _ = lax.optimization_barrier((scaled_came, state))
     (tally,) = run(
         second_adjoint_kernel, [(4, rows, 128)],
-        scaled_came, swapped(held, 0), scaled_far, *place,
+        scaled_came, swapped(held, 0), far, *place,
         model_rhs, obs_rhs, model_var, obs_var, obs_weight, state, lead,
     )
-    (end,) = run(forward_kernel, [field], state, near, far, *place, tally)
-    (tile,) = run(inner_kernel, [(8, 128)], lead_came, end, tally)
-    (sent,) = run(spread_kernel, [(8 * ranks, 128)], tile, swapped(tile, 0))
-    gathered = lax.all_to_all(sent, ("win", "band"), 0, 0, tiled=True)
+    (sent,) = run(
+        forward_kernel, [(ranks, 128)],
+        state, swapped(state, 0), crossed(state, 0, None), *place, lead_came, tally,
+    )
+    gathered = lax.all_to_all(sent, ("win", "band", "half"), 0, 0, tiled=True)
     return run(combine_kernel, [field] * 3, gathered, model_rhs, obs_rhs, model_var, obs_var, state)
 
 

time: 47.3 us -> 45.7 us (0.966)
  waiting for transfers between devices: 9.12 us -> 11.5 us
  blocking collectives: 16.4 us -> 14.5 us
  starting transfers between devices: 14.3 us -> 12.5 us
  Pallas kernels: 5.98 us -> 4.81 us
  other arithmetic: 0.06 us -> 1.11 us
    ppermute x3, waiting for transfers between devices: 8.2 us -> 10.7 us  [shifted(): lax.ppermute(value, 'win', [(source, source + step) for source in range(i...]
    all_to_all x1, blocking collectives: 16.4 us -> 14.5 us  [body(): gathered = lax.all_to_all(sent, ('win', 'band', 'half'), 0, 0, tiled=True)]
    ppermute x9 -> x7, starting transfers between devices: 10.5 us -> 8.66 us  [the longest x2 5.31 us: crossed(): return lax.ppermute(value, ('win', 'band', 'half'), pairs)]
    pallas_call x7 -> x4, Pallas kernels: 5.98 us -> 4.81 us  [run(): pl.pallas_call(kernel, out_shape=shapes, in_specs=[pl.BlockSpec(memory_sp...]
    mul x0 -> x1, other arithmetic: none -> 1.04 us  [body(): scaled = model_rhs * model_var]
  transfers between devices with their start and end apart: 12 -> 10, of which waited for: 4 -> 5; matrix products, arithmetic and copies ran while one was open for 0% -> 3% of each run, Pallas kernels for 10% -> 5%
where the time goes in v6:
time: 45.7 us; the launch traced here: 45.4 us
  blocking collectives  14.5 us (32%)
  starting transfers between devices  12.5 us (27%)
  waiting for transfers between devices  11.5 us (25%)
  Pallas kernels  4.81 us (11%)
  other arithmetic  1.11 us (2%)
  between operations  0.8 us (2%)
    all_to_all x1, blocking collectives, body(): gathered = lax.all_to_all(sent, ('win', 'band', 'half'), 0, 0, tiled=True)  14.5 us
    ppermute x3, waiting for transfers between devices, shifted(): lax.ppermute(value, 'win', [(source, source + step) for source in range(i...  10.7 us
    ppermute x2, starting transfers between devices, crossed(): return lax.ppermute(value, ('win', 'band', 'half'), pairs)  5.31 us
    pallas_call x4, Pallas kernels, run(): pl.pallas_call(kernel, out_shape=shapes, in_specs=[pl.BlockSpec(memory_sp...  4.81 us
    ppermute x3, starting transfers between devices, shifted(): lax.ppermute(value, 'win', [(source, source + step) for source in range(i...  3.86 us
    ppermute x5, starting transfers between devices, swapped(): return lax.ppermute(value, ('band', 'half'), pairs)  3.35 us
    mul x1, other arithmetic, body(): scaled = model_rhs * model_var  1.04 us
  transfers between devices with their start and end apart: 10, of which 5 were waited for; matrix products, arithmetic and copies ran while one was open for 3% of the time, Pallas kernels for 5%

profile of v6, /device:TPU:0, one launch (start us, length us, event | category | flops | bytes accessed | tf_op | source)
XLA Modules:
  0.0 45.4 jit_solution(18056766126822818972)
XLA Ops:
  0.6 0.5 %collective-permute-start.2 = (f32[1,8,1536]{2,1,0:T(8,128)}, f32[1,8,1536]{2,1,0:T(8,128)S(1)}, u32[]{:S(2)}, u32[]{:S(2)}) collective-permute-start(f32[1,8,1536]{2,1,0:T(8,128)} %depth.5), channel_id=1, source_target_pairs={{0,1},{1,0},{2,3},{3,2},{4,5},{5,4},{6,7},{7,6},{8,9},{9,8},{10,11... | collective-permute-start | bytes 147464 | tf_op jit(solution)/shard_map/ppermute | solution.py:213
  1.1 1.0 %mul.26 = f32[1,3,8,1536]{3,2,1,0:T(8,128)S(1)} multiply(f32[1,3,8,1536]{3,2,1,0:T(8,128)} %p.5, f32[1,3,8,1536]{3,2,1,0:T(8,128)} %dvar.5) | non-fusion elementwise | flops 36864 | bytes 442368 | tf_op jit(solution)/shard_map/mul | solution.py:240
  2.2 0.1 collective-permute-done.2.depth_near
  2.2 0.0 copy-done
  2.3 4.6 %collective-permute-start.3 = (f32[1,6,8,1536]{3,2,1,0:T(8,128)S(1)}, f32[1,6,8,1536]{3,2,1,0:T(8,128)S(1)}, u32[]{:S(2)}, u32[]{:S(2)}) collective-permute-start(f32[1,6,8,1536]{3,2,1,0:T(8,128)S(1)} %maximum_select_fusion), channel_id=1, source_target_pairs={{0,3},{3,0},{5,2},{6,1},{4,7},{7,4},{9,6},{10,5},{8,11},{11,8},{13... | collective-permute-start | bytes 884744 | tf_op jit(solution)/shard_map/ppermute | solution.py:223
  6.9 1.3 %collective-permute-start = (f32[1,3,8,1536]{3,2,1,0:T(8,128)S(1)}, f32[1,3,8,1536]{3,2,1,0:T(8,128)S(1)}, u32[]{:S(2)}, u32[]{:S(2)}) collective-permute-start(f32[1,3,8,1536]{3,2,1,0:T(8,128)S(1)} %copy-done), channel_id=1, source_target_pairs={{4,0},{8,4},{12,8},{16,12},{20,16},{24,20},{28,24},{5,1},{9,5},{13... | collective-permute-start | bytes 442376 | tf_op jit(solution)/shard_map/ppermute | solution.py:198
  8.2 1.3 %collective-permute-start.8 = (f32[1,3,8,1536]{3,2,1,0:T(8,128)S(1)}, f32[1,3,8,1536]{3,2,1,0:T(8,128)S(1)}, u32[]{:S(2)}, u32[]{:S(2)}) collective-permute-start(f32[1,3,8,1536]{3,2,1,0:T(8,128)S(1)} %mul.26), channel_id=1, source_target_pairs={{4,0},{8,4},{12,8},{16,12},{20,16},{24,20},{28,24},{5,1},{9,5},{13... | collective-permute-start | bytes 442376 | tf_op jit(solution)/shard_map/ppermute | solution.py:198
  9.5 7.8 %collective-permute-done.own = f32[1,3,8,1536]{3,2,1,0:T(8,128)S(1)} collective-permute-done((f32[1,3,8,1536]{3,2,1,0:T(8,128)S(1)}, f32[1,3,8,1536]{3,2,1,0:T(8,128)S(1)}, u32[]{:S(2)}, u32[]{:S(2)}) %collective-permute-start) | collective-permute-done | bytes 147488 | tf_op jit(solution)/shard_map/ppermute | solution.py:198
  17.3 0.0 collective-permute-start.1
  17.3 0.0 collective-permute-done.3.far
  17.3 0.6 %collective-permute-start.4 = (f32[1,8,1536]{2,1,0:T(8,128)S(1)}, f32[1,8,1536]{2,1,0:T(8,128)S(1)}, u32[]{:S(2)}, u32[]{:S(2)}) collective-permute-start(f32[1,8,1536]{2,1,0:T(8,128)S(1)} %slice_bitcast_fusion), channel_id=1, source_target_pairs={{0,1},{1,0},{2,3},{3,2},{4,5},{5,4},{6,7},{7,6},{8,9},{9,8},{10,11... | collective-permute-start | bytes 147464 | tf_op jit(solution)/shard_map/ppermute | solution.py:213
  17.9 0.0 copy-start.1
  18.0 0.0 copy-start.2
  18.0 0.7 %collective-permute-done.1.near = f32[1,3,8,1536]{3,2,1,0:T(8,128)S(1)} collective-permute-done((f32[1,3,8,1536]{3,2,1,0:T(8,128)S(1)}, f32[1,3,8,1536]{3,2,1,0:T(8,128)S(1)}, u32[]{:S(2)}, u32[]{:S(2)}) %collective-permute-start.1) | collective-permute-done | bytes 147488 | tf_op jit(solution)/shard_map/ppermute | solution.py:213
  18.7 0.1 collective-permute-done.4.depth_far
  18.8 0.1 broadcast_in_dim.25.spin
  18.9 0.1 broadcast_in_dim.26.inside
  19.0 0.0 copy-start.4
  19.0 1.2 %shard_map.85 = (f32[1,3,8,1536]{3,2,1,0:T(8,128)S(1)}, f32[1,3,8,1536]{3,2,1,0:T(8,128)S(1)}) custom-call(f32[1,3,8,1536]{3,2,1,0:T(8,128)S(1)} %collective-permute-done.own, f32[1,3,8,1536]{3,2,1,0:T(8,128)S(1)} %collective-permute-done.1.near, f32[1,6,8,1536]{3,2,1,0:T(8,128)S(1)} %collective-permute-done.3.far, f32[1,8,1536]{2,1,0:T(8,128)S(1)} %copy-done.5, ...), custom_call_target="tpu_custom_call" | custom-call | flops 7667712 | bytes 1916928 | tf_op jit(solution)/shard_map/pallas_call | solution.py:184
  20.2 0.0 collective-permute-done.8.own
  20.2 0.4 collective-permute-start.9
  20.6 1.3 %collective-permute-start.7 = (f32[1,3,8,1536]{3,2,1,0:T(8,128)S(1)}, f32[1,3,8,1536]{3,2,1,0:T(8,128)S(1)}, u32[]{:S(2)}, u32[]{:S(2)}) collective-permute-start(f32[1,3,8,1536]{3,2,1,0:T(8,128)S(1)} %get-tuple-element.8.lead), channel_id=1, source_target_pairs={{4,0},{8,4},{12,8},{16,12},{20,16},{24,20},{28,24},{5,1},{9,5},{13... | collective-permute-start | bytes 442376 | tf_op jit(solution)/shard_map/ppermute | solution.py:198
  21.9 0.7 %collective-permute-start.6 = (f32[1,3,8,1536]{3,2,1,0:T(8,128)S(1)}, f32[1,3,8,1536]{3,2,1,0:T(8,128)S(1)}, u32[]{:S(2)}, u32[]{:S(2)}) collective-permute-start(f32[1,3,8,1536]{3,2,1,0:T(8,128)S(1)} %get-tuple-element.7.state), channel_id=1, source_target_pairs={{1,2},{2,1},{5,6},{6,5},{9,10},{10,9},{13,14},{14,13},{17,18},{18,... | collective-permute-start | bytes 442376 | tf_op jit(solution)/shard_map/ppermute | solution.py:223
  22.6 1.8 %collective-permute-start.5 = (f32[1,3,8,1536]{3,2,1,0:T(8,128)S(1)}, f32[1,3,8,1536]{3,2,1,0:T(8,128)S(1)}, u32[]{:S(2)}, u32[]{:S(2)}) collective-permute-start(f32[1,3,8,1536]{3,2,1,0:T(8,128)S(1)} %get-tuple-element.7.state), channel_id=1, source_target_pairs={{0,1},{1,0},{2,3},{3,2},{4,5},{5,4},{6,7},{7,6},{8,9},{9,8},{10,11... | collective-permute-start | bytes 442376 | tf_op jit(solution)/shard_map/ppermute | solution.py:213
  24.4 0.0 collective-permute-done.9.near
  24.4 1.2 %shard_map.86.tally = f32[4,8,128]{2,1,0:T(8,128)S(1)} custom-call(f32[1,3,8,1536]{3,2,1,0:T(8,128)S(1)} %collective-permute-done.8.own, f32[1,3,8,1536]{3,2,1,0:T(8,128)S(1)} %collective-permute-done.9.near, f32[1,6,8,1536]{3,2,1,0:T(8,128)S(1)} %collective-permute-done.3.far, f32[1,8,1536]{2,1,0:T(8,128)S(1)} %copy-done.5, ...), custom_call_target="tpu_custom_call" | custom-call | flops 8323072 | bytes 2080768 | tf_op jit(solution)/shard_map/pallas_call | solution.py:184
  25.6 2.9 %collective-permute-done.7.lead = f32[1,3,8,1536]{3,2,1,0:T(8,128)S(1)} collective-permute-done((f32[1,3,8,1536]{3,2,1,0:T(8,128)S(1)}, f32[1,3,8,1536]{3,2,1,0:T(8,128)S(1)}, u32[]{:S(2)}, u32[]{:S(2)}) %collective-permute-start.7) | collective-permute-done | bytes 147488 | tf_op jit(solution)/shard_map/ppermute | solution.py:198
  28.6 0.0 collective-permute-done.6.far
  28.6 0.0 collective-permute-done.5.near
  28.6 1.2 %shard_map.87 = f32[32,128]{1,0:T(8,128)S(1)} custom-call(f32[1,3,8,1536]{3,2,1,0:T(8,128)S(1)} %get-tuple-element.7.state, f32[1,3,8,1536]{3,2,1,0:T(8,128)S(1)} %collective-permute-done.5.near, f32[1,3,8,1536]{3,2,1,0:T(8,128)S(1)} %collective-permute-done.6.far, f32[1,8,1536]{2,1,0:T(8,128)S(1)} %copy-done.5, ...), custom_call_target="tpu_custom_call" | custom-call | flops 4259840 | bytes 1064960 | tf_op jit(solution)/shard_map/pallas_call | solution.py:184
  29.8 14.5 %all_to_all.11 = f32[32,1,128]{2,1,0:T(1,128)S(1)} all-to-all(f32[32,1,128]{2,1,0:T(1,128)S(1)} %bitcast.8), channel_id=1, replica_groups=mesh['win'=8,'band'=2,'half'=2] {'win','band','half'}, dimensions={0} | all-to-all | bytes 32768 | tf_op jit(solution)/shard_map/all_to_all | solution.py:262
  44.2 1.2 %shard_map.88 = (f32[1,3,8,1536]{3,2,1,0:T(8,128)}, f32[1,3,8,1536]{3,2,1,0:T(8,128)}, f32[1,3,8,1536]{3,2,1,0:T(8,128)}) custom-call(f32[32,128]{1,0:T(8,128)S(1)} %bitcast.9, f32[1,3,8,1536]{3,2,1,0:T(8,128)S(1)} %copy-done, f32[1,3,8,1536]{3,2,1,0:T(8,128)S(1)} %copy-done.2, f32[1,3,8,1536]{3,2,1,0:T(8,128)S(1)} %copy-done.1, ...), custom_call_target="tpu_custom_call" | custom-call | flops 4784128 | bytes 1196032 | tf_op jit(solution)/shard_map/pallas_call | solution.py:184
  (12 shorter events, 0.1 us)
Async XLA Ops:
  0.6 1.6 %collective-permute-start.2 = (f32[1,8,1536]{2,1,0:T(8,128)}, f32[1,8,1536]{2,1,0:T(8,128)S(1)}, u32[]{:S(2)}, u32[]{:S(2)}) collective-permute-start(f32[1,8,1536]{2,1,0:T(8,128)} %depth.5), channel_id=1, source_target_pairs={{0,1},{1,0},{2,3},{3,2},{4,5},{5,4},{6,7},{7,6},{8,9},{9,8},{10,11... | collective-permute-start | bytes 147464 | tf_op jit(solution)/shard_map/ppermute | solution.py:213
  1.1 1.1 %copy-start = (f32[1,3,8,1536]{3,2,1,0:T(8,128)S(1)}, f32[1,3,8,1536]{3,2,1,0:T(8,128)}, u32[]{:S(2)}) copy-start(f32[1,3,8,1536]{3,2,1,0:T(8,128)} %p.5) | copy-start | bytes 442372
  2.2 16.7 %copy-start.3 = (f32[1,3,8,1536]{3,2,1,0:T(8,128)S(1)}, f32[1,3,8,1536]{3,2,1,0:T(8,128)}, u32[]{:S(2)}) copy-start(f32[1,3,8,1536]{3,2,1,0:T(8,128)} %hobs.3) | copy-start | bytes 442372
  2.3 15.0 %collective-permute-start.3 = (f32[1,6,8,1536]{3,2,1,0:T(8,128)S(1)}, f32[1,6,8,1536]{3,2,1,0:T(8,128)S(1)}, u32[]{:S(2)}, u32[]{:S(2)}) collective-permute-start(f32[1,6,8,1536]{3,2,1,0:T(8,128)S(1)} %maximum_select_fusion), channel_id=1, source_target_pairs={{0,3},{3,0},{5,2},{6,1},{4,7},{7,4},{9,6},{10,5},{8,11},{11,8},{13... | collective-permute-start | bytes 884744 | tf_op jit(solution)/shard_map/ppermute | solution.py:223
  6.9 10.4 %collective-permute-start = (f32[1,3,8,1536]{3,2,1,0:T(8,128)S(1)}, f32[1,3,8,1536]{3,2,1,0:T(8,128)S(1)}, u32[]{:S(2)}, u32[]{:S(2)}) collective-permute-start(f32[1,3,8,1536]{3,2,1,0:T(8,128)S(1)} %copy-done), channel_id=1, source_target_pairs={{4,0},{8,4},{12,8},{16,12},{20,16},{24,20},{28,24},{5,1},{9,5},{13... | collective-permute-start | bytes 442376 | tf_op jit(solution)/shard_map/ppermute | solution.py:198
  8.2 11.9 %collective-permute-start.8 = (f32[1,3,8,1536]{3,2,1,0:T(8,128)S(1)}, f32[1,3,8,1536]{3,2,1,0:T(8,128)S(1)}, u32[]{:S(2)}, u32[]{:S(2)}) collective-permute-start(f32[1,3,8,1536]{3,2,1,0:T(8,128)S(1)} %mul.26), channel_id=1, source_target_pairs={{4,0},{8,4},{12,8},{16,12},{20,16},{24,20},{28,24},{5,1},{9,5},{13... | collective-permute-start | bytes 442376 | tf_op jit(solution)/shard_map/ppermute | solution.py:198
  17.3 1.4 %collective-permute-start.1 = (f32[1,3,8,1536]{3,2,1,0:T(8,128)S(1)}, f32[1,3,8,1536]{3,2,1,0:T(8,128)S(1)}, u32[]{:S(2)}, u32[]{:S(2)}) collective-permute-start(f32[1,3,8,1536]{3,2,1,0:T(8,128)S(1)} %collective-permute-done.own), channel_id=1, source_target_pairs={{0,1},{1,0},{2,3},{3,2},{4,5},{5,4},{6,7},{7,6},{8,9},{9,8},{10,11... | collective-permute-start | bytes 442376 | tf_op jit(solution)/shard_map/ppermute | solution.py:213
  17.3 1.6 %copy-start.5 = (f32[1,8,1536]{2,1,0:T(8,128)S(1)}, f32[1,8,1536]{2,1,0:T(8,128)}, u32[]{:S(2)}) copy-start(f32[1,8,1536]{2,1,0:T(8,128)} %depth.5) | copy-start | bytes 147460
  17.3 1.4 %collective-permute-start.4 = (f32[1,8,1536]{2,1,0:T(8,128)S(1)}, f32[1,8,1536]{2,1,0:T(8,128)S(1)}, u32[]{:S(2)}, u32[]{:S(2)}) collective-permute-start(f32[1,8,1536]{2,1,0:T(8,128)S(1)} %slice_bitcast_fusion), channel_id=1, source_target_pairs={{0,1},{1,0},{2,3},{3,2},{4,5},{5,4},{6,7},{7,6},{8,9},{9,8},{10,11... | collective-permute-start | bytes 147464 | tf_op jit(solution)/shard_map/ppermute | solution.py:213
  17.9 1.0 %copy-start.1 = (f32[1,3,8,1536]{3,2,1,0:T(8,128)S(1)}, f32[1,3,8,1536]{3,2,1,0:T(8,128)}, u32[]{:S(2)}) copy-start(f32[1,3,8,1536]{3,2,1,0:T(8,128)} %dvar.5) | copy-start | bytes 442372
  18.0 1.0 %copy-start.2 = (f32[1,3,8,1536]{3,2,1,0:T(8,128)S(1)}, f32[1,3,8,1536]{3,2,1,0:T(8,128)}, u32[]{:S(2)}) copy-start(f32[1,3,8,1536]{3,2,1,0:T(8,128)} %m.5) | copy-start | bytes 442372
  19.0 5.4 %copy-start.4 = (f32[1,3,8,1536]{3,2,1,0:T(8,128)S(1)}, f32[1,3,8,1536]{3,2,1,0:T(8,128)}, u32[]{:S(2)}) copy-start(f32[1,3,8,1536]{3,2,1,0:T(8,128)} %rvar.3) | copy-start | bytes 442372
  20.2 4.2 %collective-permute-start.9 = (f32[1,3,8,1536]{3,2,1,0:T(8,128)S(1)}, f32[1,3,8,1536]{3,2,1,0:T(8,128)S(1)}, u32[]{:S(2)}, u32[]{:S(2)}) collective-permute-start(f32[1,3,8,1536]{3,2,1,0:T(8,128)S(1)} %collective-permute-done.8.own), channel_id=1, source_target_pairs={{0,1},{1,0},{2,3},{3,2},{4,5},{5,4},{6,7},{7,6},{8,9},{9,8},{10,11... | collective-permute-start | bytes 442376 | tf_op jit(solution)/shard_map/ppermute | solution.py:213
  20.6 8.0 %collective-permute-start.7 = (f32[1,3,8,1536]{3,2,1,0:T(8,128)S(1)}, f32[1,3,8,1536]{3,2,1,0:T(8,128)S(1)}, u32[]{:S(2)}, u32[]{:S(2)}) collective-permute-start(f32[1,3,8,1536]{3,2,1,0:T(8,128)S(1)} %get-tuple-element.8.lead), channel_id=1, source_target_pairs={{4,0},{8,4},{12,8},{16,12},{20,16},{24,20},{28,24},{5,1},{9,5},{13... | collective-permute-start | bytes 442376 | tf_op jit(solution)/shard_map/ppermute | solution.py:198
  21.9 6.7 %collective-permute-start.6 = (f32[1,3,8,1536]{3,2,1,0:T(8,128)S(1)}, f32[1,3,8,1536]{3,2,1,0:T(8,128)S(1)}, u32[]{:S(2)}, u32[]{:S(2)}) collective-permute-start(f32[1,3,8,1536]{3,2,1,0:T(8,128)S(1)} %get-tuple-element.7.state), channel_id=1, source_target_pairs={{1,2},{2,1},{5,6},{6,5},{9,10},{10,9},{13,14},{14,13},{17,18},{18,... | collective-permute-start | bytes 442376 | tf_op jit(solution)/shard_map/ppermute | solution.py:223
  22.6 6.0 %collective-permute-start.5 = (f32[1,3,8,1536]{3,2,1,0:T(8,128)S(1)}, f32[1,3,8,1536]{3,2,1,0:T(8,128)S(1)}, u32[]{:S(2)}, u32[]{:S(2)}) collective-permute-start(f32[1,3,8,1536]{3,2,1,0:T(8,128)S(1)} %get-tuple-element.7.state), channel_id=1, source_target_pairs={{0,1},{1,0},{2,3},{3,2},{4,5},{5,4},{6,7},{7,6},{8,9},{9,8},{10,11... | collective-permute-start | bytes 442376 | tf_op jit(solution)/shard_map/ppermute | solution.py:213

commit v7 on v6

--- a/solution.py
+++ b/solution.py
@@ -35,13 +35,22 @@
     return jnp.concatenate([low, own[index], high], axis=0)
 
 
+def scale_kernel(p, dvar, scaled, pv, dv, sems):
+    copies = [pltpu.make_async_copy(p, pv, sems.at[0]), pltpu.make_async_copy(dvar, dv, sems.at[1])]
+    for copy in copies:
+        copy.start()
+    for copy in copies:
+        copy.wait()
+    for part in range(3):
+        scaled[0, part] = dv[0, part] * pv[0, part]
+
+
 def stretched(depth, depth_near, depth_far):
     return 0.25 * stacked(depth, depth_near, depth_far, 0)
 
 
-def adjoint(own, near, far, far_start, depth, turn, keep):
-    outer = far.at[0, far_start:far_start + 3]
-    adj_height, adj_east, adj_north = [stacked(own.at[0], near.at[0], outer, part) for part in range(3)]
+def adjoint(own, near, far, depth, turn, keep):
+    adj_height, adj_east, adj_north = [stacked(own.at[0], near.at[0], far.at[0], part) for part in range(3)]
     for step in range(STEPS):
         adj_mid = adj_east - turn * adj_north
         adj_height = keep * (adj_height + 0.25 * (lat_gap(adj_north) + lon_gap(adj_mid)))
@@ -52,7 +61,7 @@
 
 
 def first_adjoint_kernel(own, near, far, depth, depth_near, depth_far, spin, inside, p, m, dvar, hobs, state, lead):
-    swept = adjoint(own, near, far, 0, stretched(depth, depth_near, depth_far), spin[...], inside[...])
+    swept = adjoint(own, near, far, stretched(depth, depth_near, depth_far), spin[...], inside[...])
     for part, value in enumerate(swept):
         pv, dv = p[0, part], dvar[0, part]
         ux = pv - value + hobs[0, part] * m[0, part]
@@ -63,7 +72,7 @@
 def second_adjoint_kernel(
     own, near, far, depth, depth_near, depth_far, spin, inside, p, m, dvar, rvar, hobs, state, lead, tally
 ):
-    swept = adjoint(own, near, far, 3, stretched(depth, depth_near, depth_far), spin[...], inside[...])
+    swept = adjoint(own, near, far, stretched(depth, depth_near, depth_far), spin[...], inside[...])
     first = lax.axis_index("win") == 0
     moments = [0.0, 0.0, 0.0, 0.0]
     for part, value in enumerate(swept):
@@ -213,13 +222,13 @@
     return lax.ppermute(value, ("band", "half"), pairs)
 
 
-def crossed(value, middle_step, edge_step):
+def crossed(value, ends, win_step=0):
     wins = lax.axis_size("win")
     pairs = []
     for win in range(wins):
-        for source, target, step in ((1, 2, middle_step), (2, 1, middle_step), (0, 3, edge_step), (3, 0, edge_step)):
-            if step is not None and 0 <= win + step < wins:
-                pairs.append((4 * win + source, 4 * (win + step) + target))
+        for source, target in (ends, ends[::-1]):
+            if 0 <= win + win_step < wins:
+                pairs.append((4 * win + source, 4 * (win + win_step) + target))
     return lax.ppermute(value, ("win", "band", "half"), pairs)
 
 
@@ -235,29 +244,31 @@
     inside = jnp.broadcast_to(inside[:, None], (3 * rows, width))
     spin = jnp.broadcast_to(spin[:, None], (3 * rows, width))
     field = model_rhs.shape
+    middle, outer = (1, 2), (0, 3)
+    came = shifted(model_rhs, -1)
+    came_far = crossed(model_rhs, middle, -1)
     depth_near = swapped(depth, 0)
-    came = shifted(model_rhs, -1)
-    scaled = model_rhs * model_var
-    pair = jnp.concatenate([model_rhs, scaled], axis=1)
-    edges = jnp.where(is_middle(), pair, depth_near[:, None])
-    far = crossed(edges, -1, 0)
-    place = (depth, depth_near, swapped(far[:, 0], 0), spin, inside)
-    held_scaled, _ = lax.optimization_barrier((scaled, edges))
-    scaled_came = shifted(held_scaled, -1)
+    place = (depth, depth_near, swapped(crossed(depth_near, outer), 0), spin, inside)
+    (scaled,) = run(
+        scale_kernel, [field], model_rhs, model_var, space=pltpu.HBM,
+        scratch=[pltpu.VMEM(field, jnp.float32)] * 2 + [pltpu.SemaphoreType.DMA((2,))],
+    )
+    scaled_came = shifted(scaled, -1)
+    scaled_far = crossed(swapped(scaled, 0), outer, -1)
     state, lead = run(
         first_adjoint_kernel, [field] * 2,
-        came, swapped(came, 0), far, *place, model_rhs, obs_rhs, model_var, obs_weight,
+        came, swapped(came, 0), came_far, *place, model_rhs, obs_rhs, model_var, obs_weight,
     )
     lead_came = shifted(lead, -1)
-    held, _ = lax.optimization_barrier((scaled_came, state))
+    held, held_far, _ = lax.optimization_barrier((scaled_came, scaled_far, state))
     (tally,) = run(
         second_adjoint_kernel, [(4, rows, 128)],
-        scaled_came, swapped(held, 0), far, *place,
+        scaled_came, swapped(held, 0), swapped(held_far, 0), *place,
         model_rhs, obs_rhs, model_var, obs_var, obs_weight, state, lead,
     )
     (sent,) = run(
         forward_kernel, [(ranks, 128)],
-        state, swapped(state, 0), crossed(state, 0, None), *place, lead_came, tally,
+        state, swapped(state, 0), crossed(state, middle), *place, lead_came, tally,
     )
     gathered = lax.all_to_all(sent, ("win", "band", "half"), 0, 0, tiled=True)
     return run(combine_kernel, [field] * 3, gathered, model_rhs, obs_rhs, model_var, obs_var, state)

time: 45.7 us -> 47.3 us (1.035)
  blocking collectives: 14.5 us -> 16.4 us
  Pallas kernels: 4.81 us -> 5.86 us
  other arithmetic: 1.11 us -> 0.06 us
    ppermute x3, waiting for transfers between devices: 10.7 us -> 6.82 us  [shifted(): lax.ppermute(value, 'win', [(source, source + step) for source in range(i...]
    ppermute x2 -> x4, waiting for transfers between devices: 0.01 us -> 3.24 us  [crossed(): return lax.ppermute(value, ('win', 'band', 'half'), pairs)]
    ppermute x5 -> x7, starting transfers between devices: 3.35 us -> 1.19 us  [swapped(): return lax.ppermute(value, ('band', 'half'), pairs)]
    all_to_all x1, blocking collectives: 14.5 us -> 16.4 us  [body(): gathered = lax.all_to_all(sent, ('win', 'band', 'half'), 0, 0, tiled=True)]
    ppermute x2 -> x4, starting transfers between devices: 5.31 us -> 7.12 us  [crossed(): return lax.ppermute(value, ('win', 'band', 'half'), pairs)]
    pallas_call x4 -> x5, Pallas kernels: 4.81 us -> 5.86 us  [run(): pl.pallas_call(kernel, out_shape=shapes, in_specs=[pl.BlockSpec(memory_sp...]
    mul x1 -> x0, other arithmetic: 1.04 us -> none  [body(): scaled = model_rhs * model_var]
    ppermute x5 -> x7, waiting for transfers between devices: 0.87 us -> 1.21 us  [swapped(): return lax.ppermute(value, ('band', 'half'), pairs)]
  transfers between devices with their start and end apart: 10 -> 14, of which waited for: 5 -> 5; matrix products, arithmetic and copies ran while one was open for 3% -> 0% of each run, Pallas kernels for 5% -> 7%
where the time goes in v7:
time: 47.3 us; the launch traced here: 47 us
  blocking collectives  16.4 us (35%)
  starting transfers between devices  12.3 us (26%)
  waiting for transfers between devices  11.3 us (24%)
  Pallas kernels  5.86 us (12%)
  between operations  0.88 us (2%)
    all_to_all x1, blocking collectives, body(): gathered = lax.all_to_all(sent, ('win', 'band', 'half'), 0, 0, tiled=True)  16.4 us
    ppermute x4, starting transfers between devices, crossed(): return lax.ppermute(value, ('win', 'band', 'half'), pairs)  7.12 us
    ppermute x3, waiting for transfers between devices, shifted(): lax.ppermute(value, 'win', [(source, source + step) for source in range(i...  6.82 us
    pallas_call x5, Pallas kernels, run(): pl.pallas_call(kernel, out_shape=shapes, in_specs=[pl.BlockSpec(memory_sp...  5.86 us
    ppermute x3, starting transfers between devices, shifted(): lax.ppermute(value, 'win', [(source, source + step) for source in range(i...  4.01 us
    ppermute x4, waiting for transfers between devices, crossed(): return lax.ppermute(value, ('win', 'band', 'half'), pairs)  3.24 us
    ppermute x7, waiting for transfers between devices, swapped(): return lax.ppermute(value, ('band', 'half'), pairs)  1.21 us
    ppermute x7, starting transfers between devices, swapped(): return lax.ppermute(value, ('band', 'half'), pairs)  1.19 us
  transfers between devices with their start and end apart: 14, of which 5 were waited for; matrix products, arithmetic and copies ran while one was open for 0% of the time, Pallas kernels for 7%

profile of v7, /device:TPU:0, one launch (start us, length us, event | category | flops | bytes accessed | tf_op | source)
XLA Modules:
  0.0 47.0 jit_solution(1775023477990961282)
XLA Ops:
  0.7 1.4 %collective-permute-start = (f32[1,3,8,1536]{3,2,1,0:T(8,128)}, f32[1,3,8,1536]{3,2,1,0:T(8,128)S(1)}, u32[]{:S(2)}, u32[]{:S(2)}) collective-permute-start(f32[1,3,8,1536]{3,2,1,0:T(8,128)} %p.7), channel_id=1, source_target_pairs={{4,0},{8,4},{12,8},{16,12},{20,16},{24,20},{28,24},{5,1},{9,5},{13... | collective-permute-start | bytes 442376 | tf_op jit(solution)/shard_map/ppermute | solution.py:207
  2.1 1.1 %shard_map.86 = f32[1,3,8,1536]{3,2,1,0:T(8,128)S(1)} custom-call(f32[1,3,8,1536]{3,2,1,0:T(8,128)} %p.7, f32[1,3,8,1536]{3,2,1,0:T(8,128)} %dvar.7), custom_call_target="tpu_custom_call" | custom-call | flops 1769472 | bytes 442368 | tf_op jit(solution)/shard_map/pallas_call | solution.py:193
  3.1 0.5 %collective-permute-start.10 = (f32[1,3,8,1536]{3,2,1,0:T(8,128)S(1)}, f32[1,3,8,1536]{3,2,1,0:T(8,128)S(1)}, u32[]{:S(2)}, u32[]{:S(2)}) collective-permute-start(f32[1,3,8,1536]{3,2,1,0:T(8,128)S(1)} %shard_map.86), channel_id=1, source_target_pairs={{0,1},{1,0},{2,3},{3,2},{4,5},{5,4},{6,7},{7,6},{8,9},{9,8},{10,11... | collective-permute-start | bytes 442376 | tf_op jit(solution)/shard_map/ppermute | solution.py:222
  3.7 0.1 collective-permute-start.3
  3.8 0.7 %collective-permute-start.2 = (f32[1,3,8,1536]{3,2,1,0:T(8,128)S(1)}, f32[1,3,8,1536]{3,2,1,0:T(8,128)S(1)}, u32[]{:S(2)}, u32[]{:S(2)}) collective-permute-start(f32[1,3,8,1536]{3,2,1,0:T(8,128)S(1)} %copy-done), channel_id=1, source_target_pairs={{5,2},{6,1},{9,6},{10,5},{13,10},{14,9},{17,14},{18,13},{21,18},{2... | collective-permute-start | bytes 442376 | tf_op jit(solution)/shard_map/ppermute | solution.py:232
  4.4 1.3 %collective-permute-start.9 = (f32[1,3,8,1536]{3,2,1,0:T(8,128)S(1)}, f32[1,3,8,1536]{3,2,1,0:T(8,128)S(1)}, u32[]{:S(2)}, u32[]{:S(2)}) collective-permute-start(f32[1,3,8,1536]{3,2,1,0:T(8,128)S(1)} %shard_map.86), channel_id=1, source_target_pairs={{4,0},{8,4},{12,8},{16,12},{20,16},{24,20},{28,24},{5,1},{9,5},{13... | collective-permute-start | bytes 442376 | tf_op jit(solution)/shard_map/ppermute | solution.py:207
  5.7 0.0 collective-permute-done.3.depth_near
  5.7 4.5 %collective-permute-start.4 = (f32[1,8,1536]{2,1,0:T(8,128)S(1)}, f32[1,8,1536]{2,1,0:T(8,128)S(1)}, u32[]{:S(2)}, u32[]{:S(2)}) collective-permute-start(f32[1,8,1536]{2,1,0:T(8,128)S(1)} %collective-permute-done.3.depth_near), channel_id=1, source_target_pairs={{0,3},{3,0},{4,7},{7,4},{8,11},{11,8},{12,15},{15,12},{16,19},{19,... | collective-permute-start | bytes 147464 | tf_op jit(solution)/shard_map/ppermute | solution.py:232
  10.3 0.1 collective-permute-start.1
  10.3 0.0 collective-permute-done.10
  10.4 1.3 %collective-permute-start.11 = (f32[1,3,8,1536]{3,2,1,0:T(8,128)S(1)}, f32[1,3,8,1536]{3,2,1,0:T(8,128)S(1)}, u32[]{:S(2)}, u32[]{:S(2)}) collective-permute-start(f32[1,3,8,1536]{3,2,1,0:T(8,128)S(1)} %collective-permute-done.10), channel_id=1, source_target_pairs={{4,3},{7,0},{8,7},{11,4},{12,11},{15,8},{16,15},{19,12},{20,19},{2... | collective-permute-start | bytes 442376 | tf_op jit(solution)/shard_map/ppermute | solution.py:232
  11.7 0.1 multiply_select_fusion
  11.7 0.3 collective-permute-done.4
  12.0 0.0 collective-permute-start.5
  12.0 0.0 copy-start.1
  12.0 0.0 copy-start.2
  12.1 1.2 %collective-permute-done.5.depth_far = f32[1,8,1536]{2,1,0:T(8,128)S(1)} collective-permute-done((f32[1,8,1536]{2,1,0:T(8,128)S(1)}, f32[1,8,1536]{2,1,0:T(8,128)S(1)}, u32[]{:S(2)}, u32[]{:S(2)}) %collective-permute-start.5) | collective-permute-done | bytes 49184 | tf_op jit(solution)/shard_map/ppermute | solution.py:222
  13.3 0.1 broadcast_in_dim.4.spin
  13.3 0.1 broadcast_in_dim.5.inside
  13.5 0.0 copy-start.4
  13.5 1.2 %shard_map.85 = (f32[1,3,8,1536]{3,2,1,0:T(8,128)S(1)}, f32[1,3,8,1536]{3,2,1,0:T(8,128)S(1)}) custom-call(f32[1,3,8,1536]{3,2,1,0:T(8,128)S(1)} %collective-permute-done.own, f32[1,3,8,1536]{3,2,1,0:T(8,128)S(1)} %collective-permute-done.1.near, f32[1,3,8,1536]{3,2,1,0:T(8,128)S(1)} %collective-permute-done.2.far, f32[1,8,1536]{2,1,0:T(8,128)S(1)} %copy-done.5, ...), custom_call_target="tpu_custom_call" | custom-call | flops 7077888 | bytes 1769472 | tf_op jit(solution)/shard_map/pallas_call | solution.py:193
  14.6 0.6 %collective-permute-done.9.own = f32[1,3,8,1536]{3,2,1,0:T(8,128)S(1)} collective-permute-done((f32[1,3,8,1536]{3,2,1,0:T(8,128)S(1)}, f32[1,3,8,1536]{3,2,1,0:T(8,128)S(1)}, u32[]{:S(2)}, u32[]{:S(2)}) %collective-permute-start.9) | collective-permute-done | bytes 147488 | tf_op jit(solution)/shard_map/ppermute | solution.py:207
  15.3 2.9 %collective-permute-done.11 = f32[1,3,8,1536]{3,2,1,0:T(8,128)S(1)} collective-permute-done((f32[1,3,8,1536]{3,2,1,0:T(8,128)S(1)}, f32[1,3,8,1536]{3,2,1,0:T(8,128)S(1)}, u32[]{:S(2)}, u32[]{:S(2)}) %collective-permute-start.11) | collective-permute-done | bytes 147488 | tf_op jit(solution)/shard_map/ppermute | solution.py:232
  18.2 0.5 %collective-permute-start.13 = (f32[1,3,8,1536]{3,2,1,0:T(8,128)S(1)}, f32[1,3,8,1536]{3,2,1,0:T(8,128)S(1)}, u32[]{:S(2)}, u32[]{:S(2)}) collective-permute-start(f32[1,3,8,1536]{3,2,1,0:T(8,128)S(1)} %collective-permute-done.11), channel_id=1, source_target_pairs={{0,1},{1,0},{2,3},{3,2},{4,5},{5,4},{6,7},{7,6},{8,9},{9,8},{10,11... | collective-permute-start | bytes 442376 | tf_op jit(solution)/shard_map/ppermute | solution.py:222
  18.7 0.0 collective-permute-start.6
  18.7 0.7 %collective-permute-start.7 = (f32[1,3,8,1536]{3,2,1,0:T(8,128)S(1)}, f32[1,3,8,1536]{3,2,1,0:T(8,128)S(1)}, u32[]{:S(2)}, u32[]{:S(2)}) collective-permute-start(f32[1,3,8,1536]{3,2,1,0:T(8,128)S(1)} %get-tuple-element.7.state), channel_id=1, source_target_pairs={{1,2},{2,1},{5,6},{6,5},{9,10},{10,9},{13,14},{14,13},{17,18},{18,... | collective-permute-start | bytes 442376 | tf_op jit(solution)/shard_map/ppermute | solution.py:232
  19.4 1.3 %collective-permute-start.8 = (f32[1,3,8,1536]{3,2,1,0:T(8,128)S(1)}, f32[1,3,8,1536]{3,2,1,0:T(8,128)S(1)}, u32[]{:S(2)}, u32[]{:S(2)}) collective-permute-start(f32[1,3,8,1536]{3,2,1,0:T(8,128)S(1)} %get-tuple-element.8.lead), channel_id=1, source_target_pairs={{4,0},{8,4},{12,8},{16,12},{20,16},{24,20},{28,24},{5,1},{9,5},{13... | collective-permute-start | bytes 442376 | tf_op jit(solution)/shard_map/ppermute | solution.py:207
  20.7 1.2 %shard_map.87.tally = f32[4,8,128]{2,1,0:T(8,128)S(1)} custom-call(f32[1,3,8,1536]{3,2,1,0:T(8,128)S(1)} %collective-permute-done.9.own, f32[1,3,8,1536]{3,2,1,0:T(8,128)S(1)} %collective-permute-done.12.near, f32[1,3,8,1536]{3,2,1,0:T(8,128)S(1)} %collective-permute-done.13.far, f32[1,8,1536]{2,1,0:T(8,128)S(1)} %copy-done.5, ...), custom_call_target="tpu_custom_call" | custom-call | flops 7733248 | bytes 1933312 | tf_op jit(solution)/shard_map/pallas_call | solution.py:193
  22.0 6.2 %collective-permute-done.8.lead = f32[1,3,8,1536]{3,2,1,0:T(8,128)S(1)} collective-permute-done((f32[1,3,8,1536]{3,2,1,0:T(8,128)S(1)}, f32[1,3,8,1536]{3,2,1,0:T(8,128)S(1)}, u32[]{:S(2)}, u32[]{:S(2)}) %collective-permute-start.8) | collective-permute-done | bytes 147488 | tf_op jit(solution)/shard_map/ppermute | solution.py:207
  28.2 1.2 %shard_map.88 = f32[32,128]{1,0:T(8,128)S(1)} custom-call(f32[1,3,8,1536]{3,2,1,0:T(8,128)S(1)} %get-tuple-element.7.state, f32[1,3,8,1536]{3,2,1,0:T(8,128)S(1)} %collective-permute-done.6.near, f32[1,3,8,1536]{3,2,1,0:T(8,128)S(1)} %collective-permute-done.7.far, f32[1,8,1536]{2,1,0:T(8,128)S(1)} %copy-done.5, ...), custom_call_target="tpu_custom_call" | custom-call | flops 4259840 | bytes 1064960 | tf_op jit(solution)/shard_map/pallas_call | solution.py:193
  29.3 16.4 %all_to_all.11 = f32[32,1,128]{2,1,0:T(1,128)S(1)} all-to-all(f32[32,1,128]{2,1,0:T(1,128)S(1)} %bitcast.4), channel_id=1, replica_groups=mesh['win'=8,'band'=2,'half'=2] {'win','band','half'}, dimensions={0} | all-to-all | bytes 32768 | tf_op jit(solution)/shard_map/all_to_all | solution.py:273
  45.8 1.2 %shard_map.89 = (f32[1,3,8,1536]{3,2,1,0:T(8,128)}, f32[1,3,8,1536]{3,2,1,0:T(8,128)}, f32[1,3,8,1536]{3,2,1,0:T(8,128)}) custom-call(f32[32,128]{1,0:T(8,128)S(1)} %bitcast.5, f32[1,3,8,1536]{3,2,1,0:T(8,128)S(1)} %copy-done, f32[1,3,8,1536]{3,2,1,0:T(8,128)S(1)} %copy-done.2, f32[1,3,8,1536]{3,2,1,0:T(8,128)S(1)} %copy-done.1, ...), custom_call_target="tpu_custom_call" | custom-call | flops 4784128 | bytes 1196032 | tf_op jit(solution)/shard_map/pallas_call | solution.py:193
  (18 shorter events, 0.0 us)
Async XLA Ops:
  0.6 3.1 %copy-start = (f32[1,3,8,1536]{3,2,1,0:T(8,128)S(1)}, f32[1,3,8,1536]{3,2,1,0:T(8,128)}, u32[]{:S(2)}) copy-start(f32[1,3,8,1536]{3,2,1,0:T(8,128)} %p.7) | copy-start | bytes 442372
  0.6 3.0 %copy-start.5 = (f32[1,8,1536]{2,1,0:T(8,128)S(1)}, f32[1,8,1536]{2,1,0:T(8,128)}, u32[]{:S(2)}) copy-start(f32[1,8,1536]{2,1,0:T(8,128)} %depth.5) | copy-start | bytes 147460
  0.7 9.6 %collective-permute-start = (f32[1,3,8,1536]{3,2,1,0:T(8,128)}, f32[1,3,8,1536]{3,2,1,0:T(8,128)S(1)}, u32[]{:S(2)}, u32[]{:S(2)}) collective-permute-start(f32[1,3,8,1536]{3,2,1,0:T(8,128)} %p.7), channel_id=1, source_target_pairs={{4,0},{8,4},{12,8},{16,12},{20,16},{24,20},{28,24},{5,1},{9,5},{13... | collective-permute-start | bytes 442376 | tf_op jit(solution)/shard_map/ppermute | solution.py:207
  2.1 11.3 %copy-start.3 = (f32[1,3,8,1536]{3,2,1,0:T(8,128)S(1)}, f32[1,3,8,1536]{3,2,1,0:T(8,128)}, u32[]{:S(2)}) copy-start(f32[1,3,8,1536]{3,2,1,0:T(8,128)} %hobs.3) | copy-start | bytes 442372
  3.1 7.2 %collective-permute-start.10 = (f32[1,3,8,1536]{3,2,1,0:T(8,128)S(1)}, f32[1,3,8,1536]{3,2,1,0:T(8,128)S(1)}, u32[]{:S(2)}, u32[]{:S(2)}) collective-permute-start(f32[1,3,8,1536]{3,2,1,0:T(8,128)S(1)} %shard_map.86), channel_id=1, source_target_pairs={{0,1},{1,0},{2,3},{3,2},{4,5},{5,4},{6,7},{7,6},{8,9},{9,8},{10,11... | collective-permute-start | bytes 442376 | tf_op jit(solution)/shard_map/ppermute | solution.py:222
  3.7 2.1 %collective-permute-start.3 = (f32[1,8,1536]{2,1,0:T(8,128)S(1)}, f32[1,8,1536]{2,1,0:T(8,128)S(1)}, u32[]{:S(2)}, u32[]{:S(2)}) collective-permute-start(f32[1,8,1536]{2,1,0:T(8,128)S(1)} %copy-done.5), channel_id=1, source_target_pairs={{0,1},{1,0},{2,3},{3,2},{4,5},{5,4},{6,7},{7,6},{8,9},{9,8},{10,11... | collective-permute-start | bytes 147464 | tf_op jit(solution)/shard_map/ppermute | solution.py:222
  3.8 9.5 %collective-permute-start.2 = (f32[1,3,8,1536]{3,2,1,0:T(8,128)S(1)}, f32[1,3,8,1536]{3,2,1,0:T(8,128)S(1)}, u32[]{:S(2)}, u32[]{:S(2)}) collective-permute-start(f32[1,3,8,1536]{3,2,1,0:T(8,128)S(1)} %copy-done), channel_id=1, source_target_pairs={{5,2},{6,1},{9,6},{10,5},{13,10},{14,9},{17,14},{18,13},{21,18},{2... | collective-permute-start | bytes 442376 | tf_op jit(solution)/shard_map/ppermute | solution.py:232
  4.4 10.8 %collective-permute-start.9 = (f32[1,3,8,1536]{3,2,1,0:T(8,128)S(1)}, f32[1,3,8,1536]{3,2,1,0:T(8,128)S(1)}, u32[]{:S(2)}, u32[]{:S(2)}) collective-permute-start(f32[1,3,8,1536]{3,2,1,0:T(8,128)S(1)} %shard_map.86), channel_id=1, source_target_pairs={{4,0},{8,4},{12,8},{16,12},{20,16},{24,20},{28,24},{5,1},{9,5},{13... | collective-permute-start | bytes 442376 | tf_op jit(solution)/shard_map/ppermute | solution.py:207
  5.7 6.3 %collective-permute-start.4 = (f32[1,8,1536]{2,1,0:T(8,128)S(1)}, f32[1,8,1536]{2,1,0:T(8,128)S(1)}, u32[]{:S(2)}, u32[]{:S(2)}) collective-permute-start(f32[1,8,1536]{2,1,0:T(8,128)S(1)} %collective-permute-done.3.depth_near), channel_id=1, source_target_pairs={{0,3},{3,0},{4,7},{7,4},{8,11},{11,8},{12,15},{15,12},{16,19},{19,... | collective-permute-start | bytes 147464 | tf_op jit(solution)/shard_map/ppermute | solution.py:232
  10.3 3.0 %collective-permute-start.1 = (f32[1,3,8,1536]{3,2,1,0:T(8,128)S(1)}, f32[1,3,8,1536]{3,2,1,0:T(8,128)S(1)}, u32[]{:S(2)}, u32[]{:S(2)}) collective-permute-start(f32[1,3,8,1536]{3,2,1,0:T(8,128)S(1)} %collective-permute-done.own), channel_id=1, source_target_pairs={{0,1},{1,0},{2,3},{3,2},{4,5},{5,4},{6,7},{7,6},{8,9},{9,8},{10,11... | collective-permute-start | bytes 442376 | tf_op jit(solution)/shard_map/ppermute | solution.py:222
  10.4 7.8 %collective-permute-start.11 = (f32[1,3,8,1536]{3,2,1,0:T(8,128)S(1)}, f32[1,3,8,1536]{3,2,1,0:T(8,128)S(1)}, u32[]{:S(2)}, u32[]{:S(2)}) collective-permute-start(f32[1,3,8,1536]{3,2,1,0:T(8,128)S(1)} %collective-permute-done.10), channel_id=1, source_target_pairs={{4,3},{7,0},{8,7},{11,4},{12,11},{15,8},{16,15},{19,12},{20,19},{2... | collective-permute-start | bytes 442376 | tf_op jit(solution)/shard_map/ppermute | solution.py:232
  12.0 1.2 %collective-permute-start.5 = (f32[1,8,1536]{2,1,0:T(8,128)S(1)}, f32[1,8,1536]{2,1,0:T(8,128)S(1)}, u32[]{:S(2)}, u32[]{:S(2)}) collective-permute-start(f32[1,8,1536]{2,1,0:T(8,128)S(1)} %collective-permute-done.4), channel_id=1, source_target_pairs={{0,1},{1,0},{2,3},{3,2},{4,5},{5,4},{6,7},{7,6},{8,9},{9,8},{10,11... | collective-permute-start | bytes 147464 | tf_op jit(solution)/shard_map/ppermute | solution.py:222
  12.0 1.4 %copy-start.1 = (f32[1,3,8,1536]{3,2,1,0:T(8,128)S(1)}, f32[1,3,8,1536]{3,2,1,0:T(8,128)}, u32[]{:S(2)}) copy-start(f32[1,3,8,1536]{3,2,1,0:T(8,128)} %dvar.7) | copy-start | bytes 442372
  12.0 1.4 %copy-start.2 = (f32[1,3,8,1536]{3,2,1,0:T(8,128)S(1)}, f32[1,3,8,1536]{3,2,1,0:T(8,128)}, u32[]{:S(2)}) copy-start(f32[1,3,8,1536]{3,2,1,0:T(8,128)} %m.5) | copy-start | bytes 442372
  13.5 7.2 %copy-start.4 = (f32[1,3,8,1536]{3,2,1,0:T(8,128)S(1)}, f32[1,3,8,1536]{3,2,1,0:T(8,128)}, u32[]{:S(2)}) copy-start(f32[1,3,8,1536]{3,2,1,0:T(8,128)} %rvar.3) | copy-start | bytes 442372
  18.2 2.5 %collective-permute-start.12 = (f32[1,3,8,1536]{3,2,1,0:T(8,128)S(1)}, f32[1,3,8,1536]{3,2,1,0:T(8,128)S(1)}, u32[]{:S(2)}, u32[]{:S(2)}) collective-permute-start(f32[1,3,8,1536]{3,2,1,0:T(8,128)S(1)} %collective-permute-done.9.own), channel_id=1, source_target_pairs={{0,1},{1,0},{2,3},{3,2},{4,5},{5,4},{6,7},{7,6},{8,9},{9,8},{10,11... | collective-permute-start | bytes 442376 | tf_op jit(solution)/shard_map/ppermute | solution.py:222
  18.2 2.5 %collective-permute-start.13 = (f32[1,3,8,1536]{3,2,1,0:T(8,128)S(1)}, f32[1,3,8,1536]{3,2,1,0:T(8,128)S(1)}, u32[]{:S(2)}, u32[]{:S(2)}) collective-permute-start(f32[1,3,8,1536]{3,2,1,0:T(8,128)S(1)} %collective-permute-done.11), channel_id=1, source_target_pairs={{0,1},{1,0},{2,3},{3,2},{4,5},{5,4},{6,7},{7,6},{8,9},{9,8},{10,11... | collective-permute-start | bytes 442376 | tf_op jit(solution)/shard_map/ppermute | solution.py:222
  18.7 3.2 %collective-permute-start.6 = (f32[1,3,8,1536]{3,2,1,0:T(8,128)S(1)}, f32[1,3,8,1536]{3,2,1,0:T(8,128)S(1)}, u32[]{:S(2)}, u32[]{:S(2)}) collective-permute-start(f32[1,3,8,1536]{3,2,1,0:T(8,128)S(1)} %get-tuple-element.7.state), channel_id=1, source_target_pairs={{0,1},{1,0},{2,3},{3,2},{4,5},{5,4},{6,7},{7,6},{8,9},{9,8},{10,11... | collective-permute-start | bytes 442376 | tf_op jit(solution)/shard_map/ppermute | solution.py:222
  18.7 3.2 %collective-permute-start.7 = (f32[1,3,8,1536]{3,2,1,0:T(8,128)S(1)}, f32[1,3,8,1536]{3,2,1,0:T(8,128)S(1)}, u32[]{:S(2)}, u32[]{:S(2)}) collective-permute-start(f32[1,3,8,1536]{3,2,1,0:T(8,128)S(1)} %get-tuple-element.7.state), channel_id=1, source_target_pairs={{1,2},{2,1},{5,6},{6,5},{9,10},{10,9},{13,14},{14,13},{17,18},{18,... | collective-permute-start | bytes 442376 | tf_op jit(solution)/shard_map/ppermute | solution.py:232
  19.4 8.8 %collective-permute-start.8 = (f32[1,3,8,1536]{3,2,1,0:T(8,128)S(1)}, f32[1,3,8,1536]{3,2,1,0:T(8,128)S(1)}, u32[]{:S(2)}, u32[]{:S(2)}) collective-permute-start(f32[1,3,8,1536]{3,2,1,0:T(8,128)S(1)} %get-tuple-element.8.lead), channel_id=1, source_target_pairs={{4,0},{8,4},{12,8},{16,12},{20,16},{24,20},{28,24},{5,1},{9,5},{13... | collective-permute-start | bytes 442376 | tf_op jit(solution)/shard_map/ppermute | solution.py:207

commit v8 on v4

v8 whole, which is shorter than its diff:
```python
import jax
import jax.numpy as jnp
from jax import lax
from jax.experimental import pallas as pl
from jax.experimental.pallas import tpu as pltpu
from jax.sharding import Mesh, PartitionSpec as P

GRID_ROWS = 768
STEPS = 4

mass_rate = 0.5
press_rate = 0.5
spin_rate = 0.4


def lon_gap(field):
    width = field.shape[-1]
    return pltpu.roll(field, width - 1, 1) - pltpu.roll(field, 1, 1)


def lat_gap(field):
    rows = field.shape[0]
    return pltpu.roll(field, rows - 1, 0) - pltpu.roll(field, 1, 0)


def even_lat():
    return lax.axis_index("half") == 0


def has_previous():
    return lax.axis_index("win") > 0


def stacked(own, near, far, index):
    even = even_lat()
    low = jnp.where(even, far[index], near[index])
    high = jnp.where(even, near[index], far[index])
    return jnp.concatenate([low, own[index], high], axis=0)


def prep_kernel(p, m, dvar, rvar, hobs, depth, pair, straight, local, pv, mv, dv, rv, hv, sems):
    copies = [
        pltpu.make_async_copy(source, target, sems.at[slot])
        for slot, (source, target) in enumerate(
            ((p, pv), (m, mv), (dvar, dv), (rvar, rv), (hobs, hv), (depth, straight.at[0:1]))
        )
    ]
    for copy in copies:
        copy.start()
    for copy in copies:
        copy.wait()
    for part in range(3):
        up = dv[0, part] * pv[0, part]
        seen = hv[0, part] * mv[0, part]
        pair[part] = pv[0, part]
        pair[3 + part] = up
        straight[1 + part] = pv[0, part] + seen
        local[part] = up + rv[0, part] * seen


def stretched(straight, relayed):
    even = even_lat()
    low = jnp.where(even, relayed[1], relayed[0])
    high = jnp.where(even, relayed[0], relayed[1])
    return 0.25 * jnp.concatenate([low, straight[0], high], axis=0)


def adjoint(pair, pair_near, pair_far, straight, relayed, spin, inside, base):
    depth = stretched(straight, relayed)
    turn, keep = spin[...], inside[...]
    adj_height, adj_east, adj_north = [stacked(pair, pair_near, pair_far, base + part) for part in range(3)]
    for step in range(STEPS):
        adj_mid = adj_east - turn * adj_north
        adj_height = keep * (adj_height + 0.25 * (lat_gap(adj_north) + lon_gap(adj_mid)))
        adj_north = adj_north + turn * adj_mid + depth * lat_gap(adj_height)
        adj_east = adj_mid + depth * lon_gap(adj_height)
    rows = pair.shape[1]
    return [value[rows:2 * rows] for value in (adj_height, adj_east, adj_north)]


def first_adjoint_kernel(pair, pair_near, pair_far, straight, relayed, spin, inside, state, back):
    swept = adjoint(pair, pair_near, pair_far, straight, relayed, spin, inside, 0)
    link = has_previous()
    for part, value in enumerate(swept):
        back[part] = value
        state[part] = jnp.where(link, straight[1 + part] - value, 0.0)


def second_adjoint_kernel(pair, pair_near, pair_far, straight, relayed, spin, inside, local, state, tally):
    swept = adjoint(pair, pair_near, pair_far, straight, relayed, spin, inside, 3)
    link = has_previous()
    cross = square = 0.0
    for part, value in enumerate(swept):
        zx = jnp.where(link, local[part] - value, 0.0)
        cross += lane_sum(zx * state[part])
        square += lane_sum(zx * zx)
    tally[0] = cross
    tally[1] = square


def forward_kernel(state, state_near, state_far, straight, relayed, spin, inside, end):
    depth = stretched(straight, relayed)
    turn, keep = spin[...], inside[...]
    height, east, north = [stacked(state, state_near, state_far, part) for part in range(3)]
    for step in range(STEPS):
        height = keep * (height - (lon_gap(depth * east) + lat_gap(depth * north)))
        east = east + turn * north - 0.25 * lon_gap(height)
        north = north - turn * east - 0.25 * lat_gap(height)
    rows = state.shape[1]
    for part, value in enumerate((height, east, north)):
        end[part] = value[rows:2 * rows]


def lane_sum(value):
    rows, width = value.shape
    total = value[:, :128]
    for start in range(128, width, 128):
        total = total + value[:, start:start + 128]
    return total


def inner_kernel(p, m, dvar, rvar, hobs, back, end, tally, sent):
    last = lax.axis_index("win") == lax.axis_size("win") - 1
    moments = [0.0, 0.0, 2.0 * tally[0], tally[1]]
    for part in range(3):
        dv, rv, hv = dvar[0, part], rvar[0, part], hobs[0, part]
        pv, mv = p[0, part], m[0, part]
        up, um = dv * pv, rv * mv
        ux = pv - back[part] + hv * mv
        zp = dv * up + ux - end[part]
        zm = rv * um + hv * ux
        zx = jnp.where(last, up + hv * um, 0.0)
        moments[0] += lane_sum(up * pv + um * mv)
        moments[1] += lane_sum(up * up + um * um + ux * ux)
        moments[2] += lane_sum(dv * up * up + rv * um * um + 2.0 * (zx * ux))
        moments[3] += lane_sum(zp * zp + zm * zm + zx * zx)
    lane = lax.broadcasted_iota(jnp.int32, (1, 128), 1)
    row = 0.0
    for slot, value in enumerate(moments):
        folded = jnp.sum(value, axis=0, keepdims=True)
        folded = folded + pltpu.roll(folded, 64, 1)
        folded = folded + pltpu.roll(folded, 32, 1)
        row = jnp.where(lane // 32 == slot, folded, row)
    sent[...] = jnp.broadcast_to(row, sent.shape)


def lane_sum(value):
    rows, width = value.shape
    total = value[:, :128]
    for start in range(128, width, 128):
        total = total + value[:, start:start + 128]
    return total


def two_sum(a, b):
    total = a + b
    part = total - a
    return total, (a - (total - part)) + (b - part)


def split(a):
    wide = 4097.0 * a
    top = wide - (wide - a)
    return top, a - top


def two_product(a, b):
    product = a * b
    a_top, a_low = split(a)
    b_top, b_low = split(b)
    return product, ((a_top * b_top - product) + a_top * b_low + a_low * b_top) + a_low * b_low


def pair_product(a, b):
    product, rest = two_product(a[0], b[0])
    return product, rest + (a[0] * b[1] + a[1] * b[0])


def pair_gap(a, b):
    total, rest = two_sum(a[0], -b[0])
    return total + (rest + (a[1] - b[1]))


def coefficients(gathered):
    top = jnp.sum(gathered[...], axis=0, keepdims=True)
    low = jnp.zeros_like(top)
    shift = 1
    while shift < 32:
        top, rest = two_sum(top, pltpu.roll(top, shift, 1))
        low = low + pltpu.roll(low, shift, 1) + rest
        shift *= 2
    tops = [jnp.broadcast_to(top[:, lane:lane + 1], (1, 128)) for lane in range(31, 128, 32)]
    lows = [jnp.broadcast_to(low[:, lane:lane + 1], (1, 128)) for lane in range(31, 128, 32)]
    scale = 1.0 / tops[1]
    moments = []
    for value, rest in zip(tops, lows):
        product, error = two_product(value, scale)
        moments.append((product, error + rest * scale))
    m1, m2, m3, m4 = moments
    gap = pair_gap(pair_product(m2, m4), pair_product(m3, m3))
    y1 = pair_gap(pair_product(m1, m4), pair_product(m2, m3)) / gap
    y2 = pair_gap(pair_product(m2, m2), pair_product(m1, m3)) / gap
    return y1, y2


def combine_kernel(gathered, p, m, dvar, rvar, hobs, back, dual_model, dual_obs, increment):
    y1, y2 = coefficients(gathered)
    rows, width = p.shape[2:]
    y1 = jnp.broadcast_to(jnp.concatenate([y1] * (width // 128), axis=1), (rows, width))
    y2 = jnp.broadcast_to(jnp.concatenate([y2] * (width // 128), axis=1), (rows, width))
    for part in range(3):
        pv, mv = p[0, part], m[0, part]
        dual_model[0, part] = (y1 + y2 * dvar[0, part]) * pv
        dual_obs[0, part] = (y1 + y2 * rvar[0, part]) * mv
        increment[0, part] = y2 * (pv - back[part] + hobs[0, part] * mv)


def run(kernel, out_shapes, *operands, scratch=(), space=pltpu.VMEM, work=4):
    shapes = [jax.ShapeDtypeStruct(shape, jnp.float32) for shape in out_shapes]
    size = sum(4 * operand.size for operand in operands) + sum(4 * shape.size for shape in shapes)
    if space is not pltpu.VMEM:
        operands = [pltpu.with_memory_space_constraint(operand, space) for operand in operands]
    return pl.pallas_call(
        kernel,
        out_shape=shapes,
        in_specs=[pl.BlockSpec(memory_space=space)] * len(operands),
        out_specs=[pl.BlockSpec(memory_space=pltpu.VMEM)] * len(shapes),
        scratch_shapes=scratch,
        compiler_params=pltpu.CompilerParams(vmem_limit_bytes=32 * 1024 * 1024),
        cost_estimate=pl.CostEstimate(flops=work * size, bytes_accessed=size, transcendentals=0),
    )(*operands)


def shifted(value, step):
    count = lax.axis_size("win")
    initial, last = (max(0, -step), min(count, count - step))
    return lax.ppermute(value, "win", [(source, source + step) for source in range(initial, last)])


def lat_count():
    return lax.axis_size("band") * lax.axis_size("half")


def lat_index():
    return lax.axis_index("band") * lax.axis_size("half") + lax.axis_index("half")


def swapped(value, first):
    pairs = []
    for lat in range(first, lat_count() - 1, 2):
        pairs += [(lat, lat + 1), (lat + 1, lat)]
    return lax.ppermute(value, ("band", "half"), pairs)


def crossed(value, ends, win_step=0):
    wins = lax.axis_size("win")
    pairs = []
    for win in range(wins):
        for source, target in (ends, ends[::-1]):
            if 0 <= win + win_step < wins:
                pairs.append((4 * win + source, 4 * (win + win_step) + target))
    return lax.ppermute(value, ("win", "band", "half"), pairs)


def body(model_rhs, obs_rhs, model_var, obs_var, obs_weight, depth):
    rows, width = model_rhs.shape[2:]
    ranks = lax.axis_size("win") * lat_count()
    total_rows = rows * lat_count()
    offset = (GRID_ROWS - total_rows) // 2
    local_rows = lat_index() * rows - rows + jnp.arange(3 * rows, dtype=jnp.int32)
    latitude = -jnp.pi / 2 + (local_rows.astype(jnp.float32) + offset + 0.5) * (jnp.pi / GRID_ROWS)
    inside = ((local_rows >= 0) & (local_rows < total_rows)).astype(jnp.float32)
    spin = inside * (mass_rate * spin_rate * jnp.sin(latitude))
    inside = jnp.broadcast_to(inside[:, None], (3 * rows, width))
    spin = jnp.broadcast_to(spin[:, None], (3 * rows, width))
    fields = (3, rows, width)

    middle, outer = (1, 2), (0, 3)
    pair, straight, local = run(
        prep_kernel, [(6, rows, width), (4, rows, width), fields],
        model_rhs, obs_rhs, model_var, obs_var, obs_weight, depth,
        scratch=[pltpu.VMEM(model_rhs.shape, jnp.float32)] * 5 + [pltpu.SemaphoreType.DMA((6,))],
        space=pltpu.HBM,
    )
    came = shifted(straight, 1)
    depth_near = swapped(depth, 0)
    depth_edge = crossed(depth_near, outer, 1)
    relayed = swapped(jnp.concatenate([came[:1], depth_edge]), 0)
    local, _ = lax.optimization_barrier((local, depth_near))
    local = shifted(local, 1)
    pair_near, pair_far = swapped(pair, 0), crossed(pair, middle)
    known = (pair, pair_near, pair_far, came, relayed, spin, inside)
    state, back = run(first_adjoint_kernel, [fields, fields], *known)
    back = shifted(back, -1)
    state_near, state_far = swapped(state, 0), crossed(state, middle)
    (tally,) = run(second_adjoint_kernel, [(2, rows, 128)], *known, local, state)
    (end,) = run(forward_kernel, [fields], state, state_near, state_far, came, relayed, spin, inside)
    (sent,) = run(
        inner_kernel, [(ranks, 128)],
        model_rhs, obs_rhs, model_var, obs_var, obs_weight, back, end, tally,
    )
    gathered = lax.all_to_all(sent, ("win", "band", "half"), 0, 0, tiled=True)
    return run(
        combine_kernel, [model_rhs.shape] * 3,
        gathered, model_rhs, obs_rhs, model_var, obs_var, obs_weight, back,
    )


def solution(mesh):
    wins, lats = mesh.devices.shape
    mesh = Mesh(mesh.devices.reshape(wins, lats // 2, 2), ("win", "band", "half"))
    lat = ("band", "half")
    field = P("win", None, lat, None)
    in_specs = (field,) * 5 + (P("win", lat, None),)
    return jax.shard_map(body, mesh=mesh, in_specs=in_specs, out_specs=(field,) * 3, check_vma=False)
```

time: 73.1 us -> 47.7 us (0.65)
  blocking collectives: 42.6 us -> 12.6 us
  starting transfers between devices: 15.9 us -> 21 us
    all_gather x1 -> x0, blocking collectives: 42.6 us -> none  [body(): gathered = lax.all_gather(sent, ('win', 'lat'), axis=0, tiled=True)]
    all_to_all x0 -> x1, blocking collectives: none -> 12.6 us  [body(): gathered = lax.all_to_all(sent, ('win', 'band', 'half'), 0, 0, tiled=True)]
    ppermute x2 -> x3, starting transfers between devices: 6.32 us -> 10.8 us  [shifted(): lax.ppermute(value, 'win', [(source, source + step) for source in range(i...]
    ppermute x6 -> x7, starting transfers between devices: 9.6 us -> 10.2 us  [the longest x4 5.39 us: swapped(): return lax.ppermute(value, ('band', 'half'), pairs)]
    ppermute x6 -> x7, waiting for transfers between devices: 1.19 us -> 1.71 us  [the longest x3 1.7 us: crossed(): return lax.ppermute(value, ('win', 'band', 'half'), pairs)]
    ppermute x2 -> x3, waiting for transfers between devices: 4.84 us -> 4.57 us  [shifted(): lax.ppermute(value, 'win', [(source, source + step) for source in range(i...]
  transfers between devices with their start and end apart: 8 -> 10, of which waited for: 2 -> 2; matrix products, arithmetic and copies ran while one was open for 0% -> 0% of each run, Pallas kernels for 3% -> 8%
where the time goes in v8:
time: 47.7 us; the launch traced here: 47.5 us
  starting transfers between devices  21 us (44%)
  blocking collectives  12.6 us (26%)
  Pallas kernels  6.48 us (14%)
  waiting for transfers between devices  6.28 us (13%)
  between operations  0.88 us (2%)
    all_to_all x1, blocking collectives, body(): gathered = lax.all_to_all(sent, ('win', 'band', 'half'), 0, 0, tiled=True)  12.6 us
    ppermute x3, starting transfers between devices, shifted(): lax.ppermute(value, 'win', [(source, source + step) for source in range(i...  10.8 us
    pallas_call x6, Pallas kernels, run(): pl.pallas_call(kernel, out_shape=shapes, in_specs=[pl.BlockSpec(memory_sp...  6.48 us
    ppermute x4, starting transfers between devices, swapped(): return lax.ppermute(value, ('band', 'half'), pairs)  5.39 us
    ppermute x3, starting transfers between devices, crossed(): return lax.ppermute(value, ('win', 'band', 'half'), pairs)  4.82 us
    ppermute x3, waiting for transfers between devices, shifted(): lax.ppermute(value, 'win', [(source, source + step) for source in range(i...  4.57 us
    ppermute x3, waiting for transfers between devices, crossed(): return lax.ppermute(value, ('win', 'band', 'half'), pairs)  1.7 us
  transfers between devices with their start and end apart: 10, of which 2 were waited for; matrix products, arithmetic and copies ran while one was open for 0% of the time, Pallas kernels for 8%

profile of v8, /device:TPU:0, one launch (start us, length us, event | category | flops | bytes accessed | tf_op | source)
XLA Modules:
  0.0 47.5 jit_solution(4033744898035828033)
XLA Ops:
  0.6 1.3 %shard_map.85 = (f32[6,8,1536]{2,1,0:T(8,128)S(1)}, f32[4,8,1536]{2,1,0:T(8,128)S(1)}, f32[3,8,1536]{2,1,0:T(8,128)S(1)}) custom-call(f32[1,3,8,1536]{3,2,1,0:T(8,128)} %p.5, f32[1,3,8,1536]{3,2,1,0:T(8,128)} %m.5, f32[1,3,8,1536]{3,2,1,0:T(8,128)} %dvar.5, f32[1,3,8,1536]{3,2,1,0:T(8,128)} %rvar.5, f32[1,3,8,1536]{3,2,1,0:T(8,128)} %hobs.5, f32[1,8,1536]{2,1,0:T(8,128)} %depth.1), custom_call_target="tpu_custom_call" | custom-call | flops 5701632 | bytes 1425408 | tf_op jit(solution)/shard_map/pallas_call | solution.py:223
  2.0 4.9 %collective-permute-start.2 = (f32[4,8,1536]{2,1,0:T(8,128)S(1)}, f32[4,8,1536]{2,1,0:T(8,128)S(1)}, u32[]{:S(2)}, u32[]{:S(2)}) collective-permute-start(f32[4,8,1536]{2,1,0:T(8,128)S(1)} %get-tuple-element.10), channel_id=1, source_target_pairs={{0,4},{4,8},{8,12},{12,16},{16,20},{20,24},{24,28},{1,5},{5,9},{9,... | collective-permute-start | bytes 589832 | tf_op jit(solution)/shard_map/ppermute | solution.py:237
  6.9 0.1 collective-permute-start.3
  6.9 0.7 %collective-permute-start.1 = (f32[6,8,1536]{2,1,0:T(8,128)S(1)}, f32[6,8,1536]{2,1,0:T(8,128)S(1)}, u32[]{:S(2)}, u32[]{:S(2)}) collective-permute-start(f32[6,8,1536]{2,1,0:T(8,128)S(1)} %get-tuple-element.9.pair), channel_id=1, source_target_pairs={{1,2},{2,1},{5,6},{6,5},{9,10},{10,9},{13,14},{14,13},{17,18},{18,... | collective-permute-start | bytes 884744 | tf_op jit(solution)/shard_map/ppermute | solution.py:262
  7.6 2.9 %collective-permute-start = (f32[6,8,1536]{2,1,0:T(8,128)S(1)}, f32[6,8,1536]{2,1,0:T(8,128)S(1)}, u32[]{:S(2)}, u32[]{:S(2)}) collective-permute-start(f32[6,8,1536]{2,1,0:T(8,128)S(1)} %get-tuple-element.9.pair), channel_id=1, source_target_pairs={{0,1},{1,0},{2,3},{3,2},{4,5},{5,4},{6,7},{7,6},{8,9},{9,8},{10,11... | collective-permute-start | bytes 884744 | tf_op jit(solution)/shard_map/ppermute | solution.py:252
  10.5 0.0 collective-permute-done.3
  10.5 3.5 %collective-permute-start.4 = (f32[1,8,1536]{2,1,0:T(8,128)S(1)}, f32[1,8,1536]{2,1,0:T(8,128)S(1)}, u32[]{:S(2)}, u32[]{:S(2)}) collective-permute-start(f32[1,8,1536]{2,1,0:T(8,128)S(1)} %collective-permute-done.3), channel_id=1, source_target_pairs={{0,7},{3,4},{4,11},{7,8},{8,15},{11,12},{12,19},{15,16},{16,23},{1... | collective-permute-start | bytes 147464 | tf_op jit(solution)/shard_map/ppermute | solution.py:262
  14.0 0.0 collective-permute-done.2.straight
  14.0 1.7 %collective-permute-done.4 = f32[1,8,1536]{2,1,0:T(8,128)S(1)} collective-permute-done((f32[1,8,1536]{2,1,0:T(8,128)S(1)}, f32[1,8,1536]{2,1,0:T(8,128)S(1)}, u32[]{:S(2)}, u32[]{:S(2)}) %collective-permute-start.4) | collective-permute-done | bytes 49184 | tf_op jit(solution)/shard_map/ppermute | solution.py:262
  15.8 0.1 multiply_select_fusion
  15.8 4.6 %collective-permute-start.9 = (f32[3,8,1536]{2,1,0:T(8,128)S(1)}, f32[3,8,1536]{2,1,0:T(8,128)S(1)}, u32[]{:S(2)}, u32[]{:S(2)}) collective-permute-start(f32[3,8,1536]{2,1,0:T(8,128)S(1)} %get-tuple-element.14), channel_id=1, source_target_pairs={{0,4},{4,8},{8,12},{12,16},{16,20},{20,24},{24,28},{1,5},{5,9},{9,... | collective-permute-start | bytes 442376 | tf_op jit(solution)/shard_map/ppermute | solution.py:237
  20.4 0.0 collective-permute-done.1.pair_far
  20.4 0.0 collective-permute-done.pair_near
  20.4 0.1 broadcast_in_dim.4.spin
  20.5 0.1 broadcast_in_dim.5.inside
  20.6 1.2 %shard_map.86 = (f32[3,8,1536]{2,1,0:T(8,128)S(1)}, f32[3,8,1536]{2,1,0:T(8,128)S(1)}) custom-call(f32[6,8,1536]{2,1,0:T(8,128)S(1)} %get-tuple-element.9.pair, f32[6,8,1536]{2,1,0:T(8,128)S(1)} %collective-permute-done.pair_near, f32[6,8,1536]{2,1,0:T(8,128)S(1)} %collective-permute-done.1.pair_far, f32[4,8,1536]{2,1,0:T(8,128)S(1)} %collective-permute-done.2.straight, ...), custom_call_target="tpu_custom_call" | custom-call | flops 7077888 | bytes 1769472 | tf_op jit(solution)/shard_map/pallas_call | solution.py:223
  21.8 0.7 %collective-permute-start.8 = (f32[3,8,1536]{2,1,0:T(8,128)S(1)}, f32[3,8,1536]{2,1,0:T(8,128)S(1)}, u32[]{:S(2)}, u32[]{:S(2)}) collective-permute-start(f32[3,8,1536]{2,1,0:T(8,128)S(1)} %get-tuple-element.12.state), channel_id=1, source_target_pairs={{1,2},{2,1},{5,6},{6,5},{9,10},{10,9},{13,14},{14,13},{17,18},{18,... | collective-permute-start | bytes 442376 | tf_op jit(solution)/shard_map/ppermute | solution.py:262
  22.5 2.4 %collective-permute-start.7 = (f32[3,8,1536]{2,1,0:T(8,128)S(1)}, f32[3,8,1536]{2,1,0:T(8,128)S(1)}, u32[]{:S(2)}, u32[]{:S(2)}) collective-permute-start(f32[3,8,1536]{2,1,0:T(8,128)S(1)} %get-tuple-element.12.state), channel_id=1, source_target_pairs={{0,1},{1,0},{2,3},{3,2},{4,5},{5,4},{6,7},{7,6},{8,9},{9,8},{10,11... | collective-permute-start | bytes 442376 | tf_op jit(solution)/shard_map/ppermute | solution.py:252
  24.9 1.3 %collective-permute-start.6 = (f32[3,8,1536]{2,1,0:T(8,128)S(1)}, f32[3,8,1536]{2,1,0:T(8,128)S(1)}, u32[]{:S(2)}, u32[]{:S(2)}) collective-permute-start(f32[3,8,1536]{2,1,0:T(8,128)S(1)} %get-tuple-element.11), channel_id=1, source_target_pairs={{4,0},{8,4},{12,8},{16,12},{20,16},{24,20},{28,24},{5,1},{9,5},{13... | collective-permute-start | bytes 442376 | tf_op jit(solution)/shard_map/ppermute | solution.py:237
  26.2 0.0 collective-permute-done.9.local
  26.2 1.2 %shard_map.88.tally = f32[2,8,128]{2,1,0:T(8,128)S(1)} custom-call(f32[6,8,1536]{2,1,0:T(8,128)S(1)} %get-tuple-element.9.pair, f32[6,8,1536]{2,1,0:T(8,128)S(1)} %collective-permute-done.pair_near, f32[6,8,1536]{2,1,0:T(8,128)S(1)} %collective-permute-done.1.pair_far, f32[4,8,1536]{2,1,0:T(8,128)S(1)} %collective-permute-done.2.straight, ...), custom_call_target="tpu_custom_call" | custom-call | flops 7110656 | bytes 1777664 | tf_op jit(solution)/shard_map/pallas_call | solution.py:223
  27.4 0.0 copy-start
  27.4 0.0 copy-start.1
  27.4 0.0 copy-start.2
  27.4 0.0 copy-start.3
  27.4 0.0 copy-start.4
  27.5 0.0 collective-permute-done.7.state_near
  27.5 1.2 %shard_map.87.end = f32[3,8,1536]{2,1,0:T(8,128)S(1)} custom-call(f32[3,8,1536]{2,1,0:T(8,128)S(1)} %get-tuple-element.12.state, f32[3,8,1536]{2,1,0:T(8,128)S(1)} %collective-permute-done.7.state_near, f32[3,8,1536]{2,1,0:T(8,128)S(1)} %collective-permute-done.8.state_far, f32[4,8,1536]{2,1,0:T(8,128)S(1)} %collective-permute-done.2.straight, ...), custom_call_target="tpu_custom_call" | custom-call | flops 4718592 | bytes 1179648 | tf_op jit(solution)/shard_map/pallas_call | solution.py:223
  28.7 4.6 %collective-permute-done.6.back = f32[3,8,1536]{2,1,0:T(8,128)S(1)} collective-permute-done((f32[3,8,1536]{2,1,0:T(8,128)S(1)}, f32[3,8,1536]{2,1,0:T(8,128)S(1)}, u32[]{:S(2)}, u32[]{:S(2)}) %collective-permute-start.6) | collective-permute-done | bytes 147488 | tf_op jit(solution)/shard_map/ppermute | solution.py:237
  33.3 0.4 shard_map.89
  33.6 12.6 %all_to_all.11 = f32[32,1,128]{2,1,0:T(1,128)S(1)} all-to-all(f32[32,1,128]{2,1,0:T(1,128)S(1)} %bitcast.5), channel_id=1, replica_groups=mesh['win'=8,'band'=2,'half'=2] {'win','band','half'}, dimensions={0} | all-to-all | bytes 32768 | tf_op jit(solution)/shard_map/all_to_all | solution.py:302
  46.2 1.2 %shard_map.90 = (f32[1,3,8,1536]{3,2,1,0:T(8,128)}, f32[1,3,8,1536]{3,2,1,0:T(8,128)}, f32[1,3,8,1536]{3,2,1,0:T(8,128)}) custom-call(f32[32,128]{1,0:T(8,128)S(1)} %bitcast.4, f32[1,3,8,1536]{3,2,1,0:T(8,128)S(1)} %copy-done, f32[1,3,8,1536]{3,2,1,0:T(8,128)S(1)} %copy-done.1, f32[1,3,8,1536]{3,2,1,0:T(8,128)S(1)} %copy-done.2, ...), custom_call_target="tpu_custom_call" | custom-call | flops 5373952 | bytes 1343488 | tf_op jit(solution)/shard_map/pallas_call | solution.py:223
  (13 shorter events, 0.0 us)
Async XLA Ops:
  0.6 6.2 %copy-start.5 = (f32[1,8,1536]{2,1,0:T(8,128)S(1)}, f32[1,8,1536]{2,1,0:T(8,128)}, u32[]{:S(2)}) copy-start(f32[1,8,1536]{2,1,0:T(8,128)} %depth.1) | copy-start | bytes 147460
  2.0 12.1 %collective-permute-start.2 = (f32[4,8,1536]{2,1,0:T(8,128)S(1)}, f32[4,8,1536]{2,1,0:T(8,128)S(1)}, u32[]{:S(2)}, u32[]{:S(2)}) collective-permute-start(f32[4,8,1536]{2,1,0:T(8,128)S(1)} %get-tuple-element.10), channel_id=1, source_target_pairs={{0,4},{4,8},{8,12},{12,16},{16,20},{20,24},{24,28},{1,5},{5,9},{9,... | collective-permute-start | bytes 589832 | tf_op jit(solution)/shard_map/ppermute | solution.py:237
  6.9 3.7 %collective-permute-start.3 = (f32[1,8,1536]{2,1,0:T(8,128)S(1)}, f32[1,8,1536]{2,1,0:T(8,128)S(1)}, u32[]{:S(2)}, u32[]{:S(2)}) collective-permute-start(f32[1,8,1536]{2,1,0:T(8,128)S(1)} %copy-done.5), channel_id=1, source_target_pairs={{0,1},{1,0},{2,3},{3,2},{4,5},{5,4},{6,7},{7,6},{8,9},{9,8},{10,11... | collective-permute-start | bytes 147464 | tf_op jit(solution)/shard_map/ppermute | solution.py:252
  6.9 13.5 %collective-permute-start.1 = (f32[6,8,1536]{2,1,0:T(8,128)S(1)}, f32[6,8,1536]{2,1,0:T(8,128)S(1)}, u32[]{:S(2)}, u32[]{:S(2)}) collective-permute-start(f32[6,8,1536]{2,1,0:T(8,128)S(1)} %get-tuple-element.9.pair), channel_id=1, source_target_pairs={{1,2},{2,1},{5,6},{6,5},{9,10},{10,9},{13,14},{14,13},{17,18},{18,... | collective-permute-start | bytes 884744 | tf_op jit(solution)/shard_map/ppermute | solution.py:262
  7.6 12.8 %collective-permute-start = (f32[6,8,1536]{2,1,0:T(8,128)S(1)}, f32[6,8,1536]{2,1,0:T(8,128)S(1)}, u32[]{:S(2)}, u32[]{:S(2)}) collective-permute-start(f32[6,8,1536]{2,1,0:T(8,128)S(1)} %get-tuple-element.9.pair), channel_id=1, source_target_pairs={{0,1},{1,0},{2,3},{3,2},{4,5},{5,4},{6,7},{7,6},{8,9},{9,8},{10,11... | collective-permute-start | bytes 884744 | tf_op jit(solution)/shard_map/ppermute | solution.py:252
  10.5 5.2 %collective-permute-start.4 = (f32[1,8,1536]{2,1,0:T(8,128)S(1)}, f32[1,8,1536]{2,1,0:T(8,128)S(1)}, u32[]{:S(2)}, u32[]{:S(2)}) collective-permute-start(f32[1,8,1536]{2,1,0:T(8,128)S(1)} %collective-permute-done.3), channel_id=1, source_target_pairs={{0,7},{3,4},{4,11},{7,8},{8,15},{11,12},{12,19},{15,16},{16,23},{1... | collective-permute-start | bytes 147464 | tf_op jit(solution)/shard_map/ppermute | solution.py:262
  15.7 4.7 %collective-permute-start.5 = (f32[2,8,1536]{2,1,0:T(8,128)S(1)}, f32[2,8,1536]{2,1,0:T(8,128)S(1)}, u32[]{:S(2)}, u32[]{:S(2)}) collective-permute-start(f32[2,8,1536]{2,1,0:T(8,128)S(1)} %pad_maximum_fusion), channel_id=1, source_target_pairs={{0,1},{1,0},{2,3},{3,2},{4,5},{5,4},{6,7},{7,6},{8,9},{9,8},{10,11... | collective-permute-start | bytes 294920 | tf_op jit(solution)/shard_map/ppermute | solution.py:252
  15.8 10.4 %collective-permute-start.9 = (f32[3,8,1536]{2,1,0:T(8,128)S(1)}, f32[3,8,1536]{2,1,0:T(8,128)S(1)}, u32[]{:S(2)}, u32[]{:S(2)}) collective-permute-start(f32[3,8,1536]{2,1,0:T(8,128)S(1)} %get-tuple-element.14), channel_id=1, source_target_pairs={{0,4},{4,8},{8,12},{12,16},{16,20},{20,24},{24,28},{1,5},{5,9},{9,... | collective-permute-start | bytes 442376 | tf_op jit(solution)/shard_map/ppermute | solution.py:237
  21.8 5.7 %collective-permute-start.8 = (f32[3,8,1536]{2,1,0:T(8,128)S(1)}, f32[3,8,1536]{2,1,0:T(8,128)S(1)}, u32[]{:S(2)}, u32[]{:S(2)}) collective-permute-start(f32[3,8,1536]{2,1,0:T(8,128)S(1)} %get-tuple-element.12.state), channel_id=1, source_target_pairs={{1,2},{2,1},{5,6},{6,5},{9,10},{10,9},{13,14},{14,13},{17,18},{18,... | collective-permute-start | bytes 442376 | tf_op jit(solution)/shard_map/ppermute | solution.py:262
  22.5 5.0 %collective-permute-start.7 = (f32[3,8,1536]{2,1,0:T(8,128)S(1)}, f32[3,8,1536]{2,1,0:T(8,128)S(1)}, u32[]{:S(2)}, u32[]{:S(2)}) collective-permute-start(f32[3,8,1536]{2,1,0:T(8,128)S(1)} %get-tuple-element.12.state), channel_id=1, source_target_pairs={{0,1},{1,0},{2,3},{3,2},{4,5},{5,4},{6,7},{7,6},{8,9},{9,8},{10,11... | collective-permute-start | bytes 442376 | tf_op jit(solution)/shard_map/ppermute | solution.py:252
  24.9 8.3 %collective-permute-start.6 = (f32[3,8,1536]{2,1,0:T(8,128)S(1)}, f32[3,8,1536]{2,1,0:T(8,128)S(1)}, u32[]{:S(2)}, u32[]{:S(2)}) collective-permute-start(f32[3,8,1536]{2,1,0:T(8,128)S(1)} %get-tuple-element.11), channel_id=1, source_target_pairs={{4,0},{8,4},{12,8},{16,12},{20,16},{24,20},{28,24},{5,1},{9,5},{13... | collective-permute-start | bytes 442376 | tf_op jit(solution)/shard_map/ppermute | solution.py:237
  27.4 5.8 %copy-start = (f32[1,3,8,1536]{3,2,1,0:T(8,128)S(1)}, f32[1,3,8,1536]{3,2,1,0:T(8,128)}, u32[]{:S(2)}) copy-start(f32[1,3,8,1536]{3,2,1,0:T(8,128)} %p.5) | copy-start | bytes 442372
  27.4 5.8 %copy-start.1 = (f32[1,3,8,1536]{3,2,1,0:T(8,128)S(1)}, f32[1,3,8,1536]{3,2,1,0:T(8,128)}, u32[]{:S(2)}) copy-start(f32[1,3,8,1536]{3,2,1,0:T(8,128)} %m.5) | copy-start | bytes 442372
  27.4 5.8 %copy-start.2 = (f32[1,3,8,1536]{3,2,1,0:T(8,128)S(1)}, f32[1,3,8,1536]{3,2,1,0:T(8,128)}, u32[]{:S(2)}) copy-start(f32[1,3,8,1536]{3,2,1,0:T(8,128)} %dvar.5) | copy-start | bytes 442372
  27.4 5.8 %copy-start.3 = (f32[1,3,8,1536]{3,2,1,0:T(8,128)S(1)}, f32[1,3,8,1536]{3,2,1,0:T(8,128)}, u32[]{:S(2)}) copy-start(f32[1,3,8,1536]{3,2,1,0:T(8,128)} %rvar.5) | copy-start | bytes 442372
  27.4 5.8 %copy-start.4 = (f32[1,3,8,1536]{3,2,1,0:T(8,128)S(1)}, f32[1,3,8,1536]{3,2,1,0:T(8,128)}, u32[]{:S(2)}) copy-start(f32[1,3,8,1536]{3,2,1,0:T(8,128)} %hobs.5) | copy-start | bytes 442372

commit v9 on v8

--- a/solution.py
+++ b/solution.py
@@ -58,6 +58,10 @@
         local[part] = up + rv[0, part] * seen
 
 
+def widened(tile, width):
+    return jnp.concatenate([tile[...]] * (width // 128), axis=1)
+
+
 def stretched(straight, relayed):
     even = even_lat()
     low = jnp.where(even, relayed[1], relayed[0])
@@ -67,7 +71,7 @@
 
 def adjoint(pair, pair_near, pair_far, straight, relayed, spin, inside, base):
     depth = stretched(straight, relayed)
-    turn, keep = spin[...], inside[...]
+    turn, keep = widened(spin, depth.shape[1]), widened(inside, depth.shape[1])
     adj_height, adj_east, adj_north = [stacked(pair, pair_near, pair_far, base + part) for part in range(3)]
     for step in range(STEPS):
         adj_mid = adj_east - turn * adj_north
@@ -100,7 +104,7 @@
 
 def forward_kernel(state, state_near, state_far, straight, relayed, spin, inside, end):
     depth = stretched(straight, relayed)
-    turn, keep = spin[...], inside[...]
+    turn, keep = widened(spin, depth.shape[1]), widened(inside, depth.shape[1])
     height, east, north = [stacked(state, state_near, state_far, part) for part in range(3)]
     for step in range(STEPS):
         height = keep * (height - (lon_gap(depth * east) + lat_gap(depth * north)))
@@ -271,8 +275,8 @@
     latitude = -jnp.pi / 2 + (local_rows.astype(jnp.float32) + offset + 0.5) * (jnp.pi / GRID_ROWS)
     inside = ((local_rows >= 0) & (local_rows < total_rows)).astype(jnp.float32)
     spin = inside * (mass_rate * spin_rate * jnp.sin(latitude))
-    inside = jnp.broadcast_to(inside[:, None], (3 * rows, width))
-    spin = jnp.broadcast_to(spin[:, None], (3 * rows, width))
+    inside = jnp.broadcast_to(inside[:, None], (3 * rows, 128))
+    spin = jnp.broadcast_to(spin[:, None], (3 * rows, 128))
     fields = (3, rows, width)
 
     middle, outer = (1, 2), (0, 3)
@@ -288,7 +292,8 @@
     relayed = swapped(jnp.concatenate([came[:1], depth_edge]), 0)
     local, _ = lax.optimization_barrier((local, depth_near))
     local = shifted(local, 1)
-    pair_near, pair_far = swapped(pair, 0), crossed(pair, middle)
+    held_pair, _ = lax.optimization_barrier((pair, depth_edge))
+    pair_near, pair_far = swapped(held_pair, 0), crossed(pair, middle)
     known = (pair, pair_near, pair_far, came, relayed, spin, inside)
     state, back = run(first_adjoint_kernel, [fields, fields], *known)
     back = shifted(back, -1)

time: 47.7 us -> 45.4 us (0.952)
  starting transfers between devices: 21 us -> 18.9 us
  blocking collectives: 12.6 us -> 11.9 us
  waiting for transfers between devices: 6.28 us -> 6.85 us
    ppermute x4, starting transfers between devices: 5.39 us -> 3.22 us  [swapped(): return lax.ppermute(value, ('band', 'half'), pairs)]
    all_to_all x1, blocking collectives: 12.6 us -> 11.9 us  [body(): gathered = lax.all_to_all(sent, ('win', 'band', 'half'), 0, 0, tiled=True)]
    ppermute x3, starting transfers between devices: 4.82 us -> 5.45 us  [crossed(): return lax.ppermute(value, ('win', 'band', 'half'), pairs)]
    ppermute x3, starting transfers between devices: 10.8 us -> 10.2 us  [shifted(): lax.ppermute(value, 'win', [(source, source + step) for source in range(i...]
    ppermute x4, waiting for transfers between devices: 0.01 us -> 0.53 us  [swapped(): return lax.ppermute(value, ('band', 'half'), pairs)]
  transfers between devices with their start and end apart: 10 -> 10, of which waited for: 2 -> 3; matrix products, arithmetic and copies ran while one was open for 0% -> 0% of each run, Pallas kernels for 8% -> 8%
where the time goes in v9:
time: 45.4 us; the launch traced here: 45.1 us
  starting transfers between devices  18.9 us (42%)
  blocking collectives  11.9 us (26%)
  waiting for transfers between devices  6.85 us (15%)
  Pallas kernels  6.4 us (14%)
  between operations  0.87 us (2%)
    all_to_all x1, blocking collectives, body(): gathered = lax.all_to_all(sent, ('win', 'band', 'half'), 0, 0, tiled=True)  11.9 us
    ppermute x3, starting transfers between devices, shifted(): lax.ppermute(value, 'win', [(source, source + step) for source in range(i...  10.2 us
    pallas_call x6, Pallas kernels, run(): pl.pallas_call(kernel, out_shape=shapes, in_specs=[pl.BlockSpec(memory_sp...  6.4 us
    ppermute x3, starting transfers between devices, crossed(): return lax.ppermute(value, ('win', 'band', 'half'), pairs)  5.45 us
    ppermute x3, waiting for transfers between devices, shifted(): lax.ppermute(value, 'win', [(source, source + step) for source in range(i...  4.15 us
    ppermute x4, starting transfers between devices, swapped(): return lax.ppermute(value, ('band', 'half'), pairs)  3.22 us
    ppermute x3, waiting for transfers between devices, crossed(): return lax.ppermute(value, ('win', 'band', 'half'), pairs)  2.17 us
  transfers between devices with their start and end apart: 10, of which 3 were waited for; matrix products, arithmetic and copies ran while one was open for 0% of the time, Pallas kernels for 8%

profile of v9, /device:TPU:0, one launch (start us, length us, event | category | flops | bytes accessed | tf_op | source)
XLA Modules:
  0.0 45.1 jit_solution(5457582346638950572)
XLA Ops:
  0.6 1.3 %shard_map.85 = (f32[6,8,1536]{2,1,0:T(8,128)S(1)}, f32[4,8,1536]{2,1,0:T(8,128)S(1)}, f32[3,8,1536]{2,1,0:T(8,128)S(1)}) custom-call(f32[1,3,8,1536]{3,2,1,0:T(8,128)} %p.5, f32[1,3,8,1536]{3,2,1,0:T(8,128)} %m.5, f32[1,3,8,1536]{3,2,1,0:T(8,128)} %dvar.5, f32[1,3,8,1536]{3,2,1,0:T(8,128)} %rvar.5, f32[1,3,8,1536]{3,2,1,0:T(8,128)} %hobs.5, f32[1,8,1536]{2,1,0:T(8,128)} %depth.1), custom_call_target="tpu_custom_call" | custom-call | flops 5701632 | bytes 1425408 | tf_op jit(solution)/shard_map/pallas_call | solution.py:227
  2.0 4.9 %collective-permute-start.4 = (f32[4,8,1536]{2,1,0:T(8,128)S(1)}, f32[4,8,1536]{2,1,0:T(8,128)S(1)}, u32[]{:S(2)}, u32[]{:S(2)}) collective-permute-start(f32[4,8,1536]{2,1,0:T(8,128)S(1)} %get-tuple-element.12), channel_id=1, source_target_pairs={{0,4},{4,8},{8,12},{12,16},{16,20},{20,24},{24,28},{1,5},{5,9},{9,... | collective-permute-start | bytes 589832 | tf_op jit(solution)/shard_map/ppermute | solution.py:241
  6.9 0.1 collective-permute-start
  6.9 0.7 %collective-permute-start.3 = (f32[6,8,1536]{2,1,0:T(8,128)S(1)}, f32[6,8,1536]{2,1,0:T(8,128)S(1)}, u32[]{:S(2)}, u32[]{:S(2)}) collective-permute-start(f32[6,8,1536]{2,1,0:T(8,128)S(1)} %get-tuple-element.11.pair), channel_id=1, source_target_pairs={{1,2},{2,1},{5,6},{6,5},{9,10},{10,9},{13,14},{14,13},{17,18},{18,... | collective-permute-start | bytes 884744 | tf_op jit(solution)/shard_map/ppermute | solution.py:266
  7.6 0.5 %collective-permute-done = f32[1,8,1536]{2,1,0:T(8,128)S(1)} collective-permute-done((f32[1,8,1536]{2,1,0:T(8,128)S(1)}, f32[1,8,1536]{2,1,0:T(8,128)S(1)}, u32[]{:S(2)}, u32[]{:S(2)}) %collective-permute-start) | collective-permute-done | bytes 49184 | tf_op jit(solution)/shard_map/ppermute | solution.py:256
  8.2 4.1 %collective-permute-start.1 = (f32[1,8,1536]{2,1,0:T(8,128)S(1)}, f32[1,8,1536]{2,1,0:T(8,128)S(1)}, u32[]{:S(2)}, u32[]{:S(2)}) collective-permute-start(f32[1,8,1536]{2,1,0:T(8,128)S(1)} %collective-permute-done), channel_id=1, source_target_pairs={{0,7},{3,4},{4,11},{7,8},{8,15},{11,12},{12,19},{15,16},{16,23},{1... | collective-permute-start | bytes 147464 | tf_op jit(solution)/shard_map/ppermute | solution.py:266
  12.3 2.2 %collective-permute-done.1 = f32[1,8,1536]{2,1,0:T(8,128)S(1)} collective-permute-done((f32[1,8,1536]{2,1,0:T(8,128)S(1)}, f32[1,8,1536]{2,1,0:T(8,128)S(1)}, u32[]{:S(2)}, u32[]{:S(2)}) %collective-permute-start.1) | collective-permute-done | bytes 49184 | tf_op jit(solution)/shard_map/ppermute | solution.py:266
  14.4 0.0 collective-permute-start.2
  14.4 0.0 collective-permute-done.4.straight
  14.5 0.6 %collective-permute-start.5 = (f32[2,8,1536]{2,1,0:T(8,128)S(1)}, f32[2,8,1536]{2,1,0:T(8,128)S(1)}, u32[]{:S(2)}, u32[]{:S(2)}) collective-permute-start(f32[2,8,1536]{2,1,0:T(8,128)S(1)} %pad_maximum_fusion), channel_id=1, source_target_pairs={{0,1},{1,0},{2,3},{3,2},{4,5},{5,4},{6,7},{7,6},{8,9},{9,8},{10,11... | collective-permute-start | bytes 294920 | tf_op jit(solution)/shard_map/ppermute | solution.py:256
  15.1 4.0 %collective-permute-start.9 = (f32[3,8,1536]{2,1,0:T(8,128)S(1)}, f32[3,8,1536]{2,1,0:T(8,128)S(1)}, u32[]{:S(2)}, u32[]{:S(2)}) collective-permute-start(f32[3,8,1536]{2,1,0:T(8,128)S(1)} %get-tuple-element.16), channel_id=1, source_target_pairs={{0,4},{4,8},{8,12},{12,16},{16,20},{20,24},{24,28},{1,5},{5,9},{9,... | collective-permute-start | bytes 442376 | tf_op jit(solution)/shard_map/ppermute | solution.py:241
  19.1 0.0 collective-permute-done.5.relayed
  19.1 0.0 collective-permute-done.3.pair_far
  19.1 0.0 collective-permute-done.2.pair_near
  19.1 0.1 broadcast_in_dim.4.spin
  19.2 0.1 broadcast_in_dim.5.inside
  19.3 1.2 %shard_map.86 = (f32[3,8,1536]{2,1,0:T(8,128)S(1)}, f32[3,8,1536]{2,1,0:T(8,128)S(1)}) custom-call(f32[6,8,1536]{2,1,0:T(8,128)S(1)} %get-tuple-element.11.pair, f32[6,8,1536]{2,1,0:T(8,128)S(1)} %collective-permute-done.2.pair_near, f32[6,8,1536]{2,1,0:T(8,128)S(1)} %collective-permute-done.3.pair_far, f32[4,8,1536]{2,1,0:T(8,128)S(1)} %collective-permute-done.4.straight, ...), custom_call_target="tpu_custom_call" | custom-call | flops 5996544 | bytes 1499136 | tf_op jit(solution)/shard_map/pallas_call | solution.py:227
  20.5 0.7 %collective-permute-start.8 = (f32[3,8,1536]{2,1,0:T(8,128)S(1)}, f32[3,8,1536]{2,1,0:T(8,128)S(1)}, u32[]{:S(2)}, u32[]{:S(2)}) collective-permute-start(f32[3,8,1536]{2,1,0:T(8,128)S(1)} %get-tuple-element.14.state), channel_id=1, source_target_pairs={{1,2},{2,1},{5,6},{6,5},{9,10},{10,9},{13,14},{14,13},{17,18},{18,... | collective-permute-start | bytes 442376 | tf_op jit(solution)/shard_map/ppermute | solution.py:266
  21.1 2.6 %collective-permute-start.7 = (f32[3,8,1536]{2,1,0:T(8,128)S(1)}, f32[3,8,1536]{2,1,0:T(8,128)S(1)}, u32[]{:S(2)}, u32[]{:S(2)}) collective-permute-start(f32[3,8,1536]{2,1,0:T(8,128)S(1)} %get-tuple-element.14.state), channel_id=1, source_target_pairs={{0,1},{1,0},{2,3},{3,2},{4,5},{5,4},{6,7},{7,6},{8,9},{9,8},{10,11... | collective-permute-start | bytes 442376 | tf_op jit(solution)/shard_map/ppermute | solution.py:256
  23.7 1.3 %collective-permute-start.6 = (f32[3,8,1536]{2,1,0:T(8,128)S(1)}, f32[3,8,1536]{2,1,0:T(8,128)S(1)}, u32[]{:S(2)}, u32[]{:S(2)}) collective-permute-start(f32[3,8,1536]{2,1,0:T(8,128)S(1)} %get-tuple-element.13), channel_id=1, source_target_pairs={{4,0},{8,4},{12,8},{16,12},{20,16},{24,20},{28,24},{5,1},{9,5},{13... | collective-permute-start | bytes 442376 | tf_op jit(solution)/shard_map/ppermute | solution.py:241
  25.0 0.0 collective-permute-done.9.local
  25.0 1.2 %shard_map.88.tally = f32[2,8,128]{2,1,0:T(8,128)S(1)} custom-call(f32[6,8,1536]{2,1,0:T(8,128)S(1)} %get-tuple-element.11.pair, f32[6,8,1536]{2,1,0:T(8,128)S(1)} %collective-permute-done.2.pair_near, f32[6,8,1536]{2,1,0:T(8,128)S(1)} %collective-permute-done.3.pair_far, f32[4,8,1536]{2,1,0:T(8,128)S(1)} %collective-permute-done.4.straight, ...), custom_call_target="tpu_custom_call" | custom-call | flops 6029312 | bytes 1507328 | tf_op jit(solution)/shard_map/pallas_call | solution.py:227
  26.2 0.0 copy-start
  26.2 0.0 copy-start.1
  26.2 0.0 copy-start.2
  26.2 0.0 copy-start.3
  26.2 0.0 copy-start.4
  26.3 1.2 %shard_map.87.end = f32[3,8,1536]{2,1,0:T(8,128)S(1)} custom-call(f32[3,8,1536]{2,1,0:T(8,128)S(1)} %get-tuple-element.14.state, f32[3,8,1536]{2,1,0:T(8,128)S(1)} %collective-permute-done.7.state_near, f32[3,8,1536]{2,1,0:T(8,128)S(1)} %collective-permute-done.8.state_far, f32[4,8,1536]{2,1,0:T(8,128)S(1)} %collective-permute-done.4.straight, ...), custom_call_target="tpu_custom_call" | custom-call | flops 3637248 | bytes 909312 | tf_op jit(solution)/shard_map/pallas_call | solution.py:227
  27.4 4.1 %collective-permute-done.6.back = f32[3,8,1536]{2,1,0:T(8,128)S(1)} collective-permute-done((f32[3,8,1536]{2,1,0:T(8,128)S(1)}, f32[3,8,1536]{2,1,0:T(8,128)S(1)}, u32[]{:S(2)}, u32[]{:S(2)}) %collective-permute-start.6) | collective-permute-done | bytes 147488 | tf_op jit(solution)/shard_map/ppermute | solution.py:241
  31.6 0.4 shard_map.89
  32.0 11.9 %all_to_all.11 = f32[32,1,128]{2,1,0:T(1,128)S(1)} all-to-all(f32[32,1,128]{2,1,0:T(1,128)S(1)} %bitcast.5), channel_id=1, replica_groups=mesh['win'=8,'band'=2,'half'=2] {'win','band','half'}, dimensions={0} | all-to-all | bytes 32768 | tf_op jit(solution)/shard_map/all_to_all | solution.py:307
  43.9 1.2 %shard_map.90 = (f32[1,3,8,1536]{3,2,1,0:T(8,128)}, f32[1,3,8,1536]{3,2,1,0:T(8,128)}, f32[1,3,8,1536]{3,2,1,0:T(8,128)}) custom-call(f32[32,128]{1,0:T(8,128)S(1)} %bitcast.4, f32[1,3,8,1536]{3,2,1,0:T(8,128)S(1)} %copy-done, f32[1,3,8,1536]{3,2,1,0:T(8,128)S(1)} %copy-done.1, f32[1,3,8,1536]{3,2,1,0:T(8,128)S(1)} %copy-done.2, ...), custom_call_target="tpu_custom_call" | custom-call | flops 5373952 | bytes 1343488 | tf_op jit(solution)/shard_map/pallas_call | solution.py:227
  (13 shorter events, 0.1 us)
Async XLA Ops:
  0.6 6.2 %copy-start.5 = (f32[1,8,1536]{2,1,0:T(8,128)S(1)}, f32[1,8,1536]{2,1,0:T(8,128)}, u32[]{:S(2)}) copy-start(f32[1,8,1536]{2,1,0:T(8,128)} %depth.1) | copy-start | bytes 147460
  2.0 12.5 %collective-permute-start.4 = (f32[4,8,1536]{2,1,0:T(8,128)S(1)}, f32[4,8,1536]{2,1,0:T(8,128)S(1)}, u32[]{:S(2)}, u32[]{:S(2)}) collective-permute-start(f32[4,8,1536]{2,1,0:T(8,128)S(1)} %get-tuple-element.12), channel_id=1, source_target_pairs={{0,4},{4,8},{8,12},{12,16},{16,20},{20,24},{24,28},{1,5},{5,9},{9,... | collective-permute-start | bytes 589832 | tf_op jit(solution)/shard_map/ppermute | solution.py:241
  6.9 1.3 %collective-permute-start = (f32[1,8,1536]{2,1,0:T(8,128)S(1)}, f32[1,8,1536]{2,1,0:T(8,128)S(1)}, u32[]{:S(2)}, u32[]{:S(2)}) collective-permute-start(f32[1,8,1536]{2,1,0:T(8,128)S(1)} %copy-done.5), channel_id=1, source_target_pairs={{0,1},{1,0},{2,3},{3,2},{4,5},{5,4},{6,7},{7,6},{8,9},{9,8},{10,11... | collective-permute-start | bytes 147464 | tf_op jit(solution)/shard_map/ppermute | solution.py:256
  6.9 12.2 %collective-permute-start.3 = (f32[6,8,1536]{2,1,0:T(8,128)S(1)}, f32[6,8,1536]{2,1,0:T(8,128)S(1)}, u32[]{:S(2)}, u32[]{:S(2)}) collective-permute-start(f32[6,8,1536]{2,1,0:T(8,128)S(1)} %get-tuple-element.11.pair), channel_id=1, source_target_pairs={{1,2},{2,1},{5,6},{6,5},{9,10},{10,9},{13,14},{14,13},{17,18},{18,... | collective-permute-start | bytes 884744 | tf_op jit(solution)/shard_map/ppermute | solution.py:266
  8.2 6.3 %collective-permute-start.1 = (f32[1,8,1536]{2,1,0:T(8,128)S(1)}, f32[1,8,1536]{2,1,0:T(8,128)S(1)}, u32[]{:S(2)}, u32[]{:S(2)}) collective-permute-start(f32[1,8,1536]{2,1,0:T(8,128)S(1)} %collective-permute-done), channel_id=1, source_target_pairs={{0,7},{3,4},{4,11},{7,8},{8,15},{11,12},{12,19},{15,16},{16,23},{1... | collective-permute-start | bytes 147464 | tf_op jit(solution)/shard_map/ppermute | solution.py:266
  14.4 4.7 %collective-permute-start.2 = (f32[6,8,1536]{2,1,0:T(8,128)S(1)}, f32[6,8,1536]{2,1,0:T(8,128)S(1)}, u32[]{:S(2)}, u32[]{:S(2)}) collective-permute-start(f32[6,8,1536]{2,1,0:T(8,128)S(1)} %get-tuple-element.11.pair), channel_id=1, source_target_pairs={{0,1},{1,0},{2,3},{3,2},{4,5},{5,4},{6,7},{7,6},{8,9},{9,8},{10,11... | collective-permute-start | bytes 884744 | tf_op jit(solution)/shard_map/ppermute | solution.py:256
  14.5 4.6 %collective-permute-start.5 = (f32[2,8,1536]{2,1,0:T(8,128)S(1)}, f32[2,8,1536]{2,1,0:T(8,128)S(1)}, u32[]{:S(2)}, u32[]{:S(2)}) collective-permute-start(f32[2,8,1536]{2,1,0:T(8,128)S(1)} %pad_maximum_fusion), channel_id=1, source_target_pairs={{0,1},{1,0},{2,3},{3,2},{4,5},{5,4},{6,7},{7,6},{8,9},{9,8},{10,11... | collective-permute-start | bytes 294920 | tf_op jit(solution)/shard_map/ppermute | solution.py:256
  15.1 9.9 %collective-permute-start.9 = (f32[3,8,1536]{2,1,0:T(8,128)S(1)}, f32[3,8,1536]{2,1,0:T(8,128)S(1)}, u32[]{:S(2)}, u32[]{:S(2)}) collective-permute-start(f32[3,8,1536]{2,1,0:T(8,128)S(1)} %get-tuple-element.16), channel_id=1, source_target_pairs={{0,4},{4,8},{8,12},{12,16},{16,20},{20,24},{24,28},{1,5},{5,9},{9,... | collective-permute-start | bytes 442376 | tf_op jit(solution)/shard_map/ppermute | solution.py:241
  20.5 5.8 %collective-permute-start.8 = (f32[3,8,1536]{2,1,0:T(8,128)S(1)}, f32[3,8,1536]{2,1,0:T(8,128)S(1)}, u32[]{:S(2)}, u32[]{:S(2)}) collective-permute-start(f32[3,8,1536]{2,1,0:T(8,128)S(1)} %get-tuple-element.14.state), channel_id=1, source_target_pairs={{1,2},{2,1},{5,6},{6,5},{9,10},{10,9},{13,14},{14,13},{17,18},{18,... | collective-permute-start | bytes 442376 | tf_op jit(solution)/shard_map/ppermute | solution.py:266
  21.1 5.1 %collective-permute-start.7 = (f32[3,8,1536]{2,1,0:T(8,128)S(1)}, f32[3,8,1536]{2,1,0:T(8,128)S(1)}, u32[]{:S(2)}, u32[]{:S(2)}) collective-permute-start(f32[3,8,1536]{2,1,0:T(8,128)S(1)} %get-tuple-element.14.state), channel_id=1, source_target_pairs={{0,1},{1,0},{2,3},{3,2},{4,5},{5,4},{6,7},{7,6},{8,9},{9,8},{10,11... | collective-permute-start | bytes 442376 | tf_op jit(solution)/shard_map/ppermute | solution.py:256
  23.7 7.9 %collective-permute-start.6 = (f32[3,8,1536]{2,1,0:T(8,128)S(1)}, f32[3,8,1536]{2,1,0:T(8,128)S(1)}, u32[]{:S(2)}, u32[]{:S(2)}) collective-permute-start(f32[3,8,1536]{2,1,0:T(8,128)S(1)} %get-tuple-element.13), channel_id=1, source_target_pairs={{4,0},{8,4},{12,8},{16,12},{20,16},{24,20},{28,24},{5,1},{9,5},{13... | collective-permute-start | bytes 442376 | tf_op jit(solution)/shard_map/ppermute | solution.py:241
  26.2 5.4 %copy-start = (f32[1,3,8,1536]{3,2,1,0:T(8,128)S(1)}, f32[1,3,8,1536]{3,2,1,0:T(8,128)}, u32[]{:S(2)}) copy-start(f32[1,3,8,1536]{3,2,1,0:T(8,128)} %p.5) | copy-start | bytes 442372
  26.2 5.4 %copy-start.1 = (f32[1,3,8,1536]{3,2,1,0:T(8,128)S(1)}, f32[1,3,8,1536]{3,2,1,0:T(8,128)}, u32[]{:S(2)}) copy-start(f32[1,3,8,1536]{3,2,1,0:T(8,128)} %m.5) | copy-start | bytes 442372
  26.2 5.4 %copy-start.2 = (f32[1,3,8,1536]{3,2,1,0:T(8,128)S(1)}, f32[1,3,8,1536]{3,2,1,0:T(8,128)}, u32[]{:S(2)}) copy-start(f32[1,3,8,1536]{3,2,1,0:T(8,128)} %dvar.5) | copy-start | bytes 442372
  26.2 5.4 %copy-start.3 = (f32[1,3,8,1536]{3,2,1,0:T(8,128)S(1)}, f32[1,3,8,1536]{3,2,1,0:T(8,128)}, u32[]{:S(2)}) copy-start(f32[1,3,8,1536]{3,2,1,0:T(8,128)} %rvar.5) | copy-start | bytes 442372
  26.2 5.4 %copy-start.4 = (f32[1,3,8,1536]{3,2,1,0:T(8,128)S(1)}, f32[1,3,8,1536]{3,2,1,0:T(8,128)}, u32[]{:S(2)}) copy-start(f32[1,3,8,1536]{3,2,1,0:T(8,128)} %hobs.5) | copy-start | bytes 442372

commit v10 on v9

--- a/solution.py
+++ b/solution.py
@@ -38,7 +38,7 @@
     return jnp.concatenate([low, own[index], high], axis=0)
 
 
-def prep_kernel(p, m, dvar, rvar, hobs, depth, pair, straight, local, pv, mv, dv, rv, hv, sems):
+def prep_kernel(p, m, dvar, rvar, hobs, depth, pair, straight, pv, mv, dv, rv, hv, sems):
     copies = [
         pltpu.make_async_copy(source, target, sems.at[slot])
         for slot, (source, target) in enumerate(
@@ -55,7 +55,7 @@
         pair[part] = pv[0, part]
         pair[3 + part] = up
         straight[1 + part] = pv[0, part] + seen
-        local[part] = up + rv[0, part] * seen
+        straight[4 + part] = up + rv[0, part] * seen
 
 
 def widened(tile, width):
@@ -90,19 +90,19 @@
         state[part] = jnp.where(link, straight[1 + part] - value, 0.0)
 
 
-def second_adjoint_kernel(pair, pair_near, pair_far, straight, relayed, spin, inside, local, state, tally):
+def second_adjoint_kernel(pair, pair_near, pair_far, straight, relayed, spin, inside, state, tally):
     swept = adjoint(pair, pair_near, pair_far, straight, relayed, spin, inside, 3)
     link = has_previous()
     cross = square = 0.0
     for part, value in enumerate(swept):
-        zx = jnp.where(link, local[part] - value, 0.0)
+        zx = jnp.where(link, straight[4 + part] - value, 0.0)
         cross += lane_sum(zx * state[part])
         square += lane_sum(zx * zx)
     tally[0] = cross
     tally[1] = square
 
 
-def forward_kernel(state, state_near, state_far, straight, relayed, spin, inside, end):
+def forward_kernel(state, state_far, state_near, straight, relayed, spin, inside, end):
     depth = stretched(straight, relayed)
     turn, keep = widened(spin, depth.shape[1]), widened(inside, depth.shape[1])
     height, east, north = [stacked(state, state_near, state_far, part) for part in range(3)]
@@ -280,8 +280,8 @@
     fields = (3, rows, width)
 
     middle, outer = (1, 2), (0, 3)
-    pair, straight, local = run(
-        prep_kernel, [(6, rows, width), (4, rows, width), fields],
+    pair, straight = run(
+        prep_kernel, [(6, rows, width), (7, rows, width)],
         model_rhs, obs_rhs, model_var, obs_var, obs_weight, depth,
         scratch=[pltpu.VMEM(model_rhs.shape, jnp.float32)] * 5 + [pltpu.SemaphoreType.DMA((6,))],
         space=pltpu.HBM,
@@ -290,16 +290,15 @@
     depth_near = swapped(depth, 0)
     depth_edge = crossed(depth_near, outer, 1)
     relayed = swapped(jnp.concatenate([came[:1], depth_edge]), 0)
-    local, _ = lax.optimization_barrier((local, depth_near))
-    local = shifted(local, 1)
     held_pair, _ = lax.optimization_barrier((pair, depth_edge))
     pair_near, pair_far = swapped(held_pair, 0), crossed(pair, middle)
     known = (pair, pair_near, pair_far, came, relayed, spin, inside)
     state, back = run(first_adjoint_kernel, [fields, fields], *known)
     back = shifted(back, -1)
-    state_near, state_far = swapped(state, 0), crossed(state, middle)
-    (tally,) = run(second_adjoint_kernel, [(2, rows, 128)], *known, local, state)
-    (end,) = run(forward_kernel, [fields], state, state_near, state_far, came, relayed, spin, inside)
+    state_far = crossed(state, middle)
+    (tally,) = run(second_adjoint_kernel, [(2, rows, 128)], *known, state)
+    state_near = swapped(state, 0)
+    (end,) = run(forward_kernel, [fields], state, state_far, state_near, came, relayed, spin, inside)
     (sent,) = run(
         inner_kernel, [(ranks, 128)],
         model_rhs, obs_rhs, model_var, obs_var, obs_weight, back, end, tally,

time: 45.4 us -> 43.2 us (0.952)
  starting transfers between devices: 18.9 us -> 12.2 us
  blocking collectives: 11.9 us -> 15.6 us
  waiting for transfers between devices: 6.85 us -> 7.68 us
    ppermute x3 -> x2, starting transfers between devices: 10.2 us -> 6.18 us  [shifted(): lax.ppermute(value, 'win', [(source, source + step) for source in range(i...]
    all_to_all x1, blocking collectives: 11.9 us -> 15.6 us  [body(): gathered = lax.all_to_all(sent, ('win', 'band', 'half'), 0, 0, tiled=True)]
    ppermute x4, starting transfers between devices: 3.22 us -> 0.63 us  [swapped(): return lax.ppermute(value, ('band', 'half'), pairs)]
    ppermute x4, waiting for transfers between devices: 0.53 us -> 1.59 us  [swapped(): return lax.ppermute(value, ('band', 'half'), pairs)]
    ppermute x3 -> x2, waiting for transfers between devices: 4.15 us -> 3.92 us  [shifted(): lax.ppermute(value, 'win', [(source, source + step) for source in range(i...]
  transfers between devices with their start and end apart: 10 -> 9, of which waited for: 3 -> 6; matrix products, arithmetic and copies ran while one was open for 0% -> 0% of each run, Pallas kernels for 8% -> 5%
where the time goes in v10:
time: 43.2 us; the launch traced here: 43 us
  blocking collectives  15.6 us (36%)
  starting transfers between devices  12.2 us (28%)
  waiting for transfers between devices  7.68 us (18%)
  Pallas kernels  6.39 us (15%)
  between operations  0.83 us (2%)
    all_to_all x1, blocking collectives, body(): gathered = lax.all_to_all(sent, ('win', 'band', 'half'), 0, 0, tiled=True)  15.6 us
    pallas_call x6, Pallas kernels, run(): pl.pallas_call(kernel, out_shape=shapes, in_specs=[pl.BlockSpec(memory_sp...  6.39 us
    ppermute x2, starting transfers between devices, shifted(): lax.ppermute(value, 'win', [(source, source + step) for source in range(i...  6.18 us
    ppermute x3, starting transfers between devices, crossed(): return lax.ppermute(value, ('win', 'band', 'half'), pairs)  5.43 us
    ppermute x2, waiting for transfers between devices, shifted(): lax.ppermute(value, 'win', [(source, source + step) for source in range(i...  3.92 us
    ppermute x3, waiting for transfers between devices, crossed(): return lax.ppermute(value, ('win', 'band', 'half'), pairs)  2.17 us
    ppermute x4, waiting for transfers between devices, swapped(): return lax.ppermute(value, ('band', 'half'), pairs)  1.59 us
  transfers between devices with their start and end apart: 9, of which 6 were waited for; matrix products, arithmetic and copies ran while one was open for 0% of the time, Pallas kernels for 5%

profile of v10, /device:TPU:0, one launch (start us, length us, event | category | flops | bytes accessed | tf_op | source)
XLA Modules:
  0.0 43.0 jit_solution(2930311299635514229)
XLA Ops:
  0.6 1.3 %shard_map.85 = (f32[6,8,1536]{2,1,0:T(8,128)S(1)}, f32[7,8,1536]{2,1,0:T(8,128)S(1)}) custom-call(f32[1,3,8,1536]{3,2,1,0:T(8,128)} %p.5, f32[1,3,8,1536]{3,2,1,0:T(8,128)} %m.5, f32[1,3,8,1536]{3,2,1,0:T(8,128)} %dvar.5, f32[1,3,8,1536]{3,2,1,0:T(8,128)} %rvar.5, f32[1,3,8,1536]{3,2,1,0:T(8,128)} %hobs.5, f32[1,8,1536]{2,1,0:T(8,128)} %depth.1), custom_call_target="tpu_custom_call" | custom-call | flops 5701632 | bytes 1425408 | tf_op jit(solution)/shard_map/pallas_call | solution.py:227
  2.0 4.9 %collective-permute-start.4 = (f32[7,8,1536]{2,1,0:T(8,128)S(1)}, f32[7,8,1536]{2,1,0:T(8,128)S(1)}, u32[]{:S(2)}, u32[]{:S(2)}) collective-permute-start(f32[7,8,1536]{2,1,0:T(8,128)S(1)} %get-tuple-element.10), channel_id=1, source_target_pairs={{0,4},{4,8},{8,12},{12,16},{16,20},{20,24},{24,28},{1,5},{5,9},{9,... | collective-permute-start | bytes 1032200 | tf_op jit(solution)/shard_map/ppermute | solution.py:241
  6.9 0.1 collective-permute-start
  6.9 0.7 %collective-permute-start.3 = (f32[6,8,1536]{2,1,0:T(8,128)S(1)}, f32[6,8,1536]{2,1,0:T(8,128)S(1)}, u32[]{:S(2)}, u32[]{:S(2)}) collective-permute-start(f32[6,8,1536]{2,1,0:T(8,128)S(1)} %get-tuple-element.9.pair), channel_id=1, source_target_pairs={{1,2},{2,1},{5,6},{6,5},{9,10},{10,9},{13,14},{14,13},{17,18},{18,... | collective-permute-start | bytes 884744 | tf_op jit(solution)/shard_map/ppermute | solution.py:266
  7.6 0.5 %collective-permute-done = f32[1,8,1536]{2,1,0:T(8,128)S(1)} collective-permute-done((f32[1,8,1536]{2,1,0:T(8,128)S(1)}, f32[1,8,1536]{2,1,0:T(8,128)S(1)}, u32[]{:S(2)}, u32[]{:S(2)}) %collective-permute-start) | collective-permute-done | bytes 49184 | tf_op jit(solution)/shard_map/ppermute | solution.py:256
  8.2 4.1 %collective-permute-start.1 = (f32[1,8,1536]{2,1,0:T(8,128)S(1)}, f32[1,8,1536]{2,1,0:T(8,128)S(1)}, u32[]{:S(2)}, u32[]{:S(2)}) collective-permute-start(f32[1,8,1536]{2,1,0:T(8,128)S(1)} %collective-permute-done), channel_id=1, source_target_pairs={{0,7},{3,4},{4,11},{7,8},{8,15},{11,12},{12,19},{15,16},{16,23},{1... | collective-permute-start | bytes 147464 | tf_op jit(solution)/shard_map/ppermute | solution.py:266
  12.3 2.2 %collective-permute-done.1 = f32[1,8,1536]{2,1,0:T(8,128)S(1)} collective-permute-done((f32[1,8,1536]{2,1,0:T(8,128)S(1)}, f32[1,8,1536]{2,1,0:T(8,128)S(1)}, u32[]{:S(2)}, u32[]{:S(2)}) %collective-permute-start.1) | collective-permute-done | bytes 49184 | tf_op jit(solution)/shard_map/ppermute | solution.py:266
  14.4 0.0 collective-permute-start.2
  14.4 0.3 collective-permute-done.4.straight
  14.7 0.3 collective-permute-start.5
  15.1 0.0 collective-permute-done.3.pair_far
  15.1 0.9 %collective-permute-done.2.pair_near = f32[6,8,1536]{2,1,0:T(8,128)S(1)} collective-permute-done((f32[6,8,1536]{2,1,0:T(8,128)S(1)}, f32[6,8,1536]{2,1,0:T(8,128)S(1)}, u32[]{:S(2)}, u32[]{:S(2)}) %collective-permute-start.2) | collective-permute-done | bytes 294944 | tf_op jit(solution)/shard_map/ppermute | solution.py:256
  16.0 0.1 collective-permute-done.5.relayed
  16.2 0.1 broadcast_in_dim.4.spin
  16.2 0.1 broadcast_in_dim.5.inside
  16.3 1.2 %shard_map.86 = (f32[3,8,1536]{2,1,0:T(8,128)S(1)}, f32[3,8,1536]{2,1,0:T(8,128)S(1)}) custom-call(f32[6,8,1536]{2,1,0:T(8,128)S(1)} %get-tuple-element.9.pair, f32[6,8,1536]{2,1,0:T(8,128)S(1)} %collective-permute-done.2.pair_near, f32[6,8,1536]{2,1,0:T(8,128)S(1)} %collective-permute-done.3.pair_far, f32[7,8,1536]{2,1,0:T(8,128)S(1)} %collective-permute-done.4.straight, ...), custom_call_target="tpu_custom_call" | custom-call | flops 6586368 | bytes 1646592 | tf_op jit(solution)/shard_map/pallas_call | solution.py:227
  17.5 0.2 collective-permute-start.8
  17.7 0.7 %collective-permute-start.7 = (f32[3,8,1536]{2,1,0:T(8,128)S(1)}, f32[3,8,1536]{2,1,0:T(8,128)S(1)}, u32[]{:S(2)}, u32[]{:S(2)}) collective-permute-start(f32[3,8,1536]{2,1,0:T(8,128)S(1)} %get-tuple-element.12.state), channel_id=1, source_target_pairs={{1,2},{2,1},{5,6},{6,5},{9,10},{10,9},{13,14},{14,13},{17,18},{18,... | collective-permute-start | bytes 442376 | tf_op jit(solution)/shard_map/ppermute | solution.py:266
  18.4 1.3 %collective-permute-start.6 = (f32[3,8,1536]{2,1,0:T(8,128)S(1)}, f32[3,8,1536]{2,1,0:T(8,128)S(1)}, u32[]{:S(2)}, u32[]{:S(2)}) collective-permute-start(f32[3,8,1536]{2,1,0:T(8,128)S(1)} %get-tuple-element.11), channel_id=1, source_target_pairs={{4,0},{8,4},{12,8},{16,12},{20,16},{24,20},{28,24},{5,1},{9,5},{13... | collective-permute-start | bytes 442376 | tf_op jit(solution)/shard_map/ppermute | solution.py:241
  19.7 1.2 %shard_map.88.tally = f32[2,8,128]{2,1,0:T(8,128)S(1)} custom-call(f32[6,8,1536]{2,1,0:T(8,128)S(1)} %get-tuple-element.9.pair, f32[6,8,1536]{2,1,0:T(8,128)S(1)} %collective-permute-done.2.pair_near, f32[6,8,1536]{2,1,0:T(8,128)S(1)} %collective-permute-done.3.pair_far, f32[7,8,1536]{2,1,0:T(8,128)S(1)} %collective-permute-done.4.straight, ...), custom_call_target="tpu_custom_call" | custom-call | flops 6029312 | bytes 1507328 | tf_op jit(solution)/shard_map/pallas_call | solution.py:227
  20.8 0.0 copy-start
  20.9 0.0 copy-start.1
  20.9 0.0 copy-start.2
  20.9 0.0 copy-start.3
  20.9 0.0 copy-start.4
  20.9 0.0 collective-permute-done.8.state_near
  20.9 0.0 collective-permute-done.7.state_far
  20.9 1.1 %shard_map.87.end = f32[3,8,1536]{2,1,0:T(8,128)S(1)} custom-call(f32[3,8,1536]{2,1,0:T(8,128)S(1)} %get-tuple-element.12.state, f32[3,8,1536]{2,1,0:T(8,128)S(1)} %collective-permute-done.7.state_far, f32[3,8,1536]{2,1,0:T(8,128)S(1)} %collective-permute-done.8.state_near, f32[7,8,1536]{2,1,0:T(8,128)S(1)} %collective-permute-done.4.straight, ...), custom_call_target="tpu_custom_call" | custom-call | flops 4227072 | bytes 1056768 | tf_op jit(solution)/shard_map/pallas_call | solution.py:227
  22.1 3.7 %collective-permute-done.6.back = f32[3,8,1536]{2,1,0:T(8,128)S(1)} collective-permute-done((f32[3,8,1536]{2,1,0:T(8,128)S(1)}, f32[3,8,1536]{2,1,0:T(8,128)S(1)}, u32[]{:S(2)}, u32[]{:S(2)}) %collective-permute-start.6) | collective-permute-done | bytes 147488 | tf_op jit(solution)/shard_map/ppermute | solution.py:241
  25.8 0.4 shard_map.89
  26.2 15.6 %all_to_all.11 = f32[32,1,128]{2,1,0:T(1,128)S(1)} all-to-all(f32[32,1,128]{2,1,0:T(1,128)S(1)} %bitcast.5), channel_id=1, replica_groups=mesh['win'=8,'band'=2,'half'=2] {'win','band','half'}, dimensions={0} | all-to-all | bytes 32768 | tf_op jit(solution)/shard_map/all_to_all | solution.py:306
  41.8 1.2 %shard_map.90 = (f32[1,3,8,1536]{3,2,1,0:T(8,128)}, f32[1,3,8,1536]{3,2,1,0:T(8,128)}, f32[1,3,8,1536]{3,2,1,0:T(8,128)}) custom-call(f32[32,128]{1,0:T(8,128)S(1)} %bitcast.4, f32[1,3,8,1536]{3,2,1,0:T(8,128)S(1)} %copy-done, f32[1,3,8,1536]{3,2,1,0:T(8,128)S(1)} %copy-done.1, f32[1,3,8,1536]{3,2,1,0:T(8,128)S(1)} %copy-done.2, ...), custom_call_target="tpu_custom_call" | custom-call | flops 5373952 | bytes 1343488 | tf_op jit(solution)/shard_map/pallas_call | solution.py:227
  (11 shorter events, 0.1 us)
Async XLA Ops:
  0.6 6.2 %copy-start.5 = (f32[1,8,1536]{2,1,0:T(8,128)S(1)}, f32[1,8,1536]{2,1,0:T(8,128)}, u32[]{:S(2)}) copy-start(f32[1,8,1536]{2,1,0:T(8,128)} %depth.1) | copy-start | bytes 147460
  2.0 12.7 %collective-permute-start.4 = (f32[7,8,1536]{2,1,0:T(8,128)S(1)}, f32[7,8,1536]{2,1,0:T(8,128)S(1)}, u32[]{:S(2)}, u32[]{:S(2)}) collective-permute-start(f32[7,8,1536]{2,1,0:T(8,128)S(1)} %get-tuple-element.10), channel_id=1, source_target_pairs={{0,4},{4,8},{8,12},{12,16},{16,20},{20,24},{24,28},{1,5},{5,9},{9,... | collective-permute-start | bytes 1032200 | tf_op jit(solution)/shard_map/ppermute | solution.py:241
  6.9 1.3 %collective-permute-start = (f32[1,8,1536]{2,1,0:T(8,128)S(1)}, f32[1,8,1536]{2,1,0:T(8,128)S(1)}, u32[]{:S(2)}, u32[]{:S(2)}) collective-permute-start(f32[1,8,1536]{2,1,0:T(8,128)S(1)} %copy-done.5), channel_id=1, source_target_pairs={{0,1},{1,0},{2,3},{3,2},{4,5},{5,4},{6,7},{7,6},{8,9},{9,8},{10,11... | collective-permute-start | bytes 147464 | tf_op jit(solution)/shard_map/ppermute | solution.py:256
  6.9 8.1 %collective-permute-start.3 = (f32[6,8,1536]{2,1,0:T(8,128)S(1)}, f32[6,8,1536]{2,1,0:T(8,128)S(1)}, u32[]{:S(2)}, u32[]{:S(2)}) collective-permute-start(f32[6,8,1536]{2,1,0:T(8,128)S(1)} %get-tuple-element.9.pair), channel_id=1, source_target_pairs={{1,2},{2,1},{5,6},{6,5},{9,10},{10,9},{13,14},{14,13},{17,18},{18,... | collective-permute-start | bytes 884744 | tf_op jit(solution)/shard_map/ppermute | solution.py:266
  8.2 6.3 %collective-permute-start.1 = (f32[1,8,1536]{2,1,0:T(8,128)S(1)}, f32[1,8,1536]{2,1,0:T(8,128)S(1)}, u32[]{:S(2)}, u32[]{:S(2)}) collective-permute-start(f32[1,8,1536]{2,1,0:T(8,128)S(1)} %collective-permute-done), channel_id=1, source_target_pairs={{0,7},{3,4},{4,11},{7,8},{8,15},{11,12},{12,19},{15,16},{16,23},{1... | collective-permute-start | bytes 147464 | tf_op jit(solution)/shard_map/ppermute | solution.py:266
  14.4 1.6 %collective-permute-start.2 = (f32[6,8,1536]{2,1,0:T(8,128)S(1)}, f32[6,8,1536]{2,1,0:T(8,128)S(1)}, u32[]{:S(2)}, u32[]{:S(2)}) collective-permute-start(f32[6,8,1536]{2,1,0:T(8,128)S(1)} %get-tuple-element.9.pair), channel_id=1, source_target_pairs={{0,1},{1,0},{2,3},{3,2},{4,5},{5,4},{6,7},{7,6},{8,9},{9,8},{10,11... | collective-permute-start | bytes 884744 | tf_op jit(solution)/shard_map/ppermute | solution.py:256
  14.7 1.4 %collective-permute-start.5 = (f32[2,8,1536]{2,1,0:T(8,128)S(1)}, f32[2,8,1536]{2,1,0:T(8,128)S(1)}, u32[]{:S(2)}, u32[]{:S(2)}) collective-permute-start(f32[2,8,1536]{2,1,0:T(8,128)S(1)} %pad_maximum_fusion), channel_id=1, source_target_pairs={{0,1},{1,0},{2,3},{3,2},{4,5},{5,4},{6,7},{7,6},{8,9},{9,8},{10,11... | collective-permute-start | bytes 294920 | tf_op jit(solution)/shard_map/ppermute | solution.py:256
  17.5 3.4 %collective-permute-start.8 = (f32[3,8,1536]{2,1,0:T(8,128)S(1)}, f32[3,8,1536]{2,1,0:T(8,128)S(1)}, u32[]{:S(2)}, u32[]{:S(2)}) collective-permute-start(f32[3,8,1536]{2,1,0:T(8,128)S(1)} %get-tuple-element.12.state), channel_id=1, source_target_pairs={{0,1},{1,0},{2,3},{3,2},{4,5},{5,4},{6,7},{7,6},{8,9},{9,8},{10,11... | collective-permute-start | bytes 442376 | tf_op jit(solution)/shard_map/ppermute | solution.py:256
  17.7 3.2 %collective-permute-start.7 = (f32[3,8,1536]{2,1,0:T(8,128)S(1)}, f32[3,8,1536]{2,1,0:T(8,128)S(1)}, u32[]{:S(2)}, u32[]{:S(2)}) collective-permute-start(f32[3,8,1536]{2,1,0:T(8,128)S(1)} %get-tuple-element.12.state), channel_id=1, source_target_pairs={{1,2},{2,1},{5,6},{6,5},{9,10},{10,9},{13,14},{14,13},{17,18},{18,... | collective-permute-start | bytes 442376 | tf_op jit(solution)/shard_map/ppermute | solution.py:266
  18.4 7.4 %collective-permute-start.6 = (f32[3,8,1536]{2,1,0:T(8,128)S(1)}, f32[3,8,1536]{2,1,0:T(8,128)S(1)}, u32[]{:S(2)}, u32[]{:S(2)}) collective-permute-start(f32[3,8,1536]{2,1,0:T(8,128)S(1)} %get-tuple-element.11), channel_id=1, source_target_pairs={{4,0},{8,4},{12,8},{16,12},{20,16},{24,20},{28,24},{5,1},{9,5},{13... | collective-permute-start | bytes 442376 | tf_op jit(solution)/shard_map/ppermute | solution.py:241
  20.8 4.9 %copy-start = (f32[1,3,8,1536]{3,2,1,0:T(8,128)S(1)}, f32[1,3,8,1536]{3,2,1,0:T(8,128)}, u32[]{:S(2)}) copy-start(f32[1,3,8,1536]{3,2,1,0:T(8,128)} %p.5) | copy-start | bytes 442372
  20.9 4.9 %copy-start.1 = (f32[1,3,8,1536]{3,2,1,0:T(8,128)S(1)}, f32[1,3,8,1536]{3,2,1,0:T(8,128)}, u32[]{:S(2)}) copy-start(f32[1,3,8,1536]{3,2,1,0:T(8,128)} %m.5) | copy-start | bytes 442372
  20.9 4.9 %copy-start.2 = (f32[1,3,8,1536]{3,2,1,0:T(8,128)S(1)}, f32[1,3,8,1536]{3,2,1,0:T(8,128)}, u32[]{:S(2)}) copy-start(f32[1,3,8,1536]{3,2,1,0:T(8,128)} %dvar.5) | copy-start | bytes 442372
  20.9 4.9 %copy-start.3 = (f32[1,3,8,1536]{3,2,1,0:T(8,128)S(1)}, f32[1,3,8,1536]{3,2,1,0:T(8,128)}, u32[]{:S(2)}) copy-start(f32[1,3,8,1536]{3,2,1,0:T(8,128)} %rvar.5) | copy-start | bytes 442372
  20.9 4.9 %copy-start.4 = (f32[1,3,8,1536]{3,2,1,0:T(8,128)S(1)}, f32[1,3,8,1536]{3,2,1,0:T(8,128)}, u32[]{:S(2)}) copy-start(f32[1,3,8,1536]{3,2,1,0:T(8,128)} %hobs.5) | copy-start | bytes 442372

commit v11 on v10

--- a/solution.py
+++ b/solution.py
@@ -286,12 +286,12 @@
         scratch=[pltpu.VMEM(model_rhs.shape, jnp.float32)] * 5 + [pltpu.SemaphoreType.DMA((6,))],
         space=pltpu.HBM,
     )
-    came = shifted(straight, 1)
     depth_near = swapped(depth, 0)
     depth_edge = crossed(depth_near, outer, 1)
+    pair, straight, _ = lax.optimization_barrier((pair, straight, depth_near))
+    came = shifted(straight, 1)
     relayed = swapped(jnp.concatenate([came[:1], depth_edge]), 0)
-    held_pair, _ = lax.optimization_barrier((pair, depth_edge))
-    pair_near, pair_far = swapped(held_pair, 0), crossed(pair, middle)
+    pair_near, pair_far = swapped(pair, 0), crossed(pair, middle)
     known = (pair, pair_near, pair_far, came, relayed, spin, inside)
     state, back = run(first_adjoint_kernel, [fields, fields], *known)
     back = shifted(back, -1)

time: 43.2 us -> 44.3 us (1.025)
  waiting for transfers between devices: 7.68 us -> 8.55 us
    ppermute x2, waiting for transfers between devices: 3.92 us -> 7.32 us  [shifted(): lax.ppermute(value, 'win', [(source, source + step) for source in range(i...]
    ppermute x3, waiting for transfers between devices: 2.17 us -> 0.01 us  [crossed(): return lax.ppermute(value, ('win', 'band', 'half'), pairs)]
  transfers between devices with their start and end apart: 9 -> 9, of which waited for: 6 -> 3; matrix products, arithmetic and copies ran while one was open for 0% -> 0% of each run, Pallas kernels for 5% -> 8%
where the time goes in v11:
time: 44.3 us; the launch traced here: 44 us
  blocking collectives  15.9 us (36%)
  starting transfers between devices  12.2 us (28%)
  waiting for transfers between devices  8.55 us (19%)
  Pallas kernels  6.38 us (14%)
  between operations  0.84 us (2%)
    all_to_all x1, blocking collectives, body(): gathered = lax.all_to_all(sent, ('win', 'band', 'half'), 0, 0, tiled=True)  15.9 us
    ppermute x2, waiting for transfers between devices, shifted(): lax.ppermute(value, 'win', [(source, source + step) for source in range(i...  7.32 us
    pallas_call x6, Pallas kernels, run(): pl.pallas_call(kernel, out_shape=shapes, in_specs=[pl.BlockSpec(memory_sp...  6.38 us
    ppermute x2, starting transfers between devices, shifted(): lax.ppermute(value, 'win', [(source, source + step) for source in range(i...  5.85 us
    ppermute x3, starting transfers between devices, crossed(): return lax.ppermute(value, ('win', 'band', 'half'), pairs)  5.43 us
    ppermute x4, waiting for transfers between devices, swapped(): return lax.ppermute(value, ('band', 'half'), pairs)  1.22 us
  transfers between devices with their start and end apart: 9, of which 3 were waited for; matrix products, arithmetic and copies ran while one was open for 0% of the time, Pallas kernels for 8%

profile of v11, /device:TPU:0, one launch (start us, length us, event | category | flops | bytes accessed | tf_op | source)
XLA Modules:
  0.0 44.0 jit_solution(17765947005402223863)
XLA Ops:
  0.6 0.5 %collective-permute-start = (f32[1,8,1536]{2,1,0:T(8,128)}, f32[1,8,1536]{2,1,0:T(8,128)S(1)}, u32[]{:S(2)}, u32[]{:S(2)}) collective-permute-start(f32[1,8,1536]{2,1,0:T(8,128)} %depth.1), channel_id=1, source_target_pairs={{0,1},{1,0},{2,3},{3,2},{4,5},{5,4},{6,7},{7,6},{8,9},{9,8},{10,11... | collective-permute-start | bytes 147464 | tf_op jit(solution)/shard_map/ppermute | solution.py:256
  1.1 1.3 %shard_map.85 = (f32[6,8,1536]{2,1,0:T(8,128)S(1)}, f32[7,8,1536]{2,1,0:T(8,128)S(1)}) custom-call(f32[1,3,8,1536]{3,2,1,0:T(8,128)} %p.5, f32[1,3,8,1536]{3,2,1,0:T(8,128)} %m.5, f32[1,3,8,1536]{3,2,1,0:T(8,128)} %dvar.5, f32[1,3,8,1536]{3,2,1,0:T(8,128)} %rvar.5, f32[1,3,8,1536]{3,2,1,0:T(8,128)} %hobs.5, f32[1,8,1536]{2,1,0:T(8,128)} %depth.1), custom_call_target="tpu_custom_call" | custom-call | flops 5701632 | bytes 1425408 | tf_op jit(solution)/shard_map/pallas_call | solution.py:227
  2.5 0.0 collective-permute-done
  2.5 4.6 %collective-permute-start.3 = (f32[7,8,1536]{2,1,0:T(8,128)S(1)}, f32[7,8,1536]{2,1,0:T(8,128)S(1)}, u32[]{:S(2)}, u32[]{:S(2)}) collective-permute-start(f32[7,8,1536]{2,1,0:T(8,128)S(1)} %get-tuple-element.12), channel_id=1, source_target_pairs={{0,4},{4,8},{8,12},{12,16},{16,20},{20,24},{24,28},{1,5},{5,9},{9,... | collective-permute-start | bytes 1032200 | tf_op jit(solution)/shard_map/ppermute | solution.py:241
  7.0 4.1 %collective-permute-start.4 = (f32[1,8,1536]{2,1,0:T(8,128)S(1)}, f32[1,8,1536]{2,1,0:T(8,128)S(1)}, u32[]{:S(2)}, u32[]{:S(2)}) collective-permute-start(f32[1,8,1536]{2,1,0:T(8,128)S(1)} %collective-permute-done), channel_id=1, source_target_pairs={{0,7},{3,4},{4,11},{7,8},{8,15},{11,12},{12,19},{15,16},{16,23},{1... | collective-permute-start | bytes 147464 | tf_op jit(solution)/shard_map/ppermute | solution.py:266
  11.1 0.7 %collective-permute-start.2 = (f32[6,8,1536]{2,1,0:T(8,128)S(1)}, f32[6,8,1536]{2,1,0:T(8,128)S(1)}, u32[]{:S(2)}, u32[]{:S(2)}) collective-permute-start(f32[6,8,1536]{2,1,0:T(8,128)S(1)} %get-tuple-element.11.pair), channel_id=1, source_target_pairs={{1,2},{2,1},{5,6},{6,5},{9,10},{10,9},{13,14},{14,13},{17,18},{18,... | collective-permute-start | bytes 884744 | tf_op jit(solution)/shard_map/ppermute | solution.py:266
  11.8 0.1 collective-permute-start.1
  11.9 3.5 %collective-permute-done.3.straight = f32[7,8,1536]{2,1,0:T(8,128)S(1)} collective-permute-done((f32[7,8,1536]{2,1,0:T(8,128)S(1)}, f32[7,8,1536]{2,1,0:T(8,128)S(1)}, u32[]{:S(2)}, u32[]{:S(2)}) %collective-permute-start.3) | collective-permute-done | bytes 344096 | tf_op jit(solution)/shard_map/ppermute | solution.py:241
  15.4 0.0 collective-permute-done.4
  15.4 0.1 collective-permute-start.5
  15.5 0.1 multiply_select_fusion
  15.6 0.0 collective-permute-done.2.pair_far
  15.6 0.0 collective-permute-done.1.pair_near
  15.6 1.2 %collective-permute-done.5.relayed = f32[2,8,1536]{2,1,0:T(8,128)S(1)} collective-permute-done((f32[2,8,1536]{2,1,0:T(8,128)S(1)}, f32[2,8,1536]{2,1,0:T(8,128)S(1)}, u32[]{:S(2)}, u32[]{:S(2)}) %collective-permute-start.5) | collective-permute-done | bytes 98336 | tf_op jit(solution)/shard_map/ppermute | solution.py:256
  16.8 0.1 broadcast_in_dim.4.spin
  16.9 0.1 broadcast_in_dim.5.inside
  17.0 1.2 %shard_map.86 = (f32[3,8,1536]{2,1,0:T(8,128)S(1)}, f32[3,8,1536]{2,1,0:T(8,128)S(1)}) custom-call(f32[6,8,1536]{2,1,0:T(8,128)S(1)} %get-tuple-element.11.pair, f32[6,8,1536]{2,1,0:T(8,128)S(1)} %collective-permute-done.1.pair_near, f32[6,8,1536]{2,1,0:T(8,128)S(1)} %collective-permute-done.2.pair_far, f32[7,8,1536]{2,1,0:T(8,128)S(1)} %collective-permute-done.3.straight, ...), custom_call_target="tpu_custom_call" | custom-call | flops 6586368 | bytes 1646592 | tf_op jit(solution)/shard_map/pallas_call | solution.py:227
  18.1 0.2 collective-permute-start.8
  18.3 0.7 %collective-permute-start.7 = (f32[3,8,1536]{2,1,0:T(8,128)S(1)}, f32[3,8,1536]{2,1,0:T(8,128)S(1)}, u32[]{:S(2)}, u32[]{:S(2)}) collective-permute-start(f32[3,8,1536]{2,1,0:T(8,128)S(1)} %get-tuple-element.14.state), channel_id=1, source_target_pairs={{1,2},{2,1},{5,6},{6,5},{9,10},{10,9},{13,14},{14,13},{17,18},{18,... | collective-permute-start | bytes 442376 | tf_op jit(solution)/shard_map/ppermute | solution.py:266
  19.0 1.3 %collective-permute-start.6 = (f32[3,8,1536]{2,1,0:T(8,128)S(1)}, f32[3,8,1536]{2,1,0:T(8,128)S(1)}, u32[]{:S(2)}, u32[]{:S(2)}) collective-permute-start(f32[3,8,1536]{2,1,0:T(8,128)S(1)} %get-tuple-element.13), channel_id=1, source_target_pairs={{4,0},{8,4},{12,8},{16,12},{20,16},{24,20},{28,24},{5,1},{9,5},{13... | collective-permute-start | bytes 442376 | tf_op jit(solution)/shard_map/ppermute | solution.py:241
  20.3 1.2 %shard_map.88.tally = f32[2,8,128]{2,1,0:T(8,128)S(1)} custom-call(f32[6,8,1536]{2,1,0:T(8,128)S(1)} %get-tuple-element.11.pair, f32[6,8,1536]{2,1,0:T(8,128)S(1)} %collective-permute-done.1.pair_near, f32[6,8,1536]{2,1,0:T(8,128)S(1)} %collective-permute-done.2.pair_far, f32[7,8,1536]{2,1,0:T(8,128)S(1)} %collective-permute-done.3.straight, ...), custom_call_target="tpu_custom_call" | custom-call | flops 6029312 | bytes 1507328 | tf_op jit(solution)/shard_map/pallas_call | solution.py:227
  21.5 0.0 copy-start
  21.5 0.0 copy-start.1
  21.5 0.0 copy-start.2
  21.5 0.0 copy-start.3
  21.5 0.0 copy-start.4
  21.5 0.0 collective-permute-done.8.state_near
  21.6 1.1 %shard_map.87.end = f32[3,8,1536]{2,1,0:T(8,128)S(1)} custom-call(f32[3,8,1536]{2,1,0:T(8,128)S(1)} %get-tuple-element.14.state, f32[3,8,1536]{2,1,0:T(8,128)S(1)} %collective-permute-done.7.state_far, f32[3,8,1536]{2,1,0:T(8,128)S(1)} %collective-permute-done.8.state_near, f32[7,8,1536]{2,1,0:T(8,128)S(1)} %collective-permute-done.3.straight, ...), custom_call_target="tpu_custom_call" | custom-call | flops 4227072 | bytes 1056768 | tf_op jit(solution)/shard_map/pallas_call | solution.py:227
  22.7 3.8 %collective-permute-done.6.back = f32[3,8,1536]{2,1,0:T(8,128)S(1)} collective-permute-done((f32[3,8,1536]{2,1,0:T(8,128)S(1)}, f32[3,8,1536]{2,1,0:T(8,128)S(1)}, u32[]{:S(2)}, u32[]{:S(2)}) %collective-permute-start.6) | collective-permute-done | bytes 147488 | tf_op jit(solution)/shard_map/ppermute | solution.py:241
  26.5 0.4 shard_map.89
  26.9 15.9 %all_to_all.11 = f32[32,1,128]{2,1,0:T(1,128)S(1)} all-to-all(f32[32,1,128]{2,1,0:T(1,128)S(1)} %bitcast.5), channel_id=1, replica_groups=mesh['win'=8,'band'=2,'half'=2] {'win','band','half'}, dimensions={0} | all-to-all | bytes 32768 | tf_op jit(solution)/shard_map/all_to_all | solution.py:306
  42.8 1.2 %shard_map.90 = (f32[1,3,8,1536]{3,2,1,0:T(8,128)}, f32[1,3,8,1536]{3,2,1,0:T(8,128)}, f32[1,3,8,1536]{3,2,1,0:T(8,128)}) custom-call(f32[32,128]{1,0:T(8,128)S(1)} %bitcast.4, f32[1,3,8,1536]{3,2,1,0:T(8,128)S(1)} %copy-done, f32[1,3,8,1536]{3,2,1,0:T(8,128)S(1)} %copy-done.1, f32[1,3,8,1536]{3,2,1,0:T(8,128)S(1)} %copy-done.2, ...), custom_call_target="tpu_custom_call" | custom-call | flops 5373952 | bytes 1343488 | tf_op jit(solution)/shard_map/pallas_call | solution.py:227
  (9 shorter events, 0.0 us)
Async XLA Ops:
  0.6 1.8 %collective-permute-start = (f32[1,8,1536]{2,1,0:T(8,128)}, f32[1,8,1536]{2,1,0:T(8,128)S(1)}, u32[]{:S(2)}, u32[]{:S(2)}) collective-permute-start(f32[1,8,1536]{2,1,0:T(8,128)} %depth.1), channel_id=1, source_target_pairs={{0,1},{1,0},{2,3},{3,2},{4,5},{5,4},{6,7},{7,6},{8,9},{9,8},{10,11... | collective-permute-start | bytes 147464 | tf_op jit(solution)/shard_map/ppermute | solution.py:256
  2.5 13.0 %collective-permute-start.3 = (f32[7,8,1536]{2,1,0:T(8,128)S(1)}, f32[7,8,1536]{2,1,0:T(8,128)S(1)}, u32[]{:S(2)}, u32[]{:S(2)}) collective-permute-start(f32[7,8,1536]{2,1,0:T(8,128)S(1)} %get-tuple-element.12), channel_id=1, source_target_pairs={{0,4},{4,8},{8,12},{12,16},{16,20},{20,24},{24,28},{1,5},{5,9},{9,... | collective-permute-start | bytes 1032200 | tf_op jit(solution)/shard_map/ppermute | solution.py:241
  7.0 8.4 %collective-permute-start.4 = (f32[1,8,1536]{2,1,0:T(8,128)S(1)}, f32[1,8,1536]{2,1,0:T(8,128)S(1)}, u32[]{:S(2)}, u32[]{:S(2)}) collective-permute-start(f32[1,8,1536]{2,1,0:T(8,128)S(1)} %collective-permute-done), channel_id=1, source_target_pairs={{0,7},{3,4},{4,11},{7,8},{8,15},{11,12},{12,19},{15,16},{16,23},{1... | collective-permute-start | bytes 147464 | tf_op jit(solution)/shard_map/ppermute | solution.py:266
  11.1 4.4 %collective-permute-start.2 = (f32[6,8,1536]{2,1,0:T(8,128)S(1)}, f32[6,8,1536]{2,1,0:T(8,128)S(1)}, u32[]{:S(2)}, u32[]{:S(2)}) collective-permute-start(f32[6,8,1536]{2,1,0:T(8,128)S(1)} %get-tuple-element.11.pair), channel_id=1, source_target_pairs={{1,2},{2,1},{5,6},{6,5},{9,10},{10,9},{13,14},{14,13},{17,18},{18,... | collective-permute-start | bytes 884744 | tf_op jit(solution)/shard_map/ppermute | solution.py:266
  11.8 3.8 %collective-permute-start.1 = (f32[6,8,1536]{2,1,0:T(8,128)S(1)}, f32[6,8,1536]{2,1,0:T(8,128)S(1)}, u32[]{:S(2)}, u32[]{:S(2)}) collective-permute-start(f32[6,8,1536]{2,1,0:T(8,128)S(1)} %get-tuple-element.11.pair), channel_id=1, source_target_pairs={{0,1},{1,0},{2,3},{3,2},{4,5},{5,4},{6,7},{7,6},{8,9},{9,8},{10,11... | collective-permute-start | bytes 884744 | tf_op jit(solution)/shard_map/ppermute | solution.py:256
  15.4 1.4 %collective-permute-start.5 = (f32[2,8,1536]{2,1,0:T(8,128)S(1)}, f32[2,8,1536]{2,1,0:T(8,128)S(1)}, u32[]{:S(2)}, u32[]{:S(2)}) collective-permute-start(f32[2,8,1536]{2,1,0:T(8,128)S(1)} %pad_maximum_fusion), channel_id=1, source_target_pairs={{0,1},{1,0},{2,3},{3,2},{4,5},{5,4},{6,7},{7,6},{8,9},{9,8},{10,11... | collective-permute-start | bytes 294920 | tf_op jit(solution)/shard_map/ppermute | solution.py:256
  18.1 3.4 %collective-permute-start.8 = (f32[3,8,1536]{2,1,0:T(8,128)S(1)}, f32[3,8,1536]{2,1,0:T(8,128)S(1)}, u32[]{:S(2)}, u32[]{:S(2)}) collective-permute-start(f32[3,8,1536]{2,1,0:T(8,128)S(1)} %get-tuple-element.14.state), channel_id=1, source_target_pairs={{0,1},{1,0},{2,3},{3,2},{4,5},{5,4},{6,7},{7,6},{8,9},{9,8},{10,11... | collective-permute-start | bytes 442376 | tf_op jit(solution)/shard_map/ppermute | solution.py:256
  18.3 3.2 %collective-permute-start.7 = (f32[3,8,1536]{2,1,0:T(8,128)S(1)}, f32[3,8,1536]{2,1,0:T(8,128)S(1)}, u32[]{:S(2)}, u32[]{:S(2)}) collective-permute-start(f32[3,8,1536]{2,1,0:T(8,128)S(1)} %get-tuple-element.14.state), channel_id=1, source_target_pairs={{1,2},{2,1},{5,6},{6,5},{9,10},{10,9},{13,14},{14,13},{17,18},{18,... | collective-permute-start | bytes 442376 | tf_op jit(solution)/shard_map/ppermute | solution.py:266
  19.0 7.5 %collective-permute-start.6 = (f32[3,8,1536]{2,1,0:T(8,128)S(1)}, f32[3,8,1536]{2,1,0:T(8,128)S(1)}, u32[]{:S(2)}, u32[]{:S(2)}) collective-permute-start(f32[3,8,1536]{2,1,0:T(8,128)S(1)} %get-tuple-element.13), channel_id=1, source_target_pairs={{4,0},{8,4},{12,8},{16,12},{20,16},{24,20},{28,24},{5,1},{9,5},{13... | collective-permute-start | bytes 442376 | tf_op jit(solution)/shard_map/ppermute | solution.py:241
  21.5 5.0 %copy-start = (f32[1,3,8,1536]{3,2,1,0:T(8,128)S(1)}, f32[1,3,8,1536]{3,2,1,0:T(8,128)}, u32[]{:S(2)}) copy-start(f32[1,3,8,1536]{3,2,1,0:T(8,128)} %p.5) | copy-start | bytes 442372
  21.5 5.0 %copy-start.1 = (f32[1,3,8,1536]{3,2,1,0:T(8,128)S(1)}, f32[1,3,8,1536]{3,2,1,0:T(8,128)}, u32[]{:S(2)}) copy-start(f32[1,3,8,1536]{3,2,1,0:T(8,128)} %m.5) | copy-start | bytes 442372
  21.5 5.0 %copy-start.2 = (f32[1,3,8,1536]{3,2,1,0:T(8,128)S(1)}, f32[1,3,8,1536]{3,2,1,0:T(8,128)}, u32[]{:S(2)}) copy-start(f32[1,3,8,1536]{3,2,1,0:T(8,128)} %dvar.5) | copy-start | bytes 442372
  21.5 5.0 %copy-start.3 = (f32[1,3,8,1536]{3,2,1,0:T(8,128)S(1)}, f32[1,3,8,1536]{3,2,1,0:T(8,128)}, u32[]{:S(2)}) copy-start(f32[1,3,8,1536]{3,2,1,0:T(8,128)} %rvar.5) | copy-start | bytes 442372
  21.5 5.0 %copy-start.4 = (f32[1,3,8,1536]{3,2,1,0:T(8,128)S(1)}, f32[1,3,8,1536]{3,2,1,0:T(8,128)}, u32[]{:S(2)}) copy-start(f32[1,3,8,1536]{3,2,1,0:T(8,128)} %hobs.5) | copy-start | bytes 442372

commit v12 on v9

--- a/solution.py
+++ b/solution.py
@@ -102,7 +102,7 @@
     tally[1] = square
 
 
-def forward_kernel(state, state_near, state_far, straight, relayed, spin, inside, end):
+def forward_kernel(state, state_far, state_near, straight, relayed, spin, inside, end):
     depth = stretched(straight, relayed)
     turn, keep = widened(spin, depth.shape[1]), widened(inside, depth.shape[1])
     height, east, north = [stacked(state, state_near, state_far, part) for part in range(3)]
@@ -231,7 +231,7 @@
         out_specs=[pl.BlockSpec(memory_space=pltpu.VMEM)] * len(shapes),
         scratch_shapes=scratch,
         compiler_params=pltpu.CompilerParams(vmem_limit_bytes=32 * 1024 * 1024),
-        cost_estimate=pl.CostEstimate(flops=work * size, bytes_accessed=size, transcendentals=0),
+        cost_estimate=pl.CostEstimate(flops=work * size // 4, bytes_accessed=work * size // 4, transcendentals=0),
     )(*operands)
 
 
@@ -286,20 +286,21 @@
         scratch=[pltpu.VMEM(model_rhs.shape, jnp.float32)] * 5 + [pltpu.SemaphoreType.DMA((6,))],
         space=pltpu.HBM,
     )
-    came = shifted(straight, 1)
     depth_near = swapped(depth, 0)
     depth_edge = crossed(depth_near, outer, 1)
+    pair, straight, local, _ = lax.optimization_barrier((pair, straight, local, depth_near))
+    came = shifted(straight, 1)
     relayed = swapped(jnp.concatenate([came[:1], depth_edge]), 0)
-    local, _ = lax.optimization_barrier((local, depth_near))
+    pair_near, pair_far = swapped(pair, 0), crossed(pair, middle)
+    known = (pair, pair_near, pair_far, came, relayed, spin, inside)
     local = shifted(local, 1)
-    held_pair, _ = lax.optimization_barrier((pair, depth_edge))
-    pair_near, pair_far = swapped(held_pair, 0), crossed(pair, middle)
-    known = (pair, pair_near, pair_far, came, relayed, spin, inside)
-    state, back = run(first_adjoint_kernel, [fields, fields], *known)
+    state, back = run(first_adjoint_kernel, [fields, fields], *known, work=4)
+    state, back, local = lax.optimization_barrier((state, back, local))
     back = shifted(back, -1)
-    state_near, state_far = swapped(state, 0), crossed(state, middle)
+    state_far = crossed(state, middle)
     (tally,) = run(second_adjoint_kernel, [(2, rows, 128)], *known, local, state)
-    (end,) = run(forward_kernel, [fields], state, state_near, state_far, came, relayed, spin, inside)
+    state_near = swapped(state, 0)
+    (end,) = run(forward_kernel, [fields], state, state_far, state_near, came, relayed, spin, inside)
     (sent,) = run(
         inner_kernel, [(ranks, 128)],
         model_rhs, obs_rhs, model_var, obs_var, obs_weight, back, end, tally,

time: 45.4 us -> 44.2 us (0.974)
  starting transfers between devices: 18.9 us -> 15.6 us
  blocking collectives: 11.9 us -> 14.6 us
  waiting for transfers between devices: 6.85 us -> 6.36 us
    all_to_all x1, blocking collectives: 11.9 us -> 14.6 us  [body(): gathered = lax.all_to_all(sent, ('win', 'band', 'half'), 0, 0, tiled=True)]
    ppermute x4, starting transfers between devices: 3.22 us -> 0.86 us  [swapped(): return lax.ppermute(value, ('band', 'half'), pairs)]
    ppermute x3, waiting for transfers between devices: 2.17 us -> 0.01 us  [crossed(): return lax.ppermute(value, ('win', 'band', 'half'), pairs)]
    ppermute x3, waiting for transfers between devices: 4.15 us -> 5.3 us  [shifted(): lax.ppermute(value, 'win', [(source, source + step) for source in range(i...]
    ppermute x3, starting transfers between devices: 10.2 us -> 9.27 us  [shifted(): lax.ppermute(value, 'win', [(source, source + step) for source in range(i...]
    ppermute x4, waiting for transfers between devices: 0.53 us -> 1.06 us  [swapped(): return lax.ppermute(value, ('band', 'half'), pairs)]
  transfers between devices with their start and end apart: 10 -> 10, of which waited for: 3 -> 3; matrix products, arithmetic and copies ran while one was open for 0% -> 0% of each run, Pallas kernels for 8% -> 11%
where the time goes in v12:
time: 44.2 us; the launch traced here: 44 us
  starting transfers between devices  15.6 us (35%)
  blocking collectives  14.6 us (33%)
  Pallas kernels  6.37 us (14%)
  waiting for transfers between devices  6.36 us (14%)
  between operations  0.85 us (2%)
    all_to_all x1, blocking collectives, body(): gathered = lax.all_to_all(sent, ('win', 'band', 'half'), 0, 0, tiled=True)  14.6 us
    ppermute x3, starting transfers between devices, shifted(): lax.ppermute(value, 'win', [(source, source + step) for source in range(i...  9.27 us
    pallas_call x6, Pallas kernels, run(): pl.pallas_call(kernel, out_shape=shapes, in_specs=[pl.BlockSpec(memory_sp...  6.37 us
    ppermute x3, starting transfers between devices, crossed(): return lax.ppermute(value, ('win', 'band', 'half'), pairs)  5.44 us
    ppermute x3, waiting for transfers between devices, shifted(): lax.ppermute(value, 'win', [(source, source + step) for source in range(i...  5.3 us
    ppermute x4, waiting for transfers between devices, swapped(): return lax.ppermute(value, ('band', 'half'), pairs)  1.06 us
  transfers between devices with their start and end apart: 10, of which 3 were waited for; matrix products, arithmetic and copies ran while one was open for 0% of the time, Pallas kernels for 11%

profile of v12, /device:TPU:0, one launch (start us, length us, event | category | flops | bytes accessed | tf_op | source)
XLA Modules:
  0.0 44.0 jit_solution(3235627547566382617)
XLA Ops:
  0.6 0.5 %collective-permute-start = (f32[1,8,1536]{2,1,0:T(8,128)}, f32[1,8,1536]{2,1,0:T(8,128)S(1)}, u32[]{:S(2)}, u32[]{:S(2)}) collective-permute-start(f32[1,8,1536]{2,1,0:T(8,128)} %depth.1), channel_id=1, source_target_pairs={{0,1},{1,0},{2,3},{3,2},{4,5},{5,4},{6,7},{7,6},{8,9},{9,8},{10,11... | collective-permute-start | bytes 147464 | tf_op jit(solution)/shard_map/ppermute | solution.py:256
  1.1 1.3 %shard_map.85 = (f32[6,8,1536]{2,1,0:T(8,128)S(1)}, f32[4,8,1536]{2,1,0:T(8,128)S(1)}, f32[3,8,1536]{2,1,0:T(8,128)S(1)}) custom-call(f32[1,3,8,1536]{3,2,1,0:T(8,128)} %p.5, f32[1,3,8,1536]{3,2,1,0:T(8,128)} %m.5, f32[1,3,8,1536]{3,2,1,0:T(8,128)} %dvar.5, f32[1,3,8,1536]{3,2,1,0:T(8,128)} %rvar.5, f32[1,3,8,1536]{3,2,1,0:T(8,128)} %hobs.5, f32[1,8,1536]{2,1,0:T(8,128)} %depth.1), custom_call_target="tpu_custom_call" | custom-call | flops 1425408 | bytes 1425408 | tf_op jit(solution)/shard_map/pallas_call | solution.py:227
  2.5 0.0 collective-permute-done
  2.5 4.5 %collective-permute-start.3 = (f32[4,8,1536]{2,1,0:T(8,128)S(1)}, f32[4,8,1536]{2,1,0:T(8,128)S(1)}, u32[]{:S(2)}, u32[]{:S(2)}) collective-permute-start(f32[4,8,1536]{2,1,0:T(8,128)S(1)} %get-tuple-element.18), channel_id=1, source_target_pairs={{0,4},{4,8},{8,12},{12,16},{16,20},{20,24},{24,28},{1,5},{5,9},{9,... | collective-permute-start | bytes 589832 | tf_op jit(solution)/shard_map/ppermute | solution.py:241
  7.0 4.1 %collective-permute-start.4 = (f32[1,8,1536]{2,1,0:T(8,128)S(1)}, f32[1,8,1536]{2,1,0:T(8,128)S(1)}, u32[]{:S(2)}, u32[]{:S(2)}) collective-permute-start(f32[1,8,1536]{2,1,0:T(8,128)S(1)} %collective-permute-done), channel_id=1, source_target_pairs={{0,7},{3,4},{4,11},{7,8},{8,15},{11,12},{12,19},{15,16},{16,23},{1... | collective-permute-start | bytes 147464 | tf_op jit(solution)/shard_map/ppermute | solution.py:266
  11.1 0.7 %collective-permute-start.2 = (f32[6,8,1536]{2,1,0:T(8,128)S(1)}, f32[6,8,1536]{2,1,0:T(8,128)S(1)}, u32[]{:S(2)}, u32[]{:S(2)}) collective-permute-start(f32[6,8,1536]{2,1,0:T(8,128)S(1)} %get-tuple-element.17.pair), channel_id=1, source_target_pairs={{1,2},{2,1},{5,6},{6,5},{9,10},{10,9},{13,14},{14,13},{17,18},{18,... | collective-permute-start | bytes 884744 | tf_op jit(solution)/shard_map/ppermute | solution.py:266
  11.8 0.1 collective-permute-start.1
  11.9 3.4 %collective-permute-start.6 = (f32[3,8,1536]{2,1,0:T(8,128)S(1)}, f32[3,8,1536]{2,1,0:T(8,128)S(1)}, u32[]{:S(2)}, u32[]{:S(2)}) collective-permute-start(f32[3,8,1536]{2,1,0:T(8,128)S(1)} %get-tuple-element.21), channel_id=1, source_target_pairs={{0,4},{4,8},{8,12},{12,16},{16,20},{20,24},{24,28},{1,5},{5,9},{9,... | collective-permute-start | bytes 442376 | tf_op jit(solution)/shard_map/ppermute | solution.py:241
  15.4 0.0 collective-permute-done.3.straight
  15.4 0.0 collective-permute-done.4
  15.4 0.3 collective-permute-start.5
  15.7 1.0 %collective-permute-done.5.relayed = f32[2,8,1536]{2,1,0:T(8,128)S(1)} collective-permute-done((f32[2,8,1536]{2,1,0:T(8,128)S(1)}, f32[2,8,1536]{2,1,0:T(8,128)S(1)}, u32[]{:S(2)}, u32[]{:S(2)}) %collective-permute-start.5) | collective-permute-done | bytes 98336 | tf_op jit(solution)/shard_map/ppermute | solution.py:256
  16.8 0.1 broadcast_in_dim.4.spin
  16.8 0.1 broadcast_in_dim.5.inside
  16.9 1.1 %shard_map.86 = (f32[3,8,1536]{2,1,0:T(8,128)S(1)}, f32[3,8,1536]{2,1,0:T(8,128)S(1)}) custom-call(f32[6,8,1536]{2,1,0:T(8,128)S(1)} %get-tuple-element.17.pair, f32[6,8,1536]{2,1,0:T(8,128)S(1)} %collective-permute-done.1.pair_near, f32[6,8,1536]{2,1,0:T(8,128)S(1)} %collective-permute-done.2.pair_far, f32[4,8,1536]{2,1,0:T(8,128)S(1)} %collective-permute-done.3.straight, ...), custom_call_target="tpu_custom_call" | custom-call | flops 1499136 | bytes 1499136 | tf_op jit(solution)/shard_map/pallas_call | solution.py:227
  18.1 1.0 %collective-permute-done.6.local = f32[3,8,1536]{2,1,0:T(8,128)S(1)} collective-permute-done((f32[3,8,1536]{2,1,0:T(8,128)S(1)}, f32[3,8,1536]{2,1,0:T(8,128)S(1)}, u32[]{:S(2)}, u32[]{:S(2)}) %collective-permute-start.6) | collective-permute-done | bytes 147488 | tf_op jit(solution)/shard_map/ppermute | solution.py:241
  19.1 0.0 collective-permute-start.9
  19.1 0.7 %collective-permute-start.8 = (f32[3,8,1536]{2,1,0:T(8,128)S(1)}, f32[3,8,1536]{2,1,0:T(8,128)S(1)}, u32[]{:S(2)}, u32[]{:S(2)}) collective-permute-start(f32[3,8,1536]{2,1,0:T(8,128)S(1)} %get-tuple-element.23.state), channel_id=1, source_target_pairs={{1,2},{2,1},{5,6},{6,5},{9,10},{10,9},{13,14},{14,13},{17,18},{18,... | collective-permute-start | bytes 442376 | tf_op jit(solution)/shard_map/ppermute | solution.py:266
  19.8 1.3 %collective-permute-start.7 = (f32[3,8,1536]{2,1,0:T(8,128)S(1)}, f32[3,8,1536]{2,1,0:T(8,128)S(1)}, u32[]{:S(2)}, u32[]{:S(2)}) collective-permute-start(f32[3,8,1536]{2,1,0:T(8,128)S(1)} %get-tuple-element.22), channel_id=1, source_target_pairs={{4,0},{8,4},{12,8},{16,12},{20,16},{24,20},{28,24},{5,1},{9,5},{13... | collective-permute-start | bytes 442376 | tf_op jit(solution)/shard_map/ppermute | solution.py:241
  21.1 1.2 %shard_map.88.tally = f32[2,8,128]{2,1,0:T(8,128)S(1)} custom-call(f32[6,8,1536]{2,1,0:T(8,128)S(1)} %get-tuple-element.17.pair, f32[6,8,1536]{2,1,0:T(8,128)S(1)} %collective-permute-done.1.pair_near, f32[6,8,1536]{2,1,0:T(8,128)S(1)} %collective-permute-done.2.pair_far, f32[4,8,1536]{2,1,0:T(8,128)S(1)} %collective-permute-done.3.straight, ...), custom_call_target="tpu_custom_call" | custom-call | flops 1507328 | bytes 1507328 | tf_op jit(solution)/shard_map/pallas_call | solution.py:227
  22.2 0.0 copy-start
  22.2 0.0 copy-start.1
  22.2 0.0 copy-start.2
  22.3 0.0 copy-start.3
  22.3 0.0 copy-start.4
  22.3 0.0 collective-permute-done.9.state_near
  22.3 0.0 collective-permute-done.8.state_far
  22.3 1.1 %shard_map.87.end = f32[3,8,1536]{2,1,0:T(8,128)S(1)} custom-call(f32[3,8,1536]{2,1,0:T(8,128)S(1)} %get-tuple-element.23.state, f32[3,8,1536]{2,1,0:T(8,128)S(1)} %collective-permute-done.8.state_far, f32[3,8,1536]{2,1,0:T(8,128)S(1)} %collective-permute-done.9.state_near, f32[4,8,1536]{2,1,0:T(8,128)S(1)} %collective-permute-done.3.straight, ...), custom_call_target="tpu_custom_call" | custom-call | flops 909312 | bytes 909312 | tf_op jit(solution)/shard_map/pallas_call | solution.py:227
  23.5 4.3 %collective-permute-done.7.back = f32[3,8,1536]{2,1,0:T(8,128)S(1)} collective-permute-done((f32[3,8,1536]{2,1,0:T(8,128)S(1)}, f32[3,8,1536]{2,1,0:T(8,128)S(1)}, u32[]{:S(2)}, u32[]{:S(2)}) %collective-permute-start.7) | collective-permute-done | bytes 147488 | tf_op jit(solution)/shard_map/ppermute | solution.py:241
  27.8 0.4 shard_map.89
  28.2 14.6 %all_to_all.11 = f32[32,1,128]{2,1,0:T(1,128)S(1)} all-to-all(f32[32,1,128]{2,1,0:T(1,128)S(1)} %bitcast.5), channel_id=1, replica_groups=mesh['win'=8,'band'=2,'half'=2] {'win','band','half'}, dimensions={0} | all-to-all | bytes 32768 | tf_op jit(solution)/shard_map/all_to_all | solution.py:308
  42.7 1.2 %shard_map.90 = (f32[1,3,8,1536]{3,2,1,0:T(8,128)}, f32[1,3,8,1536]{3,2,1,0:T(8,128)}, f32[1,3,8,1536]{3,2,1,0:T(8,128)}) custom-call(f32[32,128]{1,0:T(8,128)S(1)} %bitcast.4, f32[1,3,8,1536]{3,2,1,0:T(8,128)S(1)} %copy-done, f32[1,3,8,1536]{3,2,1,0:T(8,128)S(1)} %copy-done.1, f32[1,3,8,1536]{3,2,1,0:T(8,128)S(1)} %copy-done.2, ...), custom_call_target="tpu_custom_call" | custom-call | flops 1343488 | bytes 1343488 | tf_op jit(solution)/shard_map/pallas_call | solution.py:227
  (11 shorter events, 0.1 us)
Async XLA Ops:
  0.6 1.8 %collective-permute-start = (f32[1,8,1536]{2,1,0:T(8,128)}, f32[1,8,1536]{2,1,0:T(8,128)S(1)}, u32[]{:S(2)}, u32[]{:S(2)}) collective-permute-start(f32[1,8,1536]{2,1,0:T(8,128)} %depth.1), channel_id=1, source_target_pairs={{0,1},{1,0},{2,3},{3,2},{4,5},{5,4},{6,7},{7,6},{8,9},{9,8},{10,11... | collective-permute-start | bytes 147464 | tf_op jit(solution)/shard_map/ppermute | solution.py:256
  2.5 12.9 %collective-permute-start.3 = (f32[4,8,1536]{2,1,0:T(8,128)S(1)}, f32[4,8,1536]{2,1,0:T(8,128)S(1)}, u32[]{:S(2)}, u32[]{:S(2)}) collective-permute-start(f32[4,8,1536]{2,1,0:T(8,128)S(1)} %get-tuple-element.18), channel_id=1, source_target_pairs={{0,4},{4,8},{8,12},{12,16},{16,20},{20,24},{24,28},{1,5},{5,9},{9,... | collective-permute-start | bytes 589832 | tf_op jit(solution)/shard_map/ppermute | solution.py:241
  7.0 8.4 %collective-permute-start.4 = (f32[1,8,1536]{2,1,0:T(8,128)S(1)}, f32[1,8,1536]{2,1,0:T(8,128)S(1)}, u32[]{:S(2)}, u32[]{:S(2)}) collective-permute-start(f32[1,8,1536]{2,1,0:T(8,128)S(1)} %collective-permute-done), channel_id=1, source_target_pairs={{0,7},{3,4},{4,11},{7,8},{8,15},{11,12},{12,19},{15,16},{16,23},{1... | collective-permute-start | bytes 147464 | tf_op jit(solution)/shard_map/ppermute | solution.py:266
  11.1 5.6 %collective-permute-start.2 = (f32[6,8,1536]{2,1,0:T(8,128)S(1)}, f32[6,8,1536]{2,1,0:T(8,128)S(1)}, u32[]{:S(2)}, u32[]{:S(2)}) collective-permute-start(f32[6,8,1536]{2,1,0:T(8,128)S(1)} %get-tuple-element.17.pair), channel_id=1, source_target_pairs={{1,2},{2,1},{5,6},{6,5},{9,10},{10,9},{13,14},{14,13},{17,18},{18,... | collective-permute-start | bytes 884744 | tf_op jit(solution)/shard_map/ppermute | solution.py:266
  11.8 4.9 %collective-permute-start.1 = (f32[6,8,1536]{2,1,0:T(8,128)S(1)}, f32[6,8,1536]{2,1,0:T(8,128)S(1)}, u32[]{:S(2)}, u32[]{:S(2)}) collective-permute-start(f32[6,8,1536]{2,1,0:T(8,128)S(1)} %get-tuple-element.17.pair), channel_id=1, source_target_pairs={{0,1},{1,0},{2,3},{3,2},{4,5},{5,4},{6,7},{7,6},{8,9},{9,8},{10,11... | collective-permute-start | bytes 884744 | tf_op jit(solution)/shard_map/ppermute | solution.py:256
  11.9 7.2 %collective-permute-start.6 = (f32[3,8,1536]{2,1,0:T(8,128)S(1)}, f32[3,8,1536]{2,1,0:T(8,128)S(1)}, u32[]{:S(2)}, u32[]{:S(2)}) collective-permute-start(f32[3,8,1536]{2,1,0:T(8,128)S(1)} %get-tuple-element.21), channel_id=1, source_target_pairs={{0,4},{4,8},{8,12},{12,16},{16,20},{20,24},{24,28},{1,5},{5,9},{9,... | collective-permute-start | bytes 442376 | tf_op jit(solution)/shard_map/ppermute | solution.py:241
  15.4 1.4 %collective-permute-start.5 = (f32[2,8,1536]{2,1,0:T(8,128)S(1)}, f32[2,8,1536]{2,1,0:T(8,128)S(1)}, u32[]{:S(2)}, u32[]{:S(2)}) collective-permute-start(f32[2,8,1536]{2,1,0:T(8,128)S(1)} %pad_maximum_fusion), channel_id=1, source_target_pairs={{0,1},{1,0},{2,3},{3,2},{4,5},{5,4},{6,7},{7,6},{8,9},{9,8},{10,11... | collective-permute-start | bytes 294920 | tf_op jit(solution)/shard_map/ppermute | solution.py:256
  19.1 3.2 %collective-permute-start.9 = (f32[3,8,1536]{2,1,0:T(8,128)S(1)}, f32[3,8,1536]{2,1,0:T(8,128)S(1)}, u32[]{:S(2)}, u32[]{:S(2)}) collective-permute-start(f32[3,8,1536]{2,1,0:T(8,128)S(1)} %get-tuple-element.23.state), channel_id=1, source_target_pairs={{0,1},{1,0},{2,3},{3,2},{4,5},{5,4},{6,7},{7,6},{8,9},{9,8},{10,11... | collective-permute-start | bytes 442376 | tf_op jit(solution)/shard_map/ppermute | solution.py:256
  19.1 3.2 %collective-permute-start.8 = (f32[3,8,1536]{2,1,0:T(8,128)S(1)}, f32[3,8,1536]{2,1,0:T(8,128)S(1)}, u32[]{:S(2)}, u32[]{:S(2)}) collective-permute-start(f32[3,8,1536]{2,1,0:T(8,128)S(1)} %get-tuple-element.23.state), channel_id=1, source_target_pairs={{1,2},{2,1},{5,6},{6,5},{9,10},{10,9},{13,14},{14,13},{17,18},{18,... | collective-permute-start | bytes 442376 | tf_op jit(solution)/shard_map/ppermute | solution.py:266
  19.8 8.0 %collective-permute-start.7 = (f32[3,8,1536]{2,1,0:T(8,128)S(1)}, f32[3,8,1536]{2,1,0:T(8,128)S(1)}, u32[]{:S(2)}, u32[]{:S(2)}) collective-permute-start(f32[3,8,1536]{2,1,0:T(8,128)S(1)} %get-tuple-element.22), channel_id=1, source_target_pairs={{4,0},{8,4},{12,8},{16,12},{20,16},{24,20},{28,24},{5,1},{9,5},{13... | collective-permute-start | bytes 442376 | tf_op jit(solution)/shard_map/ppermute | solution.py:241
  22.2 5.5 %copy-start = (f32[1,3,8,1536]{3,2,1,0:T(8,128)S(1)}, f32[1,3,8,1536]{3,2,1,0:T(8,128)}, u32[]{:S(2)}) copy-start(f32[1,3,8,1536]{3,2,1,0:T(8,128)} %p.5) | copy-start | bytes 442372
  22.2 5.5 %copy-start.1 = (f32[1,3,8,1536]{3,2,1,0:T(8,128)S(1)}, f32[1,3,8,1536]{3,2,1,0:T(8,128)}, u32[]{:S(2)}) copy-start(f32[1,3,8,1536]{3,2,1,0:T(8,128)} %m.5) | copy-start | bytes 442372
  22.2 5.5 %copy-start.2 = (f32[1,3,8,1536]{3,2,1,0:T(8,128)S(1)}, f32[1,3,8,1536]{3,2,1,0:T(8,128)}, u32[]{:S(2)}) copy-start(f32[1,3,8,1536]{3,2,1,0:T(8,128)} %dvar.5) | copy-start | bytes 442372
  22.3 5.5 %copy-start.3 = (f32[1,3,8,1536]{3,2,1,0:T(8,128)S(1)}, f32[1,3,8,1536]{3,2,1,0:T(8,128)}, u32[]{:S(2)}) copy-start(f32[1,3,8,1536]{3,2,1,0:T(8,128)} %rvar.5) | copy-start | bytes 442372
  22.3 5.5 %copy-start.4 = (f32[1,3,8,1536]{3,2,1,0:T(8,128)S(1)}, f32[1,3,8,1536]{3,2,1,0:T(8,128)}, u32[]{:S(2)}) copy-start(f32[1,3,8,1536]{3,2,1,0:T(8,128)} %hobs.5) | copy-start | bytes 442372

commit v13 on v12

--- a/solution.py
+++ b/solution.py
@@ -295,7 +295,7 @@
     known = (pair, pair_near, pair_far, came, relayed, spin, inside)
     local = shifted(local, 1)
     state, back = run(first_adjoint_kernel, [fields, fields], *known, work=4)
-    state, back, local = lax.optimization_barrier((state, back, local))
+    back, local = lax.optimization_barrier((back, local))
     back = shifted(back, -1)
     state_far = crossed(state, middle)
     (tally,) = run(second_adjoint_kernel, [(2, rows, 128)], *known, local, state)

time: 44.2 us -> 42.1 us (0.952)
  blocking collectives: 14.6 us -> 12.7 us
  waiting for transfers between devices: 6.36 us -> 5.87 us
    all_to_all x1, blocking collectives: 14.6 us -> 12.7 us  [body(): gathered = lax.all_to_all(sent, ('win', 'band', 'half'), 0, 0, tiled=True)]
    ppermute x3, waiting for transfers between devices: 5.3 us -> 4.81 us  [shifted(): lax.ppermute(value, 'win', [(source, source + step) for source in range(i...]
where the time goes in v13:
time: 42.1 us; the launch traced here: 41.9 us
  starting transfers between devices  15.8 us (38%)
  blocking collectives  12.7 us (30%)
  Pallas kernels  6.37 us (15%)
  waiting for transfers between devices  5.87 us (14%)
  between operations  0.85 us (2%)
    all_to_all x1, blocking collectives, body(): gathered = lax.all_to_all(sent, ('win', 'band', 'half'), 0, 0, tiled=True)  12.7 us
    ppermute x3, starting transfers between devices, shifted(): lax.ppermute(value, 'win', [(source, source + step) for source in range(i...  9.26 us
    pallas_call x6, Pallas kernels, run(): pl.pallas_call(kernel, out_shape=shapes, in_specs=[pl.BlockSpec(memory_sp...  6.37 us
    ppermute x3, starting transfers between devices, crossed(): return lax.ppermute(value, ('win', 'band', 'half'), pairs)  5.44 us
    ppermute x3, waiting for transfers between devices, shifted(): lax.ppermute(value, 'win', [(source, source + step) for source in range(i...  4.81 us
    ppermute x4, starting transfers between devices, swapped(): return lax.ppermute(value, ('band', 'half'), pairs)  1.13 us
    ppermute x4, waiting for transfers between devices, swapped(): return lax.ppermute(value, ('band', 'half'), pairs)  1.06 us
  transfers between devices with their start and end apart: 10, of which 3 were waited for; matrix products, arithmetic and copies ran while one was open for 0% of the time, Pallas kernels for 11%

profile of v13, /device:TPU:0, one launch (start us, length us, event | category | flops | bytes accessed | tf_op | source)
XLA Modules:
  0.0 41.9 jit_solution(14150733725664269771)
XLA Ops:
  0.6 0.5 %collective-permute-start = (f32[1,8,1536]{2,1,0:T(8,128)}, f32[1,8,1536]{2,1,0:T(8,128)S(1)}, u32[]{:S(2)}, u32[]{:S(2)}) collective-permute-start(f32[1,8,1536]{2,1,0:T(8,128)} %depth.1), channel_id=1, source_target_pairs={{0,1},{1,0},{2,3},{3,2},{4,5},{5,4},{6,7},{7,6},{8,9},{9,8},{10,11... | collective-permute-start | bytes 147464 | tf_op jit(solution)/shard_map/ppermute | solution.py:256
  1.1 1.3 %shard_map.85 = (f32[6,8,1536]{2,1,0:T(8,128)S(1)}, f32[4,8,1536]{2,1,0:T(8,128)S(1)}, f32[3,8,1536]{2,1,0:T(8,128)S(1)}) custom-call(f32[1,3,8,1536]{3,2,1,0:T(8,128)} %p.5, f32[1,3,8,1536]{3,2,1,0:T(8,128)} %m.5, f32[1,3,8,1536]{3,2,1,0:T(8,128)} %dvar.5, f32[1,3,8,1536]{3,2,1,0:T(8,128)} %rvar.5, f32[1,3,8,1536]{3,2,1,0:T(8,128)} %hobs.5, f32[1,8,1536]{2,1,0:T(8,128)} %depth.1), custom_call_target="tpu_custom_call" | custom-call | flops 1425408 | bytes 1425408 | tf_op jit(solution)/shard_map/pallas_call | solution.py:227
  2.5 0.0 collective-permute-done
  2.5 4.5 %collective-permute-start.3 = (f32[4,8,1536]{2,1,0:T(8,128)S(1)}, f32[4,8,1536]{2,1,0:T(8,128)S(1)}, u32[]{:S(2)}, u32[]{:S(2)}) collective-permute-start(f32[4,8,1536]{2,1,0:T(8,128)S(1)} %get-tuple-element.17), channel_id=1, source_target_pairs={{0,4},{4,8},{8,12},{12,16},{16,20},{20,24},{24,28},{1,5},{5,9},{9,... | collective-permute-start | bytes 589832 | tf_op jit(solution)/shard_map/ppermute | solution.py:241
  7.0 4.1 %collective-permute-start.4 = (f32[1,8,1536]{2,1,0:T(8,128)S(1)}, f32[1,8,1536]{2,1,0:T(8,128)S(1)}, u32[]{:S(2)}, u32[]{:S(2)}) collective-permute-start(f32[1,8,1536]{2,1,0:T(8,128)S(1)} %collective-permute-done), channel_id=1, source_target_pairs={{0,7},{3,4},{4,11},{7,8},{8,15},{11,12},{12,19},{15,16},{16,23},{1... | collective-permute-start | bytes 147464 | tf_op jit(solution)/shard_map/ppermute | solution.py:266
  11.1 0.7 %collective-permute-start.2 = (f32[6,8,1536]{2,1,0:T(8,128)S(1)}, f32[6,8,1536]{2,1,0:T(8,128)S(1)}, u32[]{:S(2)}, u32[]{:S(2)}) collective-permute-start(f32[6,8,1536]{2,1,0:T(8,128)S(1)} %get-tuple-element.16.pair), channel_id=1, source_target_pairs={{1,2},{2,1},{5,6},{6,5},{9,10},{10,9},{13,14},{14,13},{17,18},{18,... | collective-permute-start | bytes 884744 | tf_op jit(solution)/shard_map/ppermute | solution.py:266
  11.8 0.1 collective-permute-start.1
  11.9 3.4 %collective-permute-start.6 = (f32[3,8,1536]{2,1,0:T(8,128)S(1)}, f32[3,8,1536]{2,1,0:T(8,128)S(1)}, u32[]{:S(2)}, u32[]{:S(2)}) collective-permute-start(f32[3,8,1536]{2,1,0:T(8,128)S(1)} %get-tuple-element.19), channel_id=1, source_target_pairs={{0,4},{4,8},{8,12},{12,16},{16,20},{20,24},{24,28},{1,5},{5,9},{9,... | collective-permute-start | bytes 442376 | tf_op jit(solution)/shard_map/ppermute | solution.py:241
  15.4 0.0 collective-permute-done.3.straight
  15.4 0.0 collective-permute-done.4
  15.4 0.3 collective-permute-start.5
  15.7 1.0 %collective-permute-done.5.relayed = f32[2,8,1536]{2,1,0:T(8,128)S(1)} collective-permute-done((f32[2,8,1536]{2,1,0:T(8,128)S(1)}, f32[2,8,1536]{2,1,0:T(8,128)S(1)}, u32[]{:S(2)}, u32[]{:S(2)}) %collective-permute-start.5) | collective-permute-done | bytes 98336 | tf_op jit(solution)/shard_map/ppermute | solution.py:256
  16.8 0.0 collective-permute-done.2.pair_far
  16.8 0.1 broadcast_in_dim.4.spin
  16.8 0.1 broadcast_in_dim.5.inside
  16.9 1.1 %shard_map.86 = (f32[3,8,1536]{2,1,0:T(8,128)S(1)}, f32[3,8,1536]{2,1,0:T(8,128)S(1)}) custom-call(f32[6,8,1536]{2,1,0:T(8,128)S(1)} %get-tuple-element.16.pair, f32[6,8,1536]{2,1,0:T(8,128)S(1)} %collective-permute-done.1.pair_near, f32[6,8,1536]{2,1,0:T(8,128)S(1)} %collective-permute-done.2.pair_far, f32[4,8,1536]{2,1,0:T(8,128)S(1)} %collective-permute-done.3.straight, ...), custom_call_target="tpu_custom_call" | custom-call | flops 1499136 | bytes 1499136 | tf_op jit(solution)/shard_map/pallas_call | solution.py:227
  18.1 0.3 collective-permute-start.9
  18.3 0.7 %collective-permute-start.8 = (f32[3,8,1536]{2,1,0:T(8,128)S(1)}, f32[3,8,1536]{2,1,0:T(8,128)S(1)}, u32[]{:S(2)}, u32[]{:S(2)}) collective-permute-start(f32[3,8,1536]{2,1,0:T(8,128)S(1)} %get-tuple-element.21.state), channel_id=1, source_target_pairs={{1,2},{2,1},{5,6},{6,5},{9,10},{10,9},{13,14},{14,13},{17,18},{18,... | collective-permute-start | bytes 442376 | tf_op jit(solution)/shard_map/ppermute | solution.py:266
  19.0 0.1 collective-permute-done.6.local
  19.1 1.3 %collective-permute-start.7 = (f32[3,8,1536]{2,1,0:T(8,128)S(1)}, f32[3,8,1536]{2,1,0:T(8,128)S(1)}, u32[]{:S(2)}, u32[]{:S(2)}) collective-permute-start(f32[3,8,1536]{2,1,0:T(8,128)S(1)} %get-tuple-element.20), channel_id=1, source_target_pairs={{4,0},{8,4},{12,8},{16,12},{20,16},{24,20},{28,24},{5,1},{9,5},{13... | collective-permute-start | bytes 442376 | tf_op jit(solution)/shard_map/ppermute | solution.py:241
  20.4 1.2 %shard_map.88.tally = f32[2,8,128]{2,1,0:T(8,128)S(1)} custom-call(f32[6,8,1536]{2,1,0:T(8,128)S(1)} %get-tuple-element.16.pair, f32[6,8,1536]{2,1,0:T(8,128)S(1)} %collective-permute-done.1.pair_near, f32[6,8,1536]{2,1,0:T(8,128)S(1)} %collective-permute-done.2.pair_far, f32[4,8,1536]{2,1,0:T(8,128)S(1)} %collective-permute-done.3.straight, ...), custom_call_target="tpu_custom_call" | custom-call | flops 1507328 | bytes 1507328 | tf_op jit(solution)/shard_map/pallas_call | solution.py:227
  21.5 0.0 copy-start
  21.6 0.0 copy-start.1
  21.6 0.0 copy-start.2
  21.6 0.0 copy-start.3
  21.6 0.0 copy-start.4
  21.6 0.0 collective-permute-done.9.state_near
  21.6 1.1 %shard_map.87.end = f32[3,8,1536]{2,1,0:T(8,128)S(1)} custom-call(f32[3,8,1536]{2,1,0:T(8,128)S(1)} %get-tuple-element.21.state, f32[3,8,1536]{2,1,0:T(8,128)S(1)} %collective-permute-done.8.state_far, f32[3,8,1536]{2,1,0:T(8,128)S(1)} %collective-permute-done.9.state_near, f32[4,8,1536]{2,1,0:T(8,128)S(1)} %collective-permute-done.3.straight, ...), custom_call_target="tpu_custom_call" | custom-call | flops 909312 | bytes 909312 | tf_op jit(solution)/shard_map/pallas_call | solution.py:227
  22.8 4.7 %collective-permute-done.7.back = f32[3,8,1536]{2,1,0:T(8,128)S(1)} collective-permute-done((f32[3,8,1536]{2,1,0:T(8,128)S(1)}, f32[3,8,1536]{2,1,0:T(8,128)S(1)}, u32[]{:S(2)}, u32[]{:S(2)}) %collective-permute-start.7) | collective-permute-done | bytes 147488 | tf_op jit(solution)/shard_map/ppermute | solution.py:241
  27.5 0.4 shard_map.89
  27.9 12.7 %all_to_all.11 = f32[32,1,128]{2,1,0:T(1,128)S(1)} all-to-all(f32[32,1,128]{2,1,0:T(1,128)S(1)} %bitcast.5), channel_id=1, replica_groups=mesh['win'=8,'band'=2,'half'=2] {'win','band','half'}, dimensions={0} | all-to-all | bytes 32768 | tf_op jit(solution)/shard_map/all_to_all | solution.py:308
  40.6 1.2 %shard_map.90 = (f32[1,3,8,1536]{3,2,1,0:T(8,128)}, f32[1,3,8,1536]{3,2,1,0:T(8,128)}, f32[1,3,8,1536]{3,2,1,0:T(8,128)}) custom-call(f32[32,128]{1,0:T(8,128)S(1)} %bitcast.4, f32[1,3,8,1536]{3,2,1,0:T(8,128)S(1)} %copy-done, f32[1,3,8,1536]{3,2,1,0:T(8,128)S(1)} %copy-done.1, f32[1,3,8,1536]{3,2,1,0:T(8,128)S(1)} %copy-done.2, ...), custom_call_target="tpu_custom_call" | custom-call | flops 1343488 | bytes 1343488 | tf_op jit(solution)/shard_map/pallas_call | solution.py:227
  (11 shorter events, 0.1 us)
Async XLA Ops:
  0.6 1.8 %collective-permute-start = (f32[1,8,1536]{2,1,0:T(8,128)}, f32[1,8,1536]{2,1,0:T(8,128)S(1)}, u32[]{:S(2)}, u32[]{:S(2)}) collective-permute-start(f32[1,8,1536]{2,1,0:T(8,128)} %depth.1), channel_id=1, source_target_pairs={{0,1},{1,0},{2,3},{3,2},{4,5},{5,4},{6,7},{7,6},{8,9},{9,8},{10,11... | collective-permute-start | bytes 147464 | tf_op jit(solution)/shard_map/ppermute | solution.py:256
  2.5 12.9 %collective-permute-start.3 = (f32[4,8,1536]{2,1,0:T(8,128)S(1)}, f32[4,8,1536]{2,1,0:T(8,128)S(1)}, u32[]{:S(2)}, u32[]{:S(2)}) collective-permute-start(f32[4,8,1536]{2,1,0:T(8,128)S(1)} %get-tuple-element.17), channel_id=1, source_target_pairs={{0,4},{4,8},{8,12},{12,16},{16,20},{20,24},{24,28},{1,5},{5,9},{9,... | collective-permute-start | bytes 589832 | tf_op jit(solution)/shard_map/ppermute | solution.py:241
  7.0 8.4 %collective-permute-start.4 = (f32[1,8,1536]{2,1,0:T(8,128)S(1)}, f32[1,8,1536]{2,1,0:T(8,128)S(1)}, u32[]{:S(2)}, u32[]{:S(2)}) collective-permute-start(f32[1,8,1536]{2,1,0:T(8,128)S(1)} %collective-permute-done), channel_id=1, source_target_pairs={{0,7},{3,4},{4,11},{7,8},{8,15},{11,12},{12,19},{15,16},{16,23},{1... | collective-permute-start | bytes 147464 | tf_op jit(solution)/shard_map/ppermute | solution.py:266
  11.1 5.6 %collective-permute-start.2 = (f32[6,8,1536]{2,1,0:T(8,128)S(1)}, f32[6,8,1536]{2,1,0:T(8,128)S(1)}, u32[]{:S(2)}, u32[]{:S(2)}) collective-permute-start(f32[6,8,1536]{2,1,0:T(8,128)S(1)} %get-tuple-element.16.pair), channel_id=1, source_target_pairs={{1,2},{2,1},{5,6},{6,5},{9,10},{10,9},{13,14},{14,13},{17,18},{18,... | collective-permute-start | bytes 884744 | tf_op jit(solution)/shard_map/ppermute | solution.py:266
  11.8 4.9 %collective-permute-start.1 = (f32[6,8,1536]{2,1,0:T(8,128)S(1)}, f32[6,8,1536]{2,1,0:T(8,128)S(1)}, u32[]{:S(2)}, u32[]{:S(2)}) collective-permute-start(f32[6,8,1536]{2,1,0:T(8,128)S(1)} %get-tuple-element.16.pair), channel_id=1, source_target_pairs={{0,1},{1,0},{2,3},{3,2},{4,5},{5,4},{6,7},{7,6},{8,9},{9,8},{10,11... | collective-permute-start | bytes 884744 | tf_op jit(solution)/shard_map/ppermute | solution.py:256
  11.9 7.2 %collective-permute-start.6 = (f32[3,8,1536]{2,1,0:T(8,128)S(1)}, f32[3,8,1536]{2,1,0:T(8,128)S(1)}, u32[]{:S(2)}, u32[]{:S(2)}) collective-permute-start(f32[3,8,1536]{2,1,0:T(8,128)S(1)} %get-tuple-element.19), channel_id=1, source_target_pairs={{0,4},{4,8},{8,12},{12,16},{16,20},{20,24},{24,28},{1,5},{5,9},{9,... | collective-permute-start | bytes 442376 | tf_op jit(solution)/shard_map/ppermute | solution.py:241
  15.4 1.4 %collective-permute-start.5 = (f32[2,8,1536]{2,1,0:T(8,128)S(1)}, f32[2,8,1536]{2,1,0:T(8,128)S(1)}, u32[]{:S(2)}, u32[]{:S(2)}) collective-permute-start(f32[2,8,1536]{2,1,0:T(8,128)S(1)} %pad_maximum_fusion), channel_id=1, source_target_pairs={{0,1},{1,0},{2,3},{3,2},{4,5},{5,4},{6,7},{7,6},{8,9},{9,8},{10,11... | collective-permute-start | bytes 294920 | tf_op jit(solution)/shard_map/ppermute | solution.py:256
  18.1 3.5 %collective-permute-start.9 = (f32[3,8,1536]{2,1,0:T(8,128)S(1)}, f32[3,8,1536]{2,1,0:T(8,128)S(1)}, u32[]{:S(2)}, u32[]{:S(2)}) collective-permute-start(f32[3,8,1536]{2,1,0:T(8,128)S(1)} %get-tuple-element.21.state), channel_id=1, source_target_pairs={{0,1},{1,0},{2,3},{3,2},{4,5},{5,4},{6,7},{7,6},{8,9},{9,8},{10,11... | collective-permute-start | bytes 442376 | tf_op jit(solution)/shard_map/ppermute | solution.py:256
  18.3 3.3 %collective-permute-start.8 = (f32[3,8,1536]{2,1,0:T(8,128)S(1)}, f32[3,8,1536]{2,1,0:T(8,128)S(1)}, u32[]{:S(2)}, u32[]{:S(2)}) collective-permute-start(f32[3,8,1536]{2,1,0:T(8,128)S(1)} %get-tuple-element.21.state), channel_id=1, source_target_pairs={{1,2},{2,1},{5,6},{6,5},{9,10},{10,9},{13,14},{14,13},{17,18},{18,... | collective-permute-start | bytes 442376 | tf_op jit(solution)/shard_map/ppermute | solution.py:266
  19.1 8.4 %collective-permute-start.7 = (f32[3,8,1536]{2,1,0:T(8,128)S(1)}, f32[3,8,1536]{2,1,0:T(8,128)S(1)}, u32[]{:S(2)}, u32[]{:S(2)}) collective-permute-start(f32[3,8,1536]{2,1,0:T(8,128)S(1)} %get-tuple-element.20), channel_id=1, source_target_pairs={{4,0},{8,4},{12,8},{16,12},{20,16},{24,20},{28,24},{5,1},{9,5},{13... | collective-permute-start | bytes 442376 | tf_op jit(solution)/shard_map/ppermute | solution.py:241
  21.5 6.0 %copy-start = (f32[1,3,8,1536]{3,2,1,0:T(8,128)S(1)}, f32[1,3,8,1536]{3,2,1,0:T(8,128)}, u32[]{:S(2)}) copy-start(f32[1,3,8,1536]{3,2,1,0:T(8,128)} %p.5) | copy-start | bytes 442372
  21.6 6.0 %copy-start.1 = (f32[1,3,8,1536]{3,2,1,0:T(8,128)S(1)}, f32[1,3,8,1536]{3,2,1,0:T(8,128)}, u32[]{:S(2)}) copy-start(f32[1,3,8,1536]{3,2,1,0:T(8,128)} %m.5) | copy-start | bytes 442372
  21.6 6.0 %copy-start.2 = (f32[1,3,8,1536]{3,2,1,0:T(8,128)S(1)}, f32[1,3,8,1536]{3,2,1,0:T(8,128)}, u32[]{:S(2)}) copy-start(f32[1,3,8,1536]{3,2,1,0:T(8,128)} %dvar.5) | copy-start | bytes 442372
  21.6 5.9 %copy-start.3 = (f32[1,3,8,1536]{3,2,1,0:T(8,128)S(1)}, f32[1,3,8,1536]{3,2,1,0:T(8,128)}, u32[]{:S(2)}) copy-start(f32[1,3,8,1536]{3,2,1,0:T(8,128)} %rvar.5) | copy-start | bytes 442372
  21.6 5.9 %copy-start.4 = (f32[1,3,8,1536]{3,2,1,0:T(8,128)S(1)}, f32[1,3,8,1536]{3,2,1,0:T(8,128)}, u32[]{:S(2)}) copy-start(f32[1,3,8,1536]{3,2,1,0:T(8,128)} %hobs.5) | copy-start | bytes 442372

commit v14 on v13

--- a/solution.py
+++ b/solution.py
@@ -102,7 +102,34 @@
     tally[1] = square
 
 
-def forward_kernel(state, state_far, state_near, straight, relayed, spin, inside, end):
+def lane_sum(value):
+    rows, width = value.shape
+    total = value[:, :128]
+    for start in range(128, width, 128):
+        total = total + value[:, start:start + 128]
+    return total
+
+
+def home_kernel(p, m, dvar, rvar, hobs, tally, back, lead, sums):
+    last = lax.axis_index("win") == lax.axis_size("win") - 1
+    moments = [0.0, 0.0, 2.0 * tally[0], tally[1]]
+    for part in range(3):
+        dv, rv, hv = dvar[0, part], rvar[0, part], hobs[0, part]
+        pv, mv = p[0, part], m[0, part]
+        up, um = dv * pv, rv * mv
+        ux = pv - back[part] + hv * mv
+        lead[part] = dv * up + ux
+        zm = rv * um + hv * ux
+        zx = jnp.where(last, up + hv * um, 0.0)
+        moments[0] += lane_sum(up * pv + um * mv)
+        moments[1] += lane_sum(up * up + um * um + ux * ux)
+        moments[2] += lane_sum(dv * up * up + rv * um * um + 2.0 * (zx * ux))
+        moments[3] += lane_sum(zm * zm + zx * zx)
+    for row, value in enumerate(moments):
+        sums[row] = value
+
+
+def closing_kernel(state_far, state_near, straight, relayed, spin, inside, state, lead, sums, sent):
     depth = stretched(straight, relayed)
     turn, keep = widened(spin, depth.shape[1]), widened(inside, depth.shape[1])
     height, east, north = [stacked(state, state_near, state_far, part) for part in range(3)]
@@ -111,33 +138,11 @@
         east = east + turn * north - 0.25 * lon_gap(height)
         north = north - turn * east - 0.25 * lat_gap(height)
     rows = state.shape[1]
+    square = 0.0
     for part, value in enumerate((height, east, north)):
-        end[part] = value[rows:2 * rows]
-
-
-def lane_sum(value):
-    rows, width = value.shape
-    total = value[:, :128]
-    for start in range(128, width, 128):
-        total = total + value[:, start:start + 128]
-    return total
-
-
-def inner_kernel(p, m, dvar, rvar, hobs, back, end, tally, sent):
-    last = lax.axis_index("win") == lax.axis_size("win") - 1
-    moments = [0.0, 0.0, 2.0 * tally[0], tally[1]]
-    for part in range(3):
-        dv, rv, hv = dvar[0, part], rvar[0, part], hobs[0, part]
-        pv, mv = p[0, part], m[0, part]
-        up, um = dv * pv, rv * mv
-        ux = pv - back[part] + hv * mv
-        zp = dv * up + ux - end[part]
-        zm = rv * um + hv * ux
-        zx = jnp.where(last, up + hv * um, 0.0)
-        moments[0] += lane_sum(up * pv + um * mv)
-        moments[1] += lane_sum(up * up + um * um + ux * ux)
-        moments[2] += lane_sum(dv * up * up + rv * um * um + 2.0 * (zx * ux))
-        moments[3] += lane_sum(zp * zp + zm * zm + zx * zx)
+        zp = lead[part] - value[rows:2 * rows]
+        square += lane_sum(zp * zp)
+    moments = [sums[0], sums[1], sums[2], sums[3] + square]
     lane = lax.broadcasted_iota(jnp.int32, (1, 128), 1)
     row = 0.0
     for slot, value in enumerate(moments):
@@ -295,16 +300,16 @@
     known = (pair, pair_near, pair_far, came, relayed, spin, inside)
     local = shifted(local, 1)
     state, back = run(first_adjoint_kernel, [fields, fields], *known, work=4)
-    back, local = lax.optimization_barrier((back, local))
+    held_state, local = lax.optimization_barrier((state, local))
     back = shifted(back, -1)
-    state_far = crossed(state, middle)
+    state_far = crossed(held_state, middle)
     (tally,) = run(second_adjoint_kernel, [(2, rows, 128)], *known, local, state)
     state_near = swapped(state, 0)
-    (end,) = run(forward_kernel, [fields], state, state_far, state_near, came, relayed, spin, inside)
-    (sent,) = run(
-        inner_kernel, [(ranks, 128)],
-        model_rhs, obs_rhs, model_var, obs_var, obs_weight, back, end, tally,
+    lead, sums = run(
+        home_kernel, [fields, (4, rows, 128)],
+        model_rhs, obs_rhs, model_var, obs_var, obs_weight, tally, back,
     )
+    (sent,) = run(closing_kernel, [(ranks, 128)], state_far, state_near, came, relayed, spin, inside, state, lead, sums)
     gathered = lax.all_to_all(sent, ("win", "band", "half"), 0, 0, tiled=True)
     return run(
         combine_kernel, [model_rhs.shape] * 3,

time: 42.1 us -> 42.1 us (level)
  waiting for transfers between devices: 5.87 us -> 3.16 us
  starting transfers between devices: 15.8 us -> 18.1 us
  blocking collectives: 12.7 us -> 13.2 us
    ppermute x3, waiting for transfers between devices: 4.81 us -> 2.1 us  [shifted(): lax.ppermute(value, 'win', [(source, source + step) for source in range(i...]
    ppermute x4, starting transfers between devices: 1.13 us -> 3.27 us  [swapped(): return lax.ppermute(value, ('band', 'half'), pairs)]
    all_to_all x1, blocking collectives: 12.7 us -> 13.2 us  [body(): gathered = lax.all_to_all(sent, ('win', 'band', 'half'), 0, 0, tiled=True)]
  transfers between devices with their start and end apart: 10 -> 10, of which waited for: 3 -> 2; matrix products, arithmetic and copies ran while one was open for 0% -> 0% of each run, Pallas kernels for 11% -> 9%
where the time goes in v14:
time: 42.1 us; the launch traced here: 41.8 us
  starting transfers between devices  18.1 us (43%)
  blocking collectives  13.2 us (31%)
  Pallas kernels  6.21 us (15%)
  waiting for transfers between devices  3.16 us (8%)
  between operations  0.86 us (2%)
    all_to_all x1, blocking collectives, body(): gathered = lax.all_to_all(sent, ('win', 'band', 'half'), 0, 0, tiled=True)  13.2 us
    ppermute x3, starting transfers between devices, shifted(): lax.ppermute(value, 'win', [(source, source + step) for source in range(i...  9.27 us
    pallas_call x6, Pallas kernels, run(): pl.pallas_call(kernel, out_shape=shapes, in_specs=[pl.BlockSpec(memory_sp...  6.21 us
    ppermute x3, starting transfers between devices, crossed(): return lax.ppermute(value, ('win', 'band', 'half'), pairs)  5.58 us
    ppermute x4, starting transfers between devices, swapped(): return lax.ppermute(value, ('band', 'half'), pairs)  3.27 us
    ppermute x3, waiting for transfers between devices, shifted(): lax.ppermute(value, 'win', [(source, source + step) for source in range(i...  2.1 us
    ppermute x4, waiting for transfers between devices, swapped(): return lax.ppermute(value, ('band', 'half'), pairs)  1.06 us
  transfers between devices with their start and end apart: 10, of which 2 were waited for; matrix products, arithmetic and copies ran while one was open for 0% of the time, Pallas kernels for 9%

profile of v14, /device:TPU:0, one launch (start us, length us, event | category | flops | bytes accessed | tf_op | source)
XLA Modules:
  0.0 41.8 jit_solution(17938017169826854804)
XLA Ops:
  0.6 0.5 %collective-permute-start = (f32[1,8,1536]{2,1,0:T(8,128)}, f32[1,8,1536]{2,1,0:T(8,128)S(1)}, u32[]{:S(2)}, u32[]{:S(2)}) collective-permute-start(f32[1,8,1536]{2,1,0:T(8,128)} %depth.1), channel_id=1, source_target_pairs={{0,1},{1,0},{2,3},{3,2},{4,5},{5,4},{6,7},{7,6},{8,9},{9,8},{10,11... | collective-permute-start | bytes 147464 | tf_op jit(solution)/shard_map/ppermute | solution.py:261
  1.1 1.3 %shard_map.85 = (f32[6,8,1536]{2,1,0:T(8,128)S(1)}, f32[4,8,1536]{2,1,0:T(8,128)S(1)}, f32[3,8,1536]{2,1,0:T(8,128)S(1)}) custom-call(f32[1,3,8,1536]{3,2,1,0:T(8,128)} %p.5, f32[1,3,8,1536]{3,2,1,0:T(8,128)} %m.5, f32[1,3,8,1536]{3,2,1,0:T(8,128)} %dvar.5, f32[1,3,8,1536]{3,2,1,0:T(8,128)} %rvar.5, f32[1,3,8,1536]{3,2,1,0:T(8,128)} %hobs.5, f32[1,8,1536]{2,1,0:T(8,128)} %depth.1), custom_call_target="tpu_custom_call" | custom-call | flops 1425408 | bytes 1425408 | tf_op jit(solution)/shard_map/pallas_call | solution.py:232
  2.5 0.0 collective-permute-done
  2.5 4.5 %collective-permute-start.3 = (f32[4,8,1536]{2,1,0:T(8,128)S(1)}, f32[4,8,1536]{2,1,0:T(8,128)S(1)}, u32[]{:S(2)}, u32[]{:S(2)}) collective-permute-start(f32[4,8,1536]{2,1,0:T(8,128)S(1)} %get-tuple-element.19), channel_id=1, source_target_pairs={{0,4},{4,8},{8,12},{12,16},{16,20},{20,24},{24,28},{1,5},{5,9},{9,... | collective-permute-start | bytes 589832 | tf_op jit(solution)/shard_map/ppermute | solution.py:246
  7.0 4.1 %collective-permute-start.4 = (f32[1,8,1536]{2,1,0:T(8,128)S(1)}, f32[1,8,1536]{2,1,0:T(8,128)S(1)}, u32[]{:S(2)}, u32[]{:S(2)}) collective-permute-start(f32[1,8,1536]{2,1,0:T(8,128)S(1)} %collective-permute-done), channel_id=1, source_target_pairs={{0,7},{3,4},{4,11},{7,8},{8,15},{11,12},{12,19},{15,16},{16,23},{1... | collective-permute-start | bytes 147464 | tf_op jit(solution)/shard_map/ppermute | solution.py:271
  11.1 0.7 %collective-permute-start.2 = (f32[6,8,1536]{2,1,0:T(8,128)S(1)}, f32[6,8,1536]{2,1,0:T(8,128)S(1)}, u32[]{:S(2)}, u32[]{:S(2)}) collective-permute-start(f32[6,8,1536]{2,1,0:T(8,128)S(1)} %get-tuple-element.18.pair), channel_id=1, source_target_pairs={{1,2},{2,1},{5,6},{6,5},{9,10},{10,9},{13,14},{14,13},{17,18},{18,... | collective-permute-start | bytes 884744 | tf_op jit(solution)/shard_map/ppermute | solution.py:271
  11.8 0.1 collective-permute-start.1
  11.9 3.4 %collective-permute-start.6 = (f32[3,8,1536]{2,1,0:T(8,128)S(1)}, f32[3,8,1536]{2,1,0:T(8,128)S(1)}, u32[]{:S(2)}, u32[]{:S(2)}) collective-permute-start(f32[3,8,1536]{2,1,0:T(8,128)S(1)} %get-tuple-element.21), channel_id=1, source_target_pairs={{0,4},{4,8},{8,12},{12,16},{16,20},{20,24},{24,28},{1,5},{5,9},{9,... | collective-permute-start | bytes 442376 | tf_op jit(solution)/shard_map/ppermute | solution.py:246
  15.4 0.0 collective-permute-done.3.straight
  15.4 0.0 collective-permute-done.4
  15.4 0.3 collective-permute-start.5
  15.7 1.0 %collective-permute-done.5.relayed = f32[2,8,1536]{2,1,0:T(8,128)S(1)} collective-permute-done((f32[2,8,1536]{2,1,0:T(8,128)S(1)}, f32[2,8,1536]{2,1,0:T(8,128)S(1)}, u32[]{:S(2)}, u32[]{:S(2)}) %collective-permute-start.5) | collective-permute-done | bytes 98336 | tf_op jit(solution)/shard_map/ppermute | solution.py:261
  16.8 0.0 collective-permute-done.2.pair_far
  16.8 0.1 broadcast_in_dim.4.spin
  16.8 0.1 broadcast_in_dim.5.inside
  16.9 1.2 %shard_map.86 = (f32[3,8,1536]{2,1,0:T(8,128)S(1)}, f32[3,8,1536]{2,1,0:T(8,128)S(1)}) custom-call(f32[6,8,1536]{2,1,0:T(8,128)S(1)} %get-tuple-element.18.pair, f32[6,8,1536]{2,1,0:T(8,128)S(1)} %collective-permute-done.1.pair_near, f32[6,8,1536]{2,1,0:T(8,128)S(1)} %collective-permute-done.2.pair_far, f32[4,8,1536]{2,1,0:T(8,128)S(1)} %collective-permute-done.3.straight, ...), custom_call_target="tpu_custom_call" | custom-call | flops 1499136 | bytes 1499136 | tf_op jit(solution)/shard_map/pallas_call | solution.py:232
  18.1 1.3 %collective-permute-start.9 = (f32[3,8,1536]{2,1,0:T(8,128)S(1)}, f32[3,8,1536]{2,1,0:T(8,128)S(1)}, u32[]{:S(2)}, u32[]{:S(2)}) collective-permute-start(f32[3,8,1536]{2,1,0:T(8,128)S(1)} %get-tuple-element.24), channel_id=1, source_target_pairs={{4,0},{8,4},{12,8},{16,12},{20,16},{24,20},{28,24},{5,1},{9,5},{13... | collective-permute-start | bytes 442376 | tf_op jit(solution)/shard_map/ppermute | solution.py:246
  19.4 0.0 collective-permute-done.6.local
  19.4 0.0 copy-start
  19.4 0.0 copy-start.1
  19.4 0.0 copy-start.2
  19.4 0.0 copy-start.3
  19.4 0.0 copy-start.4
  19.5 0.8 %collective-permute-start.7 = (f32[3,8,1536]{2,1,0:T(8,128)S(1)}, f32[3,8,1536]{2,1,0:T(8,128)S(1)}, u32[]{:S(2)}, u32[]{:S(2)}) collective-permute-start(f32[3,8,1536]{2,1,0:T(8,128)S(1)} %get-tuple-element.22.state), channel_id=1, source_target_pairs={{1,2},{2,1},{5,6},{6,5},{9,10},{10,9},{13,14},{14,13},{17,18},{18,... | collective-permute-start | bytes 442376 | tf_op jit(solution)/shard_map/ppermute | solution.py:271
  20.3 2.4 %collective-permute-start.8 = (f32[3,8,1536]{2,1,0:T(8,128)S(1)}, f32[3,8,1536]{2,1,0:T(8,128)S(1)}, u32[]{:S(2)}, u32[]{:S(2)}) collective-permute-start(f32[3,8,1536]{2,1,0:T(8,128)S(1)} %get-tuple-element.22.state), channel_id=1, source_target_pairs={{0,1},{1,0},{2,3},{3,2},{4,5},{5,4},{6,7},{7,6},{8,9},{9,8},{10,11... | collective-permute-start | bytes 442376 | tf_op jit(solution)/shard_map/ppermute | solution.py:261
  22.7 1.2 %shard_map.87.tally = f32[2,8,128]{2,1,0:T(8,128)S(1)} custom-call(f32[6,8,1536]{2,1,0:T(8,128)S(1)} %get-tuple-element.18.pair, f32[6,8,1536]{2,1,0:T(8,128)S(1)} %collective-permute-done.1.pair_near, f32[6,8,1536]{2,1,0:T(8,128)S(1)} %collective-permute-done.2.pair_far, f32[4,8,1536]{2,1,0:T(8,128)S(1)} %collective-permute-done.3.straight, ...), custom_call_target="tpu_custom_call" | custom-call | flops 1507328 | bytes 1507328 | tf_op jit(solution)/shard_map/pallas_call | solution.py:232
  23.8 2.1 %collective-permute-done.9.back = f32[3,8,1536]{2,1,0:T(8,128)S(1)} collective-permute-done((f32[3,8,1536]{2,1,0:T(8,128)S(1)}, f32[3,8,1536]{2,1,0:T(8,128)S(1)}, u32[]{:S(2)}, u32[]{:S(2)}) %collective-permute-start.9) | collective-permute-done | bytes 147488 | tf_op jit(solution)/shard_map/ppermute | solution.py:246
  26.0 0.2 shard_map.88
  26.1 0.0 collective-permute-done.7.state_far
  26.2 1.2 %shard_map.89 = f32[32,128]{1,0:T(8,128)S(1)} custom-call(f32[3,8,1536]{2,1,0:T(8,128)S(1)} %collective-permute-done.7.state_far, f32[3,8,1536]{2,1,0:T(8,128)S(1)} %collective-permute-done.8.state_near, f32[4,8,1536]{2,1,0:T(8,128)S(1)} %collective-permute-done.3.straight, f32[2,8,1536]{2,1,0:T(8,128)S(1)} %collective-permute-done.5.relayed, ...), custom_call_target="tpu_custom_call" | custom-call | flops 942080 | bytes 942080 | tf_op jit(solution)/shard_map/pallas_call | solution.py:232
  27.4 13.2 %all_to_all.11 = f32[32,1,128]{2,1,0:T(1,128)S(1)} all-to-all(f32[32,1,128]{2,1,0:T(1,128)S(1)} %bitcast.4), channel_id=1, replica_groups=mesh['win'=8,'band'=2,'half'=2] {'win','band','half'}, dimensions={0} | all-to-all | bytes 32768 | tf_op jit(solution)/shard_map/all_to_all | solution.py:313
  40.6 1.2 %shard_map.90 = (f32[1,3,8,1536]{3,2,1,0:T(8,128)}, f32[1,3,8,1536]{3,2,1,0:T(8,128)}, f32[1,3,8,1536]{3,2,1,0:T(8,128)}) custom-call(f32[32,128]{1,0:T(8,128)S(1)} %bitcast.5, f32[1,3,8,1536]{3,2,1,0:T(8,128)S(1)} %copy-done, f32[1,3,8,1536]{3,2,1,0:T(8,128)S(1)} %copy-done.1, f32[1,3,8,1536]{3,2,1,0:T(8,128)S(1)} %copy-done.2, ...), custom_call_target="tpu_custom_call" | custom-call | flops 1343488 | bytes 1343488 | tf_op jit(solution)/shard_map/pallas_call | solution.py:232
  (11 shorter events, 0.1 us)
Async XLA Ops:
  0.6 1.8 %collective-permute-start = (f32[1,8,1536]{2,1,0:T(8,128)}, f32[1,8,1536]{2,1,0:T(8,128)S(1)}, u32[]{:S(2)}, u32[]{:S(2)}) collective-permute-start(f32[1,8,1536]{2,1,0:T(8,128)} %depth.1), channel_id=1, source_target_pairs={{0,1},{1,0},{2,3},{3,2},{4,5},{5,4},{6,7},{7,6},{8,9},{9,8},{10,11... | collective-permute-start | bytes 147464 | tf_op jit(solution)/shard_map/ppermute | solution.py:261
  2.5 12.9 %collective-permute-start.3 = (f32[4,8,1536]{2,1,0:T(8,128)S(1)}, f32[4,8,1536]{2,1,0:T(8,128)S(1)}, u32[]{:S(2)}, u32[]{:S(2)}) collective-permute-start(f32[4,8,1536]{2,1,0:T(8,128)S(1)} %get-tuple-element.19), channel_id=1, source_target_pairs={{0,4},{4,8},{8,12},{12,16},{16,20},{20,24},{24,28},{1,5},{5,9},{9,... | collective-permute-start | bytes 589832 | tf_op jit(solution)/shard_map/ppermute | solution.py:246
  7.0 8.4 %collective-permute-start.4 = (f32[1,8,1536]{2,1,0:T(8,128)S(1)}, f32[1,8,1536]{2,1,0:T(8,128)S(1)}, u32[]{:S(2)}, u32[]{:S(2)}) collective-permute-start(f32[1,8,1536]{2,1,0:T(8,128)S(1)} %collective-permute-done), channel_id=1, source_target_pairs={{0,7},{3,4},{4,11},{7,8},{8,15},{11,12},{12,19},{15,16},{16,23},{1... | collective-permute-start | bytes 147464 | tf_op jit(solution)/shard_map/ppermute | solution.py:271
  11.1 5.6 %collective-permute-start.2 = (f32[6,8,1536]{2,1,0:T(8,128)S(1)}, f32[6,8,1536]{2,1,0:T(8,128)S(1)}, u32[]{:S(2)}, u32[]{:S(2)}) collective-permute-start(f32[6,8,1536]{2,1,0:T(8,128)S(1)} %get-tuple-element.18.pair), channel_id=1, source_target_pairs={{1,2},{2,1},{5,6},{6,5},{9,10},{10,9},{13,14},{14,13},{17,18},{18,... | collective-permute-start | bytes 884744 | tf_op jit(solution)/shard_map/ppermute | solution.py:271
  11.8 4.9 %collective-permute-start.1 = (f32[6,8,1536]{2,1,0:T(8,128)S(1)}, f32[6,8,1536]{2,1,0:T(8,128)S(1)}, u32[]{:S(2)}, u32[]{:S(2)}) collective-permute-start(f32[6,8,1536]{2,1,0:T(8,128)S(1)} %get-tuple-element.18.pair), channel_id=1, source_target_pairs={{0,1},{1,0},{2,3},{3,2},{4,5},{5,4},{6,7},{7,6},{8,9},{9,8},{10,11... | collective-permute-start | bytes 884744 | tf_op jit(solution)/shard_map/ppermute | solution.py:261
  11.9 7.5 %collective-permute-start.6 = (f32[3,8,1536]{2,1,0:T(8,128)S(1)}, f32[3,8,1536]{2,1,0:T(8,128)S(1)}, u32[]{:S(2)}, u32[]{:S(2)}) collective-permute-start(f32[3,8,1536]{2,1,0:T(8,128)S(1)} %get-tuple-element.21), channel_id=1, source_target_pairs={{0,4},{4,8},{8,12},{12,16},{16,20},{20,24},{24,28},{1,5},{5,9},{9,... | collective-permute-start | bytes 442376 | tf_op jit(solution)/shard_map/ppermute | solution.py:246
  15.4 1.4 %collective-permute-start.5 = (f32[2,8,1536]{2,1,0:T(8,128)S(1)}, f32[2,8,1536]{2,1,0:T(8,128)S(1)}, u32[]{:S(2)}, u32[]{:S(2)}) collective-permute-start(f32[2,8,1536]{2,1,0:T(8,128)S(1)} %pad_maximum_fusion), channel_id=1, source_target_pairs={{0,1},{1,0},{2,3},{3,2},{4,5},{5,4},{6,7},{7,6},{8,9},{9,8},{10,11... | collective-permute-start | bytes 294920 | tf_op jit(solution)/shard_map/ppermute | solution.py:261
  18.1 7.9 %collective-permute-start.9 = (f32[3,8,1536]{2,1,0:T(8,128)S(1)}, f32[3,8,1536]{2,1,0:T(8,128)S(1)}, u32[]{:S(2)}, u32[]{:S(2)}) collective-permute-start(f32[3,8,1536]{2,1,0:T(8,128)S(1)} %get-tuple-element.24), channel_id=1, source_target_pairs={{4,0},{8,4},{12,8},{16,12},{20,16},{24,20},{28,24},{5,1},{9,5},{13... | collective-permute-start | bytes 442376 | tf_op jit(solution)/shard_map/ppermute | solution.py:246
  19.4 6.5 %copy-start = (f32[1,3,8,1536]{3,2,1,0:T(8,128)S(1)}, f32[1,3,8,1536]{3,2,1,0:T(8,128)}, u32[]{:S(2)}) copy-start(f32[1,3,8,1536]{3,2,1,0:T(8,128)} %p.5) | copy-start | bytes 442372
  19.4 6.5 %copy-start.1 = (f32[1,3,8,1536]{3,2,1,0:T(8,128)S(1)}, f32[1,3,8,1536]{3,2,1,0:T(8,128)}, u32[]{:S(2)}) copy-start(f32[1,3,8,1536]{3,2,1,0:T(8,128)} %m.5) | copy-start | bytes 442372
  19.4 6.5 %copy-start.2 = (f32[1,3,8,1536]{3,2,1,0:T(8,128)S(1)}, f32[1,3,8,1536]{3,2,1,0:T(8,128)}, u32[]{:S(2)}) copy-start(f32[1,3,8,1536]{3,2,1,0:T(8,128)} %dvar.5) | copy-start | bytes 442372
  19.4 6.5 %copy-start.3 = (f32[1,3,8,1536]{3,2,1,0:T(8,128)S(1)}, f32[1,3,8,1536]{3,2,1,0:T(8,128)}, u32[]{:S(2)}) copy-start(f32[1,3,8,1536]{3,2,1,0:T(8,128)} %rvar.5) | copy-start | bytes 442372
  19.4 6.5 %copy-start.4 = (f32[1,3,8,1536]{3,2,1,0:T(8,128)S(1)}, f32[1,3,8,1536]{3,2,1,0:T(8,128)}, u32[]{:S(2)}) copy-start(f32[1,3,8,1536]{3,2,1,0:T(8,128)} %hobs.5) | copy-start | bytes 442372
  19.5 6.7 %collective-permute-start.7 = (f32[3,8,1536]{2,1,0:T(8,128)S(1)}, f32[3,8,1536]{2,1,0:T(8,128)S(1)}, u32[]{:S(2)}, u32[]{:S(2)}) collective-permute-start(f32[3,8,1536]{2,1,0:T(8,128)S(1)} %get-tuple-element.22.state), channel_id=1, source_target_pairs={{1,2},{2,1},{5,6},{6,5},{9,10},{10,9},{13,14},{14,13},{17,18},{18,... | collective-permute-start | bytes 442376 | tf_op jit(solution)/shard_map/ppermute | solution.py:271
  20.3 5.9 %collective-permute-start.8 = (f32[3,8,1536]{2,1,0:T(8,128)S(1)}, f32[3,8,1536]{2,1,0:T(8,128)S(1)}, u32[]{:S(2)}, u32[]{:S(2)}) collective-permute-start(f32[3,8,1536]{2,1,0:T(8,128)S(1)} %get-tuple-element.22.state), channel_id=1, source_target_pairs={{0,1},{1,0},{2,3},{3,2},{4,5},{5,4},{6,7},{7,6},{8,9},{9,8},{10,11... | collective-permute-start | bytes 442376 | tf_op jit(solution)/shard_map/ppermute | solution.py:261

commit v15 on v14

--- a/solution.py
+++ b/solution.py
@@ -21,6 +21,12 @@
 def lat_gap(field):
     rows = field.shape[0]
     return pltpu.roll(field, rows - 1, 0) - pltpu.roll(field, 1, 0)
+
+
+def own_lat_gap(field, rows):
+    above = jnp.concatenate([field[rows + 1:2 * rows], field[2 * rows:2 * rows + 1]], axis=0)
+    below = jnp.concatenate([field[rows - 1:rows], field[rows:2 * rows - 1]], axis=0)
+    return above - below
 
 
 def even_lat():
@@ -69,33 +75,38 @@
     return 0.25 * jnp.concatenate([low, straight[0], high], axis=0)
 
 
-def adjoint(pair, pair_near, pair_far, straight, relayed, spin, inside, base):
+def adjoint(pair, pair_far, pair_near, straight, relayed, spin, inside, base):
     depth = stretched(straight, relayed)
     turn, keep = widened(spin, depth.shape[1]), widened(inside, depth.shape[1])
     adj_height, adj_east, adj_north = [stacked(pair, pair_near, pair_far, base + part) for part in range(3)]
+    rows = pair.shape[1]
+    own = slice(rows, 2 * rows)
     for step in range(STEPS):
         adj_mid = adj_east - turn * adj_north
         adj_height = keep * (adj_height + 0.25 * (lat_gap(adj_north) + lon_gap(adj_mid)))
-        adj_north = adj_north + turn * adj_mid + depth * lat_gap(adj_height)
-        adj_east = adj_mid + depth * lon_gap(adj_height)
-    rows = pair.shape[1]
-    return [value[rows:2 * rows] for value in (adj_height, adj_east, adj_north)]
-
-
-def first_adjoint_kernel(pair, pair_near, pair_far, straight, relayed, spin, inside, state, back):
-    swept = adjoint(pair, pair_near, pair_far, straight, relayed, spin, inside, 0)
+        if step < STEPS - 1:
+            adj_north = adj_north + turn * adj_mid + depth * lat_gap(adj_height)
+            adj_east = adj_mid + depth * lon_gap(adj_height)
+    own_height, own_mid, own_depth = adj_height[own], adj_mid[own], depth[own]
+    own_north = adj_north[own] + turn[own] * own_mid + own_depth * own_lat_gap(adj_height, rows)
+    own_east = own_mid + own_depth * lon_gap(own_height)
+    return own_height, own_east, own_north
+
+
+def first_adjoint_kernel(pair, pair_far, pair_near, straight, relayed, spin, inside, state, back):
+    swept = adjoint(pair, pair_far, pair_near, straight, relayed, spin, inside, 0)
     link = has_previous()
     for part, value in enumerate(swept):
         back[part] = value
         state[part] = jnp.where(link, straight[1 + part] - value, 0.0)
 
 
-def second_adjoint_kernel(pair, pair_near, pair_far, straight, relayed, spin, inside, local, state, tally):
-    swept = adjoint(pair, pair_near, pair_far, straight, relayed, spin, inside, 3)
+def second_adjoint_kernel(pair, pair_far, pair_near, straight, relayed, spin, inside, local, late, state, tally):
+    swept = adjoint(pair, pair_far, pair_near, straight, relayed, spin, inside, 3)
     link = has_previous()
     cross = square = 0.0
     for part, value in enumerate(swept):
-        zx = jnp.where(link, local[part] - value, 0.0)
+        zx = jnp.where(link, local[part] + late[part] - value, 0.0)
         cross += lane_sum(zx * state[part])
         square += lane_sum(zx * zx)
     tally[0] = cross
@@ -135,12 +146,17 @@
     height, east, north = [stacked(state, state_near, state_far, part) for part in range(3)]
     for step in range(STEPS):
         height = keep * (height - (lon_gap(depth * east) + lat_gap(depth * north)))
-        east = east + turn * north - 0.25 * lon_gap(height)
-        north = north - turn * east - 0.25 * lat_gap(height)
+        if step < STEPS - 1:
+            east = east + turn * north - 0.25 * lon_gap(height)
+            north = north - turn * east - 0.25 * lat_gap(height)
     rows = state.shape[1]
+    own = slice(rows, 2 * rows)
+    own_height, own_turn, own_north = height[own], turn[own], north[own]
+    own_east = east[own] + own_turn * own_north - 0.25 * lon_gap(own_height)
+    own_north = own_north - own_turn * own_east - 0.25 * own_lat_gap(height, rows)
     square = 0.0
-    for part, value in enumerate((height, east, north)):
-        zp = lead[part] - value[rows:2 * rows]
+    for part, value in enumerate((own_height, own_east, own_north)):
+        zp = lead[part] - value
         square += lane_sum(zp * zp)
     moments = [sums[0], sums[1], sums[2], sums[3] + square]
     lane = lax.broadcasted_iota(jnp.int32, (1, 128), 1)
@@ -240,10 +256,13 @@
     )(*operands)
 
 
-def shifted(value, step):
-    count = lax.axis_size("win")
-    initial, last = (max(0, -step), min(count, count - step))
-    return lax.ppermute(value, "win", [(source, source + step) for source in range(initial, last)])
+def shifted(value, step, lats=(0, 1, 2, 3)):
+    wins = lax.axis_size("win")
+    pairs = []
+    for win in range(max(0, -step), min(wins, wins - step)):
+        for lat in lats:
+            pairs.append((4 * win + lat, 4 * (win + step) + lat))
+    return lax.ppermute(value, ("win", "band", "half"), pairs)
 
 
 def lat_count():
@@ -276,12 +295,10 @@
     ranks = lax.axis_size("win") * lat_count()
     total_rows = rows * lat_count()
     offset = (GRID_ROWS - total_rows) // 2
-    local_rows = lat_index() * rows - rows + jnp.arange(3 * rows, dtype=jnp.int32)
+    local_rows = lat_index() * rows - rows + lax.broadcasted_iota(jnp.int32, (3 * rows, 128), 0)
     latitude = -jnp.pi / 2 + (local_rows.astype(jnp.float32) + offset + 0.5) * (jnp.pi / GRID_ROWS)
     inside = ((local_rows >= 0) & (local_rows < total_rows)).astype(jnp.float32)
     spin = inside * (mass_rate * spin_rate * jnp.sin(latitude))
-    inside = jnp.broadcast_to(inside[:, None], (3 * rows, 128))
-    spin = jnp.broadcast_to(spin[:, None], (3 * rows, 128))
     fields = (3, rows, width)
 
     middle, outer = (1, 2), (0, 3)
@@ -297,13 +314,15 @@
     came = shifted(straight, 1)
     relayed = swapped(jnp.concatenate([came[:1], depth_edge]), 0)
     pair_near, pair_far = swapped(pair, 0), crossed(pair, middle)
-    known = (pair, pair_near, pair_far, came, relayed, spin, inside)
-    local = shifted(local, 1)
+    known = (pair, pair_far, pair_near, came, relayed, spin, inside)
+    late, local = local, shifted(local, 1, middle)
     state, back = run(first_adjoint_kernel, [fields, fields], *known, work=4)
     held_state, local = lax.optimization_barrier((state, local))
+    late, _ = lax.optimization_barrier((late, state))
+    late = shifted(late, 1, outer)
     back = shifted(back, -1)
     state_far = crossed(held_state, middle)
-    (tally,) = run(second_adjoint_kernel, [(2, rows, 128)], *known, local, state)
+    (tally,) = run(second_adjoint_kernel, [(2, rows, 128)], *known, local, late, state)
     state_near = swapped(state, 0)
     lead, sums = run(
         home_kernel, [fields, (4, rows, 128)],

time: 42.1 us -> 43.1 us (1.024)
  waiting for transfers between devices: 3.16 us -> 5.22 us
  blocking collectives: 13.2 us -> 11.6 us
  starting transfers between devices: 18.1 us -> 18.7 us
    ppermute x3 -> x4, waiting for transfers between devices: 2.1 us -> 3.81 us  [shifted(): return lax.ppermute(value, ('win', 'band', 'half'), pairs)]
    all_to_all x1, blocking collectives: 13.2 us -> 11.6 us  [body(): gathered = lax.all_to_all(sent, ('win', 'band', 'half'), 0, 0, tiled=True)]
    ppermute x3 -> x4, starting transfers between devices: 9.27 us -> 10.1 us  [shifted(): return lax.ppermute(value, ('win', 'band', 'half'), pairs)]
    ppermute x3, waiting for transfers between devices: 0.01 us -> 0.54 us  [crossed(): return lax.ppermute(value, ('win', 'band', 'half'), pairs)]
  transfers between devices with their start and end apart: 10 -> 11, of which waited for: 2 -> 4; matrix products, arithmetic and copies ran while one was open for 0% -> 0% of each run, Pallas kernels for 9% -> 9%
where the time goes in v15:
time: 43.1 us; the launch traced here: 42.9 us
  starting transfers between devices  18.7 us (43%)
  blocking collectives  11.6 us (27%)
  Pallas kernels  6.21 us (14%)
  waiting for transfers between devices  5.22 us (12%)
  between operations  0.85 us (2%)
    all_to_all x1, blocking collectives, body(): gathered = lax.all_to_all(sent, ('win', 'band', 'half'), 0, 0, tiled=True)  11.6 us
    ppermute x4, starting transfers between devices, shifted(): return lax.ppermute(value, ('win', 'band', 'half'), pairs)  10.1 us
    pallas_call x6, Pallas kernels, run(): pl.pallas_call(kernel, out_shape=shapes, in_specs=[pl.BlockSpec(memory_sp...  6.21 us
    ppermute x3, starting transfers between devices, crossed(): return lax.ppermute(value, ('win', 'band', 'half'), pairs)  5.45 us
    ppermute x4, waiting for transfers between devices, shifted(): return lax.ppermute(value, ('win', 'band', 'half'), pairs)  3.81 us
    ppermute x4, starting transfers between devices, swapped(): return lax.ppermute(value, ('band', 'half'), pairs)  3.18 us
    ppermute x4, waiting for transfers between devices, swapped(): return lax.ppermute(value, ('band', 'half'), pairs)  0.88 us
  transfers between devices with their start and end apart: 11, of which 4 were waited for; matrix products, arithmetic and copies ran while one was open for 0% of the time, Pallas kernels for 9%

profile of v15, /device:TPU:0, one launch (start us, length us, event | category | flops | bytes accessed | tf_op | source)
XLA Modules:
  0.0 42.9 jit_solution(9233158758591316015)
XLA Ops:
  0.6 0.5 %collective-permute-start = (f32[1,8,1536]{2,1,0:T(8,128)}, f32[1,8,1536]{2,1,0:T(8,128)S(1)}, u32[]{:S(2)}, u32[]{:S(2)}) collective-permute-start(f32[1,8,1536]{2,1,0:T(8,128)} %depth.1), channel_id=1, source_target_pairs={{0,1},{1,0},{2,3},{3,2},{4,5},{5,4},{6,7},{7,6},{8,9},{9,8},{10,11... | collective-permute-start | bytes 147464 | tf_op jit(solution)/shard_map/ppermute | solution.py:280
  1.1 1.3 %shard_map.85 = (f32[6,8,1536]{2,1,0:T(8,128)S(1)}, f32[4,8,1536]{2,1,0:T(8,128)S(1)}, f32[3,8,1536]{2,1,0:T(8,128)S(1)}) custom-call(f32[1,3,8,1536]{3,2,1,0:T(8,128)} %p.5, f32[1,3,8,1536]{3,2,1,0:T(8,128)} %m.5, f32[1,3,8,1536]{3,2,1,0:T(8,128)} %dvar.5, f32[1,3,8,1536]{3,2,1,0:T(8,128)} %rvar.5, f32[1,3,8,1536]{3,2,1,0:T(8,128)} %hobs.5, f32[1,8,1536]{2,1,0:T(8,128)} %depth.1), custom_call_target="tpu_custom_call" | custom-call | flops 1425408 | bytes 1425408 | tf_op jit(solution)/shard_map/pallas_call | solution.py:248
  2.5 0.0 collective-permute-done
  2.5 4.5 %collective-permute-start.3 = (f32[4,8,1536]{2,1,0:T(8,128)S(1)}, f32[4,8,1536]{2,1,0:T(8,128)S(1)}, u32[]{:S(2)}, u32[]{:S(2)}) collective-permute-start(f32[4,8,1536]{2,1,0:T(8,128)S(1)} %get-tuple-element.20), channel_id=1, source_target_pairs={{0,4},{1,5},{2,6},{3,7},{4,8},{5,9},{6,10},{7,11},{8,12},{9,13},{1... | collective-permute-start | bytes 589832 | tf_op jit(solution)/shard_map/ppermute | solution.py:265
  7.0 4.1 %collective-permute-start.4 = (f32[1,8,1536]{2,1,0:T(8,128)S(1)}, f32[1,8,1536]{2,1,0:T(8,128)S(1)}, u32[]{:S(2)}, u32[]{:S(2)}) collective-permute-start(f32[1,8,1536]{2,1,0:T(8,128)S(1)} %collective-permute-done), channel_id=1, source_target_pairs={{0,7},{3,4},{4,11},{7,8},{8,15},{11,12},{12,19},{15,16},{16,23},{1... | collective-permute-start | bytes 147464 | tf_op jit(solution)/shard_map/ppermute | solution.py:290
  11.1 0.1 sine_multiply_fusion
  11.2 0.7 %collective-permute-start.1 = (f32[6,8,1536]{2,1,0:T(8,128)S(1)}, f32[6,8,1536]{2,1,0:T(8,128)S(1)}, u32[]{:S(2)}, u32[]{:S(2)}) collective-permute-start(f32[6,8,1536]{2,1,0:T(8,128)S(1)} %get-tuple-element.19.pair), channel_id=1, source_target_pairs={{1,2},{2,1},{5,6},{6,5},{9,10},{10,9},{13,14},{14,13},{17,18},{18,... | collective-permute-start | bytes 884744 | tf_op jit(solution)/shard_map/ppermute | solution.py:290
  11.9 0.1 collective-permute-start.2
  12.0 0.7 %collective-permute-start.6 = (f32[3,8,1536]{2,1,0:T(8,128)S(1)}, f32[3,8,1536]{2,1,0:T(8,128)S(1)}, u32[]{:S(2)}, u32[]{:S(2)}) collective-permute-start(f32[3,8,1536]{2,1,0:T(8,128)S(1)} %get-tuple-element.25), channel_id=1, source_target_pairs={{1,5},{2,6},{5,9},{6,10},{9,13},{10,14},{13,17},{14,18},{17,21},{1... | collective-permute-start | bytes 442376 | tf_op jit(solution)/shard_map/ppermute | solution.py:265
  12.6 0.0 collective-permute-done.3.straight
  12.7 0.5 %collective-permute-done.4 = f32[1,8,1536]{2,1,0:T(8,128)S(1)} collective-permute-done((f32[1,8,1536]{2,1,0:T(8,128)S(1)}, f32[1,8,1536]{2,1,0:T(8,128)S(1)}, u32[]{:S(2)}, u32[]{:S(2)}) %collective-permute-start.4) | collective-permute-done | bytes 49184 | tf_op jit(solution)/shard_map/ppermute | solution.py:290
  13.2 2.5 %collective-permute-start.5 = (f32[2,8,1536]{2,1,0:T(8,128)S(1)}, f32[2,8,1536]{2,1,0:T(8,128)S(1)}, u32[]{:S(2)}, u32[]{:S(2)}) collective-permute-start(f32[2,8,1536]{2,1,0:T(8,128)S(1)} %pad_maximum_fusion), channel_id=1, source_target_pairs={{0,1},{1,0},{2,3},{3,2},{4,5},{5,4},{6,7},{7,6},{8,9},{9,8},{10,11... | collective-permute-start | bytes 294920 | tf_op jit(solution)/shard_map/ppermute | solution.py:280
  15.7 0.1 broadcast_select_fusion.spin
  15.8 0.9 %collective-permute-done.5.relayed = f32[2,8,1536]{2,1,0:T(8,128)S(1)} collective-permute-done((f32[2,8,1536]{2,1,0:T(8,128)S(1)}, f32[2,8,1536]{2,1,0:T(8,128)S(1)}, u32[]{:S(2)}, u32[]{:S(2)}) %collective-permute-start.5) | collective-permute-done | bytes 98336 | tf_op jit(solution)/shard_map/ppermute | solution.py:280
  16.7 0.1 iota.13.inside
  16.7 1.1 %shard_map.86 = (f32[3,8,1536]{2,1,0:T(8,128)S(1)}, f32[3,8,1536]{2,1,0:T(8,128)S(1)}) custom-call(f32[6,8,1536]{2,1,0:T(8,128)S(1)} %get-tuple-element.19.pair, f32[6,8,1536]{2,1,0:T(8,128)S(1)} %collective-permute-done.1.pair_far, f32[6,8,1536]{2,1,0:T(8,128)S(1)} %collective-permute-done.2.pair_near, f32[4,8,1536]{2,1,0:T(8,128)S(1)} %collective-permute-done.3.straight, ...), custom_call_target="tpu_custom_call" | custom-call | flops 1499136 | bytes 1499136 | tf_op jit(solution)/shard_map/pallas_call | solution.py:248
  17.9 3.4 %collective-permute-start.9 = (f32[3,8,1536]{2,1,0:T(8,128)S(1)}, f32[3,8,1536]{2,1,0:T(8,128)S(1)}, u32[]{:S(2)}, u32[]{:S(2)}) collective-permute-start(f32[3,8,1536]{2,1,0:T(8,128)S(1)} %get-tuple-element.25), channel_id=1, source_target_pairs={{0,4},{3,7},{4,8},{7,11},{8,12},{11,15},{12,16},{15,19},{16,20},{1... | collective-permute-start | bytes 442376 | tf_op jit(solution)/shard_map/ppermute | solution.py:265
  21.3 0.0 copy-start
  21.3 0.0 copy-start.1
  21.4 0.0 copy-start.2
  21.4 0.0 copy-start.3
  21.4 0.0 copy-start.4
  21.4 1.4 %collective-permute-start.10 = (f32[3,8,1536]{2,1,0:T(8,128)S(1)}, f32[3,8,1536]{2,1,0:T(8,128)S(1)}, u32[]{:S(2)}, u32[]{:S(2)}) collective-permute-start(f32[3,8,1536]{2,1,0:T(8,128)S(1)} %get-tuple-element.26), channel_id=1, source_target_pairs={{4,0},{5,1},{6,2},{7,3},{8,4},{9,5},{10,6},{11,7},{12,8},{13,9},{1... | collective-permute-start | bytes 442376 | tf_op jit(solution)/shard_map/ppermute | solution.py:265
  22.8 0.7 %collective-permute-start.7 = (f32[3,8,1536]{2,1,0:T(8,128)S(1)}, f32[3,8,1536]{2,1,0:T(8,128)S(1)}, u32[]{:S(2)}, u32[]{:S(2)}) collective-permute-start(f32[3,8,1536]{2,1,0:T(8,128)S(1)} %get-tuple-element.23.state), channel_id=1, source_target_pairs={{1,2},{2,1},{5,6},{6,5},{9,10},{10,9},{13,14},{14,13},{17,18},{18,... | collective-permute-start | bytes 442376 | tf_op jit(solution)/shard_map/ppermute | solution.py:290
  23.5 0.1 collective-permute-start.8
  23.6 2.0 %collective-permute-done.9.late = f32[3,8,1536]{2,1,0:T(8,128)S(1)} collective-permute-done((f32[3,8,1536]{2,1,0:T(8,128)S(1)}, f32[3,8,1536]{2,1,0:T(8,128)S(1)}, u32[]{:S(2)}, u32[]{:S(2)}) %collective-permute-start.9) | collective-permute-done | bytes 147488 | tf_op jit(solution)/shard_map/ppermute | solution.py:265
  25.6 1.2 %shard_map.87.tally = f32[2,8,128]{2,1,0:T(8,128)S(1)} custom-call(f32[6,8,1536]{2,1,0:T(8,128)S(1)} %get-tuple-element.19.pair, f32[6,8,1536]{2,1,0:T(8,128)S(1)} %collective-permute-done.1.pair_far, f32[6,8,1536]{2,1,0:T(8,128)S(1)} %collective-permute-done.2.pair_near, f32[4,8,1536]{2,1,0:T(8,128)S(1)} %collective-permute-done.3.straight, ...), custom_call_target="tpu_custom_call" | custom-call | flops 1654784 | bytes 1654784 | tf_op jit(solution)/shard_map/pallas_call | solution.py:248
  26.8 1.8 %collective-permute-done.10.back = f32[3,8,1536]{2,1,0:T(8,128)S(1)} collective-permute-done((f32[3,8,1536]{2,1,0:T(8,128)S(1)}, f32[3,8,1536]{2,1,0:T(8,128)S(1)}, u32[]{:S(2)}, u32[]{:S(2)}) %collective-permute-start.10) | collective-permute-done | bytes 147488 | tf_op jit(solution)/shard_map/ppermute | solution.py:265
  28.6 0.2 shard_map.88
  28.8 1.2 %shard_map.89 = f32[32,128]{1,0:T(8,128)S(1)} custom-call(f32[3,8,1536]{2,1,0:T(8,128)S(1)} %collective-permute-done.7.state_far, f32[3,8,1536]{2,1,0:T(8,128)S(1)} %collective-permute-done.8.state_near, f32[4,8,1536]{2,1,0:T(8,128)S(1)} %collective-permute-done.3.straight, f32[2,8,1536]{2,1,0:T(8,128)S(1)} %collective-permute-done.5.relayed, ...), custom_call_target="tpu_custom_call" | custom-call | flops 942080 | bytes 942080 | tf_op jit(solution)/shard_map/pallas_call | solution.py:248
  30.0 11.6 %all_to_all.11 = f32[32,1,128]{2,1,0:T(1,128)S(1)} all-to-all(f32[32,1,128]{2,1,0:T(1,128)S(1)} %bitcast.4), channel_id=1, replica_groups=mesh['win'=8,'band'=2,'half'=2] {'win','band','half'}, dimensions={0} | all-to-all | bytes 32768 | tf_op jit(solution)/shard_map/all_to_all | solution.py:332
  41.6 1.2 %shard_map.90 = (f32[1,3,8,1536]{3,2,1,0:T(8,128)}, f32[1,3,8,1536]{3,2,1,0:T(8,128)}, f32[1,3,8,1536]{3,2,1,0:T(8,128)}) custom-call(f32[32,128]{1,0:T(8,128)S(1)} %bitcast.5, f32[1,3,8,1536]{3,2,1,0:T(8,128)S(1)} %copy-done, f32[1,3,8,1536]{3,2,1,0:T(8,128)S(1)} %copy-done.1, f32[1,3,8,1536]{3,2,1,0:T(8,128)S(1)} %copy-done.2, ...), custom_call_target="tpu_custom_call" | custom-call | flops 1343488 | bytes 1343488 | tf_op jit(solution)/shard_map/pallas_call | solution.py:248
  (13 shorter events, 0.0 us)
Async XLA Ops:
  0.6 1.8 %collective-permute-start = (f32[1,8,1536]{2,1,0:T(8,128)}, f32[1,8,1536]{2,1,0:T(8,128)S(1)}, u32[]{:S(2)}, u32[]{:S(2)}) collective-permute-start(f32[1,8,1536]{2,1,0:T(8,128)} %depth.1), channel_id=1, source_target_pairs={{0,1},{1,0},{2,3},{3,2},{4,5},{5,4},{6,7},{7,6},{8,9},{9,8},{10,11... | collective-permute-start | bytes 147464 | tf_op jit(solution)/shard_map/ppermute | solution.py:280
  2.5 10.2 %collective-permute-start.3 = (f32[4,8,1536]{2,1,0:T(8,128)S(1)}, f32[4,8,1536]{2,1,0:T(8,128)S(1)}, u32[]{:S(2)}, u32[]{:S(2)}) collective-permute-start(f32[4,8,1536]{2,1,0:T(8,128)S(1)} %get-tuple-element.20), channel_id=1, source_target_pairs={{0,4},{1,5},{2,6},{3,7},{4,8},{5,9},{6,10},{7,11},{8,12},{9,13},{1... | collective-permute-start | bytes 589832 | tf_op jit(solution)/shard_map/ppermute | solution.py:265
  7.0 6.2 %collective-permute-start.4 = (f32[1,8,1536]{2,1,0:T(8,128)S(1)}, f32[1,8,1536]{2,1,0:T(8,128)S(1)}, u32[]{:S(2)}, u32[]{:S(2)}) collective-permute-start(f32[1,8,1536]{2,1,0:T(8,128)S(1)} %collective-permute-done), channel_id=1, source_target_pairs={{0,7},{3,4},{4,11},{7,8},{8,15},{11,12},{12,19},{15,16},{16,23},{1... | collective-permute-start | bytes 147464 | tf_op jit(solution)/shard_map/ppermute | solution.py:290
  11.2 5.5 %collective-permute-start.1 = (f32[6,8,1536]{2,1,0:T(8,128)S(1)}, f32[6,8,1536]{2,1,0:T(8,128)S(1)}, u32[]{:S(2)}, u32[]{:S(2)}) collective-permute-start(f32[6,8,1536]{2,1,0:T(8,128)S(1)} %get-tuple-element.19.pair), channel_id=1, source_target_pairs={{1,2},{2,1},{5,6},{6,5},{9,10},{10,9},{13,14},{14,13},{17,18},{18,... | collective-permute-start | bytes 884744 | tf_op jit(solution)/shard_map/ppermute | solution.py:290
  11.9 4.8 %collective-permute-start.2 = (f32[6,8,1536]{2,1,0:T(8,128)S(1)}, f32[6,8,1536]{2,1,0:T(8,128)S(1)}, u32[]{:S(2)}, u32[]{:S(2)}) collective-permute-start(f32[6,8,1536]{2,1,0:T(8,128)S(1)} %get-tuple-element.19.pair), channel_id=1, source_target_pairs={{0,1},{1,0},{2,3},{3,2},{4,5},{5,4},{6,7},{7,6},{8,9},{9,8},{10,11... | collective-permute-start | bytes 884744 | tf_op jit(solution)/shard_map/ppermute | solution.py:280
  12.0 10.9 %collective-permute-start.6 = (f32[3,8,1536]{2,1,0:T(8,128)S(1)}, f32[3,8,1536]{2,1,0:T(8,128)S(1)}, u32[]{:S(2)}, u32[]{:S(2)}) collective-permute-start(f32[3,8,1536]{2,1,0:T(8,128)S(1)} %get-tuple-element.25), channel_id=1, source_target_pairs={{1,5},{2,6},{5,9},{6,10},{9,13},{10,14},{13,17},{14,18},{17,21},{1... | collective-permute-start | bytes 442376 | tf_op jit(solution)/shard_map/ppermute | solution.py:265
  13.2 3.5 %collective-permute-start.5 = (f32[2,8,1536]{2,1,0:T(8,128)S(1)}, f32[2,8,1536]{2,1,0:T(8,128)S(1)}, u32[]{:S(2)}, u32[]{:S(2)}) collective-permute-start(f32[2,8,1536]{2,1,0:T(8,128)S(1)} %pad_maximum_fusion), channel_id=1, source_target_pairs={{0,1},{1,0},{2,3},{3,2},{4,5},{5,4},{6,7},{7,6},{8,9},{9,8},{10,11... | collective-permute-start | bytes 294920 | tf_op jit(solution)/shard_map/ppermute | solution.py:280
  17.9 7.7 %collective-permute-start.9 = (f32[3,8,1536]{2,1,0:T(8,128)S(1)}, f32[3,8,1536]{2,1,0:T(8,128)S(1)}, u32[]{:S(2)}, u32[]{:S(2)}) collective-permute-start(f32[3,8,1536]{2,1,0:T(8,128)S(1)} %get-tuple-element.25), channel_id=1, source_target_pairs={{0,4},{3,7},{4,8},{7,11},{8,12},{11,15},{12,16},{15,19},{16,20},{1... | collective-permute-start | bytes 442376 | tf_op jit(solution)/shard_map/ppermute | solution.py:265
  21.3 7.2 %copy-start = (f32[1,3,8,1536]{3,2,1,0:T(8,128)S(1)}, f32[1,3,8,1536]{3,2,1,0:T(8,128)}, u32[]{:S(2)}) copy-start(f32[1,3,8,1536]{3,2,1,0:T(8,128)} %p.5) | copy-start | bytes 442372
  21.3 7.2 %copy-start.1 = (f32[1,3,8,1536]{3,2,1,0:T(8,128)S(1)}, f32[1,3,8,1536]{3,2,1,0:T(8,128)}, u32[]{:S(2)}) copy-start(f32[1,3,8,1536]{3,2,1,0:T(8,128)} %m.5) | copy-start | bytes 442372
  21.4 7.2 %copy-start.2 = (f32[1,3,8,1536]{3,2,1,0:T(8,128)S(1)}, f32[1,3,8,1536]{3,2,1,0:T(8,128)}, u32[]{:S(2)}) copy-start(f32[1,3,8,1536]{3,2,1,0:T(8,128)} %dvar.5) | copy-start | bytes 442372
  21.4 7.2 %copy-start.3 = (f32[1,3,8,1536]{3,2,1,0:T(8,128)S(1)}, f32[1,3,8,1536]{3,2,1,0:T(8,128)}, u32[]{:S(2)}) copy-start(f32[1,3,8,1536]{3,2,1,0:T(8,128)} %rvar.5) | copy-start | bytes 442372
  21.4 7.2 %copy-start.4 = (f32[1,3,8,1536]{3,2,1,0:T(8,128)S(1)}, f32[1,3,8,1536]{3,2,1,0:T(8,128)}, u32[]{:S(2)}) copy-start(f32[1,3,8,1536]{3,2,1,0:T(8,128)} %hobs.5) | copy-start | bytes 442372
  21.4 7.2 %collective-permute-start.10 = (f32[3,8,1536]{2,1,0:T(8,128)S(1)}, f32[3,8,1536]{2,1,0:T(8,128)S(1)}, u32[]{:S(2)}, u32[]{:S(2)}) collective-permute-start(f32[3,8,1536]{2,1,0:T(8,128)S(1)} %get-tuple-element.26), channel_id=1, source_target_pairs={{4,0},{5,1},{6,2},{7,3},{8,4},{9,5},{10,6},{11,7},{12,8},{13,9},{1... | collective-permute-start | bytes 442376 | tf_op jit(solution)/shard_map/ppermute | solution.py:265
  22.8 5.9 %collective-permute-start.7 = (f32[3,8,1536]{2,1,0:T(8,128)S(1)}, f32[3,8,1536]{2,1,0:T(8,128)S(1)}, u32[]{:S(2)}, u32[]{:S(2)}) collective-permute-start(f32[3,8,1536]{2,1,0:T(8,128)S(1)} %get-tuple-element.23.state), channel_id=1, source_target_pairs={{1,2},{2,1},{5,6},{6,5},{9,10},{10,9},{13,14},{14,13},{17,18},{18,... | collective-permute-start | bytes 442376 | tf_op jit(solution)/shard_map/ppermute | solution.py:290
  23.5 5.3 %collective-permute-start.8 = (f32[3,8,1536]{2,1,0:T(8,128)S(1)}, f32[3,8,1536]{2,1,0:T(8,128)S(1)}, u32[]{:S(2)}, u32[]{:S(2)}) collective-permute-start(f32[3,8,1536]{2,1,0:T(8,128)S(1)} %get-tuple-element.23.state), channel_id=1, source_target_pairs={{0,1},{1,0},{2,3},{3,2},{4,5},{5,4},{6,7},{7,6},{8,9},{9,8},{10,11... | collective-permute-start | bytes 442376 | tf_op jit(solution)/shard_map/ppermute | solution.py:280

commit v16 on v14

--- a/solution.py
+++ b/solution.py
@@ -129,19 +129,72 @@
         sums[row] = value
 
 
-def closing_kernel(state_far, state_near, straight, relayed, spin, inside, state, lead, sums, sent):
+def forward(height, east, north, depth, turn, keep, gap):
+    for step in range(STEPS):
+        height = keep * (height - (lon_gap(depth * east) + gap(depth * north)))
+        east = east + turn * north - 0.25 * lon_gap(height)
+        north = north - turn * east - 0.25 * gap(height)
+    return height, east, north
+
+
+def inner_forward_kernel(state, state_near, straight, relayed, spin, inside, lead, rest):
     depth = stretched(straight, relayed)
     turn, keep = widened(spin, depth.shape[1]), widened(inside, depth.shape[1])
-    height, east, north = [stacked(state, state_near, state_far, part) for part in range(3)]
-    for step in range(STEPS):
-        height = keep * (height - (lon_gap(depth * east) + lat_gap(depth * north)))
-        east = east + turn * north - 0.25 * lon_gap(height)
-        north = north - turn * east - 0.25 * lat_gap(height)
+    even = even_lat()
     rows = state.shape[1]
+    fields = []
+    for part in range(3):
+        low = jnp.where(even, 0.0, state_near[part])
+        high = jnp.where(even, state_near[part], 0.0)
+        fields.append(jnp.concatenate([low, state[part], high], axis=0))
+    for part, value in enumerate(forward(*fields, depth, turn, keep, lat_gap)):
+        rest[part] = lead[part] - value[rows:2 * rows]
+
+
+def open_lat_gap(field):
+    rows = field.shape[0]
+    row = lax.broadcasted_iota(jnp.int32, field.shape, 0)
+    above = jnp.where(row < rows - 1, pltpu.roll(field, rows - 1, 0), 0.0)
+    below = jnp.where(row > 0, pltpu.roll(field, 1, 0), 0.0)
+    return above - below
+
+
+def closing_kernel(state_far, rest, straight, relayed, spin, inside, sums, sent, remainder):
+    even = even_lat()
+    rows, width = state_far.shape[1:]
+    middle = lax.axis_index("band") != lax.axis_index("half")
+
+    @pl.when(middle)
+    def _():
+        depth = jnp.where(
+            even,
+            jnp.concatenate([relayed[1], straight[0]], axis=0),
+            jnp.concatenate([straight[0], relayed[1]], axis=0),
+        )
+        turn, keep = [
+            jnp.where(even, factor[:2 * rows], factor[rows:])
+            for factor in (widened(spin, width), widened(inside, width))
+        ]
+        empty = jnp.zeros((rows, width), jnp.float32)
+        fields = [
+            jnp.where(
+                even,
+                jnp.concatenate([state_far[part], empty], axis=0),
+                jnp.concatenate([empty, state_far[part]], axis=0),
+            )
+            for part in range(3)
+        ]
+        for part, value in enumerate(forward(*fields, 0.25 * depth, turn, keep, open_lat_gap)):
+            remainder[part] = rest[part] - jnp.where(even, value[rows:], value[:rows])
+
+    @pl.when(jnp.logical_not(middle))
+    def _():
+        for part in range(3):
+            remainder[part] = rest[part]
+
     square = 0.0
-    for part, value in enumerate((height, east, north)):
-        zp = lead[part] - value[rows:2 * rows]
-        square += lane_sum(zp * zp)
+    for part in range(3):
+        square += lane_sum(remainder[part] * remainder[part])
     moments = [sums[0], sums[1], sums[2], sums[3] + square]
     lane = lax.broadcasted_iota(jnp.int32, (1, 128), 1)
     row = 0.0
@@ -212,19 +265,29 @@
     return y1, y2
 
 
-def combine_kernel(gathered, p, m, dvar, rvar, hobs, back, dual_model, dual_obs, increment):
+def combine_kernel(gathered, p, m, dvar, rvar, hobs, back, dual_model, dual_obs, increment, first, second, third, sems):
     y1, y2 = coefficients(gathered)
     rows, width = p.shape[2:]
     y1 = jnp.broadcast_to(jnp.concatenate([y1] * (width // 128), axis=1), (rows, width))
     y2 = jnp.broadcast_to(jnp.concatenate([y2] * (width // 128), axis=1), (rows, width))
-    for part in range(3):
-        pv, mv = p[0, part], m[0, part]
-        dual_model[0, part] = (y1 + y2 * dvar[0, part]) * pv
-        dual_obs[0, part] = (y1 + y2 * rvar[0, part]) * mv
-        increment[0, part] = y2 * (pv - back[part] + hobs[0, part] * mv)
-
-
-def run(kernel, out_shapes, *operands, scratch=(), space=pltpu.VMEM, work=4):
+    copies = [
+        pltpu.make_async_copy(source, target, sems.at[slot])
+        for slot, (source, target) in enumerate(((first, dual_model), (second, dual_obs), (third, increment)))
+    ]
+    for part in range(3):
+        first[0, part] = (y1 + y2 * dvar[0, part]) * p[0, part]
+    copies[0].start()
+    for part in range(3):
+        second[0, part] = (y1 + y2 * rvar[0, part]) * m[0, part]
+    copies[1].start()
+    for part in range(3):
+        third[0, part] = y2 * (p[0, part] - back[part] + hobs[0, part] * m[0, part])
+    copies[2].start()
+    for copy in copies:
+        copy.wait()
+
+
+def run(kernel, out_shapes, *operands, scratch=(), space=pltpu.VMEM, target=pltpu.VMEM, work=4):
     shapes = [jax.ShapeDtypeStruct(shape, jnp.float32) for shape in out_shapes]
     size = sum(4 * operand.size for operand in operands) + sum(4 * shape.size for shape in shapes)
     if space is not pltpu.VMEM:
@@ -233,7 +296,7 @@
         kernel,
         out_shape=shapes,
         in_specs=[pl.BlockSpec(memory_space=space)] * len(operands),
-        out_specs=[pl.BlockSpec(memory_space=pltpu.VMEM)] * len(shapes),
+        out_specs=[pl.BlockSpec(memory_space=target)] * len(shapes),
         scratch_shapes=scratch,
         compiler_params=pltpu.CompilerParams(vmem_limit_bytes=32 * 1024 * 1024),
         cost_estimate=pl.CostEstimate(flops=work * size // 4, bytes_accessed=work * size // 4, transcendentals=0),
@@ -276,12 +339,10 @@
     ranks = lax.axis_size("win") * lat_count()
     total_rows = rows * lat_count()
     offset = (GRID_ROWS - total_rows) // 2
-    local_rows = lat_index() * rows - rows + jnp.arange(3 * rows, dtype=jnp.int32)
+    local_rows = lat_index() * rows - rows + lax.broadcasted_iota(jnp.int32, (3 * rows, 128), 0)
     latitude = -jnp.pi / 2 + (local_rows.astype(jnp.float32) + offset + 0.5) * (jnp.pi / GRID_ROWS)
     inside = ((local_rows >= 0) & (local_rows < total_rows)).astype(jnp.float32)
     spin = inside * (mass_rate * spin_rate * jnp.sin(latitude))
-    inside = jnp.broadcast_to(inside[:, None], (3 * rows, 128))
-    spin = jnp.broadcast_to(spin[:, None], (3 * rows, 128))
     fields = (3, rows, width)
 
     middle, outer = (1, 2), (0, 3)
@@ -309,11 +370,16 @@
         home_kernel, [fields, (4, rows, 128)],
         model_rhs, obs_rhs, model_var, obs_var, obs_weight, tally, back,
     )
-    (sent,) = run(closing_kernel, [(ranks, 128)], state_far, state_near, came, relayed, spin, inside, state, lead, sums)
+    (rest,) = run(inner_forward_kernel, [fields], state, state_near, came, relayed, spin, inside, lead)
+    (sent,) = run(
+        closing_kernel, [(ranks, 128)], state_far, rest, came, relayed, spin, inside, sums,
+        scratch=[pltpu.VMEM(fields, jnp.float32)],
+    )
     gathered = lax.all_to_all(sent, ("win", "band", "half"), 0, 0, tiled=True)
     return run(
         combine_kernel, [model_rhs.shape] * 3,
-        gathered, model_rhs, obs_rhs, model_var, obs_var, obs_weight, back,
+        gathered, model_rhs, obs_rhs, model_var, obs_var, obs_weight, back, target=pltpu.HBM,
+        scratch=[pltpu.VMEM(model_rhs.shape, jnp.float32)] * 3 + [pltpu.SemaphoreType.DMA((3,))],
     )
 
 

time: 42.1 us -> 42.2 us (level)
  starting transfers between devices: 18.1 us -> 15.8 us
  waiting for transfers between devices: 3.16 us -> 5.43 us
    ppermute x3, waiting for transfers between devices: 2.1 us -> 4.39 us  [shifted(): lax.ppermute(value, 'win', [(source, source + step) for source in range(i...]
    ppermute x4, starting transfers between devices: 3.27 us -> 1.13 us  [swapped(): return lax.ppermute(value, ('band', 'half'), pairs)]
    pallas_call x6 -> x7, Pallas kernels: 6.21 us -> 6.39 us  [run(): pl.pallas_call(kernel, out_shape=shapes, in_specs=[pl.BlockSpec(memory_sp...]
  transfers between devices with their start and end apart: 10 -> 10, of which waited for: 2 -> 2; matrix products, arithmetic and copies ran while one was open for 0% -> 1% of each run, Pallas kernels for 9% -> 12%
where the time goes in v16:
time: 42.2 us; the launch traced here: 41.9 us
  starting transfers between devices  15.8 us (37%)
  blocking collectives  13.1 us (31%)
  Pallas kernels  6.39 us (15%)
  waiting for transfers between devices  5.43 us (13%)
  between operations  0.84 us (2%)
    all_to_all x1, blocking collectives, body(): gathered = lax.all_to_all(sent, ('win', 'band', 'half'), 0, 0, tiled=True)  13.1 us
    ppermute x3, starting transfers between devices, shifted(): lax.ppermute(value, 'win', [(source, source + step) for source in range(i...  9.27 us
    pallas_call x7, Pallas kernels, run(): pl.pallas_call(kernel, out_shape=shapes, in_specs=[pl.BlockSpec(memory_sp...  6.39 us
    ppermute x3, starting transfers between devices, crossed(): return lax.ppermute(value, ('win', 'band', 'half'), pairs)  5.44 us
    ppermute x3, waiting for transfers between devices, shifted(): lax.ppermute(value, 'win', [(source, source + step) for source in range(i...  4.39 us
    ppermute x4, starting transfers between devices, swapped(): return lax.ppermute(value, ('band', 'half'), pairs)  1.13 us
    ppermute x4, waiting for transfers between devices, swapped(): return lax.ppermute(value, ('band', 'half'), pairs)  1.03 us
  transfers between devices with their start and end apart: 10, of which 2 were waited for; matrix products, arithmetic and copies ran while one was open for 1% of the time, Pallas kernels for 12%

profile of v16, /device:TPU:0, one launch (start us, length us, event | category | flops | bytes accessed | tf_op | source)
XLA Modules:
  0.0 41.9 jit_solution(5409558371389437446)
XLA Ops:
  0.6 0.5 %collective-permute-start = (f32[1,8,1536]{2,1,0:T(8,128)}, f32[1,8,1536]{2,1,0:T(8,128)S(1)}, u32[]{:S(2)}, u32[]{:S(2)}) collective-permute-start(f32[1,8,1536]{2,1,0:T(8,128)} %depth.1), channel_id=1, source_target_pairs={{0,1},{1,0},{2,3},{3,2},{4,5},{5,4},{6,7},{7,6},{8,9},{9,8},{10,11... | collective-permute-start | bytes 147464 | tf_op jit(solution)/shard_map/ppermute | solution.py:324
  1.1 1.3 %shard_map.85 = (f32[6,8,1536]{2,1,0:T(8,128)S(1)}, f32[4,8,1536]{2,1,0:T(8,128)S(1)}, f32[3,8,1536]{2,1,0:T(8,128)S(1)}) custom-call(f32[1,3,8,1536]{3,2,1,0:T(8,128)} %p.5, f32[1,3,8,1536]{3,2,1,0:T(8,128)} %m.5, f32[1,3,8,1536]{3,2,1,0:T(8,128)} %dvar.5, f32[1,3,8,1536]{3,2,1,0:T(8,128)} %rvar.5, f32[1,3,8,1536]{3,2,1,0:T(8,128)} %hobs.5, f32[1,8,1536]{2,1,0:T(8,128)} %depth.1), custom_call_target="tpu_custom_call" | custom-call | flops 1425408 | bytes 1425408 | tf_op jit(solution)/shard_map/pallas_call | solution.py:295
  2.5 0.0 collective-permute-done
  2.5 4.5 %collective-permute-start.3 = (f32[4,8,1536]{2,1,0:T(8,128)S(1)}, f32[4,8,1536]{2,1,0:T(8,128)S(1)}, u32[]{:S(2)}, u32[]{:S(2)}) collective-permute-start(f32[4,8,1536]{2,1,0:T(8,128)S(1)} %get-tuple-element.19), channel_id=1, source_target_pairs={{0,4},{4,8},{8,12},{12,16},{16,20},{20,24},{24,28},{1,5},{5,9},{9,... | collective-permute-start | bytes 589832 | tf_op jit(solution)/shard_map/ppermute | solution.py:309
  7.0 4.1 %collective-permute-start.4 = (f32[1,8,1536]{2,1,0:T(8,128)S(1)}, f32[1,8,1536]{2,1,0:T(8,128)S(1)}, u32[]{:S(2)}, u32[]{:S(2)}) collective-permute-start(f32[1,8,1536]{2,1,0:T(8,128)S(1)} %collective-permute-done), channel_id=1, source_target_pairs={{0,7},{3,4},{4,11},{7,8},{8,15},{11,12},{12,19},{15,16},{16,23},{1... | collective-permute-start | bytes 147464 | tf_op jit(solution)/shard_map/ppermute | solution.py:334
  11.1 0.1 sine_multiply_fusion
  11.2 0.7 %collective-permute-start.2 = (f32[6,8,1536]{2,1,0:T(8,128)S(1)}, f32[6,8,1536]{2,1,0:T(8,128)S(1)}, u32[]{:S(2)}, u32[]{:S(2)}) collective-permute-start(f32[6,8,1536]{2,1,0:T(8,128)S(1)} %get-tuple-element.18.pair), channel_id=1, source_target_pairs={{1,2},{2,1},{5,6},{6,5},{9,10},{10,9},{13,14},{14,13},{17,18},{18,... | collective-permute-start | bytes 884744 | tf_op jit(solution)/shard_map/ppermute | solution.py:334
  11.9 0.1 collective-permute-start.1
  12.0 3.4 %collective-permute-start.6 = (f32[3,8,1536]{2,1,0:T(8,128)S(1)}, f32[3,8,1536]{2,1,0:T(8,128)S(1)}, u32[]{:S(2)}, u32[]{:S(2)}) collective-permute-start(f32[3,8,1536]{2,1,0:T(8,128)S(1)} %get-tuple-element.21), channel_id=1, source_target_pairs={{0,4},{4,8},{8,12},{12,16},{16,20},{20,24},{24,28},{1,5},{5,9},{9,... | collective-permute-start | bytes 442376 | tf_op jit(solution)/shard_map/ppermute | solution.py:309
  15.4 0.0 collective-permute-done.3.straight
  15.4 0.0 collective-permute-done.4
  15.4 0.3 collective-permute-start.5
  15.7 0.1 broadcast_select_fusion.spin
  15.8 1.0 %collective-permute-done.5.relayed = f32[2,8,1536]{2,1,0:T(8,128)S(1)} collective-permute-done((f32[2,8,1536]{2,1,0:T(8,128)S(1)}, f32[2,8,1536]{2,1,0:T(8,128)S(1)}, u32[]{:S(2)}, u32[]{:S(2)}) %collective-permute-start.5) | collective-permute-done | bytes 98336 | tf_op jit(solution)/shard_map/ppermute | solution.py:324
  16.8 0.0 collective-permute-done.2.pair_far
  16.8 0.1 iota.13.inside
  16.9 1.2 %shard_map.86 = (f32[3,8,1536]{2,1,0:T(8,128)S(1)}, f32[3,8,1536]{2,1,0:T(8,128)S(1)}) custom-call(f32[6,8,1536]{2,1,0:T(8,128)S(1)} %get-tuple-element.18.pair, f32[6,8,1536]{2,1,0:T(8,128)S(1)} %collective-permute-done.1.pair_near, f32[6,8,1536]{2,1,0:T(8,128)S(1)} %collective-permute-done.2.pair_far, f32[4,8,1536]{2,1,0:T(8,128)S(1)} %collective-permute-done.3.straight, ...), custom_call_target="tpu_custom_call" | custom-call | flops 1499136 | bytes 1499136 | tf_op jit(solution)/shard_map/pallas_call | solution.py:295
  18.1 1.3 %collective-permute-start.9 = (f32[3,8,1536]{2,1,0:T(8,128)S(1)}, f32[3,8,1536]{2,1,0:T(8,128)S(1)}, u32[]{:S(2)}, u32[]{:S(2)}) collective-permute-start(f32[3,8,1536]{2,1,0:T(8,128)S(1)} %get-tuple-element.24), channel_id=1, source_target_pairs={{4,0},{8,4},{12,8},{16,12},{20,16},{24,20},{28,24},{5,1},{9,5},{13... | collective-permute-start | bytes 442376 | tf_op jit(solution)/shard_map/ppermute | solution.py:309
  19.4 0.0 copy-start
  19.4 0.0 copy-start.1
  19.4 0.0 copy-start.2
  19.4 0.0 copy-start.3
  19.4 0.0 copy-start.4
  19.4 0.3 collective-permute-start.8
  19.7 0.7 %collective-permute-start.7 = (f32[3,8,1536]{2,1,0:T(8,128)S(1)}, f32[3,8,1536]{2,1,0:T(8,128)S(1)}, u32[]{:S(2)}, u32[]{:S(2)}) collective-permute-start(f32[3,8,1536]{2,1,0:T(8,128)S(1)} %get-tuple-element.22.state), channel_id=1, source_target_pairs={{1,2},{2,1},{5,6},{6,5},{9,10},{10,9},{13,14},{14,13},{17,18},{18,... | collective-permute-start | bytes 442376 | tf_op jit(solution)/shard_map/ppermute | solution.py:334
  20.4 1.2 %shard_map.87.tally = f32[2,8,128]{2,1,0:T(8,128)S(1)} custom-call(f32[6,8,1536]{2,1,0:T(8,128)S(1)} %get-tuple-element.18.pair, f32[6,8,1536]{2,1,0:T(8,128)S(1)} %collective-permute-done.1.pair_near, f32[6,8,1536]{2,1,0:T(8,128)S(1)} %collective-permute-done.2.pair_far, f32[4,8,1536]{2,1,0:T(8,128)S(1)} %collective-permute-done.3.straight, ...), custom_call_target="tpu_custom_call" | custom-call | flops 1507328 | bytes 1507328 | tf_op jit(solution)/shard_map/pallas_call | solution.py:295
  21.5 4.4 %collective-permute-done.9.back = f32[3,8,1536]{2,1,0:T(8,128)S(1)} collective-permute-done((f32[3,8,1536]{2,1,0:T(8,128)S(1)}, f32[3,8,1536]{2,1,0:T(8,128)S(1)}, u32[]{:S(2)}, u32[]{:S(2)}) %collective-permute-start.9) | collective-permute-done | bytes 147488 | tf_op jit(solution)/shard_map/ppermute | solution.py:309
  25.9 0.2 shard_map.88
  26.1 1.1 %shard_map.89.rest = f32[3,8,1536]{2,1,0:T(8,128)S(1)} custom-call(f32[3,8,1536]{2,1,0:T(8,128)S(1)} %get-tuple-element.22.state, f32[3,8,1536]{2,1,0:T(8,128)S(1)} %collective-permute-done.8.state_near, f32[4,8,1536]{2,1,0:T(8,128)S(1)} %collective-permute-done.3.straight, f32[2,8,1536]{2,1,0:T(8,128)S(1)} %collective-permute-done.5.relayed, ...), custom_call_target="tpu_custom_call" | custom-call | flops 909312 | bytes 909312 | tf_op jit(solution)/shard_map/pallas_call | solution.py:295
  27.3 0.2 shard_map.90
  27.5 13.1 %all_to_all.11 = f32[32,1,128]{2,1,0:T(1,128)S(1)} all-to-all(f32[32,1,128]{2,1,0:T(1,128)S(1)} %bitcast.5), channel_id=1, replica_groups=mesh['win'=8,'band'=2,'half'=2] {'win','band','half'}, dimensions={0} | all-to-all | bytes 32768 | tf_op jit(solution)/shard_map/all_to_all | solution.py:378
  40.6 1.3 %shard_map.91 = (f32[1,3,8,1536]{3,2,1,0:T(8,128)}, f32[1,3,8,1536]{3,2,1,0:T(8,128)}, f32[1,3,8,1536]{3,2,1,0:T(8,128)}) custom-call(f32[32,128]{1,0:T(8,128)S(1)} %bitcast.4, f32[1,3,8,1536]{3,2,1,0:T(8,128)S(1)} %copy-done, f32[1,3,8,1536]{3,2,1,0:T(8,128)S(1)} %copy-done.1, f32[1,3,8,1536]{3,2,1,0:T(8,128)S(1)} %copy-done.2, ...), custom_call_target="tpu_custom_call" | custom-call | flops 1343488 | bytes 1343488 | tf_op jit(solution)/shard_map/pallas_call | solution.py:295
  (12 shorter events, 0.1 us)
Async XLA Ops:
  0.6 1.8 %collective-permute-start = (f32[1,8,1536]{2,1,0:T(8,128)}, f32[1,8,1536]{2,1,0:T(8,128)S(1)}, u32[]{:S(2)}, u32[]{:S(2)}) collective-permute-start(f32[1,8,1536]{2,1,0:T(8,128)} %depth.1), channel_id=1, source_target_pairs={{0,1},{1,0},{2,3},{3,2},{4,5},{5,4},{6,7},{7,6},{8,9},{9,8},{10,11... | collective-permute-start | bytes 147464 | tf_op jit(solution)/shard_map/ppermute | solution.py:324
  2.5 12.9 %collective-permute-start.3 = (f32[4,8,1536]{2,1,0:T(8,128)S(1)}, f32[4,8,1536]{2,1,0:T(8,128)S(1)}, u32[]{:S(2)}, u32[]{:S(2)}) collective-permute-start(f32[4,8,1536]{2,1,0:T(8,128)S(1)} %get-tuple-element.19), channel_id=1, source_target_pairs={{0,4},{4,8},{8,12},{12,16},{16,20},{20,24},{24,28},{1,5},{5,9},{9,... | collective-permute-start | bytes 589832 | tf_op jit(solution)/shard_map/ppermute | solution.py:309
  7.0 8.4 %collective-permute-start.4 = (f32[1,8,1536]{2,1,0:T(8,128)S(1)}, f32[1,8,1536]{2,1,0:T(8,128)S(1)}, u32[]{:S(2)}, u32[]{:S(2)}) collective-permute-start(f32[1,8,1536]{2,1,0:T(8,128)S(1)} %collective-permute-done), channel_id=1, source_target_pairs={{0,7},{3,4},{4,11},{7,8},{8,15},{11,12},{12,19},{15,16},{16,23},{1... | collective-permute-start | bytes 147464 | tf_op jit(solution)/shard_map/ppermute | solution.py:334
  11.2 5.6 %collective-permute-start.2 = (f32[6,8,1536]{2,1,0:T(8,128)S(1)}, f32[6,8,1536]{2,1,0:T(8,128)S(1)}, u32[]{:S(2)}, u32[]{:S(2)}) collective-permute-start(f32[6,8,1536]{2,1,0:T(8,128)S(1)} %get-tuple-element.18.pair), channel_id=1, source_target_pairs={{1,2},{2,1},{5,6},{6,5},{9,10},{10,9},{13,14},{14,13},{17,18},{18,... | collective-permute-start | bytes 884744 | tf_op jit(solution)/shard_map/ppermute | solution.py:334
  11.9 4.9 %collective-permute-start.1 = (f32[6,8,1536]{2,1,0:T(8,128)S(1)}, f32[6,8,1536]{2,1,0:T(8,128)S(1)}, u32[]{:S(2)}, u32[]{:S(2)}) collective-permute-start(f32[6,8,1536]{2,1,0:T(8,128)S(1)} %get-tuple-element.18.pair), channel_id=1, source_target_pairs={{0,1},{1,0},{2,3},{3,2},{4,5},{5,4},{6,7},{7,6},{8,9},{9,8},{10,11... | collective-permute-start | bytes 884744 | tf_op jit(solution)/shard_map/ppermute | solution.py:324
  12.0 7.7 %collective-permute-start.6 = (f32[3,8,1536]{2,1,0:T(8,128)S(1)}, f32[3,8,1536]{2,1,0:T(8,128)S(1)}, u32[]{:S(2)}, u32[]{:S(2)}) collective-permute-start(f32[3,8,1536]{2,1,0:T(8,128)S(1)} %get-tuple-element.21), channel_id=1, source_target_pairs={{0,4},{4,8},{8,12},{12,16},{16,20},{20,24},{24,28},{1,5},{5,9},{9,... | collective-permute-start | bytes 442376 | tf_op jit(solution)/shard_map/ppermute | solution.py:309
  15.4 1.4 %collective-permute-start.5 = (f32[2,8,1536]{2,1,0:T(8,128)S(1)}, f32[2,8,1536]{2,1,0:T(8,128)S(1)}, u32[]{:S(2)}, u32[]{:S(2)}) collective-permute-start(f32[2,8,1536]{2,1,0:T(8,128)S(1)} %pad_maximum_fusion), channel_id=1, source_target_pairs={{0,1},{1,0},{2,3},{3,2},{4,5},{5,4},{6,7},{7,6},{8,9},{9,8},{10,11... | collective-permute-start | bytes 294920 | tf_op jit(solution)/shard_map/ppermute | solution.py:324
  18.1 7.9 %collective-permute-start.9 = (f32[3,8,1536]{2,1,0:T(8,128)S(1)}, f32[3,8,1536]{2,1,0:T(8,128)S(1)}, u32[]{:S(2)}, u32[]{:S(2)}) collective-permute-start(f32[3,8,1536]{2,1,0:T(8,128)S(1)} %get-tuple-element.24), channel_id=1, source_target_pairs={{4,0},{8,4},{12,8},{16,12},{20,16},{24,20},{28,24},{5,1},{9,5},{13... | collective-permute-start | bytes 442376 | tf_op jit(solution)/shard_map/ppermute | solution.py:309
  19.4 6.6 %copy-start = (f32[1,3,8,1536]{3,2,1,0:T(8,128)S(1)}, f32[1,3,8,1536]{3,2,1,0:T(8,128)}, u32[]{:S(2)}) copy-start(f32[1,3,8,1536]{3,2,1,0:T(8,128)} %p.5) | copy-start | bytes 442372
  19.4 6.5 %copy-start.1 = (f32[1,3,8,1536]{3,2,1,0:T(8,128)S(1)}, f32[1,3,8,1536]{3,2,1,0:T(8,128)}, u32[]{:S(2)}) copy-start(f32[1,3,8,1536]{3,2,1,0:T(8,128)} %m.5) | copy-start | bytes 442372
  19.4 6.5 %copy-start.2 = (f32[1,3,8,1536]{3,2,1,0:T(8,128)S(1)}, f32[1,3,8,1536]{3,2,1,0:T(8,128)}, u32[]{:S(2)}) copy-start(f32[1,3,8,1536]{3,2,1,0:T(8,128)} %dvar.5) | copy-start | bytes 442372
  19.4 6.5 %copy-start.3 = (f32[1,3,8,1536]{3,2,1,0:T(8,128)S(1)}, f32[1,3,8,1536]{3,2,1,0:T(8,128)}, u32[]{:S(2)}) copy-start(f32[1,3,8,1536]{3,2,1,0:T(8,128)} %rvar.5) | copy-start | bytes 442372
  19.4 6.5 %copy-start.4 = (f32[1,3,8,1536]{3,2,1,0:T(8,128)S(1)}, f32[1,3,8,1536]{3,2,1,0:T(8,128)}, u32[]{:S(2)}) copy-start(f32[1,3,8,1536]{3,2,1,0:T(8,128)} %hobs.5) | copy-start | bytes 442372
  19.4 6.7 %collective-permute-start.8 = (f32[3,8,1536]{2,1,0:T(8,128)S(1)}, f32[3,8,1536]{2,1,0:T(8,128)S(1)}, u32[]{:S(2)}, u32[]{:S(2)}) collective-permute-start(f32[3,8,1536]{2,1,0:T(8,128)S(1)} %get-tuple-element.22.state), channel_id=1, source_target_pairs={{0,1},{1,0},{2,3},{3,2},{4,5},{5,4},{6,7},{7,6},{8,9},{9,8},{10,11... | collective-permute-start | bytes 442376 | tf_op jit(solution)/shard_map/ppermute | solution.py:324
  19.7 7.6 %collective-permute-start.7 = (f32[3,8,1536]{2,1,0:T(8,128)S(1)}, f32[3,8,1536]{2,1,0:T(8,128)S(1)}, u32[]{:S(2)}, u32[]{:S(2)}) collective-permute-start(f32[3,8,1536]{2,1,0:T(8,128)S(1)} %get-tuple-element.22.state), channel_id=1, source_target_pairs={{1,2},{2,1},{5,6},{6,5},{9,10},{10,9},{13,14},{14,13},{17,18},{18,... | collective-permute-start | bytes 442376 | tf_op jit(solution)/shard_map/ppermute | solution.py:334

commit v17 on v16

--- a/solution.py
+++ b/solution.py
@@ -62,15 +62,16 @@
     return jnp.concatenate([tile[...]] * (width // 128), axis=1)
 
 
-def stretched(straight, relayed):
+def stretch_kernel(straight, depth_far, depth):
     even = even_lat()
-    low = jnp.where(even, relayed[1], relayed[0])
-    high = jnp.where(even, relayed[0], relayed[1])
-    return 0.25 * jnp.concatenate([low, straight[0], high], axis=0)
-
-
-def adjoint(pair, pair_near, pair_far, straight, relayed, spin, inside, base):
-    depth = stretched(straight, relayed)
+    rows = straight.shape[1]
+    depth[0:rows] = 0.25 * jnp.where(even, depth_far[0], straight[4])
+    depth[rows:2 * rows] = 0.25 * straight[0]
+    depth[2 * rows:] = 0.25 * jnp.where(even, straight[4], depth_far[0])
+
+
+def adjoint(pair, pair_near, pair_far, straight, depth, spin, inside, base):
+    depth = depth[...]
     turn, keep = widened(spin, depth.shape[1]), widened(inside, depth.shape[1])
     adj_height, adj_east, adj_north = [stacked(pair, pair_near, pair_far, base + part) for part in range(3)]
     for step in range(STEPS):
@@ -82,16 +83,16 @@
     return [value[rows:2 * rows] for value in (adj_height, adj_east, adj_north)]
 
 
-def first_adjoint_kernel(pair, pair_near, pair_far, straight, relayed, spin, inside, state, back):
-    swept = adjoint(pair, pair_near, pair_far, straight, relayed, spin, inside, 0)
+def first_adjoint_kernel(pair, pair_near, pair_far, straight, depth, spin, inside, state, back):
+    swept = adjoint(pair, pair_near, pair_far, straight, depth, spin, inside, 0)
     link = has_previous()
     for part, value in enumerate(swept):
         back[part] = value
         state[part] = jnp.where(link, straight[1 + part] - value, 0.0)
 
 
-def second_adjoint_kernel(pair, pair_near, pair_far, straight, relayed, spin, inside, local, state, tally):
-    swept = adjoint(pair, pair_near, pair_far, straight, relayed, spin, inside, 3)
+def second_adjoint_kernel(pair, pair_near, pair_far, straight, depth, spin, inside, local, state, tally):
+    swept = adjoint(pair, pair_near, pair_far, straight, depth, spin, inside, 3)
     link = has_previous()
     cross = square = 0.0
     for part, value in enumerate(swept):
@@ -137,8 +138,8 @@
     return height, east, north
 
 
-def inner_forward_kernel(state, state_near, straight, relayed, spin, inside, lead, rest):
-    depth = stretched(straight, relayed)
+def inner_forward_kernel(state, state_near, straight, depth, spin, inside, lead, rest):
+    depth = depth[...]
     turn, keep = widened(spin, depth.shape[1]), widened(inside, depth.shape[1])
     even = even_lat()
     rows = state.shape[1]
@@ -159,18 +160,14 @@
     return above - below
 
 
-def closing_kernel(state_far, rest, straight, relayed, spin, inside, sums, sent, remainder):
+def closing_kernel(state_far, rest, straight, depth, spin, inside, sums, sent, remainder):
     even = even_lat()
     rows, width = state_far.shape[1:]
     middle = lax.axis_index("band") != lax.axis_index("half")
 
     @pl.when(middle)
     def _():
-        depth = jnp.where(
-            even,
-            jnp.concatenate([relayed[1], straight[0]], axis=0),
-            jnp.concatenate([straight[0], relayed[1]], axis=0),
-        )
+        quarter = jnp.where(even, depth[:2 * rows], depth[rows:])
         turn, keep = [
             jnp.where(even, factor[:2 * rows], factor[rows:])
             for factor in (widened(spin, width), widened(inside, width))
@@ -184,7 +181,7 @@
             )
             for part in range(3)
         ]
-        for part, value in enumerate(forward(*fields, 0.25 * depth, turn, keep, open_lat_gap)):
+        for part, value in enumerate(forward(*fields, quarter, turn, keep, open_lat_gap)):
             remainder[part] = rest[part] - jnp.where(even, value[rows:], value[:rows])
 
     @pl.when(jnp.logical_not(middle))
@@ -324,14 +321,17 @@
     return lax.ppermute(value, ("band", "half"), pairs)
 
 
-def crossed(value, ends, win_step=0):
+def sent_on(value, steps, win_step):
     wins = lax.axis_size("win")
     pairs = []
-    for win in range(wins):
-        for source, target in (ends, ends[::-1]):
-            if 0 <= win + win_step < wins:
-                pairs.append((4 * win + source, 4 * (win + win_step) + target))
+    for win in range(wins - win_step):
+        for source, target in steps:
+            pairs.append((4 * win + source, 4 * (win + win_step) + target))
     return lax.ppermute(value, ("win", "band", "half"), pairs)
+
+
+def crossed(value, ends):
+    return sent_on(value, (ends, ends[::-1]), 0)
 
 
 def body(model_rhs, obs_rhs, model_var, obs_var, obs_weight, depth):
@@ -345,7 +345,7 @@
     spin = inside * (mass_rate * spin_rate * jnp.sin(latitude))
     fields = (3, rows, width)
 
-    middle, outer = (1, 2), (0, 3)
+    middle = (1, 2)
     pair, straight, local = run(
         prep_kernel, [(6, rows, width), (4, rows, width), fields],
         model_rhs, obs_rhs, model_var, obs_var, obs_weight, depth,
@@ -353,12 +353,12 @@
         space=pltpu.HBM,
     )
     depth_near = swapped(depth, 0)
-    depth_edge = crossed(depth_near, outer, 1)
+    depth_far = sent_on(depth_near, ((0, 2), (3, 1)), 1)
     pair, straight, local, _ = lax.optimization_barrier((pair, straight, local, depth_near))
-    came = shifted(straight, 1)
-    relayed = swapped(jnp.concatenate([came[:1], depth_edge]), 0)
+    came = shifted(jnp.concatenate([straight, depth_near]), 1)
     pair_near, pair_far = swapped(pair, 0), crossed(pair, middle)
-    known = (pair, pair_near, pair_far, came, relayed, spin, inside)
+    (stretched,) = run(stretch_kernel, [(3 * rows, width)], came, depth_far, work=100000)
+    known = (pair, pair_near, pair_far, came, stretched, spin, inside)
     local = shifted(local, 1)
     state, back = run(first_adjoint_kernel, [fields, fields], *known, work=4)
     held_state, local = lax.optimization_barrier((state, local))
@@ -370,9 +370,9 @@
         home_kernel, [fields, (4, rows, 128)],
         model_rhs, obs_rhs, model_var, obs_var, obs_weight, tally, back,
     )
-    (rest,) = run(inner_forward_kernel, [fields], state, state_near, came, relayed, spin, inside, lead)
+    (rest,) = run(inner_forward_kernel, [fields], state, state_near, came, stretched, spin, inside, lead)
     (sent,) = run(
-        closing_kernel, [(ranks, 128)], state_far, rest, came, relayed, spin, inside, sums,
+        closing_kernel, [(ranks, 128)], state_far, rest, came, stretched, spin, inside, sums,
         scratch=[pltpu.VMEM(fields, jnp.float32)],
     )
     gathered = lax.all_to_all(sent, ("win", "band", "half"), 0, 0, tiled=True)

time: 42.2 us -> 42.9 us (1.017)
  blocking collectives: 13.1 us -> 14.5 us
  waiting for transfers between devices: 5.43 us -> 4.66 us
    all_to_all x1, blocking collectives: 13.1 us -> 14.5 us  [body(): gathered = lax.all_to_all(sent, ('win', 'band', 'half'), 0, 0, tiled=True)]
    ppermute x4 -> x3, waiting for transfers between devices: 1.03 us -> 0.01 us  [swapped(): return lax.ppermute(value, ('band', 'half'), pairs)]
    ppermute x4 -> x3, starting transfers between devices: 1.13 us -> 1.06 us  [swapped(): return lax.ppermute(value, ('band', 'half'), pairs)]
    pallas_call x7 -> x8, Pallas kernels: 6.39 us -> 6.37 us  [run(): pl.pallas_call(kernel, out_shape=shapes, in_specs=[pl.BlockSpec(memory_sp...]
  transfers between devices with their start and end apart: 10 -> 9, of which waited for: 2 -> 2; matrix products, arithmetic and copies ran while one was open for 1% -> 0% of each run, Pallas kernels for 12% -> 12%
where the time goes in v17:
time: 42.9 us; the launch traced here: 42.6 us
  starting transfers between devices  16 us (37%)
  blocking collectives  14.5 us (34%)
  Pallas kernels  6.37 us (15%)
  waiting for transfers between devices  4.66 us (11%)
  between operations  0.86 us (2%)
    all_to_all x1, blocking collectives, body(): gathered = lax.all_to_all(sent, ('win', 'band', 'half'), 0, 0, tiled=True)  14.5 us
    ppermute x3, starting transfers between devices, shifted(): lax.ppermute(value, 'win', [(source, source + step) for source in range(i...  9.27 us
    pallas_call x8, Pallas kernels, run(): pl.pallas_call(kernel, out_shape=shapes, in_specs=[pl.BlockSpec(memory_sp...  6.37 us
    ppermute x3, starting transfers between devices, sent_on(): return lax.ppermute(value, ('win', 'band', 'half'), pairs)  5.67 us
    ppermute x3, waiting for transfers between devices, shifted(): lax.ppermute(value, 'win', [(source, source + step) for source in range(i...  4.64 us
    ppermute x3, starting transfers between devices, swapped(): return lax.ppermute(value, ('band', 'half'), pairs)  1.06 us
  transfers between devices with their start and end apart: 9, of which 2 were waited for; matrix products, arithmetic and copies ran while one was open for 0% of the time, Pallas kernels for 12%

profile of v17, /device:TPU:0, one launch (start us, length us, event | category | flops | bytes accessed | tf_op | source)
XLA Modules:
  0.0 42.6 jit_solution(4055617717780922369)
XLA Ops:
  0.6 0.5 %collective-permute-start = (f32[1,8,1536]{2,1,0:T(8,128)}, f32[1,8,1536]{2,1,0:T(8,128)S(1)}, u32[]{:S(2)}, u32[]{:S(2)}) collective-permute-start(f32[1,8,1536]{2,1,0:T(8,128)} %depth.1), channel_id=1, source_target_pairs={{0,1},{1,0},{2,3},{3,2},{4,5},{5,4},{6,7},{7,6},{8,9},{9,8},{10,11... | collective-permute-start | bytes 147464 | tf_op jit(solution)/shard_map/ppermute | solution.py:321
  1.2 1.3 %shard_map.85 = (f32[6,8,1536]{2,1,0:T(8,128)S(1)}, f32[4,8,1536]{2,1,0:T(8,128)S(1)}, f32[3,8,1536]{2,1,0:T(8,128)S(1)}) custom-call(f32[1,3,8,1536]{3,2,1,0:T(8,128)} %p.5, f32[1,3,8,1536]{3,2,1,0:T(8,128)} %m.5, f32[1,3,8,1536]{3,2,1,0:T(8,128)} %dvar.5, f32[1,3,8,1536]{3,2,1,0:T(8,128)} %rvar.5, f32[1,3,8,1536]{3,2,1,0:T(8,128)} %hobs.5, f32[1,8,1536]{2,1,0:T(8,128)} %depth.1), custom_call_target="tpu_custom_call" | custom-call | flops 1425408 | bytes 1425408 | tf_op jit(solution)/shard_map/pallas_call | solution.py:292
  2.5 0.0 collective-permute-done
  2.5 4.5 %collective-permute-start.3 = (f32[5,8,1536]{2,1,0:T(8,128)S(1)}, f32[5,8,1536]{2,1,0:T(8,128)S(1)}, u32[]{:S(2)}, u32[]{:S(2)}) collective-permute-start(f32[5,8,1536]{2,1,0:T(8,128)S(1)} %pad_maximum_fusion), channel_id=1, source_target_pairs={{0,4},{4,8},{8,12},{12,16},{16,20},{20,24},{24,28},{1,5},{5,9},{9,... | collective-permute-start | bytes 737288 | tf_op jit(solution)/shard_map/ppermute | solution.py:306
  7.1 0.1 sine_multiply_fusion
  7.1 4.3 %collective-permute-start.4 = (f32[1,8,1536]{2,1,0:T(8,128)S(1)}, f32[1,8,1536]{2,1,0:T(8,128)S(1)}, u32[]{:S(2)}, u32[]{:S(2)}) collective-permute-start(f32[1,8,1536]{2,1,0:T(8,128)S(1)} %collective-permute-done), channel_id=1, source_target_pairs={{0,6},{3,5},{4,10},{7,9},{8,14},{11,13},{12,18},{15,17},{16,22},{1... | collective-permute-start | bytes 147464 | tf_op jit(solution)/shard_map/ppermute | solution.py:330
  11.5 0.1 broadcast_select_fusion.spin
  11.5 0.7 %collective-permute-start.2 = (f32[6,8,1536]{2,1,0:T(8,128)S(1)}, f32[6,8,1536]{2,1,0:T(8,128)S(1)}, u32[]{:S(2)}, u32[]{:S(2)}) collective-permute-start(f32[6,8,1536]{2,1,0:T(8,128)S(1)} %get-tuple-element.18.pair), channel_id=1, source_target_pairs={{1,2},{2,1},{5,6},{6,5},{9,10},{10,9},{13,14},{14,13},{17,18},{18,... | collective-permute-start | bytes 884744 | tf_op jit(solution)/shard_map/ppermute | solution.py:330
  12.2 0.1 collective-permute-start.1
  12.3 3.4 %collective-permute-start.5 = (f32[3,8,1536]{2,1,0:T(8,128)S(1)}, f32[3,8,1536]{2,1,0:T(8,128)S(1)}, u32[]{:S(2)}, u32[]{:S(2)}) collective-permute-start(f32[3,8,1536]{2,1,0:T(8,128)S(1)} %get-tuple-element.21), channel_id=1, source_target_pairs={{0,4},{4,8},{8,12},{12,16},{16,20},{20,24},{24,28},{1,5},{5,9},{9,... | collective-permute-start | bytes 442376 | tf_op jit(solution)/shard_map/ppermute | solution.py:306
  15.7 0.0 collective-permute-done.4.depth_far
  15.7 0.0 collective-permute-done.3.straight
  15.8 0.0 collective-permute-done.2.pair_far
  15.8 0.1 iota.13.inside
  15.9 1.1 %shard_map.87 = (f32[3,8,1536]{2,1,0:T(8,128)S(1)}, f32[3,8,1536]{2,1,0:T(8,128)S(1)}) custom-call(f32[6,8,1536]{2,1,0:T(8,128)S(1)} %get-tuple-element.18.pair, f32[6,8,1536]{2,1,0:T(8,128)S(1)} %collective-permute-done.1.pair_near, f32[6,8,1536]{2,1,0:T(8,128)S(1)} %collective-permute-done.2.pair_far, f32[5,8,1536]{2,1,0:T(8,128)S(1)} %collective-permute-done.3.straight, ...), custom_call_target="tpu_custom_call" | custom-call | flops 1597440 | bytes 1597440 | tf_op jit(solution)/shard_map/pallas_call | solution.py:292
  17.0 1.3 %collective-permute-start.8 = (f32[3,8,1536]{2,1,0:T(8,128)S(1)}, f32[3,8,1536]{2,1,0:T(8,128)S(1)}, u32[]{:S(2)}, u32[]{:S(2)}) collective-permute-start(f32[3,8,1536]{2,1,0:T(8,128)S(1)} %get-tuple-element.24), channel_id=1, source_target_pairs={{4,0},{8,4},{12,8},{16,12},{20,16},{24,20},{28,24},{5,1},{9,5},{13... | collective-permute-start | bytes 442376 | tf_op jit(solution)/shard_map/ppermute | solution.py:306
  18.3 0.0 copy-start
  18.3 0.0 copy-start.1
  18.3 0.0 copy-start.2
  18.3 0.0 copy-start.3
  18.4 0.0 copy-start.4
  18.4 0.5 %collective-permute-start.7 = (f32[3,8,1536]{2,1,0:T(8,128)S(1)}, f32[3,8,1536]{2,1,0:T(8,128)S(1)}, u32[]{:S(2)}, u32[]{:S(2)}) collective-permute-start(f32[3,8,1536]{2,1,0:T(8,128)S(1)} %get-tuple-element.22.state), channel_id=1, source_target_pairs={{0,1},{1,0},{2,3},{3,2},{4,5},{5,4},{6,7},{7,6},{8,9},{9,8},{10,11... | collective-permute-start | bytes 442376 | tf_op jit(solution)/shard_map/ppermute | solution.py:321
  18.8 0.6 %collective-permute-done.5.local = f32[3,8,1536]{2,1,0:T(8,128)S(1)} collective-permute-done((f32[3,8,1536]{2,1,0:T(8,128)S(1)}, f32[3,8,1536]{2,1,0:T(8,128)S(1)}, u32[]{:S(2)}, u32[]{:S(2)}) %collective-permute-start.5) | collective-permute-done | bytes 147488 | tf_op jit(solution)/shard_map/ppermute | solution.py:306
  19.5 0.7 %collective-permute-start.6 = (f32[3,8,1536]{2,1,0:T(8,128)S(1)}, f32[3,8,1536]{2,1,0:T(8,128)S(1)}, u32[]{:S(2)}, u32[]{:S(2)}) collective-permute-start(f32[3,8,1536]{2,1,0:T(8,128)S(1)} %get-tuple-element.22.state), channel_id=1, source_target_pairs={{1,2},{2,1},{5,6},{6,5},{9,10},{10,9},{13,14},{14,13},{17,18},{18,... | collective-permute-start | bytes 442376 | tf_op jit(solution)/shard_map/ppermute | solution.py:330
  20.1 1.1 %shard_map.88.tally = f32[2,8,128]{2,1,0:T(8,128)S(1)} custom-call(f32[6,8,1536]{2,1,0:T(8,128)S(1)} %get-tuple-element.18.pair, f32[6,8,1536]{2,1,0:T(8,128)S(1)} %collective-permute-done.1.pair_near, f32[6,8,1536]{2,1,0:T(8,128)S(1)} %collective-permute-done.2.pair_far, f32[5,8,1536]{2,1,0:T(8,128)S(1)} %collective-permute-done.3.straight, ...), custom_call_target="tpu_custom_call" | custom-call | flops 1605632 | bytes 1605632 | tf_op jit(solution)/shard_map/pallas_call | solution.py:292
  21.3 4.0 %collective-permute-done.8.back = f32[3,8,1536]{2,1,0:T(8,128)S(1)} collective-permute-done((f32[3,8,1536]{2,1,0:T(8,128)S(1)}, f32[3,8,1536]{2,1,0:T(8,128)S(1)}, u32[]{:S(2)}, u32[]{:S(2)}) %collective-permute-start.8) | collective-permute-done | bytes 147488 | tf_op jit(solution)/shard_map/ppermute | solution.py:306
  25.3 0.2 shard_map.89
  25.5 0.0 collective-permute-done.7.state_near
  25.5 1.1 %shard_map.90.rest = f32[3,8,1536]{2,1,0:T(8,128)S(1)} custom-call(f32[3,8,1536]{2,1,0:T(8,128)S(1)} %get-tuple-element.22.state, f32[3,8,1536]{2,1,0:T(8,128)S(1)} %collective-permute-done.7.state_near, f32[5,8,1536]{2,1,0:T(8,128)S(1)} %collective-permute-done.3.straight, f32[24,1536]{1,0:T(8,128)S(1)} %shard_map.86.depth, ...), custom_call_target="tpu_custom_call" | custom-call | flops 1007616 | bytes 1007616 | tf_op jit(solution)/shard_map/pallas_call | solution.py:292
  26.7 0.2 shard_map.91
  26.9 14.5 %all_to_all.11 = f32[32,1,128]{2,1,0:T(1,128)S(1)} all-to-all(f32[32,1,128]{2,1,0:T(1,128)S(1)} %bitcast.5), channel_id=1, replica_groups=mesh['win'=8,'band'=2,'half'=2] {'win','band','half'}, dimensions={0} | all-to-all | bytes 32768 | tf_op jit(solution)/shard_map/all_to_all | solution.py:378
  41.3 1.3 %shard_map.92 = (f32[1,3,8,1536]{3,2,1,0:T(8,128)}, f32[1,3,8,1536]{3,2,1,0:T(8,128)}, f32[1,3,8,1536]{3,2,1,0:T(8,128)}) custom-call(f32[32,128]{1,0:T(8,128)S(1)} %bitcast.4, f32[1,3,8,1536]{3,2,1,0:T(8,128)S(1)} %copy-done, f32[1,3,8,1536]{3,2,1,0:T(8,128)S(1)} %copy-done.1, f32[1,3,8,1536]{3,2,1,0:T(8,128)S(1)} %copy-done.2, ...), custom_call_target="tpu_custom_call" | custom-call | flops 1343488 | bytes 1343488 | tf_op jit(solution)/shard_map/pallas_call | solution.py:292
  (10 shorter events, 0.1 us)
Async XLA Ops:
  0.6 1.8 %collective-permute-start = (f32[1,8,1536]{2,1,0:T(8,128)}, f32[1,8,1536]{2,1,0:T(8,128)S(1)}, u32[]{:S(2)}, u32[]{:S(2)}) collective-permute-start(f32[1,8,1536]{2,1,0:T(8,128)} %depth.1), channel_id=1, source_target_pairs={{0,1},{1,0},{2,3},{3,2},{4,5},{5,4},{6,7},{7,6},{8,9},{9,8},{10,11... | collective-permute-start | bytes 147464 | tf_op jit(solution)/shard_map/ppermute | solution.py:321
  2.5 13.2 %collective-permute-start.3 = (f32[5,8,1536]{2,1,0:T(8,128)S(1)}, f32[5,8,1536]{2,1,0:T(8,128)S(1)}, u32[]{:S(2)}, u32[]{:S(2)}) collective-permute-start(f32[5,8,1536]{2,1,0:T(8,128)S(1)} %pad_maximum_fusion), channel_id=1, source_target_pairs={{0,4},{4,8},{8,12},{12,16},{16,20},{20,24},{24,28},{1,5},{5,9},{9,... | collective-permute-start | bytes 737288 | tf_op jit(solution)/shard_map/ppermute | solution.py:306
  7.1 8.6 %collective-permute-start.4 = (f32[1,8,1536]{2,1,0:T(8,128)S(1)}, f32[1,8,1536]{2,1,0:T(8,128)S(1)}, u32[]{:S(2)}, u32[]{:S(2)}) collective-permute-start(f32[1,8,1536]{2,1,0:T(8,128)S(1)} %collective-permute-done), channel_id=1, source_target_pairs={{0,6},{3,5},{4,10},{7,9},{8,14},{11,13},{12,18},{15,17},{16,22},{1... | collective-permute-start | bytes 147464 | tf_op jit(solution)/shard_map/ppermute | solution.py:330
  11.5 4.2 %collective-permute-start.2 = (f32[6,8,1536]{2,1,0:T(8,128)S(1)}, f32[6,8,1536]{2,1,0:T(8,128)S(1)}, u32[]{:S(2)}, u32[]{:S(2)}) collective-permute-start(f32[6,8,1536]{2,1,0:T(8,128)S(1)} %get-tuple-element.18.pair), channel_id=1, source_target_pairs={{1,2},{2,1},{5,6},{6,5},{9,10},{10,9},{13,14},{14,13},{17,18},{18,... | collective-permute-start | bytes 884744 | tf_op jit(solution)/shard_map/ppermute | solution.py:330
  12.2 3.6 %collective-permute-start.1 = (f32[6,8,1536]{2,1,0:T(8,128)S(1)}, f32[6,8,1536]{2,1,0:T(8,128)S(1)}, u32[]{:S(2)}, u32[]{:S(2)}) collective-permute-start(f32[6,8,1536]{2,1,0:T(8,128)S(1)} %get-tuple-element.18.pair), channel_id=1, source_target_pairs={{0,1},{1,0},{2,3},{3,2},{4,5},{5,4},{6,7},{7,6},{8,9},{9,8},{10,11... | collective-permute-start | bytes 884744 | tf_op jit(solution)/shard_map/ppermute | solution.py:321
  12.3 7.2 %collective-permute-start.5 = (f32[3,8,1536]{2,1,0:T(8,128)S(1)}, f32[3,8,1536]{2,1,0:T(8,128)S(1)}, u32[]{:S(2)}, u32[]{:S(2)}) collective-permute-start(f32[3,8,1536]{2,1,0:T(8,128)S(1)} %get-tuple-element.21), channel_id=1, source_target_pairs={{0,4},{4,8},{8,12},{12,16},{16,20},{20,24},{24,28},{1,5},{5,9},{9,... | collective-permute-start | bytes 442376 | tf_op jit(solution)/shard_map/ppermute | solution.py:306
  17.0 8.3 %collective-permute-start.8 = (f32[3,8,1536]{2,1,0:T(8,128)S(1)}, f32[3,8,1536]{2,1,0:T(8,128)S(1)}, u32[]{:S(2)}, u32[]{:S(2)}) collective-permute-start(f32[3,8,1536]{2,1,0:T(8,128)S(1)} %get-tuple-element.24), channel_id=1, source_target_pairs={{4,0},{8,4},{12,8},{16,12},{20,16},{24,20},{28,24},{5,1},{9,5},{13... | collective-permute-start | bytes 442376 | tf_op jit(solution)/shard_map/ppermute | solution.py:306
  18.3 7.0 %copy-start = (f32[1,3,8,1536]{3,2,1,0:T(8,128)S(1)}, f32[1,3,8,1536]{3,2,1,0:T(8,128)}, u32[]{:S(2)}) copy-start(f32[1,3,8,1536]{3,2,1,0:T(8,128)} %p.5) | copy-start | bytes 442372
  18.3 7.0 %copy-start.1 = (f32[1,3,8,1536]{3,2,1,0:T(8,128)S(1)}, f32[1,3,8,1536]{3,2,1,0:T(8,128)}, u32[]{:S(2)}) copy-start(f32[1,3,8,1536]{3,2,1,0:T(8,128)} %m.5) | copy-start | bytes 442372
  18.3 7.0 %copy-start.2 = (f32[1,3,8,1536]{3,2,1,0:T(8,128)S(1)}, f32[1,3,8,1536]{3,2,1,0:T(8,128)}, u32[]{:S(2)}) copy-start(f32[1,3,8,1536]{3,2,1,0:T(8,128)} %dvar.5) | copy-start | bytes 442372
  18.3 7.0 %copy-start.3 = (f32[1,3,8,1536]{3,2,1,0:T(8,128)S(1)}, f32[1,3,8,1536]{3,2,1,0:T(8,128)}, u32[]{:S(2)}) copy-start(f32[1,3,8,1536]{3,2,1,0:T(8,128)} %rvar.5) | copy-start | bytes 442372
  18.4 7.0 %copy-start.4 = (f32[1,3,8,1536]{3,2,1,0:T(8,128)S(1)}, f32[1,3,8,1536]{3,2,1,0:T(8,128)}, u32[]{:S(2)}) copy-start(f32[1,3,8,1536]{3,2,1,0:T(8,128)} %hobs.5) | copy-start | bytes 442372
  18.4 7.1 %collective-permute-start.7 = (f32[3,8,1536]{2,1,0:T(8,128)S(1)}, f32[3,8,1536]{2,1,0:T(8,128)S(1)}, u32[]{:S(2)}, u32[]{:S(2)}) collective-permute-start(f32[3,8,1536]{2,1,0:T(8,128)S(1)} %get-tuple-element.22.state), channel_id=1, source_target_pairs={{0,1},{1,0},{2,3},{3,2},{4,5},{5,4},{6,7},{7,6},{8,9},{9,8},{10,11... | collective-permute-start | bytes 442376 | tf_op jit(solution)/shard_map/ppermute | solution.py:321
  19.5 7.2 %collective-permute-start.6 = (f32[3,8,1536]{2,1,0:T(8,128)S(1)}, f32[3,8,1536]{2,1,0:T(8,128)S(1)}, u32[]{:S(2)}, u32[]{:S(2)}) collective-permute-start(f32[3,8,1536]{2,1,0:T(8,128)S(1)} %get-tuple-element.22.state), channel_id=1, source_target_pairs={{1,2},{2,1},{5,6},{6,5},{9,10},{10,9},{13,14},{14,13},{17,18},{18,... | collective-permute-start | bytes 442376 | tf_op jit(solution)/shard_map/ppermute | solution.py:330

commit v18 on v16

--- a/solution.py
+++ b/solution.py
@@ -93,26 +93,44 @@
 def second_adjoint_kernel(pair, pair_near, pair_far, straight, relayed, spin, inside, local, state, tally):
     swept = adjoint(pair, pair_near, pair_far, straight, relayed, spin, inside, 3)
     link = has_previous()
-    cross = square = 0.0
+    zero = jnp.zeros((pair.shape[1], 128), jnp.float32)
+    cross = square = (zero, zero)
     for part, value in enumerate(swept):
         zx = jnp.where(link, local[part] - value, 0.0)
-        cross += lane_sum(zx * state[part])
-        square += lane_sum(zx * zx)
-    tally[0] = cross
-    tally[1] = square
+        cross = gathered_in(cross, zx * state[part])
+        square = gathered_in(square, zx * zx)
+    for slot, value in enumerate(cross + square):
+        tally[slot] = value
 
 
 def lane_sum(value):
-    rows, width = value.shape
-    total = value[:, :128]
-    for start in range(128, width, 128):
-        total = total + value[:, start:start + 128]
-    return total
+    tiles = [value[:, start:start + 128] for start in range(0, value.shape[1], 128)]
+    while len(tiles) > 1:
+        tiles = [sum(tiles[at:at + 2]) for at in range(0, len(tiles), 2)]
+    return tiles[0]
+
+
+def two_sum(a, b):
+    total = a + b
+    part = total - a
+    return total, (a - (total - part)) + (b - part)
+
+
+def gathered_in(pair, value):
+    total, rest = two_sum(pair[0], lane_sum(value))
+    return total, pair[1] + rest
+
+
+def folded(pair, shift, axis):
+    total, rest = two_sum(pair[0], pltpu.roll(pair[0], shift, axis))
+    return total, pair[1] + pltpu.roll(pair[1], shift, axis) + rest
 
 
 def home_kernel(p, m, dvar, rvar, hobs, tally, back, lead, sums):
     last = lax.axis_index("win") == lax.axis_size("win") - 1
-    moments = [0.0, 0.0, 2.0 * tally[0], tally[1]]
+    zero = jnp.zeros_like(tally[0])
+    m1 = m2 = (zero, zero)
+    m3, m4 = (2.0 * tally[0], 2.0 * tally[1]), (tally[2], tally[3])
     for part in range(3):
         dv, rv, hv = dvar[0, part], rvar[0, part], hobs[0, part]
         pv, mv = p[0, part], m[0, part]
@@ -121,12 +139,12 @@
         lead[part] = dv * up + ux
         zm = rv * um + hv * ux
         zx = jnp.where(last, up + hv * um, 0.0)
-        moments[0] += lane_sum(up * pv + um * mv)
-        moments[1] += lane_sum(up * up + um * um + ux * ux)
-        moments[2] += lane_sum(dv * up * up + rv * um * um + 2.0 * (zx * ux))
-        moments[3] += lane_sum(zm * zm + zx * zx)
-    for row, value in enumerate(moments):
-        sums[row] = value
+        m1 = gathered_in(m1, up * pv + um * mv)
+        m2 = gathered_in(m2, up * up + um * um + ux * ux)
+        m3 = gathered_in(m3, dv * up * up + rv * um * um + 2.0 * (zx * ux))
+        m4 = gathered_in(m4, zm * zm + zx * zx)
+    for slot, value in enumerate(m1 + m2 + m3 + m4):
+        sums[slot] = value
 
 
 def forward(height, east, north, depth, turn, keep, gap):
@@ -192,32 +210,17 @@
         for part in range(3):
             remainder[part] = rest[part]
 
-    square = 0.0
-    for part in range(3):
-        square += lane_sum(remainder[part] * remainder[part])
-    moments = [sums[0], sums[1], sums[2], sums[3] + square]
-    lane = lax.broadcasted_iota(jnp.int32, (1, 128), 1)
+    moments = [(sums[slot], sums[slot + 1]) for slot in range(0, 8, 2)]
+    for part in range(3):
+        moments[3] = gathered_in(moments[3], remainder[part] * remainder[part])
+    lane = lax.broadcasted_iota(jnp.int32, (rows, 128), 1) // 16
     row = 0.0
-    for slot, value in enumerate(moments):
-        folded = jnp.sum(value, axis=0, keepdims=True)
-        folded = folded + pltpu.roll(folded, 64, 1)
-        folded = folded + pltpu.roll(folded, 32, 1)
-        row = jnp.where(lane // 32 == slot, folded, row)
-    sent[...] = jnp.broadcast_to(row, sent.shape)
-
-
-def lane_sum(value):
-    rows, width = value.shape
-    total = value[:, :128]
-    for start in range(128, width, 128):
-        total = total + value[:, start:start + 128]
-    return total
-
-
-def two_sum(a, b):
-    total = a + b
-    part = total - a
-    return total, (a - (total - part)) + (b - part)
+    for slot, pair in enumerate(moments):
+        for axis, shift in ((0, 4), (0, 2), (0, 1), (1, 64), (1, 32), (1, 16)):
+            pair = folded(pair, shift, axis)
+        row = jnp.where(lane == slot, pair[0], jnp.where(lane == slot + 4, pair[1], row))
+    for start in range(0, sent.shape[0], rows):
+        sent[start:start + rows] = row
 
 
 def split(a):
@@ -244,15 +247,20 @@
 
 
 def coefficients(gathered):
-    top = jnp.sum(gathered[...], axis=0, keepdims=True)
-    low = jnp.zeros_like(top)
-    shift = 1
-    while shift < 32:
-        top, rest = two_sum(top, pltpu.roll(top, shift, 1))
-        low = low + pltpu.roll(low, shift, 1) + rest
-        shift *= 2
-    tops = [jnp.broadcast_to(top[:, lane:lane + 1], (1, 128)) for lane in range(31, 128, 32)]
-    lows = [jnp.broadcast_to(low[:, lane:lane + 1], (1, 128)) for lane in range(31, 128, 32)]
+    pair = gathered[0:8], jnp.zeros((8, 128), jnp.float32)
+    for start in range(8, gathered.shape[0], 8):
+        total, rest = two_sum(pair[0], gathered[start:start + 8])
+        pair = total, pair[1] + rest
+    for axis, shift in ((0, 4), (0, 2), (0, 1), (1, 1), (1, 2), (1, 4), (1, 8)):
+        pair = folded(pair, shift, axis)
+    tops, lows = [], []
+    for lane in range(15, 64, 16):
+        top, low = [
+            jnp.broadcast_to(value[0:1, at:at + 1], (1, 128))
+            for value, at in ((pair[0], lane), (pair[1] + pltpu.roll(pair[0], 64, 1), lane))
+        ]
+        tops.append(top)
+        lows.append(low)
     scale = 1.0 / tops[1]
     moments = []
     for value, rest in zip(tops, lows):
@@ -364,10 +372,10 @@
     held_state, local = lax.optimization_barrier((state, local))
     back = shifted(back, -1)
     state_far = crossed(held_state, middle)
-    (tally,) = run(second_adjoint_kernel, [(2, rows, 128)], *known, local, state)
+    (tally,) = run(second_adjoint_kernel, [(4, rows, 128)], *known, local, state)
     state_near = swapped(state, 0)
     lead, sums = run(
-        home_kernel, [fields, (4, rows, 128)],
+        home_kernel, [fields, (8, rows, 128)],
         model_rhs, obs_rhs, model_var, obs_var, obs_weight, tally, back,
     )
     (rest,) = run(inner_forward_kernel, [fields], state, state_near, came, relayed, spin, inside, lead)

time: 42.2 us -> 42.2 us (level)
  no operation moved by 1% of the time
where the time goes in v18:
time: 42.2 us; the launch traced here: 42 us
  starting transfers between devices  15.8 us (37%)
  blocking collectives  13.1 us (31%)
  Pallas kernels  6.48 us (15%)
  waiting for transfers between devices  5.43 us (13%)
  between operations  0.84 us (2%)
    all_to_all x1, blocking collectives, body(): gathered = lax.all_to_all(sent, ('win', 'band', 'half'), 0, 0, tiled=True)  13.1 us
    ppermute x3, starting transfers between devices, shifted(): lax.ppermute(value, 'win', [(source, source + step) for source in range(i...  9.27 us
    pallas_call x7, Pallas kernels, run(): pl.pallas_call(kernel, out_shape=shapes, in_specs=[pl.BlockSpec(memory_sp...  6.48 us
    ppermute x3, starting transfers between devices, crossed(): return lax.ppermute(value, ('win', 'band', 'half'), pairs)  5.44 us
    ppermute x3, waiting for transfers between devices, shifted(): lax.ppermute(value, 'win', [(source, source + step) for source in range(i...  4.39 us
    ppermute x4, starting transfers between devices, swapped(): return lax.ppermute(value, ('band', 'half'), pairs)  1.13 us
    ppermute x4, waiting for transfers between devices, swapped(): return lax.ppermute(value, ('band', 'half'), pairs)  1.03 us
  transfers between devices with their start and end apart: 10, of which 2 were waited for; matrix products, arithmetic and copies ran while one was open for 1% of the time, Pallas kernels for 12%

profile of v18, /device:TPU:0, one launch (start us, length us, event | category | flops | bytes accessed | tf_op | source)
XLA Modules:
  0.0 42.0 jit_solution(12053496750097640792)
XLA Ops:
  0.6 0.5 %collective-permute-start = (f32[1,8,1536]{2,1,0:T(8,128)}, f32[1,8,1536]{2,1,0:T(8,128)S(1)}, u32[]{:S(2)}, u32[]{:S(2)}) collective-permute-start(f32[1,8,1536]{2,1,0:T(8,128)} %depth.1), channel_id=1, source_target_pairs={{0,1},{1,0},{2,3},{3,2},{4,5},{5,4},{6,7},{7,6},{8,9},{9,8},{10,11... | collective-permute-start | bytes 147464 | tf_op jit(solution)/shard_map/ppermute | solution.py:332
  1.1 1.3 %shard_map.85 = (f32[6,8,1536]{2,1,0:T(8,128)S(1)}, f32[4,8,1536]{2,1,0:T(8,128)S(1)}, f32[3,8,1536]{2,1,0:T(8,128)S(1)}) custom-call(f32[1,3,8,1536]{3,2,1,0:T(8,128)} %p.5, f32[1,3,8,1536]{3,2,1,0:T(8,128)} %m.5, f32[1,3,8,1536]{3,2,1,0:T(8,128)} %dvar.5, f32[1,3,8,1536]{3,2,1,0:T(8,128)} %rvar.5, f32[1,3,8,1536]{3,2,1,0:T(8,128)} %hobs.5, f32[1,8,1536]{2,1,0:T(8,128)} %depth.1), custom_call_target="tpu_custom_call" | custom-call | flops 1425408 | bytes 1425408 | tf_op jit(solution)/shard_map/pallas_call | solution.py:303
  2.5 0.0 collective-permute-done
  2.5 4.5 %collective-permute-start.3 = (f32[4,8,1536]{2,1,0:T(8,128)S(1)}, f32[4,8,1536]{2,1,0:T(8,128)S(1)}, u32[]{:S(2)}, u32[]{:S(2)}) collective-permute-start(f32[4,8,1536]{2,1,0:T(8,128)S(1)} %get-tuple-element.19), channel_id=1, source_target_pairs={{0,4},{4,8},{8,12},{12,16},{16,20},{20,24},{24,28},{1,5},{5,9},{9,... | collective-permute-start | bytes 589832 | tf_op jit(solution)/shard_map/ppermute | solution.py:317
  7.0 4.1 %collective-permute-start.4 = (f32[1,8,1536]{2,1,0:T(8,128)S(1)}, f32[1,8,1536]{2,1,0:T(8,128)S(1)}, u32[]{:S(2)}, u32[]{:S(2)}) collective-permute-start(f32[1,8,1536]{2,1,0:T(8,128)S(1)} %collective-permute-done), channel_id=1, source_target_pairs={{0,7},{3,4},{4,11},{7,8},{8,15},{11,12},{12,19},{15,16},{16,23},{1... | collective-permute-start | bytes 147464 | tf_op jit(solution)/shard_map/ppermute | solution.py:342
  11.1 0.1 sine_multiply_fusion
  11.2 0.7 %collective-permute-start.2 = (f32[6,8,1536]{2,1,0:T(8,128)S(1)}, f32[6,8,1536]{2,1,0:T(8,128)S(1)}, u32[]{:S(2)}, u32[]{:S(2)}) collective-permute-start(f32[6,8,1536]{2,1,0:T(8,128)S(1)} %get-tuple-element.18.pair), channel_id=1, source_target_pairs={{1,2},{2,1},{5,6},{6,5},{9,10},{10,9},{13,14},{14,13},{17,18},{18,... | collective-permute-start | bytes 884744 | tf_op jit(solution)/shard_map/ppermute | solution.py:342
  11.9 0.1 collective-permute-start.1
  12.0 3.4 %collective-permute-start.6 = (f32[3,8,1536]{2,1,0:T(8,128)S(1)}, f32[3,8,1536]{2,1,0:T(8,128)S(1)}, u32[]{:S(2)}, u32[]{:S(2)}) collective-permute-start(f32[3,8,1536]{2,1,0:T(8,128)S(1)} %get-tuple-element.21), channel_id=1, source_target_pairs={{0,4},{4,8},{8,12},{12,16},{16,20},{20,24},{24,28},{1,5},{5,9},{9,... | collective-permute-start | bytes 442376 | tf_op jit(solution)/shard_map/ppermute | solution.py:317
  15.4 0.0 collective-permute-done.3.straight
  15.4 0.0 collective-permute-done.4
  15.4 0.3 collective-permute-start.5
  15.7 0.1 broadcast_select_fusion.spin
  15.8 1.0 %collective-permute-done.5.relayed = f32[2,8,1536]{2,1,0:T(8,128)S(1)} collective-permute-done((f32[2,8,1536]{2,1,0:T(8,128)S(1)}, f32[2,8,1536]{2,1,0:T(8,128)S(1)}, u32[]{:S(2)}, u32[]{:S(2)}) %collective-permute-start.5) | collective-permute-done | bytes 98336 | tf_op jit(solution)/shard_map/ppermute | solution.py:332
  16.8 0.0 collective-permute-done.2.pair_far
  16.8 0.1 iota.13.inside
  16.9 1.2 %shard_map.86 = (f32[3,8,1536]{2,1,0:T(8,128)S(1)}, f32[3,8,1536]{2,1,0:T(8,128)S(1)}) custom-call(f32[6,8,1536]{2,1,0:T(8,128)S(1)} %get-tuple-element.18.pair, f32[6,8,1536]{2,1,0:T(8,128)S(1)} %collective-permute-done.1.pair_near, f32[6,8,1536]{2,1,0:T(8,128)S(1)} %collective-permute-done.2.pair_far, f32[4,8,1536]{2,1,0:T(8,128)S(1)} %collective-permute-done.3.straight, ...), custom_call_target="tpu_custom_call" | custom-call | flops 1499136 | bytes 1499136 | tf_op jit(solution)/shard_map/pallas_call | solution.py:303
  18.1 1.3 %collective-permute-start.9 = (f32[3,8,1536]{2,1,0:T(8,128)S(1)}, f32[3,8,1536]{2,1,0:T(8,128)S(1)}, u32[]{:S(2)}, u32[]{:S(2)}) collective-permute-start(f32[3,8,1536]{2,1,0:T(8,128)S(1)} %get-tuple-element.24), channel_id=1, source_target_pairs={{4,0},{8,4},{12,8},{16,12},{20,16},{24,20},{28,24},{5,1},{9,5},{13... | collective-permute-start | bytes 442376 | tf_op jit(solution)/shard_map/ppermute | solution.py:317
  19.4 0.0 copy-start
  19.4 0.0 copy-start.1
  19.4 0.0 copy-start.2
  19.4 0.0 copy-start.3
  19.4 0.0 copy-start.4
  19.4 0.3 collective-permute-start.8
  19.7 0.7 %collective-permute-start.7 = (f32[3,8,1536]{2,1,0:T(8,128)S(1)}, f32[3,8,1536]{2,1,0:T(8,128)S(1)}, u32[]{:S(2)}, u32[]{:S(2)}) collective-permute-start(f32[3,8,1536]{2,1,0:T(8,128)S(1)} %get-tuple-element.22.state), channel_id=1, source_target_pairs={{1,2},{2,1},{5,6},{6,5},{9,10},{10,9},{13,14},{14,13},{17,18},{18,... | collective-permute-start | bytes 442376 | tf_op jit(solution)/shard_map/ppermute | solution.py:342
  20.4 1.2 %shard_map.87.tally = f32[4,8,128]{2,1,0:T(8,128)S(1)} custom-call(f32[6,8,1536]{2,1,0:T(8,128)S(1)} %get-tuple-element.18.pair, f32[6,8,1536]{2,1,0:T(8,128)S(1)} %collective-permute-done.1.pair_near, f32[6,8,1536]{2,1,0:T(8,128)S(1)} %collective-permute-done.2.pair_far, f32[4,8,1536]{2,1,0:T(8,128)S(1)} %collective-permute-done.3.straight, ...), custom_call_target="tpu_custom_call" | custom-call | flops 1515520 | bytes 1515520 | tf_op jit(solution)/shard_map/pallas_call | solution.py:303
  21.5 4.4 %collective-permute-done.9.back = f32[3,8,1536]{2,1,0:T(8,128)S(1)} collective-permute-done((f32[3,8,1536]{2,1,0:T(8,128)S(1)}, f32[3,8,1536]{2,1,0:T(8,128)S(1)}, u32[]{:S(2)}, u32[]{:S(2)}) %collective-permute-start.9) | collective-permute-done | bytes 147488 | tf_op jit(solution)/shard_map/ppermute | solution.py:317
  25.9 0.2 shard_map.88
  26.1 1.2 %shard_map.89.rest = f32[3,8,1536]{2,1,0:T(8,128)S(1)} custom-call(f32[3,8,1536]{2,1,0:T(8,128)S(1)} %get-tuple-element.22.state, f32[3,8,1536]{2,1,0:T(8,128)S(1)} %collective-permute-done.8.state_near, f32[4,8,1536]{2,1,0:T(8,128)S(1)} %collective-permute-done.3.straight, f32[2,8,1536]{2,1,0:T(8,128)S(1)} %collective-permute-done.5.relayed, ...), custom_call_target="tpu_custom_call" | custom-call | flops 909312 | bytes 909312 | tf_op jit(solution)/shard_map/pallas_call | solution.py:303
  27.3 0.3 shard_map.90
  27.6 13.1 %all_to_all.11 = f32[32,1,128]{2,1,0:T(1,128)S(1)} all-to-all(f32[32,1,128]{2,1,0:T(1,128)S(1)} %bitcast.5), channel_id=1, replica_groups=mesh['win'=8,'band'=2,'half'=2] {'win','band','half'}, dimensions={0} | all-to-all | bytes 32768 | tf_op jit(solution)/shard_map/all_to_all | solution.py:386
  40.7 1.3 %shard_map.91 = (f32[1,3,8,1536]{3,2,1,0:T(8,128)}, f32[1,3,8,1536]{3,2,1,0:T(8,128)}, f32[1,3,8,1536]{3,2,1,0:T(8,128)}) custom-call(f32[32,128]{1,0:T(8,128)S(1)} %bitcast.4, f32[1,3,8,1536]{3,2,1,0:T(8,128)S(1)} %copy-done, f32[1,3,8,1536]{3,2,1,0:T(8,128)S(1)} %copy-done.1, f32[1,3,8,1536]{3,2,1,0:T(8,128)S(1)} %copy-done.2, ...), custom_call_target="tpu_custom_call" | custom-call | flops 1343488 | bytes 1343488 | tf_op jit(solution)/shard_map/pallas_call | solution.py:303
  (12 shorter events, 0.1 us)
Async XLA Ops:
  0.6 1.8 %collective-permute-start = (f32[1,8,1536]{2,1,0:T(8,128)}, f32[1,8,1536]{2,1,0:T(8,128)S(1)}, u32[]{:S(2)}, u32[]{:S(2)}) collective-permute-start(f32[1,8,1536]{2,1,0:T(8,128)} %depth.1), channel_id=1, source_target_pairs={{0,1},{1,0},{2,3},{3,2},{4,5},{5,4},{6,7},{7,6},{8,9},{9,8},{10,11... | collective-permute-start | bytes 147464 | tf_op jit(solution)/shard_map/ppermute | solution.py:332
  2.5 12.9 %collective-permute-start.3 = (f32[4,8,1536]{2,1,0:T(8,128)S(1)}, f32[4,8,1536]{2,1,0:T(8,128)S(1)}, u32[]{:S(2)}, u32[]{:S(2)}) collective-permute-start(f32[4,8,1536]{2,1,0:T(8,128)S(1)} %get-tuple-element.19), channel_id=1, source_target_pairs={{0,4},{4,8},{8,12},{12,16},{16,20},{20,24},{24,28},{1,5},{5,9},{9,... | collective-permute-start | bytes 589832 | tf_op jit(solution)/shard_map/ppermute | solution.py:317
  7.0 8.4 %collective-permute-start.4 = (f32[1,8,1536]{2,1,0:T(8,128)S(1)}, f32[1,8,1536]{2,1,0:T(8,128)S(1)}, u32[]{:S(2)}, u32[]{:S(2)}) collective-permute-start(f32[1,8,1536]{2,1,0:T(8,128)S(1)} %collective-permute-done), channel_id=1, source_target_pairs={{0,7},{3,4},{4,11},{7,8},{8,15},{11,12},{12,19},{15,16},{16,23},{1... | collective-permute-start | bytes 147464 | tf_op jit(solution)/shard_map/ppermute | solution.py:342
  11.2 5.6 %collective-permute-start.2 = (f32[6,8,1536]{2,1,0:T(8,128)S(1)}, f32[6,8,1536]{2,1,0:T(8,128)S(1)}, u32[]{:S(2)}, u32[]{:S(2)}) collective-permute-start(f32[6,8,1536]{2,1,0:T(8,128)S(1)} %get-tuple-element.18.pair), channel_id=1, source_target_pairs={{1,2},{2,1},{5,6},{6,5},{9,10},{10,9},{13,14},{14,13},{17,18},{18,... | collective-permute-start | bytes 884744 | tf_op jit(solution)/shard_map/ppermute | solution.py:342
  11.9 4.9 %collective-permute-start.1 = (f32[6,8,1536]{2,1,0:T(8,128)S(1)}, f32[6,8,1536]{2,1,0:T(8,128)S(1)}, u32[]{:S(2)}, u32[]{:S(2)}) collective-permute-start(f32[6,8,1536]{2,1,0:T(8,128)S(1)} %get-tuple-element.18.pair), channel_id=1, source_target_pairs={{0,1},{1,0},{2,3},{3,2},{4,5},{5,4},{6,7},{7,6},{8,9},{9,8},{10,11... | collective-permute-start | bytes 884744 | tf_op jit(solution)/shard_map/ppermute | solution.py:332
  12.0 7.7 %collective-permute-start.6 = (f32[3,8,1536]{2,1,0:T(8,128)S(1)}, f32[3,8,1536]{2,1,0:T(8,128)S(1)}, u32[]{:S(2)}, u32[]{:S(2)}) collective-permute-start(f32[3,8,1536]{2,1,0:T(8,128)S(1)} %get-tuple-element.21), channel_id=1, source_target_pairs={{0,4},{4,8},{8,12},{12,16},{16,20},{20,24},{24,28},{1,5},{5,9},{9,... | collective-permute-start | bytes 442376 | tf_op jit(solution)/shard_map/ppermute | solution.py:317
  15.4 1.4 %collective-permute-start.5 = (f32[2,8,1536]{2,1,0:T(8,128)S(1)}, f32[2,8,1536]{2,1,0:T(8,128)S(1)}, u32[]{:S(2)}, u32[]{:S(2)}) collective-permute-start(f32[2,8,1536]{2,1,0:T(8,128)S(1)} %pad_maximum_fusion), channel_id=1, source_target_pairs={{0,1},{1,0},{2,3},{3,2},{4,5},{5,4},{6,7},{7,6},{8,9},{9,8},{10,11... | collective-permute-start | bytes 294920 | tf_op jit(solution)/shard_map/ppermute | solution.py:332
  18.1 7.9 %collective-permute-start.9 = (f32[3,8,1536]{2,1,0:T(8,128)S(1)}, f32[3,8,1536]{2,1,0:T(8,128)S(1)}, u32[]{:S(2)}, u32[]{:S(2)}) collective-permute-start(f32[3,8,1536]{2,1,0:T(8,128)S(1)} %get-tuple-element.24), channel_id=1, source_target_pairs={{4,0},{8,4},{12,8},{16,12},{20,16},{24,20},{28,24},{5,1},{9,5},{13... | collective-permute-start | bytes 442376 | tf_op jit(solution)/shard_map/ppermute | solution.py:317
  19.4 6.6 %copy-start = (f32[1,3,8,1536]{3,2,1,0:T(8,128)S(1)}, f32[1,3,8,1536]{3,2,1,0:T(8,128)}, u32[]{:S(2)}) copy-start(f32[1,3,8,1536]{3,2,1,0:T(8,128)} %p.5) | copy-start | bytes 442372
  19.4 6.5 %copy-start.1 = (f32[1,3,8,1536]{3,2,1,0:T(8,128)S(1)}, f32[1,3,8,1536]{3,2,1,0:T(8,128)}, u32[]{:S(2)}) copy-start(f32[1,3,8,1536]{3,2,1,0:T(8,128)} %m.5) | copy-start | bytes 442372
  19.4 6.5 %copy-start.2 = (f32[1,3,8,1536]{3,2,1,0:T(8,128)S(1)}, f32[1,3,8,1536]{3,2,1,0:T(8,128)}, u32[]{:S(2)}) copy-start(f32[1,3,8,1536]{3,2,1,0:T(8,128)} %dvar.5) | copy-start | bytes 442372
  19.4 6.5 %copy-start.3 = (f32[1,3,8,1536]{3,2,1,0:T(8,128)S(1)}, f32[1,3,8,1536]{3,2,1,0:T(8,128)}, u32[]{:S(2)}) copy-start(f32[1,3,8,1536]{3,2,1,0:T(8,128)} %rvar.5) | copy-start | bytes 442372
  19.4 6.5 %copy-start.4 = (f32[1,3,8,1536]{3,2,1,0:T(8,128)S(1)}, f32[1,3,8,1536]{3,2,1,0:T(8,128)}, u32[]{:S(2)}) copy-start(f32[1,3,8,1536]{3,2,1,0:T(8,128)} %hobs.5) | copy-start | bytes 442372
  19.4 6.7 %collective-permute-start.8 = (f32[3,8,1536]{2,1,0:T(8,128)S(1)}, f32[3,8,1536]{2,1,0:T(8,128)S(1)}, u32[]{:S(2)}, u32[]{:S(2)}) collective-permute-start(f32[3,8,1536]{2,1,0:T(8,128)S(1)} %get-tuple-element.22.state), channel_id=1, source_target_pairs={{0,1},{1,0},{2,3},{3,2},{4,5},{5,4},{6,7},{7,6},{8,9},{9,8},{10,11... | collective-permute-start | bytes 442376 | tf_op jit(solution)/shard_map/ppermute | solution.py:332
  19.7 7.6 %collective-permute-start.7 = (f32[3,8,1536]{2,1,0:T(8,128)S(1)}, f32[3,8,1536]{2,1,0:T(8,128)S(1)}, u32[]{:S(2)}, u32[]{:S(2)}) collective-permute-start(f32[3,8,1536]{2,1,0:T(8,128)S(1)} %get-tuple-element.22.state), channel_id=1, source_target_pairs={{1,2},{2,1},{5,6},{6,5},{9,10},{10,9},{13,14},{14,13},{17,18},{18,... | collective-permute-start | bytes 442376 | tf_op jit(solution)/shard_map/ppermute | solution.py:342

commit v19 on v18

--- a/solution.py
+++ b/solution.py
@@ -58,8 +58,8 @@
         local[part] = up + rv[0, part] * seen
 
 
-def widened(tile, width):
-    return jnp.concatenate([tile[...]] * (width // 128), axis=1)
+def widened(factors, index, width):
+    return jnp.concatenate([factors[index]] * (width // 128), axis=1)
 
 
 def stretched(straight, relayed):
@@ -69,9 +69,9 @@
     return 0.25 * jnp.concatenate([low, straight[0], high], axis=0)
 
 
-def adjoint(pair, pair_near, pair_far, straight, relayed, spin, inside, base):
+def adjoint(pair, pair_near, pair_far, straight, relayed, spin, base):
     depth = stretched(straight, relayed)
-    turn, keep = widened(spin, depth.shape[1]), widened(inside, depth.shape[1])
+    turn, keep = widened(spin, 0, depth.shape[1]), widened(spin, 1, depth.shape[1])
     adj_height, adj_east, adj_north = [stacked(pair, pair_near, pair_far, base + part) for part in range(3)]
     for step in range(STEPS):
         adj_mid = adj_east - turn * adj_north
@@ -82,16 +82,16 @@
     return [value[rows:2 * rows] for value in (adj_height, adj_east, adj_north)]
 
 
-def first_adjoint_kernel(pair, pair_near, pair_far, straight, relayed, spin, inside, state, back):
-    swept = adjoint(pair, pair_near, pair_far, straight, relayed, spin, inside, 0)
+def first_adjoint_kernel(pair, pair_near, pair_far, straight, relayed, spin, state, back):
+    swept = adjoint(pair, pair_near, pair_far, straight, relayed, spin, 0)
     link = has_previous()
     for part, value in enumerate(swept):
         back[part] = value
         state[part] = jnp.where(link, straight[1 + part] - value, 0.0)
 
 
-def second_adjoint_kernel(pair, pair_near, pair_far, straight, relayed, spin, inside, local, state, tally):
-    swept = adjoint(pair, pair_near, pair_far, straight, relayed, spin, inside, 3)
+def second_adjoint_kernel(pair, pair_near, pair_far, straight, relayed, spin, local, state, tally):
+    swept = adjoint(pair, pair_near, pair_far, straight, relayed, spin, 3)
     link = has_previous()
     zero = jnp.zeros((pair.shape[1], 128), jnp.float32)
     cross = square = (zero, zero)
@@ -155,9 +155,9 @@
     return height, east, north
 
 
-def inner_forward_kernel(state, state_near, straight, relayed, spin, inside, lead, rest):
+def inner_forward_kernel(state, state_near, straight, relayed, spin, lead, rest):
     depth = stretched(straight, relayed)
-    turn, keep = widened(spin, depth.shape[1]), widened(inside, depth.shape[1])
+    turn, keep = widened(spin, 0, depth.shape[1]), widened(spin, 1, depth.shape[1])
     even = even_lat()
     rows = state.shape[1]
     fields = []
@@ -177,7 +177,7 @@
     return above - below
 
 
-def closing_kernel(state_far, rest, straight, relayed, spin, inside, sums, sent, remainder):
+def closing_kernel(state_far, rest, straight, relayed, spin, sums, sent, remainder):
     even = even_lat()
     rows, width = state_far.shape[1:]
     middle = lax.axis_index("band") != lax.axis_index("half")
@@ -191,7 +191,7 @@
         )
         turn, keep = [
             jnp.where(even, factor[:2 * rows], factor[rows:])
-            for factor in (widened(spin, width), widened(inside, width))
+            for factor in (widened(spin, 0, width), widened(spin, 1, width))
         ]
         empty = jnp.zeros((rows, width), jnp.float32)
         fields = [
@@ -273,26 +273,16 @@
     return y1, y2
 
 
-def combine_kernel(gathered, p, m, dvar, rvar, hobs, back, dual_model, dual_obs, increment, first, second, third, sems):
+def combine_kernel(gathered, p, m, dvar, rvar, hobs, back, dual_model, dual_obs, increment):
     y1, y2 = coefficients(gathered)
     rows, width = p.shape[2:]
     y1 = jnp.broadcast_to(jnp.concatenate([y1] * (width // 128), axis=1), (rows, width))
     y2 = jnp.broadcast_to(jnp.concatenate([y2] * (width // 128), axis=1), (rows, width))
-    copies = [
-        pltpu.make_async_copy(source, target, sems.at[slot])
-        for slot, (source, target) in enumerate(((first, dual_model), (second, dual_obs), (third, increment)))
-    ]
-    for part in range(3):
-        first[0, part] = (y1 + y2 * dvar[0, part]) * p[0, part]
-    copies[0].start()
-    for part in range(3):
-        second[0, part] = (y1 + y2 * rvar[0, part]) * m[0, part]
-    copies[1].start()
-    for part in range(3):
-        third[0, part] = y2 * (p[0, part] - back[part] + hobs[0, part] * m[0, part])
-    copies[2].start()
-    for copy in copies:
-        copy.wait()
+    for part in range(3):
+        pv, mv = p[0, part], m[0, part]
+        dual_model[0, part] = (y1 + y2 * dvar[0, part]) * pv
+        dual_obs[0, part] = (y1 + y2 * rvar[0, part]) * mv
+        increment[0, part] = y2 * (pv - back[part] + hobs[0, part] * mv)
 
 
 def run(kernel, out_shapes, *operands, scratch=(), space=pltpu.VMEM, target=pltpu.VMEM, work=4):
@@ -349,8 +339,9 @@
     offset = (GRID_ROWS - total_rows) // 2
     local_rows = lat_index() * rows - rows + lax.broadcasted_iota(jnp.int32, (3 * rows, 128), 0)
     latitude = -jnp.pi / 2 + (local_rows.astype(jnp.float32) + offset + 0.5) * (jnp.pi / GRID_ROWS)
-    inside = ((local_rows >= 0) & (local_rows < total_rows)).astype(jnp.float32)
-    spin = inside * (mass_rate * spin_rate * jnp.sin(latitude))
+    inside = (local_rows >= 0) & (local_rows < total_rows)
+    spin = jnp.where(inside, mass_rate * spin_rate * jnp.sin(latitude), 0.0)
+    spin = jnp.stack([spin, inside.astype(jnp.float32)])
     fields = (3, rows, width)
 
     middle, outer = (1, 2), (0, 3)
@@ -366,7 +357,7 @@
     came = shifted(straight, 1)
     relayed = swapped(jnp.concatenate([came[:1], depth_edge]), 0)
     pair_near, pair_far = swapped(pair, 0), crossed(pair, middle)
-    known = (pair, pair_near, pair_far, came, relayed, spin, inside)
+    known = (pair, pair_near, pair_far, came, relayed, spin)
     local = shifted(local, 1)
     state, back = run(first_adjoint_kernel, [fields, fields], *known, work=4)
     held_state, local = lax.optimization_barrier((state, local))
@@ -378,16 +369,15 @@
         home_kernel, [fields, (8, rows, 128)],
         model_rhs, obs_rhs, model_var, obs_var, obs_weight, tally, back,
     )
-    (rest,) = run(inner_forward_kernel, [fields], state, state_near, came, relayed, spin, inside, lead)
+    (rest,) = run(inner_forward_kernel, [fields], state, state_near, came, relayed, spin, lead)
     (sent,) = run(
-        closing_kernel, [(ranks, 128)], state_far, rest, came, relayed, spin, inside, sums,
+        closing_kernel, [(ranks, 128)], state_far, rest, came, relayed, spin, sums,
         scratch=[pltpu.VMEM(fields, jnp.float32)],
     )
     gathered = lax.all_to_all(sent, ("win", "band", "half"), 0, 0, tiled=True)
     return run(
         combine_kernel, [model_rhs.shape] * 3,
-        gathered, model_rhs, obs_rhs, model_var, obs_var, obs_weight, back, target=pltpu.HBM,
-        scratch=[pltpu.VMEM(model_rhs.shape, jnp.float32)] * 3 + [pltpu.SemaphoreType.DMA((3,))],
+        gathered, model_rhs, obs_rhs, model_var, obs_var, obs_weight, back,
     )
 
 

time: 42.2 us -> 42.1 us (level)
  no operation moved by 1% of the time
where the time goes in v19:
time: 42.1 us; the launch traced here: 41.9 us
  starting transfers between devices  15.8 us (38%)
  blocking collectives  13.1 us (31%)
  Pallas kernels  6.45 us (15%)
  waiting for transfers between devices  5.43 us (13%)
  between operations  0.84 us (2%)
    all_to_all x1, blocking collectives, body(): gathered = lax.all_to_all(sent, ('win', 'band', 'half'), 0, 0, tiled=True)  13.1 us
    ppermute x3, starting transfers between devices, shifted(): lax.ppermute(value, 'win', [(source, source + step) for source in range(i...  9.21 us
    pallas_call x7, Pallas kernels, run(): pl.pallas_call(kernel, out_shape=shapes, in_specs=[pl.BlockSpec(memory_sp...  6.45 us
    ppermute x3, starting transfers between devices, crossed(): return lax.ppermute(value, ('win', 'band', 'half'), pairs)  5.46 us
    ppermute x3, waiting for transfers between devices, shifted(): lax.ppermute(value, 'win', [(source, source + step) for source in range(i...  4.4 us
    ppermute x4, starting transfers between devices, swapped(): return lax.ppermute(value, ('band', 'half'), pairs)  1.13 us
    ppermute x4, waiting for transfers between devices, swapped(): return lax.ppermute(value, ('band', 'half'), pairs)  1.03 us
  transfers between devices with their start and end apart: 10, of which 2 were waited for; matrix products, arithmetic and copies ran while one was open for 1% of the time, Pallas kernels for 12%

profile of v19, /device:TPU:0, one launch (start us, length us, event | category | flops | bytes accessed | tf_op | source)
XLA Modules:
  0.0 41.9 jit_solution(16185590774119367923)
XLA Ops:
  0.6 0.5 %collective-permute-start = (f32[1,8,1536]{2,1,0:T(8,128)}, f32[1,8,1536]{2,1,0:T(8,128)S(1)}, u32[]{:S(2)}, u32[]{:S(2)}) collective-permute-start(f32[1,8,1536]{2,1,0:T(8,128)} %depth.1), channel_id=1, source_target_pairs={{0,1},{1,0},{2,3},{3,2},{4,5},{5,4},{6,7},{7,6},{8,9},{9,8},{10,11... | collective-permute-start | bytes 147464 | tf_op jit(solution)/shard_map/ppermute | solution.py:322
  1.2 1.3 %shard_map.85 = (f32[6,8,1536]{2,1,0:T(8,128)S(1)}, f32[4,8,1536]{2,1,0:T(8,128)S(1)}, f32[3,8,1536]{2,1,0:T(8,128)S(1)}) custom-call(f32[1,3,8,1536]{3,2,1,0:T(8,128)} %p.5, f32[1,3,8,1536]{3,2,1,0:T(8,128)} %m.5, f32[1,3,8,1536]{3,2,1,0:T(8,128)} %dvar.5, f32[1,3,8,1536]{3,2,1,0:T(8,128)} %rvar.5, f32[1,3,8,1536]{3,2,1,0:T(8,128)} %hobs.5, f32[1,8,1536]{2,1,0:T(8,128)} %depth.1), custom_call_target="tpu_custom_call" | custom-call | flops 1425408 | bytes 1425408 | tf_op jit(solution)/shard_map/pallas_call | solution.py:293
  2.5 0.0 collective-permute-done
  2.5 4.5 %collective-permute-start.3 = (f32[4,8,1536]{2,1,0:T(8,128)S(1)}, f32[4,8,1536]{2,1,0:T(8,128)S(1)}, u32[]{:S(2)}, u32[]{:S(2)}) collective-permute-start(f32[4,8,1536]{2,1,0:T(8,128)S(1)} %get-tuple-element.19), channel_id=1, source_target_pairs={{0,4},{4,8},{8,12},{12,16},{16,20},{20,24},{24,28},{1,5},{5,9},{9,... | collective-permute-start | bytes 589832 | tf_op jit(solution)/shard_map/ppermute | solution.py:307
  7.0 4.1 %collective-permute-start.4 = (f32[1,8,1536]{2,1,0:T(8,128)S(1)}, f32[1,8,1536]{2,1,0:T(8,128)S(1)}, u32[]{:S(2)}, u32[]{:S(2)}) collective-permute-start(f32[1,8,1536]{2,1,0:T(8,128)S(1)} %collective-permute-done), channel_id=1, source_target_pairs={{0,7},{3,4},{4,11},{7,8},{8,15},{11,12},{12,19},{15,16},{16,23},{1... | collective-permute-start | bytes 147464 | tf_op jit(solution)/shard_map/ppermute | solution.py:332
  11.2 0.1 broadcast_select_fusion
  11.2 0.7 %collective-permute-start.2 = (f32[6,8,1536]{2,1,0:T(8,128)S(1)}, f32[6,8,1536]{2,1,0:T(8,128)S(1)}, u32[]{:S(2)}, u32[]{:S(2)}) collective-permute-start(f32[6,8,1536]{2,1,0:T(8,128)S(1)} %get-tuple-element.18.pair), channel_id=1, source_target_pairs={{1,2},{2,1},{5,6},{6,5},{9,10},{10,9},{13,14},{14,13},{17,18},{18,... | collective-permute-start | bytes 884744 | tf_op jit(solution)/shard_map/ppermute | solution.py:332
  11.9 0.1 collective-permute-start.1
  12.0 3.4 %collective-permute-start.6 = (f32[3,8,1536]{2,1,0:T(8,128)S(1)}, f32[3,8,1536]{2,1,0:T(8,128)S(1)}, u32[]{:S(2)}, u32[]{:S(2)}) collective-permute-start(f32[3,8,1536]{2,1,0:T(8,128)S(1)} %get-tuple-element.21), channel_id=1, source_target_pairs={{0,4},{4,8},{8,12},{12,16},{16,20},{20,24},{24,28},{1,5},{5,9},{9,... | collective-permute-start | bytes 442376 | tf_op jit(solution)/shard_map/ppermute | solution.py:307
  15.4 0.0 collective-permute-done.3.straight
  15.4 0.0 collective-permute-done.4
  15.5 0.3 collective-permute-start.5
  15.7 0.1 iota.13
  15.8 1.0 %collective-permute-done.5.relayed = f32[2,8,1536]{2,1,0:T(8,128)S(1)} collective-permute-done((f32[2,8,1536]{2,1,0:T(8,128)S(1)}, f32[2,8,1536]{2,1,0:T(8,128)S(1)}, u32[]{:S(2)}, u32[]{:S(2)}) %collective-permute-start.5) | collective-permute-done | bytes 98336 | tf_op jit(solution)/shard_map/ppermute | solution.py:322
  16.8 0.0 collective-permute-done.2.pair_far
  16.8 0.0 collective-permute-done.1.pair_near
  16.8 1.2 %shard_map.86 = (f32[3,8,1536]{2,1,0:T(8,128)S(1)}, f32[3,8,1536]{2,1,0:T(8,128)S(1)}) custom-call(f32[6,8,1536]{2,1,0:T(8,128)S(1)} %get-tuple-element.18.pair, f32[6,8,1536]{2,1,0:T(8,128)S(1)} %collective-permute-done.1.pair_near, f32[6,8,1536]{2,1,0:T(8,128)S(1)} %collective-permute-done.2.pair_far, f32[4,8,1536]{2,1,0:T(8,128)S(1)} %collective-permute-done.3.straight, ...), custom_call_target="tpu_custom_call" | custom-call | flops 1499136 | bytes 1499136 | tf_op jit(solution)/shard_map/pallas_call | solution.py:293
  18.0 1.3 %collective-permute-start.9 = (f32[3,8,1536]{2,1,0:T(8,128)S(1)}, f32[3,8,1536]{2,1,0:T(8,128)S(1)}, u32[]{:S(2)}, u32[]{:S(2)}) collective-permute-start(f32[3,8,1536]{2,1,0:T(8,128)S(1)} %get-tuple-element.24), channel_id=1, source_target_pairs={{4,0},{8,4},{12,8},{16,12},{20,16},{24,20},{28,24},{5,1},{9,5},{13... | collective-permute-start | bytes 442376 | tf_op jit(solution)/shard_map/ppermute | solution.py:307
  19.3 0.0 copy-start
  19.3 0.0 copy-start.1
  19.3 0.0 copy-start.2
  19.3 0.0 copy-start.3
  19.4 0.0 copy-start.4
  19.4 0.3 collective-permute-start.8
  19.6 0.7 %collective-permute-start.7 = (f32[3,8,1536]{2,1,0:T(8,128)S(1)}, f32[3,8,1536]{2,1,0:T(8,128)S(1)}, u32[]{:S(2)}, u32[]{:S(2)}) collective-permute-start(f32[3,8,1536]{2,1,0:T(8,128)S(1)} %get-tuple-element.22.state), channel_id=1, source_target_pairs={{1,2},{2,1},{5,6},{6,5},{9,10},{10,9},{13,14},{14,13},{17,18},{18,... | collective-permute-start | bytes 442376 | tf_op jit(solution)/shard_map/ppermute | solution.py:332
  20.3 1.2 %shard_map.87.tally = f32[4,8,128]{2,1,0:T(8,128)S(1)} custom-call(f32[6,8,1536]{2,1,0:T(8,128)S(1)} %get-tuple-element.18.pair, f32[6,8,1536]{2,1,0:T(8,128)S(1)} %collective-permute-done.1.pair_near, f32[6,8,1536]{2,1,0:T(8,128)S(1)} %collective-permute-done.2.pair_far, f32[4,8,1536]{2,1,0:T(8,128)S(1)} %collective-permute-done.3.straight, ...), custom_call_target="tpu_custom_call" | custom-call | flops 1515520 | bytes 1515520 | tf_op jit(solution)/shard_map/pallas_call | solution.py:293
  21.5 4.4 %collective-permute-done.9.back = f32[3,8,1536]{2,1,0:T(8,128)S(1)} collective-permute-done((f32[3,8,1536]{2,1,0:T(8,128)S(1)}, f32[3,8,1536]{2,1,0:T(8,128)S(1)}, u32[]{:S(2)}, u32[]{:S(2)}) %collective-permute-start.9) | collective-permute-done | bytes 147488 | tf_op jit(solution)/shard_map/ppermute | solution.py:307
  25.9 0.2 shard_map.88
  26.1 1.1 %shard_map.89.rest = f32[3,8,1536]{2,1,0:T(8,128)S(1)} custom-call(f32[3,8,1536]{2,1,0:T(8,128)S(1)} %get-tuple-element.22.state, f32[3,8,1536]{2,1,0:T(8,128)S(1)} %collective-permute-done.8.state_near, f32[4,8,1536]{2,1,0:T(8,128)S(1)} %collective-permute-done.3.straight, f32[2,8,1536]{2,1,0:T(8,128)S(1)} %collective-permute-done.5.relayed, ...), custom_call_target="tpu_custom_call" | custom-call | flops 909312 | bytes 909312 | tf_op jit(solution)/shard_map/pallas_call | solution.py:293
  27.3 0.3 shard_map.90
  27.5 13.1 %all_to_all.11 = f32[32,1,128]{2,1,0:T(1,128)S(1)} all-to-all(f32[32,1,128]{2,1,0:T(1,128)S(1)} %bitcast.5), channel_id=1, replica_groups=mesh['win'=8,'band'=2,'half'=2] {'win','band','half'}, dimensions={0} | all-to-all | bytes 32768 | tf_op jit(solution)/shard_map/all_to_all | solution.py:377
  40.6 1.2 %shard_map.91 = (f32[1,3,8,1536]{3,2,1,0:T(8,128)}, f32[1,3,8,1536]{3,2,1,0:T(8,128)}, f32[1,3,8,1536]{3,2,1,0:T(8,128)}) custom-call(f32[32,128]{1,0:T(8,128)S(1)} %bitcast.4, f32[1,3,8,1536]{3,2,1,0:T(8,128)S(1)} %copy-done, f32[1,3,8,1536]{3,2,1,0:T(8,128)S(1)} %copy-done.1, f32[1,3,8,1536]{3,2,1,0:T(8,128)S(1)} %copy-done.2, ...), custom_call_target="tpu_custom_call" | custom-call | flops 1343488 | bytes 1343488 | tf_op jit(solution)/shard_map/pallas_call | solution.py:293
  (13 shorter events, 0.1 us)
Async XLA Ops:
  0.6 1.9 %collective-permute-start = (f32[1,8,1536]{2,1,0:T(8,128)}, f32[1,8,1536]{2,1,0:T(8,128)S(1)}, u32[]{:S(2)}, u32[]{:S(2)}) collective-permute-start(f32[1,8,1536]{2,1,0:T(8,128)} %depth.1), channel_id=1, source_target_pairs={{0,1},{1,0},{2,3},{3,2},{4,5},{5,4},{6,7},{7,6},{8,9},{9,8},{10,11... | collective-permute-start | bytes 147464 | tf_op jit(solution)/shard_map/ppermute | solution.py:322
  2.5 12.9 %collective-permute-start.3 = (f32[4,8,1536]{2,1,0:T(8,128)S(1)}, f32[4,8,1536]{2,1,0:T(8,128)S(1)}, u32[]{:S(2)}, u32[]{:S(2)}) collective-permute-start(f32[4,8,1536]{2,1,0:T(8,128)S(1)} %get-tuple-element.19), channel_id=1, source_target_pairs={{0,4},{4,8},{8,12},{12,16},{16,20},{20,24},{24,28},{1,5},{5,9},{9,... | collective-permute-start | bytes 589832 | tf_op jit(solution)/shard_map/ppermute | solution.py:307
  7.0 8.4 %collective-permute-start.4 = (f32[1,8,1536]{2,1,0:T(8,128)S(1)}, f32[1,8,1536]{2,1,0:T(8,128)S(1)}, u32[]{:S(2)}, u32[]{:S(2)}) collective-permute-start(f32[1,8,1536]{2,1,0:T(8,128)S(1)} %collective-permute-done), channel_id=1, source_target_pairs={{0,7},{3,4},{4,11},{7,8},{8,15},{11,12},{12,19},{15,16},{16,23},{1... | collective-permute-start | bytes 147464 | tf_op jit(solution)/shard_map/ppermute | solution.py:332
  11.2 5.6 %collective-permute-start.2 = (f32[6,8,1536]{2,1,0:T(8,128)S(1)}, f32[6,8,1536]{2,1,0:T(8,128)S(1)}, u32[]{:S(2)}, u32[]{:S(2)}) collective-permute-start(f32[6,8,1536]{2,1,0:T(8,128)S(1)} %get-tuple-element.18.pair), channel_id=1, source_target_pairs={{1,2},{2,1},{5,6},{6,5},{9,10},{10,9},{13,14},{14,13},{17,18},{18,... | collective-permute-start | bytes 884744 | tf_op jit(solution)/shard_map/ppermute | solution.py:332
  11.9 4.9 %collective-permute-start.1 = (f32[6,8,1536]{2,1,0:T(8,128)S(1)}, f32[6,8,1536]{2,1,0:T(8,128)S(1)}, u32[]{:S(2)}, u32[]{:S(2)}) collective-permute-start(f32[6,8,1536]{2,1,0:T(8,128)S(1)} %get-tuple-element.18.pair), channel_id=1, source_target_pairs={{0,1},{1,0},{2,3},{3,2},{4,5},{5,4},{6,7},{7,6},{8,9},{9,8},{10,11... | collective-permute-start | bytes 884744 | tf_op jit(solution)/shard_map/ppermute | solution.py:322
  12.0 7.7 %collective-permute-start.6 = (f32[3,8,1536]{2,1,0:T(8,128)S(1)}, f32[3,8,1536]{2,1,0:T(8,128)S(1)}, u32[]{:S(2)}, u32[]{:S(2)}) collective-permute-start(f32[3,8,1536]{2,1,0:T(8,128)S(1)} %get-tuple-element.21), channel_id=1, source_target_pairs={{0,4},{4,8},{8,12},{12,16},{16,20},{20,24},{24,28},{1,5},{5,9},{9,... | collective-permute-start | bytes 442376 | tf_op jit(solution)/shard_map/ppermute | solution.py:307
  15.5 1.4 %collective-permute-start.5 = (f32[2,8,1536]{2,1,0:T(8,128)S(1)}, f32[2,8,1536]{2,1,0:T(8,128)S(1)}, u32[]{:S(2)}, u32[]{:S(2)}) collective-permute-start(f32[2,8,1536]{2,1,0:T(8,128)S(1)} %pad_maximum_fusion), channel_id=1, source_target_pairs={{0,1},{1,0},{2,3},{3,2},{4,5},{5,4},{6,7},{7,6},{8,9},{9,8},{10,11... | collective-permute-start | bytes 294920 | tf_op jit(solution)/shard_map/ppermute | solution.py:322
  18.0 7.9 %collective-permute-start.9 = (f32[3,8,1536]{2,1,0:T(8,128)S(1)}, f32[3,8,1536]{2,1,0:T(8,128)S(1)}, u32[]{:S(2)}, u32[]{:S(2)}) collective-permute-start(f32[3,8,1536]{2,1,0:T(8,128)S(1)} %get-tuple-element.24), channel_id=1, source_target_pairs={{4,0},{8,4},{12,8},{16,12},{20,16},{24,20},{28,24},{5,1},{9,5},{13... | collective-permute-start | bytes 442376 | tf_op jit(solution)/shard_map/ppermute | solution.py:307
  19.3 6.6 %copy-start = (f32[1,3,8,1536]{3,2,1,0:T(8,128)S(1)}, f32[1,3,8,1536]{3,2,1,0:T(8,128)}, u32[]{:S(2)}) copy-start(f32[1,3,8,1536]{3,2,1,0:T(8,128)} %p.5) | copy-start | bytes 442372
  19.3 6.5 %copy-start.1 = (f32[1,3,8,1536]{3,2,1,0:T(8,128)S(1)}, f32[1,3,8,1536]{3,2,1,0:T(8,128)}, u32[]{:S(2)}) copy-start(f32[1,3,8,1536]{3,2,1,0:T(8,128)} %m.5) | copy-start | bytes 442372
  19.3 6.5 %copy-start.2 = (f32[1,3,8,1536]{3,2,1,0:T(8,128)S(1)}, f32[1,3,8,1536]{3,2,1,0:T(8,128)}, u32[]{:S(2)}) copy-start(f32[1,3,8,1536]{3,2,1,0:T(8,128)} %dvar.5) | copy-start | bytes 442372
  19.3 6.5 %copy-start.3 = (f32[1,3,8,1536]{3,2,1,0:T(8,128)S(1)}, f32[1,3,8,1536]{3,2,1,0:T(8,128)}, u32[]{:S(2)}) copy-start(f32[1,3,8,1536]{3,2,1,0:T(8,128)} %rvar.5) | copy-start | bytes 442372
  19.4 6.5 %copy-start.4 = (f32[1,3,8,1536]{3,2,1,0:T(8,128)S(1)}, f32[1,3,8,1536]{3,2,1,0:T(8,128)}, u32[]{:S(2)}) copy-start(f32[1,3,8,1536]{3,2,1,0:T(8,128)} %hobs.5) | copy-start | bytes 442372
  19.4 6.7 %collective-permute-start.8 = (f32[3,8,1536]{2,1,0:T(8,128)S(1)}, f32[3,8,1536]{2,1,0:T(8,128)S(1)}, u32[]{:S(2)}, u32[]{:S(2)}) collective-permute-start(f32[3,8,1536]{2,1,0:T(8,128)S(1)} %get-tuple-element.22.state), channel_id=1, source_target_pairs={{0,1},{1,0},{2,3},{3,2},{4,5},{5,4},{6,7},{7,6},{8,9},{9,8},{10,11... | collective-permute-start | bytes 442376 | tf_op jit(solution)/shard_map/ppermute | solution.py:322
  19.6 7.6 %collective-permute-start.7 = (f32[3,8,1536]{2,1,0:T(8,128)S(1)}, f32[3,8,1536]{2,1,0:T(8,128)S(1)}, u32[]{:S(2)}, u32[]{:S(2)}) collective-permute-start(f32[3,8,1536]{2,1,0:T(8,128)S(1)} %get-tuple-element.22.state), channel_id=1, source_target_pairs={{1,2},{2,1},{5,6},{6,5},{9,10},{10,9},{13,14},{14,13},{17,18},{18,... | collective-permute-start | bytes 442376 | tf_op jit(solution)/shard_map/ppermute | solution.py:332

commit v20 on v18

--- a/solution.py
+++ b/solution.py
@@ -155,7 +155,7 @@
     return height, east, north
 
 
-def inner_forward_kernel(state, state_near, straight, relayed, spin, inside, lead, rest):
+def inner_forward_kernel(state, state_near, straight, relayed, spin, inside, rest):
     depth = stretched(straight, relayed)
     turn, keep = widened(spin, depth.shape[1]), widened(inside, depth.shape[1])
     even = even_lat()
@@ -166,7 +166,7 @@
         high = jnp.where(even, state_near[part], 0.0)
         fields.append(jnp.concatenate([low, state[part], high], axis=0))
     for part, value in enumerate(forward(*fields, depth, turn, keep, lat_gap)):
-        rest[part] = lead[part] - value[rows:2 * rows]
+        rest[part] = value[rows:2 * rows]
 
 
 def open_lat_gap(field):
@@ -177,7 +177,7 @@
     return above - below
 
 
-def closing_kernel(state_far, rest, straight, relayed, spin, inside, sums, sent, remainder):
+def closing_kernel(state_far, rest, straight, relayed, spin, inside, lead, sums, sent, remainder):
     even = even_lat()
     rows, width = state_far.shape[1:]
     middle = lax.axis_index("band") != lax.axis_index("half")
@@ -203,12 +203,12 @@
             for part in range(3)
         ]
         for part, value in enumerate(forward(*fields, 0.25 * depth, turn, keep, open_lat_gap)):
-            remainder[part] = rest[part] - jnp.where(even, value[rows:], value[:rows])
+            remainder[part] = lead[part] - rest[part] - jnp.where(even, value[rows:], value[:rows])
 
     @pl.when(jnp.logical_not(middle))
     def _():
         for part in range(3):
-            remainder[part] = rest[part]
+            remainder[part] = lead[part] - rest[part]
 
     moments = [(sums[slot], sums[slot + 1]) for slot in range(0, 8, 2)]
     for part in range(3):
@@ -378,9 +378,9 @@
         home_kernel, [fields, (8, rows, 128)],
         model_rhs, obs_rhs, model_var, obs_var, obs_weight, tally, back,
     )
-    (rest,) = run(inner_forward_kernel, [fields], state, state_near, came, relayed, spin, inside, lead)
+    (rest,) = run(inner_forward_kernel, [fields], state, state_near, came, relayed, spin, inside)
     (sent,) = run(
-        closing_kernel, [(ranks, 128)], state_far, rest, came, relayed, spin, inside, sums,
+        closing_kernel, [(ranks, 128)], state_far, rest, came, relayed, spin, inside, lead, sums,
         scratch=[pltpu.VMEM(fields, jnp.float32)],
     )
     gathered = lax.all_to_all(sent, ("win", "band", "half"), 0, 0, tiled=True)

time: 42.2 us -> 42 us (level)
  waiting for transfers between devices: 5.43 us -> 4.61 us
  blocking collectives: 13.1 us -> 13.7 us
    ppermute x3, waiting for transfers between devices: 4.39 us -> 3.57 us  [shifted(): lax.ppermute(value, 'win', [(source, source + step) for source in range(i...]
    all_to_all x1, blocking collectives: 13.1 us -> 13.7 us  [body(): gathered = lax.all_to_all(sent, ('win', 'band', 'half'), 0, 0, tiled=True)]
where the time goes in v20:
time: 42 us; the launch traced here: 41.8 us
  starting transfers between devices  15.8 us (38%)
  blocking collectives  13.7 us (33%)
  Pallas kernels  6.49 us (15%)
  waiting for transfers between devices  4.61 us (11%)
  between operations  0.85 us (2%)
    all_to_all x1, blocking collectives, body(): gathered = lax.all_to_all(sent, ('win', 'band', 'half'), 0, 0, tiled=True)  13.7 us
    ppermute x3, starting transfers between devices, shifted(): lax.ppermute(value, 'win', [(source, source + step) for source in range(i...  9.26 us
    pallas_call x7, Pallas kernels, run(): pl.pallas_call(kernel, out_shape=shapes, in_specs=[pl.BlockSpec(memory_sp...  6.49 us
    ppermute x3, starting transfers between devices, crossed(): return lax.ppermute(value, ('win', 'band', 'half'), pairs)  5.45 us
    ppermute x3, waiting for transfers between devices, shifted(): lax.ppermute(value, 'win', [(source, source + step) for source in range(i...  3.57 us
    ppermute x4, starting transfers between devices, swapped(): return lax.ppermute(value, ('band', 'half'), pairs)  1.13 us
    ppermute x4, waiting for transfers between devices, swapped(): return lax.ppermute(value, ('band', 'half'), pairs)  1.03 us
  transfers between devices with their start and end apart: 10, of which 2 were waited for; matrix products, arithmetic and copies ran while one was open for 1% of the time, Pallas kernels for 12%

profile of v20, /device:TPU:0, one launch (start us, length us, event | category | flops | bytes accessed | tf_op | source)
XLA Modules:
  0.0 41.8 jit_solution(11078452234380339728)
XLA Ops:
  0.6 0.5 %collective-permute-start = (f32[1,8,1536]{2,1,0:T(8,128)}, f32[1,8,1536]{2,1,0:T(8,128)S(1)}, u32[]{:S(2)}, u32[]{:S(2)}) collective-permute-start(f32[1,8,1536]{2,1,0:T(8,128)} %depth.1), channel_id=1, source_target_pairs={{0,1},{1,0},{2,3},{3,2},{4,5},{5,4},{6,7},{7,6},{8,9},{9,8},{10,11... | collective-permute-start | bytes 147464 | tf_op jit(solution)/shard_map/ppermute | solution.py:332
  1.1 1.3 %shard_map.85 = (f32[6,8,1536]{2,1,0:T(8,128)S(1)}, f32[4,8,1536]{2,1,0:T(8,128)S(1)}, f32[3,8,1536]{2,1,0:T(8,128)S(1)}) custom-call(f32[1,3,8,1536]{3,2,1,0:T(8,128)} %p.5, f32[1,3,8,1536]{3,2,1,0:T(8,128)} %m.5, f32[1,3,8,1536]{3,2,1,0:T(8,128)} %dvar.5, f32[1,3,8,1536]{3,2,1,0:T(8,128)} %rvar.5, f32[1,3,8,1536]{3,2,1,0:T(8,128)} %hobs.5, f32[1,8,1536]{2,1,0:T(8,128)} %depth.1), custom_call_target="tpu_custom_call" | custom-call | flops 1425408 | bytes 1425408 | tf_op jit(solution)/shard_map/pallas_call | solution.py:303
  2.5 0.0 collective-permute-done
  2.5 4.5 %collective-permute-start.3 = (f32[4,8,1536]{2,1,0:T(8,128)S(1)}, f32[4,8,1536]{2,1,0:T(8,128)S(1)}, u32[]{:S(2)}, u32[]{:S(2)}) collective-permute-start(f32[4,8,1536]{2,1,0:T(8,128)S(1)} %get-tuple-element.19), channel_id=1, source_target_pairs={{0,4},{4,8},{8,12},{12,16},{16,20},{20,24},{24,28},{1,5},{5,9},{9,... | collective-permute-start | bytes 589832 | tf_op jit(solution)/shard_map/ppermute | solution.py:317
  7.0 4.1 %collective-permute-start.4 = (f32[1,8,1536]{2,1,0:T(8,128)S(1)}, f32[1,8,1536]{2,1,0:T(8,128)S(1)}, u32[]{:S(2)}, u32[]{:S(2)}) collective-permute-start(f32[1,8,1536]{2,1,0:T(8,128)S(1)} %collective-permute-done), channel_id=1, source_target_pairs={{0,7},{3,4},{4,11},{7,8},{8,15},{11,12},{12,19},{15,16},{16,23},{1... | collective-permute-start | bytes 147464 | tf_op jit(solution)/shard_map/ppermute | solution.py:342
  11.1 0.1 sine_multiply_fusion
  11.2 0.7 %collective-permute-start.2 = (f32[6,8,1536]{2,1,0:T(8,128)S(1)}, f32[6,8,1536]{2,1,0:T(8,128)S(1)}, u32[]{:S(2)}, u32[]{:S(2)}) collective-permute-start(f32[6,8,1536]{2,1,0:T(8,128)S(1)} %get-tuple-element.18.pair), channel_id=1, source_target_pairs={{1,2},{2,1},{5,6},{6,5},{9,10},{10,9},{13,14},{14,13},{17,18},{18,... | collective-permute-start | bytes 884744 | tf_op jit(solution)/shard_map/ppermute | solution.py:342
  11.9 0.1 collective-permute-start.1
  12.0 3.4 %collective-permute-start.6 = (f32[3,8,1536]{2,1,0:T(8,128)S(1)}, f32[3,8,1536]{2,1,0:T(8,128)S(1)}, u32[]{:S(2)}, u32[]{:S(2)}) collective-permute-start(f32[3,8,1536]{2,1,0:T(8,128)S(1)} %get-tuple-element.21), channel_id=1, source_target_pairs={{0,4},{4,8},{8,12},{12,16},{16,20},{20,24},{24,28},{1,5},{5,9},{9,... | collective-permute-start | bytes 442376 | tf_op jit(solution)/shard_map/ppermute | solution.py:317
  15.4 0.0 collective-permute-done.3.straight
  15.4 0.0 collective-permute-done.4
  15.4 0.3 collective-permute-start.5
  15.7 0.1 broadcast_select_fusion.spin
  15.8 1.0 %collective-permute-done.5.relayed = f32[2,8,1536]{2,1,0:T(8,128)S(1)} collective-permute-done((f32[2,8,1536]{2,1,0:T(8,128)S(1)}, f32[2,8,1536]{2,1,0:T(8,128)S(1)}, u32[]{:S(2)}, u32[]{:S(2)}) %collective-permute-start.5) | collective-permute-done | bytes 98336 | tf_op jit(solution)/shard_map/ppermute | solution.py:332
  16.8 0.0 collective-permute-done.2.pair_far
  16.8 0.1 iota.13.inside
  16.9 1.2 %shard_map.86 = (f32[3,8,1536]{2,1,0:T(8,128)S(1)}, f32[3,8,1536]{2,1,0:T(8,128)S(1)}) custom-call(f32[6,8,1536]{2,1,0:T(8,128)S(1)} %get-tuple-element.18.pair, f32[6,8,1536]{2,1,0:T(8,128)S(1)} %collective-permute-done.1.pair_near, f32[6,8,1536]{2,1,0:T(8,128)S(1)} %collective-permute-done.2.pair_far, f32[4,8,1536]{2,1,0:T(8,128)S(1)} %collective-permute-done.3.straight, ...), custom_call_target="tpu_custom_call" | custom-call | flops 1499136 | bytes 1499136 | tf_op jit(solution)/shard_map/pallas_call | solution.py:303
  18.1 0.3 collective-permute-start.8
  18.3 1.3 %collective-permute-start.9 = (f32[3,8,1536]{2,1,0:T(8,128)S(1)}, f32[3,8,1536]{2,1,0:T(8,128)S(1)}, u32[]{:S(2)}, u32[]{:S(2)}) collective-permute-start(f32[3,8,1536]{2,1,0:T(8,128)S(1)} %get-tuple-element.24), channel_id=1, source_target_pairs={{4,0},{8,4},{12,8},{16,12},{20,16},{24,20},{28,24},{5,1},{9,5},{13... | collective-permute-start | bytes 442376 | tf_op jit(solution)/shard_map/ppermute | solution.py:317
  19.6 0.7 %collective-permute-start.7 = (f32[3,8,1536]{2,1,0:T(8,128)S(1)}, f32[3,8,1536]{2,1,0:T(8,128)S(1)}, u32[]{:S(2)}, u32[]{:S(2)}) collective-permute-start(f32[3,8,1536]{2,1,0:T(8,128)S(1)} %get-tuple-element.22.state), channel_id=1, source_target_pairs={{1,2},{2,1},{5,6},{6,5},{9,10},{10,9},{13,14},{14,13},{17,18},{18,... | collective-permute-start | bytes 442376 | tf_op jit(solution)/shard_map/ppermute | solution.py:342
  20.3 1.2 %shard_map.88.tally = f32[4,8,128]{2,1,0:T(8,128)S(1)} custom-call(f32[6,8,1536]{2,1,0:T(8,128)S(1)} %get-tuple-element.18.pair, f32[6,8,1536]{2,1,0:T(8,128)S(1)} %collective-permute-done.1.pair_near, f32[6,8,1536]{2,1,0:T(8,128)S(1)} %collective-permute-done.2.pair_far, f32[4,8,1536]{2,1,0:T(8,128)S(1)} %collective-permute-done.3.straight, ...), custom_call_target="tpu_custom_call" | custom-call | flops 1515520 | bytes 1515520 | tf_op jit(solution)/shard_map/pallas_call | solution.py:303
  21.5 0.0 copy-start
  21.5 0.0 copy-start.1
  21.5 0.0 copy-start.2
  21.5 0.0 copy-start.3
  21.5 0.0 copy-start.4
  21.5 1.2 %shard_map.87.rest = f32[3,8,1536]{2,1,0:T(8,128)S(1)} custom-call(f32[3,8,1536]{2,1,0:T(8,128)S(1)} %get-tuple-element.22.state, f32[3,8,1536]{2,1,0:T(8,128)S(1)} %collective-permute-done.8.state_near, f32[4,8,1536]{2,1,0:T(8,128)S(1)} %collective-permute-done.3.straight, f32[2,8,1536]{2,1,0:T(8,128)S(1)} %collective-permute-done.5.relayed, ...), custom_call_target="tpu_custom_call" | custom-call | flops 761856 | bytes 761856 | tf_op jit(solution)/shard_map/pallas_call | solution.py:303
  22.7 3.6 %collective-permute-done.9.back = f32[3,8,1536]{2,1,0:T(8,128)S(1)} collective-permute-done((f32[3,8,1536]{2,1,0:T(8,128)S(1)}, f32[3,8,1536]{2,1,0:T(8,128)S(1)}, u32[]{:S(2)}, u32[]{:S(2)}) %collective-permute-start.9) | collective-permute-done | bytes 147488 | tf_op jit(solution)/shard_map/ppermute | solution.py:317
  26.3 0.2 shard_map.89
  26.5 0.3 shard_map.90
  26.8 13.7 %all_to_all.11 = f32[32,1,128]{2,1,0:T(1,128)S(1)} all-to-all(f32[32,1,128]{2,1,0:T(1,128)S(1)} %bitcast.5), channel_id=1, replica_groups=mesh['win'=8,'band'=2,'half'=2] {'win','band','half'}, dimensions={0} | all-to-all | bytes 32768 | tf_op jit(solution)/shard_map/all_to_all | solution.py:386
  40.5 1.3 %shard_map.91 = (f32[1,3,8,1536]{3,2,1,0:T(8,128)}, f32[1,3,8,1536]{3,2,1,0:T(8,128)}, f32[1,3,8,1536]{3,2,1,0:T(8,128)}) custom-call(f32[32,128]{1,0:T(8,128)S(1)} %bitcast.4, f32[1,3,8,1536]{3,2,1,0:T(8,128)S(1)} %copy-done, f32[1,3,8,1536]{3,2,1,0:T(8,128)S(1)} %copy-done.1, f32[1,3,8,1536]{3,2,1,0:T(8,128)S(1)} %copy-done.2, ...), custom_call_target="tpu_custom_call" | custom-call | flops 1343488 | bytes 1343488 | tf_op jit(solution)/shard_map/pallas_call | solution.py:303
  (12 shorter events, 0.0 us)
Async XLA Ops:
  0.6 1.8 %collective-permute-start = (f32[1,8,1536]{2,1,0:T(8,128)}, f32[1,8,1536]{2,1,0:T(8,128)S(1)}, u32[]{:S(2)}, u32[]{:S(2)}) collective-permute-start(f32[1,8,1536]{2,1,0:T(8,128)} %depth.1), channel_id=1, source_target_pairs={{0,1},{1,0},{2,3},{3,2},{4,5},{5,4},{6,7},{7,6},{8,9},{9,8},{10,11... | collective-permute-start | bytes 147464 | tf_op jit(solution)/shard_map/ppermute | solution.py:332
  2.5 12.9 %collective-permute-start.3 = (f32[4,8,1536]{2,1,0:T(8,128)S(1)}, f32[4,8,1536]{2,1,0:T(8,128)S(1)}, u32[]{:S(2)}, u32[]{:S(2)}) collective-permute-start(f32[4,8,1536]{2,1,0:T(8,128)S(1)} %get-tuple-element.19), channel_id=1, source_target_pairs={{0,4},{4,8},{8,12},{12,16},{16,20},{20,24},{24,28},{1,5},{5,9},{9,... | collective-permute-start | bytes 589832 | tf_op jit(solution)/shard_map/ppermute | solution.py:317
  7.0 8.4 %collective-permute-start.4 = (f32[1,8,1536]{2,1,0:T(8,128)S(1)}, f32[1,8,1536]{2,1,0:T(8,128)S(1)}, u32[]{:S(2)}, u32[]{:S(2)}) collective-permute-start(f32[1,8,1536]{2,1,0:T(8,128)S(1)} %collective-permute-done), channel_id=1, source_target_pairs={{0,7},{3,4},{4,11},{7,8},{8,15},{11,12},{12,19},{15,16},{16,23},{1... | collective-permute-start | bytes 147464 | tf_op jit(solution)/shard_map/ppermute | solution.py:342
  11.2 5.6 %collective-permute-start.2 = (f32[6,8,1536]{2,1,0:T(8,128)S(1)}, f32[6,8,1536]{2,1,0:T(8,128)S(1)}, u32[]{:S(2)}, u32[]{:S(2)}) collective-permute-start(f32[6,8,1536]{2,1,0:T(8,128)S(1)} %get-tuple-element.18.pair), channel_id=1, source_target_pairs={{1,2},{2,1},{5,6},{6,5},{9,10},{10,9},{13,14},{14,13},{17,18},{18,... | collective-permute-start | bytes 884744 | tf_op jit(solution)/shard_map/ppermute | solution.py:342
  11.9 4.9 %collective-permute-start.1 = (f32[6,8,1536]{2,1,0:T(8,128)S(1)}, f32[6,8,1536]{2,1,0:T(8,128)S(1)}, u32[]{:S(2)}, u32[]{:S(2)}) collective-permute-start(f32[6,8,1536]{2,1,0:T(8,128)S(1)} %get-tuple-element.18.pair), channel_id=1, source_target_pairs={{0,1},{1,0},{2,3},{3,2},{4,5},{5,4},{6,7},{7,6},{8,9},{9,8},{10,11... | collective-permute-start | bytes 884744 | tf_op jit(solution)/shard_map/ppermute | solution.py:332
  12.0 7.7 %collective-permute-start.6 = (f32[3,8,1536]{2,1,0:T(8,128)S(1)}, f32[3,8,1536]{2,1,0:T(8,128)S(1)}, u32[]{:S(2)}, u32[]{:S(2)}) collective-permute-start(f32[3,8,1536]{2,1,0:T(8,128)S(1)} %get-tuple-element.21), channel_id=1, source_target_pairs={{0,4},{4,8},{8,12},{12,16},{16,20},{20,24},{24,28},{1,5},{5,9},{9,... | collective-permute-start | bytes 442376 | tf_op jit(solution)/shard_map/ppermute | solution.py:317
  15.4 1.4 %collective-permute-start.5 = (f32[2,8,1536]{2,1,0:T(8,128)S(1)}, f32[2,8,1536]{2,1,0:T(8,128)S(1)}, u32[]{:S(2)}, u32[]{:S(2)}) collective-permute-start(f32[2,8,1536]{2,1,0:T(8,128)S(1)} %pad_maximum_fusion), channel_id=1, source_target_pairs={{0,1},{1,0},{2,3},{3,2},{4,5},{5,4},{6,7},{7,6},{8,9},{9,8},{10,11... | collective-permute-start | bytes 294920 | tf_op jit(solution)/shard_map/ppermute | solution.py:332
  18.1 3.5 %collective-permute-start.8 = (f32[3,8,1536]{2,1,0:T(8,128)S(1)}, f32[3,8,1536]{2,1,0:T(8,128)S(1)}, u32[]{:S(2)}, u32[]{:S(2)}) collective-permute-start(f32[3,8,1536]{2,1,0:T(8,128)S(1)} %get-tuple-element.22.state), channel_id=1, source_target_pairs={{0,1},{1,0},{2,3},{3,2},{4,5},{5,4},{6,7},{7,6},{8,9},{9,8},{10,11... | collective-permute-start | bytes 442376 | tf_op jit(solution)/shard_map/ppermute | solution.py:332
  18.3 7.9 %collective-permute-start.9 = (f32[3,8,1536]{2,1,0:T(8,128)S(1)}, f32[3,8,1536]{2,1,0:T(8,128)S(1)}, u32[]{:S(2)}, u32[]{:S(2)}) collective-permute-start(f32[3,8,1536]{2,1,0:T(8,128)S(1)} %get-tuple-element.24), channel_id=1, source_target_pairs={{4,0},{8,4},{12,8},{16,12},{20,16},{24,20},{28,24},{5,1},{9,5},{13... | collective-permute-start | bytes 442376 | tf_op jit(solution)/shard_map/ppermute | solution.py:317
  19.6 6.9 %collective-permute-start.7 = (f32[3,8,1536]{2,1,0:T(8,128)S(1)}, f32[3,8,1536]{2,1,0:T(8,128)S(1)}, u32[]{:S(2)}, u32[]{:S(2)}) collective-permute-start(f32[3,8,1536]{2,1,0:T(8,128)S(1)} %get-tuple-element.22.state), channel_id=1, source_target_pairs={{1,2},{2,1},{5,6},{6,5},{9,10},{10,9},{13,14},{14,13},{17,18},{18,... | collective-permute-start | bytes 442376 | tf_op jit(solution)/shard_map/ppermute | solution.py:342
  21.5 4.8 %copy-start = (f32[1,3,8,1536]{3,2,1,0:T(8,128)S(1)}, f32[1,3,8,1536]{3,2,1,0:T(8,128)}, u32[]{:S(2)}) copy-start(f32[1,3,8,1536]{3,2,1,0:T(8,128)} %p.5) | copy-start | bytes 442372
  21.5 4.8 %copy-start.1 = (f32[1,3,8,1536]{3,2,1,0:T(8,128)S(1)}, f32[1,3,8,1536]{3,2,1,0:T(8,128)}, u32[]{:S(2)}) copy-start(f32[1,3,8,1536]{3,2,1,0:T(8,128)} %m.5) | copy-start | bytes 442372
  21.5 4.8 %copy-start.2 = (f32[1,3,8,1536]{3,2,1,0:T(8,128)S(1)}, f32[1,3,8,1536]{3,2,1,0:T(8,128)}, u32[]{:S(2)}) copy-start(f32[1,3,8,1536]{3,2,1,0:T(8,128)} %dvar.5) | copy-start | bytes 442372
  21.5 4.8 %copy-start.3 = (f32[1,3,8,1536]{3,2,1,0:T(8,128)S(1)}, f32[1,3,8,1536]{3,2,1,0:T(8,128)}, u32[]{:S(2)}) copy-start(f32[1,3,8,1536]{3,2,1,0:T(8,128)} %rvar.5) | copy-start | bytes 442372
  21.5 4.8 %copy-start.4 = (f32[1,3,8,1536]{3,2,1,0:T(8,128)S(1)}, f32[1,3,8,1536]{3,2,1,0:T(8,128)}, u32[]{:S(2)}) copy-start(f32[1,3,8,1536]{3,2,1,0:T(8,128)} %hobs.5) | copy-start | bytes 442372
